TPU v7x, 512 devices: a whole 4x8x8 slice. The times are simulated.
512 devices in a mesh: seq: 128 (over y, z, core), fsdp: 4 (over x).
Axes of the slice: x: 4, y: 8, z: 8, core: 2. Of those that a mesh axis runs over, the one named last changes fastest.
Arguments:
- tokens: bfloat16 [4, 16384, 2048], P('fsdp', 'seq'), may hold values from -14 to 14
- w_qkv: bfloat16 [2048, 3, 1024], P(None, None, 'fsdp'), may hold values from -0.125 to 0.125
- w_feature: bfloat16 [8, 128, 16], replicated, may hold values from -2 to 2
- norm_gain: float32 [1024], replicated, may hold values from 0.5 to 1.5
- log_decay: float32 [4, 8, 16384], P('fsdp', None, 'seq'), may hold values from -1.5 to 0
- pattern: int32 [4, 256, 3], P('fsdp', 'seq'), may hold values from 1 to 255, as said below
Outputs:
- mixed: bfloat16 [4, 16384, 1024], P('fsdp', 'seq')
Inputs may be any that keep to these rules, and one draw needn't show every extreme that they name: `pattern`: the 3 blocks of query block b are distinct, none is among the first 1 block or equal to b - 1, b or b + 1, and each lies in a segment at most 3 segments from b's segment; the first lies exactly 3 segments later where that segment exists, else 3 segments earlier.
All inputs are finite; a program needn't handle non-finite values.
Results may differ from a plain program's by a relative error of at most 0.0097.
The roundings to bfloat16 on the way count: a program that leaves them out, or rounds other values in their place, can miss the bound.
Values may be sent and summed in bfloat16 or wider, within the bound.
No kernel may reach another device: no remote copies, remote signals or barrier semaphores. Data moves between devices by JAX's collectives and lax.ppermute only.
A program may use at most 64 MiB of HBM per device.

v0:
```python
import jax
import jax.numpy as jnp
from jax import lax
from jax.sharding import PartitionSpec as P

HALF_HEADS = 8
DH = 128
F = 16
HD = 1024
BS = 64
G = 1
R = 3
RD = 3
TOK_DEV = 128
NB_DEV = 2


epsilon = 1e-06
masked_score = -1e30


def from_behind(value, axis, steps):
    count = lax.axis_size(axis)
    initial, last = (max(0, -steps), min(count, count - steps))
    return lax.ppermute(value, axis, [(source, source + steps) for source in range(initial, last)])


def spread(array, axis, root):
    mine = lax.axis_index(axis) == root
    return lax.psum(jnp.where(mine, array, jnp.zeros_like(array)), axis)


def entering(value, axis, join, neutral):
    count, mine = (lax.axis_size(axis), lax.axis_index(axis))
    pieces = jax.tree.map(lambda part: lax.all_gather(part, axis), value)
    running = jax.tree.map(
        lambda part, zero: jnp.full_like(part, 0) + jnp.asarray(zero, part.dtype), value, neutral
    )

    def lap(position, running):
        longer = join(running, jax.tree.map(lambda part: part[position], pieces))
        return jax.tree.map(lambda new, old: jnp.where(position < mine, new, old), longer, running)

    return lax.fori_loop(0, count - 1, lap, running)


def feature_map(projected_head, w_feature):
    logits = jnp.einsum(
        "thd,hdf->htf", projected_head, w_feature, preferred_element_type=jnp.float32
    )
    return jax.nn.softmax(logits, axis=-1).astype(jnp.bfloat16)


def combine_states(earlier, following):
    return (earlier[0] * following[0], following[0][:, None, None] * earlier[1] + following[1])


def neighbour_piece(pair_rows, offset):
    return from_behind(pair_rows, "seq", -offset)


def per_device(tokens, w_qkv, w_feature, norm_gain, log_decay, pattern):
    projected = jnp.einsum(
        "btd,dkc->btkc",
        tokens,
        lax.all_gather(w_qkv, "fsdp", axis=2, tiled=True),
        preferred_element_type=jnp.float32,
    ).astype(jnp.bfloat16)
    queries = projected[0, :, 0].reshape(TOK_DEV, HALF_HEADS, DH)
    key_rows = projected[0, :, 1].reshape(TOK_DEV, HALF_HEADS, DH)
    values = projected[0, :, 2].reshape(TOK_DEV, HALF_HEADS, DH)
    pair_rows = projected[:, :, 1:3].reshape(1, TOK_DEV, 2 * HD)
    pieces = []
    for offset in range(-RD, RD + 1):
        if offset == 0:
            pieces.append(pair_rows)
        else:
            pieces.append(neighbour_piece(pair_rows, offset))
    region = jnp.concatenate(pieces, axis=1)
    global_rows = spread(pair_rows[0, : G * BS], "seq", 0)
    phi_query = feature_map(queries, w_feature)
    phi_key = feature_map(key_rows, w_feature)
    log_steps = log_decay[0]
    cumulative = jnp.cumsum(log_steps, axis=1)
    final_log = cumulative[:, -1:]
    weighted_key = (
        jnp.exp(final_log - cumulative)[:, :, None] * phi_key.astype(jnp.float32)
    ).astype(jnp.bfloat16)
    local_state = jnp.einsum(
        "htf,thd->hfd", weighted_key, values, preferred_element_type=jnp.float32
    )
    identity = (jnp.ones((HALF_HEADS,), jnp.float32), jnp.zeros((HALF_HEADS, F, DH), jnp.float32))
    carried_pair = entering(
        (jnp.exp(final_log[:, 0]), local_state), "seq", combine_states, identity
    )
    carried = carried_pair[1]
    scores = jnp.einsum("htf,hsf->hts", phi_query, phi_key, preferred_element_type=jnp.float32)
    log_gap = cumulative[:, :, None] - cumulative[:, None, :]
    causal = jnp.arange(TOK_DEV)[:, None] >= jnp.arange(TOK_DEV)[None, :]
    decay_matrix = jnp.where(causal[None], jnp.exp(jnp.minimum(log_gap, 0.0)), 0.0)
    mixing = (scores * decay_matrix).astype(jnp.bfloat16)
    local_term = jnp.einsum("hts,shd->thd", mixing, values, preferred_element_type=jnp.float32)
    carried_term = jnp.einsum(
        "htf,hfd->thd", phi_query.astype(jnp.float32), carried, precision=lax.Precision.HIGHEST
    )
    carried_term = carried_term * jnp.exp(cumulative).T[:, :, None]
    linear = local_term + carried_term
    normed = linear * lax.rsqrt(jnp.mean(linear * linear, axis=-1, keepdims=True) + epsilon)
    normed = normed * norm_gain.reshape(HALF_HEADS, DH)
    device = lax.axis_index("seq")
    block_total = lax.axis_size("seq") * NB_DEV
    window_blocks = region[0].reshape((2 * RD + 1) * NB_DEV, BS, 2 * HD)
    query_blocks = device * NB_DEV + jnp.arange(NB_DEV, dtype=jnp.int32)
    near_blocks = query_blocks[:, None] + jnp.arange(-1, 2, dtype=jnp.int32)[None, :]
    usable_near = (near_blocks >= G) & (near_blocks < block_total)
    chosen = jnp.concatenate([near_blocks, pattern[0]], axis=1) - (device - RD) * NB_DEV
    chosen = jnp.clip(chosen, 0, (2 * RD + 1) * NB_DEV - 1)
    usable = jnp.concatenate([usable_near, jnp.ones((NB_DEV, R), dtype=bool)], axis=1)
    usable_keys = jnp.repeat(usable, BS, axis=1)
    picked = jnp.take(window_blocks, chosen, axis=0).reshape(
        NB_DEV, (3 + R) * BS, 2, HALF_HEADS, DH
    )
    global_split = global_rows.reshape(G * BS, 2, HALF_HEADS, DH)
    query_rows = queries.reshape(NB_DEV, BS, HALF_HEADS, DH)
    score_scale = DH ** (-0.5)
    near_scores = (
        jnp.einsum(
            "nqhd,nkhd->nhqk", query_rows, picked[:, :, 0], preferred_element_type=jnp.float32
        )
        * score_scale
    )
    near_scores = jnp.where(usable_keys[:, None, None, :], near_scores, masked_score)
    far_scores = (
        jnp.einsum(
            "nqhd,khd->nhqk", query_rows, global_split[:, 0], preferred_element_type=jnp.float32
        )
        * score_scale
    )
    scores_all = jnp.concatenate([near_scores, far_scores], axis=-1)
    highest = jnp.max(scores_all, axis=-1, keepdims=True)
    exponent = jnp.exp(scores_all - highest)
    denominator = jnp.sum(exponent, axis=-1, keepdims=True)
    soft_weights = (exponent / denominator).astype(jnp.bfloat16)
    near_count = (3 + R) * BS
    sparse = jnp.einsum(
        "nhqk,nkhd->nqhd",
        soft_weights[..., :near_count],
        picked[:, :, 1],
        preferred_element_type=jnp.float32,
    )
    sparse = sparse + jnp.einsum(
        "nhqk,khd->nqhd",
        soft_weights[..., near_count:],
        global_split[:, 1],
        preferred_element_type=jnp.float32,
    )
    sparse = sparse.reshape(TOK_DEV, HALF_HEADS, DH)
    return (normed + sparse).astype(jnp.bfloat16).reshape(1, TOK_DEV, HD)


def solution(mesh):
    placed = (
        P("fsdp", "seq", None),
        P(None, None, "fsdp"),
        P(),
        P(),
        P("fsdp", None, "seq"),
        P("fsdp", "seq", None),
    )
    return jax.shard_map(
        per_device, mesh=mesh, in_specs=placed, out_specs=P("fsdp", "seq", None), check_vma=False
    )
```

profile of v0, /device:TPU:1, one launch (start us, length us, event | category | flops | bytes accessed | tf_op | source)
XLA Modules:
  0.0 615.2 jit_solution(8857086100503208488)
XLA Ops:
  7.9 133.8 %all-gather.5.cloned.1.call-done = bf16[2048,3,1024]{2,0,1:T(8,128)(2,1)} async-done(((bf16[2048,3,256]{2,0,1:T(8,128)(2,1)}), bf16[2048,3,1024]{2,0,1:T(8,128)(2,1)}) %all-gather.5.cloned.1.call-update) | async-done | bytes 12582928 | tf_op jit(solution)/shard_map/all_gather | solution.py:66
  141.6 6.4 %fusion.7 = bf16[1,128,3,1024]{3,1,2,0:T(8,128)(2,1)S(1)} fusion(bf16[2048,3,1024]{2,0,1:T(8,128)(2,1)} %all-gather.5.cloned.1.call-done, bf16[1,128,2048]{2,1,0:T(8,128)(2,1)S(1)} %copy-done), kind=kOutput, calls=%fused_computation.17 | convolution fusion | flops 1611005952 | bytes 13893632 | tf_op jit(solution)/shard_map/btd,dkc->btkc/dot_general | solution.py:63
  152.1 1.3 dynamic-slice
  154.3 249.7 %all-reduce.1 = f32[1024]{0:T(1024)S(1)} all-reduce(f32[1024]{0:T(1024)S(1)} %dynamic-update-slice), channel_id=2, replica_groups=mesh['seq'=128,'fsdp'=4] {'seq'}, use_global_device_ids=true, to_apply=%add.1 | all-reduce | flops 1024 | bytes 8192
  404.7 2.1 collective-permute-start
  406.8 2.1 collective-permute-start.1
  408.9 1.9 collective-permute-start.2
  410.9 6.2 %collective-permute-start.3 = (bf16[1,128,2048]{1,2,0:T(8,128)(2,1)S(1)}, bf16[1,128,2048]{1,2,0:T(8,128)(2,1)S(1)}, u32[]{:S(2)}, u32[]{:S(2)}) collective-permute-start(bf16[1,128,2048]{1,2,0:T(8,128)(2,1)S(1)} %bitcast.122), channel_id=1, source_target_pairs={{4,0},{8,4},{12,8},{16,12},{20,16},{24,20},{28,24},{32,28},{36,32}... | collective-permute-start | bytes 1572872 | tf_op jit(solution)/shard_map/ppermute | solution.py:25
  417.1 1.3 collective-permute-start.4
  419.0 1.1 fusion.37
  420.4 1.3 collective-permute-start.5
  421.7 1.9 constant_dynamic-update-slice_fusion.6
  423.6 1.1 collective-permute-done.1
  424.7 1.9 constant_dynamic-update-slice_fusion.5
  426.6 8.0 %collective-permute-done.2 = bf16[1,128,2048]{1,2,0:T(8,128)(2,1)} collective-permute-done((bf16[1,128,2048]{1,2,0:T(8,128)(2,1)S(1)}, bf16[1,128,2048]{1,2,0:T(8,128)(2,1)}, u32[]{:S(2)}, u32[]{:S(2)}) %collective-permute-start.2) | collective-permute-done | bytes 524320 | tf_op jit(solution)/shard_map/ppermute | solution.py:25
  434.6 1.9 constant_dynamic-update-slice_fusion.4
  437.4 1.0 constant_dynamic-update-slice_fusion.2
  439.3 5.4 collective-permute-done.5
  445.5 6.2 %copy.54 = bf16[1,896,2048]{2,1,0:T(8,128)(2,1)} copy(bf16[1,896,2048]{1,2,0:T(8,128)(2,1)} %constant_dynamic-update-slice_fusion) | data formatting | bytes 7340032 | tf_op jit(solution)/shard_map/concatenate | solution.py:79
  451.7 4.6 gather_fusion
  456.4 3.0 copy.70
  463.5 20.4 %all-gather.7.cloned.1.call-done = f32[1024,16,128]{2,1,0:T(8,128)} async-done(((f32[8,16,128]{2,1,0:T(8,128)}), f32[1024,16,128]{2,1,0:T(8,128)}) %all-gather.7.cloned.1.call-update) | async-done | bytes 8388624 | tf_op jit(solution)/shard_map/all_gather | solution.py:35
  484.0 122.4 %while.14 = (s32[]{:T(128)}, f32[8,16,128]{2,1,0:T(8,128)S(1)}, s32[]{:T(128)}, f32[128,8]{1,0:T(8,128)S(1)}, f32[128,8,16,128]{3,2,1,0:T(8,128)}, /*index=5*/s32[]{:T(128)}, s32[]{:T(128)}) while((s32[]{:T(128)}, f32[8,16,128]{2,1,0:T(8,128)S(1)}, s32[]{:T(128)}, f32[128,8]{1,0:T(8,128)S(1)}, f32[128,8,16,128]{3,2,1,0:T(8,128)}, ...), condition=%wide.region_6.7_spmd.clone, body=%wide.region_5.6_spmd.clone.sunk | while | flops 65540 | bytes 196809 | solution.py:44
  484.9 0.9 fusion.58
  485.9 0.9 fusion.58
  486.8 0.9 fusion.58
  487.8 0.9 fusion.58
  489.7 0.9 fusion.58
  491.7 0.9 fusion.58
  492.6 0.9 fusion.58
  493.6 0.9 fusion.58
  494.6 0.9 fusion.58
  495.5 0.9 fusion.58
  496.5 0.9 fusion.58
  497.5 0.9 fusion.58
  498.4 0.9 fusion.58
  499.4 0.9 fusion.58
  500.3 0.9 fusion.58
  501.3 0.9 fusion.58
  502.3 0.9 fusion.58
  503.2 0.9 fusion.58
  504.2 0.9 fusion.58
  505.2 0.9 fusion.58
  506.1 0.9 fusion.58
  508.1 0.9 fusion.58
  510.0 0.9 fusion.58
  511.0 0.9 fusion.58
  511.9 0.9 fusion.58
  512.9 0.9 fusion.58
  513.8 0.9 fusion.58
  514.8 0.9 fusion.58
  515.8 0.9 fusion.58
  516.7 0.9 fusion.58
  517.7 0.9 fusion.58
  518.7 0.9 fusion.58
  519.6 0.9 fusion.58
  520.6 0.9 fusion.58
  521.6 0.9 fusion.58
  522.5 0.9 fusion.58
  523.5 0.9 fusion.58
  524.5 0.9 fusion.58
  526.4 0.9 fusion.58
  528.3 0.9 fusion.58
  529.3 0.9 fusion.58
  (301 shorter events, 96.6 us)
Async XLA Ops:
  6.5 135.1 %copy-start = (bf16[1,128,2048]{2,1,0:T(8,128)(2,1)S(1)}, bf16[1,128,2048]{2,1,0:T(8,128)(2,1)}, u32[]{:S(2)}) copy-start(bf16[1,128,2048]{2,1,0:T(8,128)(2,1)} %param.8) | copy-start | bytes 1572868
  6.5 0.8 copy-start.6
  6.5 135.1 %all-gather.5.cloned.1.call-start = ((), (), s32[]{:S(2)}) async-start(), calls=%async_computation | async-start | bytes 15728640 | tf_op jit(solution)/shard_map/all_gather | solution.py:66
  7.3 411.7 %all-reduce.4.cloned.1.call-start = ((), (), s32[]{:S(2)}) async-start(), calls=%async_computation.1 | async-start | bytes 524288 | tf_op jit(solution)/shard_map/psum | solution.py:30
  148.0 1.5 copy-start.7
  148.1 2.8 copy-start.5
  149.4 334.5 %all-gather.7.cloned.1.call-start = ((), (), s32[]{:S(2)}) async-start(), calls=%async_computation.2 | async-start | bytes 8454144 | tf_op jit(solution)/shard_map/all_gather | solution.py:35
  149.7 268.6 %copy-start.8 = (f32[8,128,16]{1,2,0:T(8,128)}, f32[8,128,16]{1,2,0:T(8,128)S(1)}, u32[]{:S(2)}) copy-start(f32[8,128,16]{1,2,0:T(8,128)S(1)} %fusion.26) | copy-start | bytes 196612
  149.8 0.9 copy-start.10
  404.7 15.7 %collective-permute-start = (bf16[1,128,2048]{1,2,0:T(8,128)(2,1)S(1)}, bf16[1,128,2048]{1,2,0:T(8,128)(2,1)}, u32[]{:S(2)}, u32[]{:S(2)}) collective-permute-start(bf16[1,128,2048]{1,2,0:T(8,128)(2,1)S(1)} %bitcast.119), channel_id=1, source_target_pairs={{0,12},{4,16},{8,20},{12,24},{16,28},{20,32},{24,36},{28,40},{32,4... | collective-permute-start | bytes 1572872 | tf_op jit(solution)/shard_map/ppermute | solution.py:25
  406.8 17.9 %collective-permute-start.1 = (bf16[1,128,2048]{1,2,0:T(8,128)(2,1)S(1)}, bf16[1,128,2048]{1,2,0:T(8,128)(2,1)}, u32[]{:S(2)}, u32[]{:S(2)}) collective-permute-start(bf16[1,128,2048]{1,2,0:T(8,128)(2,1)S(1)} %bitcast.120), channel_id=1, source_target_pairs={{0,8},{4,12},{8,16},{12,20},{16,24},{20,28},{24,32},{28,36},{32,40... | collective-permute-start | bytes 1572872 | tf_op jit(solution)/shard_map/ppermute | solution.py:25
  408.9 25.7 %collective-permute-start.2 = (bf16[1,128,2048]{1,2,0:T(8,128)(2,1)S(1)}, bf16[1,128,2048]{1,2,0:T(8,128)(2,1)}, u32[]{:S(2)}, u32[]{:S(2)}) collective-permute-start(bf16[1,128,2048]{1,2,0:T(8,128)(2,1)S(1)} %bitcast.121), channel_id=1, source_target_pairs={{0,4},{4,8},{8,12},{12,16},{16,20},{20,24},{24,28},{28,32},{32,36}... | collective-permute-start | bytes 1572872 | tf_op jit(solution)/shard_map/ppermute | solution.py:25
  410.9 26.5 %collective-permute-start.3 = (bf16[1,128,2048]{1,2,0:T(8,128)(2,1)S(1)}, bf16[1,128,2048]{1,2,0:T(8,128)(2,1)S(1)}, u32[]{:S(2)}, u32[]{:S(2)}) collective-permute-start(bf16[1,128,2048]{1,2,0:T(8,128)(2,1)S(1)} %bitcast.122), channel_id=1, source_target_pairs={{4,0},{8,4},{12,8},{16,12},{20,16},{24,20},{28,24},{32,28},{36,32}... | collective-permute-start | bytes 1572872 | tf_op jit(solution)/shard_map/ppermute | solution.py:25
  417.1 21.3 %collective-permute-start.4 = (bf16[1,128,2048]{1,2,0:T(8,128)(2,1)S(1)}, bf16[1,128,2048]{1,2,0:T(8,128)(2,1)S(1)}, u32[]{:S(2)}, u32[]{:S(2)}) collective-permute-start(bf16[1,128,2048]{1,2,0:T(8,128)(2,1)S(1)} %bitcast.123), channel_id=1, source_target_pairs={{8,0},{12,4},{16,8},{20,12},{24,16},{28,20},{32,24},{36,28},{40,32... | collective-permute-start | bytes 1572872 | tf_op jit(solution)/shard_map/ppermute | solution.py:25
  420.4 24.3 %collective-permute-start.5 = (bf16[1,128,2048]{1,2,0:T(8,128)(2,1)S(1)}, bf16[1,128,2048]{1,2,0:T(8,128)(2,1)S(1)}, u32[]{:S(2)}, u32[]{:S(2)}) collective-permute-start(bf16[1,128,2048]{1,2,0:T(8,128)(2,1)S(1)} %bitcast.124), channel_id=1, source_target_pairs={{12,0},{16,4},{20,8},{24,12},{28,16},{32,20},{36,24},{40,28},{44,3... | collective-permute-start | bytes 1572872 | tf_op jit(solution)/shard_map/ppermute | solution.py:25
  459.4 0.8 copy-start.3
  461.8 1.0 copy-start.1
  462.8 144.2 %copy-start.2 = (pred[128,128]{1,0:T(8,128)(4,1)S(1)}, pred[128,128]{1,0:T(8,128)(4,1)}, u32[]{:S(2)}) copy-start(pred[128,128]{1,0:T(8,128)(4,1)} %iota_compare_fusion) | copy-start | bytes 49156
  462.8 144.2 %copy-start.9 = (f32[8,128,16]{1,2,0:T(8,128)S(1)}, f32[8,128,16]{1,2,0:T(8,128)}, u32[]{:S(2)}) copy-start(f32[8,128,16]{1,2,0:T(8,128)} %copy-done.8) | copy-start | bytes 196612
  462.8 144.2 %copy-start.11 = (f32[8,128]{1,0:T(8,128)S(1)}, f32[8,128]{1,0:T(8,128)}, u32[]{:S(2)}) copy-start(f32[8,128]{1,0:T(8,128)} %copy-done.10) | copy-start | bytes 12292
  463.0 144.6 %copy-start.4 = (f32[1024]{0:T(1024)S(1)}, f32[1024]{0:T(1024)}, u32[]{:S(2)}) copy-start(f32[1024]{0:T(1024)} %param.11) | copy-start | bytes 12292
Sparse Core Ops, SparseCore 0:
  9.5 132.1 all-gather.4
  149.5 190.8 all-reduce.3
  343.6 140.3 all-gather.6
where the time goes:
time: 622 us; the launch traced here: 615 us
  blocking collectives  250 us (40%)
  waiting for transfers between devices  169 us (27%)
  other arithmetic  121 us (19%)
  local copies, waits for them, and re-layouts  30.3 us (5%)
  starting transfers between devices  15 us (2%)
  between operations  14.2 us (2%)
  matrix products  11.5 us (2%)
    unnamed x1, blocking collectives  250 us
    all_gather x1, waiting for transfers between devices, per_device(): lax.all_gather(w_qkv, 'fsdp', axis=2, tiled=True)  134 us
    select_n x127, other arithmetic, lap(): jnp.where(position < mine, new, old)  117 us
    all_gather x1, waiting for transfers between devices, entering(): pieces = jax.tree.map(lambda part: lax.all_gather(part, axis), value)  20.4 us
    ppermute x6, starting transfers between devices, from_behind(): lax.ppermute(value, axis, [(source, source + steps) for source in range(i...  14.9 us
    ppermute x6, waiting for transfers between devices, from_behind(): lax.ppermute(value, axis, [(source, source + steps) for source in range(i...  14.5 us
    unnamed x38, local copies, waits for them, and re-layouts  13.4 us
  transfers between devices with their start and end apart: 9, of which 5 were waited for; matrix products, arithmetic and copies ran while one was open for 6% of the time, Pallas kernels for 0%

commit v1 on v0

v1 whole, which is shorter than its diff:
```python
import jax
import jax.numpy as jnp
from jax import lax
from jax.experimental import pallas as pl
from jax.experimental.pallas import tpu as pltpu
from jax.sharding import PartitionSpec as P

HALF_HEADS = 8
DH = 128
F = 16
HD = 1024
D = 2048
BS = 64
R = 3
TOK = 128
NB = 2
DOCS = 4
EPS = 1e-06
MASKED = -1e30
CHIPS = 64
ROWS = 208
BF = jnp.bfloat16
F32 = jnp.float32
HIGH = lax.Precision.HIGHEST


def nt(a, b):
    return lax.dot_general(a, b, (((1,), (1,)), ((), ())), preferred_element_type=F32)


def mm(a, b, precision=None):
    return jnp.dot(a, b, preferred_element_type=F32, precision=precision)


def softmax0(logits):
    top = jnp.max(logits, axis=0, keepdims=True)
    e = jnp.exp(logits - top)
    return e / jnp.sum(e, axis=0, keepdims=True)


def split2(a):
    hi = a.astype(BF)
    return hi, (a - hi.astype(F32)).astype(BF)


def split3(a):
    hi, rest = a.astype(BF), None
    rest = a - hi.astype(F32)
    mid = rest.astype(BF)
    return hi, mid, (rest - mid.astype(F32)).astype(BF)


def cumulative_of(steps):
    row = lax.broadcasted_iota(jnp.int32, (TOK, TOK), 0)
    col = lax.broadcasted_iota(jnp.int32, (TOK, TOK), 1)
    return mm(steps, jnp.where(row <= col, 1.0, 0.0).astype(F32), HIGH)


def project_kernel(scal, t0, ta, tb, td1, td2, w, kv_own, kv_other, kvq_other, q_own, rows):
    c, x = scal[0], scal[1]
    rows[0:128] = t0[...]
    rows[128:256] = ta[...]
    rows[256:320] = td1[...]
    rows[320:384] = td2[...]
    rows[384:512] = tb[...]
    parts = [mm(rows[...], w[k]).astype(BF) for k in range(3)]
    first = c == 0
    for r in range(DOCS):
        n = lax.rem(x - r + DOCS, DOCS)
        own, other = [], []
        for k in range(3):
            lo = parts[k][r * TOK : (r + 1) * TOK, :DH]
            hi = parts[k][r * TOK : (r + 1) * TOK, DH:]
            own.append(jnp.where(first, lo, hi))
            other.append(jnp.where(first, hi, lo))
        q_own[n] = own[0]
        kv_own[n, :, :DH] = own[1]
        kv_own[n, :, DH:] = own[2]
        kv_other[n, :, :DH] = other[1]
        kv_other[n, :, DH:] = other[2]
        kvq_other[n, :, :DH] = other[1]
        kvq_other[n, :, DH : 2 * DH] = other[2]
        kvq_other[n, :, 2 * DH :] = other[0]


def states_kernel(scal, kv_own, kvq_mate, steps, wft, out, state0):
    c, h = scal[0], scal[5]
    first = c == 0
    cum = cumulative_of(steps[...])
    feature = wft[h]
    states, decays = [], []
    for n in range(DOCS):
        own = kv_own[n]
        mate = kvq_mate[n, :, : 2 * DH]
        segs = (jnp.where(first, own, mate), jnp.where(first, mate, own))
        local = []
        for s in range(2):
            phi = softmax0(nt(feature, segs[s][:, :DH])).astype(BF).astype(F32)
            line = cum[2 * n + s : 2 * n + s + 1]
            final = line[:, TOK - 1 :]
            weighted = (jnp.exp(final - line) * phi).astype(BF)
            local.append(mm(weighted, segs[s][:, DH:]))
        last0 = jnp.broadcast_to(cum[2 * n : 2 * n + 1, TOK - 1 :], (1, TOK))
        last1 = jnp.broadcast_to(cum[2 * n + 1 : 2 * n + 2, TOK - 1 :], (1, TOK))
        state0[n] = local[0]
        states.append(jnp.exp(last1) * local[0] + local[1])
        decays.append(last0 + last1)
        for half in range(2):
            out[2 * n + half, 144:176] = segs[0][32 * half : 32 * half + 32, :DH]
            out[2 * n + half, 176:208] = segs[0][32 * half : 32 * half + 32, DH:]
    put_states(out, jnp.concatenate(states, axis=0), decays)


def put_states(out, state, decays):
    hi, lo = split2(state)
    three = split3(jnp.concatenate(decays, axis=0))
    tail = jnp.concatenate(
        [p.astype(F32) for p in three] + [jnp.zeros((4, TOK), F32)], axis=0
    ).astype(BF)
    for peer in range(8):
        out[peer, 0:64] = hi
        out[peer, 64:128] = lo
        out[peer, 128:144] = tail


def get_states(got, peer):
    state = got[peer, 0:64].astype(F32) + got[peer, 64:128].astype(F32)
    tail = got[peer, 128:144].astype(F32)
    decay = (tail[0:4] + tail[4:8]) + tail[8:12]
    wide = jnp.concatenate(
        [jnp.broadcast_to(decay[n : n + 1], (F, TOK)) for n in range(DOCS)], axis=0
    )
    return state, decay, wide


def row_kernel(scal, got, out, inner, outer):
    z = scal[3]
    total = jnp.zeros((64, TOK), F32)
    before = jnp.zeros((64, TOK), F32)
    decays = jnp.zeros((4, TOK), F32)
    reach = jnp.zeros((64, TOK), F32)
    for peer in range(8):
        state, decay, wide = get_states(got, peer)
        grow = jnp.exp(wide)
        use = peer < z
        before = jnp.where(use, before * grow + state, before)
        reach = jnp.where(use, reach + wide, reach)
        total = total * grow + state
        decays = decays + decay
    inner[...] = before
    outer[...] = jnp.exp(reach)
    put_states(out, total, [decays])
    for peer in range(8):
        out[peer, 144:208] = got[0, 144:208]


def attend_kernel(
    scal, pat, kv_own, q_own, kvq_mate, zps, zpx, zms, zmx, tws, twx, glob, got, inner, outer,
    state0, steps, wft, gain, out, win, qs,
):
    c, q, y, h = scal[0], scal[2], scal[4], scal[5]
    mate = 1 - c
    for n in range(DOCS):
        win[n, 3 + c] = kv_own[n]
        win[n, 3 + mate] = kvq_mate[n, :, : 2 * DH]
        win[n, 1 + c] = zps[n]
        win[n, 1 + mate] = zpx[n]
        win[n, 5 + c] = zms[n]
        win[n, 5 + mate] = zmx[n]
        win[n, 7 * mate] = tws[n]
        win[n, 7 * c] = twx[n]
        qs[n, c] = q_own[n]
        qs[n, mate] = kvq_mate[n, :, 2 * DH :]

    before = jnp.zeros((64, TOK), F32)
    for peer in range(8):
        state, _, wide = get_states(got, peer)
        before = jnp.where(peer < y, before * jnp.exp(wide) + state, before)
    entering = inner[...] + outer[...] * before

    cum = cumulative_of(steps[...])
    cum_t = cum.T
    feature = wft[h]
    row = lax.broadcasted_iota(jnp.int32, (TOK, TOK), 0)
    col = lax.broadcasted_iota(jnp.int32, (TOK, TOK), 1)
    causal = row >= col
    gains = gain[h]
    lane = lax.broadcasted_iota(jnp.int32, (1, 7 * BS), 1)
    scale = DH ** (-0.5)
    for n in range(DOCS):
        carried = entering[F * n : F * n + F]
        for s in range(2):
            line = cum[2 * n + s : 2 * n + s + 1]
            column = cum_t[:, 2 * n + s : 2 * n + s + 1]
            queries = qs[n, s]
            keys = win[n, 3 + s, :, :DH]
            values = win[n, 3 + s, :, DH:]
            phi_q = softmax0(nt(feature, queries)).astype(BF).astype(F32).T
            phi_k = softmax0(nt(feature, keys)).astype(BF)
            decay = jnp.where(causal, jnp.exp(jnp.minimum(column - line, 0.0)), 0.0)
            mixing = (mm(phi_q.astype(BF), phi_k) * decay).astype(BF)
            linear = mm(mixing, values) + mm(phi_q, carried, HIGH) * jnp.exp(column)
            carried = jnp.exp(line[:, TOK - 1 :]) * carried + state0[n]
            square = jnp.mean(linear * linear, axis=1, keepdims=True)
            normed = linear * lax.rsqrt(square + EPS) * gains
            for half in range(2):
                j = 2 * s + half
                block = 4 * q + j
                picks = [win[n, 3 + (j + d) // 2 if j + d >= 0 else 2, pl.ds(BS * ((j + d) % 2), BS)] for d in (-1, 0, 1)]
                for k in range(R):
                    place = pat[12 * n + 3 * j + k]
                    picks.append(
                        win[n, lax.div(place, 2), pl.ds(pl.multiple_of(BS * lax.rem(place, 2), BS), BS)]
                    )
                near = jnp.concatenate(picks, axis=0)
                gk = jnp.concatenate([glob[2 * n, 0:32], glob[2 * n + 1, 0:32]], axis=0)
                gv = jnp.concatenate([glob[2 * n, 32:64], glob[2 * n + 1, 32:64]], axis=0)
                all_k = jnp.concatenate([near[:, :DH], gk], axis=0)
                all_v = jnp.concatenate([near[:, DH:], gv], axis=0)
                scores = nt(queries[half * BS : half * BS + BS], all_k) * scale
                bad = (
                    ((lane < BS) & (block < 2))
                    | ((lane >= BS) & (lane < 2 * BS) & (block < 1))
                    | ((lane >= 2 * BS) & (lane < 3 * BS) & (block > 4 * CHIPS - 2))
                )
                scores = jnp.where(bad, MASKED, scores)
                top = jnp.max(scores, axis=1, keepdims=True)
                e = jnp.exp(scores - top)
                soft = (e / jnp.sum(e, axis=1, keepdims=True)).astype(BF)
                sparse = mm(soft, all_v)
                out[2 * n + s, half * BS : half * BS + BS] = (
                    normed[half * BS : half * BS + BS] + sparse
                ).astype(BF)


def call(kernel, outs, scratch, n_smem, *args):
    vmem = pl.BlockSpec(memory_space=pltpu.VMEM)
    smem = pl.BlockSpec(memory_space=pltpu.SMEM)
    return pl.pallas_call(
        kernel,
        out_shape=outs,
        in_specs=[smem] * n_smem + [vmem] * (len(args) - n_smem),
        out_specs=[vmem] * len(outs),
        scratch_shapes=scratch,
        compiler_params=pltpu.CompilerParams(vmem_limit_bytes=28 * 2**20),
    )(*args)


def shape(dims, dtype):
    return jax.ShapeDtypeStruct(dims, dtype)


def pairs(move):
    found = []
    for q in range(CHIPS):
        for c in range(2):
            to, core = move(q, c)
            if 0 <= to < CHIPS:
                found.append((2 * q + c, 2 * to + core))
    return found


XC = [[(2 * q + c) * 4 + x for x in range(4) for c in range(2)] for q in range(CHIPS)]
ZS = [[(8 * y + z) * 2 + c for z in range(8)] for y in range(8) for c in range(2)]
YS = [[(8 * y + z) * 2 + c for y in range(8)] for z in range(8) for c in range(2)]


def exchange(a, axis, groups):
    return lax.all_to_all(a, axis, 0, 0, tiled=True, axis_index_groups=groups)


def per_device(tokens, w_qkv, w_feature, norm_gain, log_decay, pattern):
    x = lax.axis_index("fsdp")
    s = lax.axis_index("seq")
    c, q = s % 2, s // 2
    z, y = q % 8, q // 8
    h = 2 * x + c
    scal = jnp.stack([c, x, q, z, y, h]).astype(jnp.int32)
    t0 = tokens[0]
    up = [(i, (i + 1) % 4) for i in range(4)]
    down = [(i, (i - 1) % 4) for i in range(4)]
    ta = lax.ppermute(t0, "fsdp", up)
    tb = lax.ppermute(t0, "fsdp", down)
    td1 = lax.ppermute(ta[:64], "fsdp", up)
    td2 = lax.ppermute(tb[64:], "fsdp", down)

    small = jnp.concatenate(
        [
            log_decay[0][:, None, :],
            jnp.broadcast_to(
                jnp.pad(pattern.reshape(1, 1, 6).astype(F32), ((0, 0), (0, 0), (0, 122))),
                (8, 1, TOK),
            ),
            jnp.zeros((8, 6, TOK), F32),
        ],
        axis=1,
    )
    got0 = exchange(small, ("seq", "fsdp"), XC)
    steps = got0[:, 0]
    pat = got0[:, 1, :6].astype(jnp.int32).reshape(48) - (4 * q - 6)
    pat = jnp.clip(pat, 0, 15).astype(jnp.int32)

    w3 = w_qkv.transpose(1, 0, 2)
    wft = w_feature.transpose(0, 2, 1)
    kv_own, kv_other, kvq_other, q_own = call(
        project_kernel,
        [
            shape((DOCS, TOK, 2 * DH), BF),
            shape((DOCS, TOK, 2 * DH), BF),
            shape((DOCS, TOK, 3 * DH), BF),
            shape((DOCS, TOK, DH), BF),
        ],
        [pltpu.VMEM((4 * TOK, D), BF)],
        1,
        scal, t0, ta, tb, td1, td2, w3,
    )
    kvq_mate = lax.ppermute(kvq_other, "seq", pairs(lambda q, c: (q, 1 - c)))
    zps = lax.ppermute(kv_own, "seq", pairs(lambda q, c: (q + 1, c)))
    zms = lax.ppermute(kv_own, "seq", pairs(lambda q, c: (q - 1, c)))
    zpx = lax.ppermute(kv_other, "seq", pairs(lambda q, c: (q + 1, 1 - c)))
    zmx = lax.ppermute(kv_other, "seq", pairs(lambda q, c: (q - 1, 1 - c)))
    tws = lax.ppermute(kv_own, "seq", pairs(lambda q, c: (q + 2, 1) if c else (q - 2, 0)))
    twx = lax.ppermute(kv_other, "seq", pairs(lambda q, c: (q + 2, 0) if c else (q - 2, 1)))

    send1, state0 = call(
        states_kernel,
        [shape((8, ROWS, TOK), BF), shape((DOCS, F, DH), F32)],
        [],
        1,
        scal, kv_own, kvq_mate, steps, wft,
    )
    got1 = exchange(send1, "seq", ZS)
    send2, inner, outer = call(
        row_kernel,
        [shape((8, ROWS, TOK), BF), shape((64, TOK), F32), shape((64, TOK), F32)],
        [],
        1,
        scal, got1,
    )
    got2 = exchange(send2, "seq", YS)
    glob = exchange(jnp.broadcast_to(got2[0, 144:208][None], (8, 64, TOK)), "seq", ZS)

    [out] = call(
        attend_kernel,
        [shape((8, TOK, DH), BF)],
        [pltpu.VMEM((DOCS, 8, TOK, 2 * DH), BF), pltpu.VMEM((DOCS, 2, TOK, DH), BF)],
        2,
        scal, pat, kv_own, q_own, kvq_mate, zps, zpx, zms, zmx, tws, twx, glob, got2, inner, outer,
        state0, steps, wft, norm_gain.reshape(HALF_HEADS, 1, DH),
    )
    mixed = exchange(out, ("seq", "fsdp"), XC)
    return mixed.transpose(1, 0, 2).reshape(1, TOK, HD)


def solution(mesh):
    placed = (
        P("fsdp", "seq", None),
        P(None, None, "fsdp"),
        P(),
        P(),
        P("fsdp", None, "seq"),
        P("fsdp", "seq", None),
    )
    return jax.shard_map(
        per_device, mesh=mesh, in_specs=placed, out_specs=P("fsdp", "seq", None), check_vma=False
    )
```

time: 622 us -> 139 us (0.22)
  blocking collectives: 250 us -> 42.1 us
  waiting for transfers between devices: 169 us -> 17.9 us
  other arithmetic: 121 us -> 0.1 us
  starting transfers between devices: 15 us -> 56.2 us
  local copies, waits for them, and re-layouts: 30.3 us -> 5.03 us
  Pallas kernels: 0 us -> 15.4 us
  between operations: 14.2 us -> 0.25 us
  matrix products: 11.5 us -> 0 us
    unnamed x1 -> x0, blocking collectives: 250 us -> none
    all_gather x2 -> x0, waiting for transfers between devices: 154 us -> none  [the longest x1 134 us: per_device(): lax.all_gather(w_qkv, 'fsdp', axis=2, tiled=True)]
    select_n x130 -> x0, other arithmetic: 118 us -> none  [the longest x127 117 us: lap(): jnp.where(position < mine, new, old)]
    all_to_all x0 -> x3, blocking collectives: none -> 42.1 us  [exchange(): return lax.all_to_all(a, axis, 0, 0, tiled=True, axis_index_groups=groups)]
    ppermute x6 -> x11, starting transfers between devices: 14.9 us -> 41.5 us  [the longest x1 6.45 us: per_device(): lax.ppermute(kv_own, 'seq', pairs(lambda q, c: (q + 2, 1) if c else (q -...]
    pallas_call x0 -> x4, Pallas kernels: none -> 15.4 us  [call(): pl.pallas_call(kernel, out_shape=outs, in_specs=[smem] * n_smem + [vmem]...]
    all_to_all x0 -> x2, starting transfers between devices: none -> 14.7 us  [exchange(): return lax.all_to_all(a, axis, 0, 0, tiled=True, axis_index_groups=groups)]
    unnamed x38 -> x12, local copies, waits for them, and re-layouts: 13.4 us -> 2.95 us
  transfers between devices with their start and end apart: 9 -> 13, of which waited for: 5 -> 6; matrix products, arithmetic and copies ran while one was open for 6% -> 1% of each run, Pallas kernels for 0% -> 0%
where the time goes in v1:
time: 139 us; the launch traced here: 137 us
  starting transfers between devices  56.2 us (40%)
  blocking collectives  42.1 us (30%)
  waiting for transfers between devices  17.9 us (13%)
  Pallas kernels  15.4 us (11%)
  local copies, waits for them, and re-layouts  5.03 us (4%)
    all_to_all x3, blocking collectives, exchange(): return lax.all_to_all(a, axis, 0, 0, tiled=True, axis_index_groups=groups)  42.1 us
    pallas_call x4, Pallas kernels, call(): pl.pallas_call(kernel, out_shape=outs, in_specs=[smem] * n_smem + [vmem]...  15.4 us
    all_to_all x2, starting transfers between devices, exchange(): return lax.all_to_all(a, axis, 0, 0, tiled=True, axis_index_groups=groups)  14.7 us
    ppermute x1, waiting for transfers between devices, per_device(): zmx = lax.ppermute(kv_other, 'seq', pairs(lambda q, c: (q - 1, 1 - c)))  6.71 us
    ppermute x1, starting transfers between devices, per_device(): lax.ppermute(kv_own, 'seq', pairs(lambda q, c: (q + 2, 1) if c else (q -...  6.45 us
    ppermute x1, starting transfers between devices, per_device(): kvq_mate = lax.ppermute(kvq_other, 'seq', pairs(lambda q, c: (q, 1 - c)))  6.18 us
    ppermute x1, starting transfers between devices, per_device(): td1 = lax.ppermute(ta[:64], 'fsdp', up)  5.97 us
    ppermute x1, waiting for transfers between devices, per_device(): ta = lax.ppermute(t0, 'fsdp', up)  4.84 us
  transfers between devices with their start and end apart: 13, of which 6 were waited for; matrix products, arithmetic and copies ran while one was open for 1% of the time, Pallas kernels for 0%

profile of v1, /device:TPU:1, one launch (start us, length us, event | category | flops | bytes accessed | tf_op | source)
XLA Modules:
  0.0 136.9 jit_solution(17792268890080994335)
XLA Ops:
  0.0 0.0 copy-start.5
  0.0 0.0 copy-start.4
  0.0 0.0 copy-start.2
  0.0 4.1 %collective-permute-start = (bf16[128,2048]{1,0:T(8,128)(2,1)}, bf16[128,2048]{1,0:T(8,128)(2,1)S(1)}, u32[]{:S(2)}, u32[]{:S(2)}) collective-permute-start(bf16[128,2048]{1,0:T(8,128)(2,1)} %bitcast.21), channel_id=1, source_target_pairs={{0,1},{1,2},{2,3},{3,0},{4,5},{5,6},{6,7},{7,4},{8,9},{9,10},{10,1... | collective-permute-start | bytes 1572872 | tf_op jit(solution)/shard_map/ppermute | solution.py:282
  4.1 3.2 %collective-permute-start.1 = (bf16[128,2048]{1,0:T(8,128)(2,1)}, bf16[128,2048]{1,0:T(8,128)(2,1)S(1)}, u32[]{:S(2)}, u32[]{:S(2)}) collective-permute-start(bf16[128,2048]{1,0:T(8,128)(2,1)} %bitcast.22), channel_id=1, source_target_pairs={{0,3},{1,0},{2,1},{3,2},{4,7},{5,4},{6,5},{7,6},{8,11},{9,8},{10,9... | collective-permute-start | bytes 1572872 | tf_op jit(solution)/shard_map/ppermute | solution.py:283
  7.3 4.8 %collective-permute-done.ta = bf16[128,2048]{1,0:T(8,128)(2,1)S(1)} collective-permute-done((bf16[128,2048]{1,0:T(8,128)(2,1)}, bf16[128,2048]{1,0:T(8,128)(2,1)S(1)}, u32[]{:S(2)}, u32[]{:S(2)}) %collective-permute-start) | collective-permute-done | bytes 524320 | tf_op jit(solution)/shard_map/ppermute | solution.py:282
  12.2 6.0 %collective-permute-start.2 = (bf16[64,2048]{1,0:T(8,128)(2,1)S(1)}, bf16[64,2048]{1,0:T(8,128)(2,1)S(1)}, u32[]{:S(2)}, u32[]{:S(2)}) collective-permute-start(bf16[64,2048]{1,0:T(8,128)(2,1)S(1)} %slice.21), channel_id=1, source_target_pairs={{0,1},{1,2},{2,3},{3,0},{4,5},{5,6},{6,7},{7,4},{8,9},{9,10},{10,1... | collective-permute-start | bytes 786440 | tf_op jit(solution)/shard_map/ppermute | solution.py:284
  18.1 0.0 collective-permute-done.1.tb
  18.2 4.1 %collective-permute-start.3 = (bf16[64,2048]{1,0:T(8,128)(2,1)S(1)}, bf16[64,2048]{1,0:T(8,128)(2,1)S(1)}, u32[]{:S(2)}, u32[]{:S(2)}) collective-permute-start(bf16[64,2048]{1,0:T(8,128)(2,1)S(1)} %slice.22), channel_id=1, source_target_pairs={{0,3},{1,0},{2,1},{3,2},{4,7},{5,4},{6,5},{7,6},{8,11},{9,8},{10,9... | collective-permute-start | bytes 786440 | tf_op jit(solution)/shard_map/ppermute | solution.py:285
  22.3 0.1 stack.27.scal
  22.4 1.6 %collective-permute-done.2.td1 = bf16[64,2048]{1,0:T(8,128)(2,1)S(1)} collective-permute-done((bf16[64,2048]{1,0:T(8,128)(2,1)S(1)}, bf16[64,2048]{1,0:T(8,128)(2,1)S(1)}, u32[]{:S(2)}, u32[]{:S(2)}) %collective-permute-start.2) | collective-permute-done | bytes 262176 | tf_op jit(solution)/shard_map/ppermute | solution.py:284
  24.0 2.2 %collective-permute-done.3.td2 = bf16[64,2048]{1,0:T(8,128)(2,1)S(1)} collective-permute-done((bf16[64,2048]{1,0:T(8,128)(2,1)S(1)}, bf16[64,2048]{1,0:T(8,128)(2,1)S(1)}, u32[]{:S(2)}, u32[]{:S(2)}) %collective-permute-start.3) | collective-permute-done | bytes 262176 | tf_op jit(solution)/shard_map/ppermute | solution.py:285
  26.2 0.0 copy-start
  26.2 1.9 %copy-done = bf16[2048,3,256]{2,0,1:T(8,128)(2,1)S(1)} copy-done((bf16[2048,3,256]{2,0,1:T(8,128)(2,1)S(1)}, bf16[2048,3,256]{2,0,1:T(8,128)(2,1)}, u32[]{:S(2)}) %copy-start) | copy-done | bytes 3145752
  28.1 0.0 copy-start.1
  28.1 1.0 copy-done.1
  29.2 0.0 copy-start.3
  29.2 2.3 %shard_map.64 = (bf16[4,128,256]{2,1,0:T(8,128)(2,1)S(1)}, bf16[4,128,256]{2,1,0:T(8,128)(2,1)S(1)}, bf16[4,128,384]{2,1,0:T(8,128)(2,1)S(1)}, bf16[4,128,128]{2,1,0:T(8,128)(2,1)S(1)}) custom-call(s32[6]{0:T(128)S(1)} %stack.27.scal, bf16[128,2048]{1,0:T(8,128)(2,1)S(1)} %bitcast.23, bf16[128,2048]{1,0:T(8,128)(2,1)S(1)} %collective-permute-done.ta, ...), custom_call_target="tpu_custom_call" | custom-call | tf_op jit(solution)/shard_map/pallas_call | solution.py:239
  31.5 6.2 %collective-permute-start.4 = (bf16[4,128,384]{2,1,0:T(8,128)(2,1)S(1)}, bf16[4,128,384]{2,1,0:T(8,128)(2,1)S(1)}, u32[]{:S(2)}, u32[]{:S(2)}) collective-permute-start(bf16[4,128,384]{2,1,0:T(8,128)(2,1)S(1)} %get-tuple-element.16), channel_id=1, source_target_pairs={{0,4},{4,0},{8,12},{12,8},{16,20},{20,16},{24,28},{28,24},{32,36},... | collective-permute-start | bytes 1179656 | tf_op jit(solution)/shard_map/ppermute | solution.py:317
  37.7 0.0 copy-done.5
  37.7 0.1 convert_element_type.22
  37.8 0.1 pad.7.clone
  37.9 0.0 copy-done.4
  37.9 0.1 maximum_maximum_fusion
  38.0 9.6 %all_to_all.25 = f32[8,8,128]{2,1,0:T(8,128)S(1)} all-to-all(f32[8,8,128]{2,1,0:T(8,128)S(1)} %maximum_maximum_fusion), channel_id=1, replica_groups={{0,4,1,5,2,6,3,7},{8,12,9,13,10,14,11,15},{16,20,17,21,18,22,19,23},{24..., dimensions={0} | all-to-all | bytes 65536 | tf_op jit(solution)/shard_map/all_to_all | solution.py:269
  47.5 0.0 collective-permute-done.4.kvq_mate
  47.6 0.0 copy-done.2
  47.6 2.1 %shard_map.65 = (bf16[8,208,128]{2,1,0:T(8,128)(2,1)S(1)}, f32[4,16,128]{2,1,0:T(8,128)S(1)}) custom-call(s32[6]{0:T(128)S(1)} %stack.27.scal, bf16[4,128,256]{2,1,0:T(8,128)(2,1)S(1)} %get-tuple-element.14.kv_own, bf16[4,128,384]{2,1,0:T(8,128)(2,1)S(1)} %collective-permute-done.4.kvq_mate, f32[8,128]{1,0:T(8,128)S(1)} %bitcast.26, ...), custom_call_target="tpu_custom_call" | custom-call | tf_op jit(solution)/shard_map/pallas_call | solution.py:239
  49.6 23.5 %all_to_all.26.got = bf16[8,208,128]{2,1,0:T(8,128)(2,1)S(1)} all-to-all(bf16[8,208,128]{2,1,0:T(8,128)(2,1)S(1)} %get-tuple-element.18), channel_id=1, replica_groups={{0,8,16,24,32,40,48,56},{4,12,20,28,36,44,52,60},{64,72,80,88,96,104,11..., dimensions={0} | all-to-all | bytes 851968 | tf_op jit(solution)/shard_map/all_to_all | solution.py:269
  73.1 1.4 %shard_map.66 = (bf16[8,208,128]{2,1,0:T(8,128)(2,1)}, f32[64,128]{1,0:T(8,128)S(1)}, f32[64,128]{1,0:T(8,128)S(1)}) custom-call(s32[6]{0:T(128)S(1)} %stack.27.scal, bf16[8,208,128]{2,1,0:T(8,128)(2,1)S(1)} %all_to_all.26.got), custom_call_target="tpu_custom_call" | custom-call | tf_op jit(solution)/shard_map/pallas_call | solution.py:239
  74.5 6.8 %all-to-all-start.2 = ((bf16[8,208,128]{2,1,0:T(8,128)(2,1)}), bf16[8,208,128]{2,1,0:T(8,128)(2,1)S(1)}, u32[]{:S(2)}, u32[]{:S(2)}) async-start(bf16[8,208,128]{2,1,0:T(8,128)(2,1)} %get-tuple-element.19), calls=%async_computation.2 | async-start | bytes 851968 | tf_op jit(solution)/shard_map/all_to_all | solution.py:269
  81.3 3.9 %collective-permute-start.10 = (bf16[4,128,256]{2,1,0:T(8,128)(2,1)S(1)}, bf16[4,128,256]{2,1,0:T(8,128)(2,1)S(1)}, u32[]{:S(2)}, u32[]{:S(2)}) collective-permute-start(bf16[4,128,256]{2,1,0:T(8,128)(2,1)S(1)} %get-tuple-element.17), channel_id=1, source_target_pairs={{4,16},{12,24},{16,4},{20,32},{24,12},{28,40},{32,20},{36,48},{40,... | collective-permute-start | bytes 786440 | tf_op jit(solution)/shard_map/ppermute | solution.py:323
  85.2 2.8 %collective-permute-start.5 = (bf16[4,128,256]{2,1,0:T(8,128)(2,1)S(1)}, bf16[4,128,256]{2,1,0:T(8,128)(2,1)S(1)}, u32[]{:S(2)}, u32[]{:S(2)}) collective-permute-start(bf16[4,128,256]{2,1,0:T(8,128)(2,1)S(1)} %get-tuple-element.14.kv_own), channel_id=1, source_target_pairs={{0,8},{4,12},{8,16},{12,20},{16,24},{20,28},{24,32},{28,36},{32,40... | collective-permute-start | bytes 786440 | tf_op jit(solution)/shard_map/ppermute | solution.py:318
  88.0 2.2 %collective-permute-start.6 = (bf16[4,128,256]{2,1,0:T(8,128)(2,1)S(1)}, bf16[4,128,256]{2,1,0:T(8,128)(2,1)S(1)}, u32[]{:S(2)}, u32[]{:S(2)}) collective-permute-start(bf16[4,128,256]{2,1,0:T(8,128)(2,1)S(1)} %get-tuple-element.17), channel_id=1, source_target_pairs={{0,12},{4,8},{8,20},{12,16},{16,28},{20,24},{24,36},{28,32},{32,44... | collective-permute-start | bytes 786440 | tf_op jit(solution)/shard_map/ppermute | solution.py:320
  90.3 1.3 collective-permute-start.7
  91.6 1.3 collective-permute-start.8
  92.9 0.1 collective-permute-done.10.twx
  92.9 6.5 %collective-permute-start.9 = (bf16[4,128,256]{2,1,0:T(8,128)(2,1)S(1)}, bf16[4,128,256]{2,1,0:T(8,128)(2,1)S(1)}, u32[]{:S(2)}, u32[]{:S(2)}) collective-permute-start(bf16[4,128,256]{2,1,0:T(8,128)(2,1)S(1)} %get-tuple-element.14.kv_own), channel_id=1, source_target_pairs={{4,20},{12,28},{16,0},{20,36},{24,8},{28,44},{32,16},{36,52},{40,2... | collective-permute-start | bytes 786440 | tf_op jit(solution)/shard_map/ppermute | solution.py:322
  99.4 0.0 all-to-all-done.2.got
  99.4 0.7 broadcast_in_dim.21
  100.1 7.9 %all-to-all-start.3 = ((bf16[8,64,128]{2,1,0:T(8,128)(2,1)}), bf16[8,64,128]{2,1,0:T(8,128)(2,1)S(1)}, u32[]{:S(2)}, u32[]{:S(2)}) async-start(bf16[8,64,128]{2,1,0:T(8,128)(2,1)} %broadcast_in_dim.21), calls=%async_computation.3 | async-start | bytes 262144 | tf_op jit(solution)/shard_map/all_to_all | solution.py:269
  108.0 0.1 min.12.pat
  108.1 0.0 collective-permute-done.5.zps
  108.1 0.0 collective-permute-done.6.zpx
  108.1 0.0 collective-permute-done.7.zms
  108.1 6.7 %collective-permute-done.8.zmx = bf16[4,128,256]{2,1,0:T(8,128)(2,1)S(1)} collective-permute-done((bf16[4,128,256]{2,1,0:T(8,128)(2,1)S(1)}, bf16[4,128,256]{2,1,0:T(8,128)(2,1)S(1)}, u32[]{:S(2)}, u32[]{:S(2)}) %collective-permute-start.8) | collective-permute-done | bytes 262176 | tf_op jit(solution)/shard_map/ppermute | solution.py:321
  114.8 0.0 collective-permute-done.9.tws
  114.8 2.5 %all-to-all-done.3.glob = bf16[8,64,128]{2,1,0:T(8,128)(2,1)S(1)} async-done(((bf16[8,64,128]{2,1,0:T(8,128)(2,1)}), bf16[8,64,128]{2,1,0:T(8,128)(2,1)S(1)}, u32[]{:S(2)}, u32[]{:S(2)}) %all-to-all-start.3) | async-done | bytes 131104 | tf_op jit(solution)/shard_map/all_to_all | solution.py:269
  117.3 0.0 copy-done.3
  117.3 9.6 %shard_map.67 = bf16[8,128,128]{2,1,0:T(8,128)(2,1)S(1)} custom-call(s32[6]{0:T(128)S(1)} %stack.27.scal, s32[48]{0:T(128)S(1)} %min.12.pat, bf16[4,128,256]{2,1,0:T(8,128)(2,1)S(1)} %get-tuple-element.14.kv_own, bf16[4,128,128]{2,1,0:T(8,128)(2,1)S(1)} %get-tuple-element.15.q_own, bf16[4,128,384]{2,1,0:T(8,128)(2,1)S(1)} %collective-permute-done.4.kvq_mate, ...), custom_call_target="tpu_custom_call" | custom-call | tf_op jit(solution)/shard_map/pallas_call | solution.py:239
  126.9 9.0 %all_to_all.27 = bf16[8,128,128]{2,1,0:T(8,128)(2,1)S(1)} all-to-all(bf16[8,128,128]{2,1,0:T(8,128)(2,1)S(1)} %shard_map.67), channel_id=1, replica_groups={{0,4,1,5,2,6,3,7},{8,12,9,13,10,14,11,15},{16,20,17,21,18,22,19,23},{24..., dimensions={0} | all-to-all | bytes 524288 | tf_op jit(solution)/shard_map/all_to_all | solution.py:269
  135.9 0.2 copy.10
  136.1 0.9 copy.11
  (9 shorter events, 0.1 us)
Async XLA Ops:
  0.0 37.7 %copy-start.5 = (s32[1,2,3]{2,1,0:T(2,128)S(1)}, s32[1,2,3]{2,1,0:T(2,128)}, u32[]{:S(2)}) copy-start(s32[1,2,3]{2,1,0:T(2,128)} %param.11) | copy-start | bytes 76
  0.0 37.9 %copy-start.4 = (f32[1,8,128]{2,1,0:T(8,128)S(1)}, f32[1,8,128]{2,1,0:T(8,128)}, u32[]{:S(2)}) copy-start(f32[1,8,128]{2,1,0:T(8,128)} %param.10) | copy-start | bytes 12292
  0.0 47.5 %copy-start.2 = (bf16[8,128,16]{1,2,0:T(8,128)(2,1)S(1)}, bf16[8,128,16]{1,2,0:T(8,128)(2,1)}, u32[]{:S(2)}) copy-start(bf16[8,128,16]{1,2,0:T(8,128)(2,1)} %param.8) | copy-start | bytes 98308
  0.0 12.1 %collective-permute-start = (bf16[128,2048]{1,0:T(8,128)(2,1)}, bf16[128,2048]{1,0:T(8,128)(2,1)S(1)}, u32[]{:S(2)}, u32[]{:S(2)}) collective-permute-start(bf16[128,2048]{1,0:T(8,128)(2,1)} %bitcast.21), channel_id=1, source_target_pairs={{0,1},{1,2},{2,3},{3,0},{4,5},{5,6},{6,7},{7,4},{8,9},{9,10},{10,1... | collective-permute-start | bytes 1572872 | tf_op jit(solution)/shard_map/ppermute | solution.py:282
  4.1 14.0 %collective-permute-start.1 = (bf16[128,2048]{1,0:T(8,128)(2,1)}, bf16[128,2048]{1,0:T(8,128)(2,1)S(1)}, u32[]{:S(2)}, u32[]{:S(2)}) collective-permute-start(bf16[128,2048]{1,0:T(8,128)(2,1)} %bitcast.22), channel_id=1, source_target_pairs={{0,3},{1,0},{2,1},{3,2},{4,7},{5,4},{6,5},{7,6},{8,11},{9,8},{10,9... | collective-permute-start | bytes 1572872 | tf_op jit(solution)/shard_map/ppermute | solution.py:283
  12.2 11.9 %collective-permute-start.2 = (bf16[64,2048]{1,0:T(8,128)(2,1)S(1)}, bf16[64,2048]{1,0:T(8,128)(2,1)S(1)}, u32[]{:S(2)}, u32[]{:S(2)}) collective-permute-start(bf16[64,2048]{1,0:T(8,128)(2,1)S(1)} %slice.21), channel_id=1, source_target_pairs={{0,1},{1,2},{2,3},{3,0},{4,5},{5,6},{6,7},{7,4},{8,9},{9,10},{10,1... | collective-permute-start | bytes 786440 | tf_op jit(solution)/shard_map/ppermute | solution.py:284
  18.2 8.1 %collective-permute-start.3 = (bf16[64,2048]{1,0:T(8,128)(2,1)S(1)}, bf16[64,2048]{1,0:T(8,128)(2,1)S(1)}, u32[]{:S(2)}, u32[]{:S(2)}) collective-permute-start(bf16[64,2048]{1,0:T(8,128)(2,1)S(1)} %slice.22), channel_id=1, source_target_pairs={{0,3},{1,0},{2,1},{3,2},{4,7},{5,4},{6,5},{7,6},{8,11},{9,8},{10,9... | collective-permute-start | bytes 786440 | tf_op jit(solution)/shard_map/ppermute | solution.py:285
  26.2 1.9 %copy-start = (bf16[2048,3,256]{2,0,1:T(8,128)(2,1)S(1)}, bf16[2048,3,256]{2,0,1:T(8,128)(2,1)}, u32[]{:S(2)}) copy-start(bf16[2048,3,256]{2,0,1:T(8,128)(2,1)} %param.7) | copy-start | bytes 9437188
  28.1 1.0 copy-start.1
  29.2 88.1 %copy-start.3 = (f32[1024]{0:T(1024)S(1)}, f32[1024]{0:T(1024)}, u32[]{:S(2)}) copy-start(f32[1024]{0:T(1024)} %param.9) | copy-start | bytes 12292
  31.5 16.0 %collective-permute-start.4 = (bf16[4,128,384]{2,1,0:T(8,128)(2,1)S(1)}, bf16[4,128,384]{2,1,0:T(8,128)(2,1)S(1)}, u32[]{:S(2)}, u32[]{:S(2)}) collective-permute-start(bf16[4,128,384]{2,1,0:T(8,128)(2,1)S(1)} %get-tuple-element.16), channel_id=1, source_target_pairs={{0,4},{4,0},{8,12},{12,8},{16,20},{20,16},{24,28},{28,24},{32,36},... | collective-permute-start | bytes 1179656 | tf_op jit(solution)/shard_map/ppermute | solution.py:317
  74.5 24.9 %all-to-all-start.2 = ((bf16[8,208,128]{2,1,0:T(8,128)(2,1)}), bf16[8,208,128]{2,1,0:T(8,128)(2,1)S(1)}, u32[]{:S(2)}, u32[]{:S(2)}) async-start(bf16[8,208,128]{2,1,0:T(8,128)(2,1)} %get-tuple-element.19), calls=%async_computation.2 | async-start | bytes 851968 | tf_op jit(solution)/shard_map/all_to_all | solution.py:269
  81.3 11.6 %collective-permute-start.10 = (bf16[4,128,256]{2,1,0:T(8,128)(2,1)S(1)}, bf16[4,128,256]{2,1,0:T(8,128)(2,1)S(1)}, u32[]{:S(2)}, u32[]{:S(2)}) collective-permute-start(bf16[4,128,256]{2,1,0:T(8,128)(2,1)S(1)} %get-tuple-element.17), channel_id=1, source_target_pairs={{4,16},{12,24},{16,4},{20,32},{24,12},{28,40},{32,20},{36,48},{40,... | collective-permute-start | bytes 786440 | tf_op jit(solution)/shard_map/ppermute | solution.py:323
  85.2 22.9 %collective-permute-start.5 = (bf16[4,128,256]{2,1,0:T(8,128)(2,1)S(1)}, bf16[4,128,256]{2,1,0:T(8,128)(2,1)S(1)}, u32[]{:S(2)}, u32[]{:S(2)}) collective-permute-start(bf16[4,128,256]{2,1,0:T(8,128)(2,1)S(1)} %get-tuple-element.14.kv_own), channel_id=1, source_target_pairs={{0,8},{4,12},{8,16},{12,20},{16,24},{20,28},{24,32},{28,36},{32,40... | collective-permute-start | bytes 786440 | tf_op jit(solution)/shard_map/ppermute | solution.py:318
  88.0 20.1 %collective-permute-start.6 = (bf16[4,128,256]{2,1,0:T(8,128)(2,1)S(1)}, bf16[4,128,256]{2,1,0:T(8,128)(2,1)S(1)}, u32[]{:S(2)}, u32[]{:S(2)}) collective-permute-start(bf16[4,128,256]{2,1,0:T(8,128)(2,1)S(1)} %get-tuple-element.17), channel_id=1, source_target_pairs={{0,12},{4,8},{8,20},{12,16},{16,28},{20,24},{24,36},{28,32},{32,44... | collective-permute-start | bytes 786440 | tf_op jit(solution)/shard_map/ppermute | solution.py:320
  90.3 17.8 %collective-permute-start.7 = (bf16[4,128,256]{2,1,0:T(8,128)(2,1)S(1)}, bf16[4,128,256]{2,1,0:T(8,128)(2,1)S(1)}, u32[]{:S(2)}, u32[]{:S(2)}) collective-permute-start(bf16[4,128,256]{2,1,0:T(8,128)(2,1)S(1)} %get-tuple-element.14.kv_own), channel_id=1, source_target_pairs={{8,0},{12,4},{16,8},{20,12},{24,16},{28,20},{32,24},{36,28},{40,32... | collective-permute-start | bytes 786440 | tf_op jit(solution)/shard_map/ppermute | solution.py:319
  91.6 23.3 %collective-permute-start.8 = (bf16[4,128,256]{2,1,0:T(8,128)(2,1)S(1)}, bf16[4,128,256]{2,1,0:T(8,128)(2,1)S(1)}, u32[]{:S(2)}, u32[]{:S(2)}) collective-permute-start(bf16[4,128,256]{2,1,0:T(8,128)(2,1)S(1)} %get-tuple-element.17), channel_id=1, source_target_pairs={{8,4},{12,0},{16,12},{20,8},{24,20},{28,16},{32,28},{36,24},{40,36... | collective-permute-start | bytes 786440 | tf_op jit(solution)/shard_map/ppermute | solution.py:321
  92.9 21.9 %collective-permute-start.9 = (bf16[4,128,256]{2,1,0:T(8,128)(2,1)S(1)}, bf16[4,128,256]{2,1,0:T(8,128)(2,1)S(1)}, u32[]{:S(2)}, u32[]{:S(2)}) collective-permute-start(bf16[4,128,256]{2,1,0:T(8,128)(2,1)S(1)} %get-tuple-element.14.kv_own), channel_id=1, source_target_pairs={{4,20},{12,28},{16,0},{20,36},{24,8},{28,44},{32,16},{36,52},{40,2... | collective-permute-start | bytes 786440 | tf_op jit(solution)/shard_map/ppermute | solution.py:322
  100.1 17.2 %all-to-all-start.3 = ((bf16[8,64,128]{2,1,0:T(8,128)(2,1)}), bf16[8,64,128]{2,1,0:T(8,128)(2,1)S(1)}, u32[]{:S(2)}, u32[]{:S(2)}) async-start(bf16[8,64,128]{2,1,0:T(8,128)(2,1)} %broadcast_in_dim.21), calls=%async_computation.3 | async-start | bytes 262144 | tf_op jit(solution)/shard_map/all_to_all | solution.py:269

commit v2 on v1

--- a/solution.py
+++ b/solution.py
@@ -56,34 +56,45 @@
     return mm(steps, jnp.where(row <= col, 1.0, 0.0).astype(F32), HIGH)
 
 
-def project_kernel(scal, t0, ta, tb, td1, td2, w, kv_own, kv_other, kvq_other, q_own, rows):
+def project_kernel(
+    scal, t0, at, ab, bt, bb, dt, db, ext, w, kv_own, kv_other, kvq_other, q_own, ext_own, rows, wv, sems
+):
     c, x = scal[0], scal[1]
-    rows[0:128] = t0[...]
-    rows[128:256] = ta[...]
-    rows[256:320] = td1[...]
-    rows[320:384] = td2[...]
-    rows[384:512] = tb[...]
-    parts = [mm(rows[...], w[k]).astype(BF) for k in range(3)]
+    places = [(t0, 0, 128), (at, 128, 64), (ab, 192, 64), (bt, 384, 64), (bb, 448, 64), (ext, 512, 32), (dt, 256, 64), (db, 320, 64)]
+    copies = [pltpu.make_async_copy(w.at[0], wv.at[0], sems.at[8])]
+    copies += [
+        pltpu.make_async_copy(ref, rows.at[pl.ds(start, size)], sems.at[i])
+        for i, (ref, start, size) in enumerate(places)
+    ]
+    copies += [pltpu.make_async_copy(w.at[k], wv.at[k], sems.at[8 + k]) for k in (1, 2)]
+    for copy in copies:
+        copy.start()
     first = c == 0
-    for r in range(DOCS):
-        n = lax.rem(x - r + DOCS, DOCS)
-        own, other = [], []
-        for k in range(3):
-            lo = parts[k][r * TOK : (r + 1) * TOK, :DH]
-            hi = parts[k][r * TOK : (r + 1) * TOK, DH:]
-            own.append(jnp.where(first, lo, hi))
-            other.append(jnp.where(first, hi, lo))
-        q_own[n] = own[0]
-        kv_own[n, :, :DH] = own[1]
-        kv_own[n, :, DH:] = own[2]
-        kv_other[n, :, :DH] = other[1]
-        kv_other[n, :, DH:] = other[2]
-        kvq_other[n, :, :DH] = other[1]
-        kvq_other[n, :, DH : 2 * DH] = other[2]
-        kvq_other[n, :, 2 * DH :] = other[0]
-
-
-def states_kernel(scal, kv_own, kvq_mate, steps, wft, out, state0):
+    for copy in copies[:9]:
+        copy.wait()
+    for k in range(3):
+        if k:
+            copies[8 + k].wait()
+        part = mm(rows[...], wv[k]).astype(BF)
+        for r in range(DOCS):
+            n = lax.rem(x - r + DOCS, DOCS)
+            lo = part[r * TOK : (r + 1) * TOK, :DH]
+            hi = part[r * TOK : (r + 1) * TOK, DH:]
+            own = jnp.where(first, lo, hi)
+            other = jnp.where(first, hi, lo)
+            if k == 0:
+                q_own[n] = own
+                kvq_other[n, :, 2 * DH :] = other
+            else:
+                here = slice((k - 1) * DH, k * DH)
+                kv_own[n, :, here] = own
+                kv_other[n, :, here] = other
+                kvq_other[n, :, here] = other
+        if k:
+            ext_own[(k - 1) * 32 : k * 32] = jnp.where(first, part[512:, :DH], part[512:, DH:])
+
+
+def states_kernel(scal, kv_own, kvq_mate, ext_own, steps, wft, out, state0):
     c, h = scal[0], scal[5]
     first = c == 0
     cum = cumulative_of(steps[...])
@@ -105,10 +116,9 @@
         state0[n] = local[0]
         states.append(jnp.exp(last1) * local[0] + local[1])
         decays.append(last0 + last1)
-        for half in range(2):
-            out[2 * n + half, 144:176] = segs[0][32 * half : 32 * half + 32, :DH]
-            out[2 * n + half, 176:208] = segs[0][32 * half : 32 * half + 32, DH:]
     put_states(out, jnp.concatenate(states, axis=0), decays)
+    for peer in range(8):
+        out[peer, 144:208] = ext_own[...]
 
 
 def put_states(out, state, decays):
@@ -133,7 +143,7 @@
     return state, decay, wide
 
 
-def row_kernel(scal, got, out, inner, outer):
+def row_kernel(scal, got, h0, h1, h2, h3, h4, h5, out, inner, outer):
     z = scal[3]
     total = jnp.zeros((64, TOK), F32)
     before = jnp.zeros((64, TOK), F32)
@@ -155,7 +165,7 @@
 
 
 def attend_kernel(
-    scal, pat, kv_own, q_own, kvq_mate, zps, zpx, zms, zmx, tws, twx, glob, got, inner, outer,
+    scal, pat, kv_own, q_own, kvq_mate, zps, zpx, zms, zmx, tws, twx, got, inner, outer,
     state0, steps, wft, gain, out, win, qs,
 ):
     c, q, y, h = scal[0], scal[2], scal[4], scal[5]
@@ -189,6 +199,12 @@
     scale = DH ** (-0.5)
     for n in range(DOCS):
         carried = entering[F * n : F * n + F]
+        glob = [
+            jnp.concatenate(
+                [got[peer, at : at + 32].astype(F32)[8 * n : 8 * n + 8] for peer in range(8)], axis=0
+            ).astype(BF)
+            for at in (144, 176)
+        ]
         for s in range(2):
             line = cum[2 * n + s : 2 * n + s + 1]
             column = cum_t[:, 2 * n + s : 2 * n + s + 1]
@@ -213,10 +229,8 @@
                         win[n, lax.div(place, 2), pl.ds(pl.multiple_of(BS * lax.rem(place, 2), BS), BS)]
                     )
                 near = jnp.concatenate(picks, axis=0)
-                gk = jnp.concatenate([glob[2 * n, 0:32], glob[2 * n + 1, 0:32]], axis=0)
-                gv = jnp.concatenate([glob[2 * n, 32:64], glob[2 * n + 1, 32:64]], axis=0)
-                all_k = jnp.concatenate([near[:, :DH], gk], axis=0)
-                all_v = jnp.concatenate([near[:, DH:], gv], axis=0)
+                all_k = jnp.concatenate([near[:, :DH], glob[0]], axis=0)
+                all_v = jnp.concatenate([near[:, DH:], glob[1]], axis=0)
                 scores = nt(queries[half * BS : half * BS + BS], all_k) * scale
                 bad = (
                     ((lane < BS) & (block < 2))
@@ -233,14 +247,13 @@
                 ).astype(BF)
 
 
-def call(kernel, outs, scratch, n_smem, *args):
-    vmem = pl.BlockSpec(memory_space=pltpu.VMEM)
-    smem = pl.BlockSpec(memory_space=pltpu.SMEM)
+def call(kernel, outs, scratch, spaces, *args):
+    kinds = {"s": pltpu.SMEM, "v": pltpu.VMEM, "a": pl.ANY}
     return pl.pallas_call(
         kernel,
         out_shape=outs,
-        in_specs=[smem] * n_smem + [vmem] * (len(args) - n_smem),
-        out_specs=[vmem] * len(outs),
+        in_specs=[pl.BlockSpec(memory_space=kinds[k]) for k in spaces],
+        out_specs=[pl.BlockSpec(memory_space=pltpu.VMEM)] * len(outs),
         scratch_shapes=scratch,
         compiler_params=pltpu.CompilerParams(vmem_limit_bytes=28 * 2**20),
     )(*args)
@@ -263,6 +276,7 @@
 XC = [[(2 * q + c) * 4 + x for x in range(4) for c in range(2)] for q in range(CHIPS)]
 ZS = [[(8 * y + z) * 2 + c for z in range(8)] for y in range(8) for c in range(2)]
 YS = [[(8 * y + z) * 2 + c for y in range(8)] for z in range(8) for c in range(2)]
+YC = [[(8 * y + z) * 2 + c for y in range(8) for c in range(2)] for z in range(8)]
 
 
 def exchange(a, axis, groups):
@@ -279,40 +293,45 @@
     t0 = tokens[0]
     up = [(i, (i + 1) % 4) for i in range(4)]
     down = [(i, (i - 1) % 4) for i in range(4)]
-    ta = lax.ppermute(t0, "fsdp", up)
-    tb = lax.ppermute(t0, "fsdp", down)
-    td1 = lax.ppermute(ta[:64], "fsdp", up)
-    td2 = lax.ppermute(tb[64:], "fsdp", down)
-
-    small = jnp.concatenate(
-        [
-            log_decay[0][:, None, :],
-            jnp.broadcast_to(
-                jnp.pad(pattern.reshape(1, 1, 6).astype(F32), ((0, 0), (0, 0), (0, 122))),
-                (8, 1, TOK),
-            ),
-            jnp.zeros((8, 6, TOK), F32),
-        ],
-        axis=1,
-    )
+    top, bottom = t0[:64], t0[64:]
+    at = lax.ppermute(top, "fsdp", up)
+    bb = lax.ppermute(bottom, "fsdp", down)
+    ab = lax.ppermute(bottom, "fsdp", up)
+    bt = lax.ppermute(top, "fsdp", down)
+    dt = lax.ppermute(at, "fsdp", up)
+    db = lax.ppermute(bb, "fsdp", down)
+
+    scattered = exchange(top.reshape(16, 64, TOK), "seq", YC)[0]
+    three = split3(log_decay[0])
+    wanted = jnp.broadcast_to(
+        jnp.pad(pattern.reshape(1, 6).astype(BF), ((0, 0), (0, TOK - 6))), (8, TOK)
+    )
+    small = jnp.stack([*three, wanted] + [jnp.zeros((8, TOK), BF)] * 12, axis=1)
+    small = jnp.concatenate([small, jnp.broadcast_to(scattered[None], (8, 64, TOK))], axis=1)
     got0 = exchange(small, ("seq", "fsdp"), XC)
-    steps = got0[:, 0]
-    pat = got0[:, 1, :6].astype(jnp.int32).reshape(48) - (4 * q - 6)
+    steps = (got0[:, 0].astype(F32) + got0[:, 1].astype(F32)) + got0[:, 2].astype(F32)
+    pat = got0[:, 3, :6].astype(jnp.int32).reshape(48) - (4 * q - 6)
     pat = jnp.clip(pat, 0, 15).astype(jnp.int32)
+    ext = got0[:, 16:].reshape(32, D)
 
     w3 = w_qkv.transpose(1, 0, 2)
     wft = w_feature.transpose(0, 2, 1)
-    kv_own, kv_other, kvq_other, q_own = call(
+    kv_own, kv_other, kvq_other, q_own, ext_own = call(
         project_kernel,
         [
             shape((DOCS, TOK, 2 * DH), BF),
             shape((DOCS, TOK, 2 * DH), BF),
             shape((DOCS, TOK, 3 * DH), BF),
             shape((DOCS, TOK, DH), BF),
+            shape((64, DH), BF),
         ],
-        [pltpu.VMEM((4 * TOK, D), BF)],
-        1,
-        scal, t0, ta, tb, td1, td2, w3,
+        [
+            pltpu.VMEM((4 * TOK + 32, D), BF),
+            pltpu.VMEM((3, D, 2 * DH), BF),
+            pltpu.SemaphoreType.DMA((11,)),
+        ],
+        "saaaaaaaaa",
+        scal, t0, at, ab, bt, bb, dt, db, ext, w3,
     )
     kvq_mate = lax.ppermute(kvq_other, "seq", pairs(lambda q, c: (q, 1 - c)))
     zps = lax.ppermute(kv_own, "seq", pairs(lambda q, c: (q + 1, c)))
@@ -321,31 +340,31 @@
     zmx = lax.ppermute(kv_other, "seq", pairs(lambda q, c: (q - 1, 1 - c)))
     tws = lax.ppermute(kv_own, "seq", pairs(lambda q, c: (q + 2, 1) if c else (q - 2, 0)))
     twx = lax.ppermute(kv_other, "seq", pairs(lambda q, c: (q + 2, 0) if c else (q - 2, 1)))
+    halo = (zps, zpx, zms, zmx, tws, twx)
 
     send1, state0 = call(
         states_kernel,
         [shape((8, ROWS, TOK), BF), shape((DOCS, F, DH), F32)],
         [],
-        1,
-        scal, kv_own, kvq_mate, steps, wft,
+        "svvvvv",
+        scal, kv_own, kvq_mate, ext_own, steps, wft,
     )
     got1 = exchange(send1, "seq", ZS)
     send2, inner, outer = call(
         row_kernel,
         [shape((8, ROWS, TOK), BF), shape((64, TOK), F32), shape((64, TOK), F32)],
         [],
-        1,
-        scal, got1,
+        "sv" + "a" * 6,
+        scal, got1, *halo,
     )
     got2 = exchange(send2, "seq", YS)
-    glob = exchange(jnp.broadcast_to(got2[0, 144:208][None], (8, 64, TOK)), "seq", ZS)
 
     [out] = call(
         attend_kernel,
         [shape((8, TOK, DH), BF)],
         [pltpu.VMEM((DOCS, 8, TOK, 2 * DH), BF), pltpu.VMEM((DOCS, 2, TOK, DH), BF)],
-        2,
-        scal, pat, kv_own, q_own, kvq_mate, zps, zpx, zms, zmx, tws, twx, glob, got2, inner, outer,
+        "ss" + "v" * 16,
+        scal, pat, kv_own, q_own, kvq_mate, *halo, got2, inner, outer,
         state0, steps, wft, norm_gain.reshape(HALF_HEADS, 1, DH),
     )
     mixed = exchange(out, ("seq", "fsdp"), XC)

time: 139 us -> 159 us (1.14)
  blocking collectives: 42.1 us -> 10.2 us
  waiting for transfers between devices: 17.9 us -> 36.8 us
  starting transfers between devices: 56.2 us -> 73.2 us
  local copies, waits for them, and re-layouts: 5.03 us -> 14.1 us
  other arithmetic: 0.1 us -> 4.07 us
  Pallas kernels: 15.4 us -> 19.2 us
    all_to_all x3 -> x1, blocking collectives: 42.1 us -> 10.2 us  [exchange(): return lax.all_to_all(a, axis, 0, 0, tiled=True, axis_index_groups=groups)]
    all_to_all x2 -> x4, starting transfers between devices: 14.7 us -> 34.8 us  [exchange(): return lax.all_to_all(a, axis, 0, 0, tiled=True, axis_index_groups=groups)]
    all_to_all x2 -> x4, waiting for transfers between devices: 2.46 us -> 19.8 us  [exchange(): return lax.all_to_all(a, axis, 0, 0, tiled=True, axis_index_groups=groups)]
    ppermute x4 -> x6, waiting for transfers between devices: 8.68 us -> 0.31 us  [the longest x1 0.3 us: per_device(): at = lax.ppermute(top, 'fsdp', up)]
    ppermute x1, waiting for transfers between devices: 0.01 us -> 5.39 us  [per_device(): zms = lax.ppermute(kv_own, 'seq', pairs(lambda q, c: (q - 1, c)))]
    ppermute x1, waiting for transfers between devices: 0.09 us -> 4.79 us  [per_device(): lax.ppermute(kv_other, 'seq', pairs(lambda q, c: (q + 2, 0) if c else (q...]
    slice x3, local copies, waits for them, and re-layouts: 0.04 us -> 4.48 us  [the longest x1 2.04 us: per_device(): top, bottom = (t0[:64], t0[64:])]
    pallas_call x4, Pallas kernels: 15.4 us -> 19.2 us  [call(): pl.pallas_call(kernel, out_shape=outs, in_specs=[pl.BlockSpec(memory_spac...]
  transfers between devices with their start and end apart: 13 -> 17, of which waited for: 6 -> 7; matrix products, arithmetic and copies ran while one was open for 1% -> 8% of each run, Pallas kernels for 0% -> 0%
where the time goes in v2:
time: 159 us; the launch traced here: 158 us
  starting transfers between devices  73.2 us (46%)
  waiting for transfers between devices  36.8 us (23%)
  Pallas kernels  19.2 us (12%)
  local copies, waits for them, and re-layouts  14.1 us (9%)
  blocking collectives  10.2 us (6%)
  other arithmetic  4.07 us (3%)
    all_to_all x4, starting transfers between devices, exchange(): return lax.all_to_all(a, axis, 0, 0, tiled=True, axis_index_groups=groups)  34.8 us
    all_to_all x4, waiting for transfers between devices, exchange(): return lax.all_to_all(a, axis, 0, 0, tiled=True, axis_index_groups=groups)  19.8 us
    pallas_call x4, Pallas kernels, call(): pl.pallas_call(kernel, out_shape=outs, in_specs=[pl.BlockSpec(memory_spac...  19.2 us
    all_to_all x1, blocking collectives, exchange(): return lax.all_to_all(a, axis, 0, 0, tiled=True, axis_index_groups=groups)  10.2 us
    ppermute x1, waiting for transfers between devices, per_device(): zmx = lax.ppermute(kv_other, 'seq', pairs(lambda q, c: (q - 1, 1 - c)))  6.05 us
    ppermute x1, waiting for transfers between devices, per_device(): zms = lax.ppermute(kv_own, 'seq', pairs(lambda q, c: (q - 1, c)))  5.39 us
    ppermute x1, starting transfers between devices, per_device(): lax.ppermute(kv_own, 'seq', pairs(lambda q, c: (q + 2, 1) if c else (q -...  5.2 us
    ppermute x1, starting transfers between devices, per_device(): lax.ppermute(kv_other, 'seq', pairs(lambda q, c: (q + 2, 0) if c else (q...  5.08 us
  transfers between devices with their start and end apart: 17, of which 7 were waited for; matrix products, arithmetic and copies ran while one was open for 8% of the time, Pallas kernels for 0%

profile of v2, /device:TPU:1, one launch (start us, length us, event | category | flops | bytes accessed | tf_op | source)
XLA Modules:
  0.0 158.0 jit_solution(3552021264659302605)
XLA Ops:
  0.0 2.0 %slice_bitcast_fusion = (bf16[64,2048]{1,0:T(8,128)(2,1)}, bf16[64,2048]{1,0:T(8,128)(2,1)}, bf16[1,64,2048]{2,1,0:T(8,128)(2,1)S(1)}) fusion(bf16[1,128,2048]{2,1,0:T(8,128)(2,1)} %param.6), kind=kLoop, calls=%fused_computation | loop fusion | bytes 1310720 | tf_op jit(solution)/shard_map/slice | solution.py:296
  2.0 0.8 reshape.90
  2.9 10.8 %all-to-all-start = ((bf16[16,64,128]{2,1,0:T(8,128)(2,1)}), bf16[16,64,128]{2,1,0:T(8,128)(2,1)}, u32[]{:S(2)}, u32[]{:S(2)}) async-start(bf16[16,64,128]{2,1,0:T(8,128)(2,1)} %reshape.90), calls=%async_computation | async-start | bytes 524288 | tf_op jit(solution)/shard_map/all_to_all | solution.py:283
  13.7 2.2 %collective-permute-start.3 = (bf16[64,2048]{1,0:T(8,128)(2,1)}, bf16[64,2048]{1,0:T(8,128)(2,1)S(1)}, u32[]{:S(2)}, u32[]{:S(2)}) collective-permute-start(bf16[64,2048]{1,0:T(8,128)(2,1)} %get-tuple-element.25), channel_id=1, source_target_pairs={{0,3},{1,0},{2,1},{3,2},{4,7},{5,4},{6,5},{7,6},{8,11},{9,8},{10,9... | collective-permute-start | bytes 786440 | tf_op jit(solution)/shard_map/ppermute | solution.py:298
  15.9 3.1 %collective-permute-start.1 = (bf16[64,2048]{1,0:T(8,128)(2,1)}, bf16[64,2048]{1,0:T(8,128)(2,1)}, u32[]{:S(2)}, u32[]{:S(2)}) collective-permute-start(bf16[64,2048]{1,0:T(8,128)(2,1)} %get-tuple-element.25), channel_id=1, source_target_pairs={{0,1},{1,2},{2,3},{3,0},{4,5},{5,6},{6,7},{7,4},{8,9},{9,10},{10,1... | collective-permute-start | bytes 786440 | tf_op jit(solution)/shard_map/ppermute | solution.py:299
  19.0 3.4 %collective-permute-start.2 = (bf16[64,2048]{1,0:T(8,128)(2,1)}, bf16[64,2048]{1,0:T(8,128)(2,1)}, u32[]{:S(2)}, u32[]{:S(2)}) collective-permute-start(bf16[64,2048]{1,0:T(8,128)(2,1)} %get-tuple-element.26), channel_id=1, source_target_pairs={{0,3},{1,0},{2,1},{3,2},{4,7},{5,4},{6,5},{7,6},{8,11},{9,8},{10,9... | collective-permute-start | bytes 786440 | tf_op jit(solution)/shard_map/ppermute | solution.py:300
  22.4 1.9 %collective-permute-start = (bf16[64,2048]{1,0:T(8,128)(2,1)}, bf16[64,2048]{1,0:T(8,128)(2,1)}, u32[]{:S(2)}, u32[]{:S(2)}) collective-permute-start(bf16[64,2048]{1,0:T(8,128)(2,1)} %get-tuple-element.26), channel_id=1, source_target_pairs={{0,1},{1,2},{2,3},{3,0},{4,5},{5,6},{6,7},{7,4},{8,9},{9,10},{10,1... | collective-permute-start | bytes 786440 | tf_op jit(solution)/shard_map/ppermute | solution.py:297
  24.3 0.7 convert_element_type.104
  25.0 0.1 convert_element_type.105
  25.1 1.3 convert_element_type.99
  26.4 1.4 subtract_convert_fusion
  27.7 0.0 collective-permute-done.3.bb
  27.7 4.6 %collective-permute-start.5 = (bf16[64,2048]{1,0:T(8,128)(2,1)S(1)}, bf16[64,2048]{1,0:T(8,128)(2,1)}, u32[]{:S(2)}, u32[]{:S(2)}) collective-permute-start(bf16[64,2048]{1,0:T(8,128)(2,1)S(1)} %collective-permute-done.3.bb), channel_id=1, source_target_pairs={{0,3},{1,0},{2,1},{3,2},{4,7},{5,4},{6,5},{7,6},{8,11},{9,8},{10,9... | collective-permute-start | bytes 786440 | tf_op jit(solution)/shard_map/ppermute | solution.py:302
  32.3 0.3 collective-permute-done.at
  32.6 1.9 %collective-permute-start.4 = (bf16[64,2048]{1,0:T(8,128)(2,1)}, bf16[64,2048]{1,0:T(8,128)(2,1)}, u32[]{:S(2)}, u32[]{:S(2)}) collective-permute-start(bf16[64,2048]{1,0:T(8,128)(2,1)} %collective-permute-done.at), channel_id=1, source_target_pairs={{0,1},{1,2},{2,3},{3,0},{4,5},{5,6},{6,7},{7,4},{8,9},{9,10},{10,1... | collective-permute-start | bytes 786440 | tf_op jit(solution)/shard_map/ppermute | solution.py:301
  34.5 0.0 all-to-all-done
  34.5 0.7 slice_bitcast_fusion.1
  35.3 0.6 stack_broadcast_in_dim.2
  35.9 0.6 concatenate.9
  36.5 2.6 %concatenate.11 = bf16[8,80,128]{2,1,0:T(8,128)(2,1)} concatenate(bf16[8,1,128]{2,1,0:T(2,128)(2,1)} %convert_element_type.99, bf16[8,1,128]{2,1,0:T(2,128)(2,1)} %get-tuple-element.32, bf16[8,1,128]{2,1,0:T(2,128)(2,1)} %get-tuple-element.31, bf16[8,1,128]{2,1,0:T(2,128)(2,1)} %stack_broadcast_in_dim.2, bf16[8,4,128]{2,1,0:T(4,128)(2,1)} %concatenate.9, ...), dimensions={1} | concatenate | bytes 327680 | tf_op jit(solution)/shard_map/concatenate | solution.py:310
  39.1 6.4 %all-to-all-start.1 = ((bf16[8,80,128]{2,1,0:T(8,128)(2,1)}), bf16[8,80,128]{2,1,0:T(8,128)(2,1)}, u32[]{:S(2)}, u32[]{:S(2)}) async-start(bf16[8,80,128]{2,1,0:T(8,128)(2,1)} %concatenate.11), calls=%async_computation.1 | async-start | bytes 327680 | tf_op jit(solution)/shard_map/all_to_all | solution.py:283
  45.5 0.1 stack.30.scal
  45.6 5.6 %all-to-all-done.1 = bf16[8,80,128]{2,1,0:T(8,128)(2,1)} async-done(((bf16[8,80,128]{2,1,0:T(8,128)(2,1)}), bf16[8,80,128]{2,1,0:T(8,128)(2,1)}, u32[]{:S(2)}, u32[]{:S(2)}) %all-to-all-start.1) | async-done | bytes 163872 | tf_op jit(solution)/shard_map/all_to_all | solution.py:283
  51.2 1.6 slice.42
  52.8 1.0 reshape.91.ext
  53.7 0.0 collective-permute-done.1.ab
  53.8 0.0 collective-permute-done.2.bt
  53.8 0.0 collective-permute-done.5.db
  53.8 0.0 collective-permute-done.4.dt
  53.8 0.0 copy-start.1
  53.8 1.0 copy-done.1
  54.9 0.9 copy-done.3
  55.8 5.4 %shard_map.64 = (bf16[4,128,256]{2,1,0:T(8,128)(2,1)S(1)}, bf16[4,128,256]{2,1,0:T(8,128)(2,1)S(1)}, bf16[4,128,384]{2,1,0:T(8,128)(2,1)S(1)}, bf16[4,128,128]{2,1,0:T(8,128)(2,1)S(1)}, bf16[64,128]{1,0:T(8,128)(2,1)S(1)}) custom-call(s32[6]{0:T(128)S(1)} %stack.30.scal, bf16[128,2048]{1,0:T(8,128)(2,1)S(1)} %bitcast.24, ...), custom_call_target="tpu_custom_call" | custom-call | tf_op jit(solution)/shard_map/pallas_call | solution.py:252
  61.2 0.0 copy-start.9
  61.2 0.0 copy-start.5
  61.2 0.0 copy-start.8
  61.3 2.9 %collective-permute-start.6 = (bf16[4,128,384]{2,1,0:T(8,128)(2,1)S(1)}, bf16[4,128,384]{2,1,0:T(8,128)(2,1)S(1)}, u32[]{:S(2)}, u32[]{:S(2)}) collective-permute-start(bf16[4,128,384]{2,1,0:T(8,128)(2,1)S(1)} %get-tuple-element.17), channel_id=1, source_target_pairs={{0,4},{4,0},{8,12},{12,8},{16,20},{20,16},{24,28},{28,24},{32,36},... | collective-permute-start | bytes 1179656 | tf_op jit(solution)/shard_map/ppermute | solution.py:336
  64.2 0.9 fusion.4
  65.1 0.4 collective-permute-done.6.kvq_mate
  65.5 0.0 copy-done.4
  65.5 2.8 %shard_map.65 = (bf16[8,208,128]{2,1,0:T(8,128)(2,1)}, f32[4,16,128]{2,1,0:T(8,128)S(1)}) custom-call(s32[6]{0:T(128)S(1)} %stack.30.scal, bf16[4,128,256]{2,1,0:T(8,128)(2,1)S(1)} %get-tuple-element.15.kv_own, bf16[4,128,384]{2,1,0:T(8,128)(2,1)S(1)} %collective-permute-done.6.kvq_mate, bf16[64,128]{1,0:T(8,128)(2,1)S(1)} %get-tuple-element.19.ext_own, ...), custom_call_target="tpu_custom_call" | custom-call | tf_op jit(solution)/shard_map/pallas_call | solution.py:252
  68.4 10.2 %all-to-all-start.2 = ((bf16[8,208,128]{2,1,0:T(8,128)(2,1)}), bf16[8,208,128]{2,1,0:T(8,128)(2,1)S(1)}, u32[]{:S(2)}, u32[]{:S(2)}) async-start(bf16[8,208,128]{2,1,0:T(8,128)(2,1)} %get-tuple-element.20), calls=%async_computation.2 | async-start | bytes 851968 | tf_op jit(solution)/shard_map/all_to_all | solution.py:283
  78.6 5.1 %collective-permute-start.12 = (bf16[4,128,256]{2,1,0:T(8,128)(2,1)}, bf16[4,128,256]{2,1,0:T(8,128)(2,1)S(1)}, u32[]{:S(2)}, u32[]{:S(2)}) collective-permute-start(bf16[4,128,256]{2,1,0:T(8,128)(2,1)} %copy-done.9), channel_id=1, source_target_pairs={{4,16},{12,24},{16,4},{20,32},{24,12},{28,40},{32,20},{36,48},{40,... | collective-permute-start | bytes 786440 | tf_op jit(solution)/shard_map/ppermute | solution.py:342
  83.6 1.3 collective-permute-start.10
  84.9 4.3 %collective-permute-start.8 = (bf16[4,128,256]{2,1,0:T(8,128)(2,1)}, bf16[4,128,256]{2,1,0:T(8,128)(2,1)S(1)}, u32[]{:S(2)}, u32[]{:S(2)}) collective-permute-start(bf16[4,128,256]{2,1,0:T(8,128)(2,1)} %copy-done.9), channel_id=1, source_target_pairs={{0,12},{4,8},{8,20},{12,16},{16,28},{20,24},{24,36},{28,32},{32,44... | collective-permute-start | bytes 786440 | tf_op jit(solution)/shard_map/ppermute | solution.py:339
  89.2 5.2 %collective-permute-start.11 = (bf16[4,128,256]{2,1,0:T(8,128)(2,1)S(1)}, bf16[4,128,256]{2,1,0:T(8,128)(2,1)S(1)}, u32[]{:S(2)}, u32[]{:S(2)}) collective-permute-start(bf16[4,128,256]{2,1,0:T(8,128)(2,1)S(1)} %get-tuple-element.15.kv_own), channel_id=1, source_target_pairs={{4,20},{12,28},{16,0},{20,36},{24,8},{28,44},{32,16},{36,52},{40,2... | collective-permute-start | bytes 786440 | tf_op jit(solution)/shard_map/ppermute | solution.py:341
  94.4 1.3 collective-permute-start.9
  95.7 4.8 %collective-permute-done.12.h5.twx = bf16[4,128,256]{2,1,0:T(8,128)(2,1)S(1)} collective-permute-done((bf16[4,128,256]{2,1,0:T(8,128)(2,1)}, bf16[4,128,256]{2,1,0:T(8,128)(2,1)S(1)}, u32[]{:S(2)}, u32[]{:S(2)}) %collective-permute-start.12) | collective-permute-done | bytes 262176 | tf_op jit(solution)/shard_map/ppermute | solution.py:342
  100.5 1.3 collective-permute-start.7
  101.8 6.1 %collective-permute-done.10.h3.zmx = bf16[4,128,256]{2,1,0:T(8,128)(2,1)S(1)} collective-permute-done((bf16[4,128,256]{2,1,0:T(8,128)(2,1)}, bf16[4,128,256]{2,1,0:T(8,128)(2,1)S(1)}, u32[]{:S(2)}, u32[]{:S(2)}) %collective-permute-start.10) | collective-permute-done | bytes 262176 | tf_op jit(solution)/shard_map/ppermute | solution.py:340
  107.9 0.0 collective-permute-done.8.h1.zpx
  107.9 0.0 collective-permute-done.11.h4.tws
  107.9 5.4 %collective-permute-done.9.h2.zms = bf16[4,128,256]{2,1,0:T(8,128)(2,1)S(1)} collective-permute-done((bf16[4,128,256]{2,1,0:T(8,128)(2,1)S(1)}, bf16[4,128,256]{2,1,0:T(8,128)(2,1)S(1)}, u32[]{:S(2)}, u32[]{:S(2)}) %collective-permute-start.9) | collective-permute-done | bytes 262176 | tf_op jit(solution)/shard_map/ppermute | solution.py:338
  113.3 0.0 collective-permute-done.7.h0.zps
  113.3 0.0 all-to-all-done.2.got
  113.3 1.4 shard_map.66
  114.7 7.4 %all-to-all-start.3 = ((bf16[8,208,128]{2,1,0:T(8,128)(2,1)}), bf16[8,208,128]{2,1,0:T(8,128)(2,1)S(1)}, u32[]{:S(2)}, u32[]{:S(2)}) async-start(bf16[8,208,128]{2,1,0:T(8,128)(2,1)} %get-tuple-element.21), calls=%async_computation.3 | async-start | bytes 851968 | tf_op jit(solution)/shard_map/all_to_all | solution.py:283
  122.0 0.7 fusion.2
  122.8 0.1 min.12.pat
  122.9 14.2 %all-to-all-done.3.got = bf16[8,208,128]{2,1,0:T(8,128)(2,1)S(1)} async-done(((bf16[8,208,128]{2,1,0:T(8,128)(2,1)}), bf16[8,208,128]{2,1,0:T(8,128)(2,1)S(1)}, u32[]{:S(2)}, u32[]{:S(2)}) %all-to-all-start.3) | async-done | bytes 426016 | tf_op jit(solution)/shard_map/all_to_all | solution.py:283
  137.1 9.6 %shard_map.67 = bf16[8,128,128]{2,1,0:T(8,128)(2,1)S(1)} custom-call(s32[6]{0:T(128)S(1)} %stack.30.scal, s32[48]{0:T(128)S(1)} %min.12.pat, bf16[4,128,256]{2,1,0:T(8,128)(2,1)S(1)} %get-tuple-element.15.kv_own, bf16[4,128,128]{2,1,0:T(8,128)(2,1)S(1)} %copy-done.7, bf16[4,128,384]{2,1,0:T(8,128)(2,1)S(1)} %collective-permute-done.6.kvq_mate, ...), custom_call_target="tpu_custom_call" | custom-call | tf_op jit(solution)/shard_map/pallas_call | solution.py:252
  146.7 10.2 %all_to_all.25 = bf16[8,128,128]{2,1,0:T(8,128)(2,1)S(1)} all-to-all(bf16[8,128,128]{2,1,0:T(8,128)(2,1)S(1)} %shard_map.67), channel_id=1, replica_groups={{0,4,1,5,2,6,3,7},{8,12,9,13,10,14,11,15},{16,20,17,21,18,22,19,23},{24..., dimensions={0} | all-to-all | bytes 524288 | tf_op jit(solution)/shard_map/all_to_all | solution.py:283
  156.9 0.2 copy.13
  157.1 0.9 copy.14
  (17 shorter events, 0.1 us)
Async XLA Ops:
  0.0 53.8 %copy-start = (bf16[2048,3,256]{2,0,1:T(8,128)(2,1)S(1)}, bf16[2048,3,256]{2,0,1:T(8,128)(2,1)}, u32[]{:S(2)}) copy-start(bf16[2048,3,256]{2,0,1:T(8,128)(2,1)} %param.7) | copy-start | bytes 9437188
  2.9 31.7 %all-to-all-start = ((bf16[16,64,128]{2,1,0:T(8,128)(2,1)}), bf16[16,64,128]{2,1,0:T(8,128)(2,1)}, u32[]{:S(2)}, u32[]{:S(2)}) async-start(bf16[16,64,128]{2,1,0:T(8,128)(2,1)} %reshape.90), calls=%async_computation | async-start | bytes 524288 | tf_op jit(solution)/shard_map/all_to_all | solution.py:283
  13.7 14.1 %collective-permute-start.3 = (bf16[64,2048]{1,0:T(8,128)(2,1)}, bf16[64,2048]{1,0:T(8,128)(2,1)S(1)}, u32[]{:S(2)}, u32[]{:S(2)}) collective-permute-start(bf16[64,2048]{1,0:T(8,128)(2,1)} %get-tuple-element.25), channel_id=1, source_target_pairs={{0,3},{1,0},{2,1},{3,2},{4,7},{5,4},{6,5},{7,6},{8,11},{9,8},{10,9... | collective-permute-start | bytes 786440 | tf_op jit(solution)/shard_map/ppermute | solution.py:298
  15.9 37.9 %collective-permute-start.1 = (bf16[64,2048]{1,0:T(8,128)(2,1)}, bf16[64,2048]{1,0:T(8,128)(2,1)}, u32[]{:S(2)}, u32[]{:S(2)}) collective-permute-start(bf16[64,2048]{1,0:T(8,128)(2,1)} %get-tuple-element.25), channel_id=1, source_target_pairs={{0,1},{1,2},{2,3},{3,0},{4,5},{5,6},{6,7},{7,4},{8,9},{9,10},{10,1... | collective-permute-start | bytes 786440 | tf_op jit(solution)/shard_map/ppermute | solution.py:299
  19.0 34.8 %collective-permute-start.2 = (bf16[64,2048]{1,0:T(8,128)(2,1)}, bf16[64,2048]{1,0:T(8,128)(2,1)}, u32[]{:S(2)}, u32[]{:S(2)}) collective-permute-start(bf16[64,2048]{1,0:T(8,128)(2,1)} %get-tuple-element.26), channel_id=1, source_target_pairs={{0,3},{1,0},{2,1},{3,2},{4,7},{5,4},{6,5},{7,6},{8,11},{9,8},{10,9... | collective-permute-start | bytes 786440 | tf_op jit(solution)/shard_map/ppermute | solution.py:300
  22.4 10.2 %collective-permute-start = (bf16[64,2048]{1,0:T(8,128)(2,1)}, bf16[64,2048]{1,0:T(8,128)(2,1)}, u32[]{:S(2)}, u32[]{:S(2)}) collective-permute-start(bf16[64,2048]{1,0:T(8,128)(2,1)} %get-tuple-element.26), channel_id=1, source_target_pairs={{0,1},{1,2},{2,3},{3,0},{4,5},{5,6},{6,7},{7,4},{8,9},{9,10},{10,1... | collective-permute-start | bytes 786440 | tf_op jit(solution)/shard_map/ppermute | solution.py:297
  27.7 26.0 %copy-start.2 = (bf16[64,2048]{1,0:T(8,128)(2,1)}, bf16[64,2048]{1,0:T(8,128)(2,1)S(1)}, u32[]{:S(2)}) copy-start(bf16[64,2048]{1,0:T(8,128)(2,1)S(1)} %collective-permute-done.3.bb) | copy-start | bytes 786436
  27.7 26.0 %collective-permute-start.5 = (bf16[64,2048]{1,0:T(8,128)(2,1)S(1)}, bf16[64,2048]{1,0:T(8,128)(2,1)}, u32[]{:S(2)}, u32[]{:S(2)}) collective-permute-start(bf16[64,2048]{1,0:T(8,128)(2,1)S(1)} %collective-permute-done.3.bb), channel_id=1, source_target_pairs={{0,3},{1,0},{2,1},{3,2},{4,7},{5,4},{6,5},{7,6},{8,11},{9,8},{10,9... | collective-permute-start | bytes 786440 | tf_op jit(solution)/shard_map/ppermute | solution.py:302
  32.6 21.2 %collective-permute-start.4 = (bf16[64,2048]{1,0:T(8,128)(2,1)}, bf16[64,2048]{1,0:T(8,128)(2,1)}, u32[]{:S(2)}, u32[]{:S(2)}) collective-permute-start(bf16[64,2048]{1,0:T(8,128)(2,1)} %collective-permute-done.at), channel_id=1, source_target_pairs={{0,1},{1,2},{2,3},{3,0},{4,5},{5,6},{6,7},{7,4},{8,9},{9,10},{10,1... | collective-permute-start | bytes 786440 | tf_op jit(solution)/shard_map/ppermute | solution.py:301
  39.1 12.1 %all-to-all-start.1 = ((bf16[8,80,128]{2,1,0:T(8,128)(2,1)}), bf16[8,80,128]{2,1,0:T(8,128)(2,1)}, u32[]{:S(2)}, u32[]{:S(2)}) async-start(bf16[8,80,128]{2,1,0:T(8,128)(2,1)} %concatenate.11), calls=%async_computation.1 | async-start | bytes 327680 | tf_op jit(solution)/shard_map/all_to_all | solution.py:283
  53.8 1.0 copy-start.1
  54.9 0.9 copy-start.3
  55.8 9.7 %copy-start.4 = (bf16[8,128,16]{1,2,0:T(8,128)(2,1)S(1)}, bf16[8,128,16]{1,2,0:T(8,128)(2,1)}, u32[]{:S(2)}) copy-start(bf16[8,128,16]{1,2,0:T(8,128)(2,1)} %param.8) | copy-start | bytes 98308
  61.2 7.2 %copy-start.6 = (bf16[4,128,128]{2,1,0:T(8,128)(2,1)}, bf16[4,128,128]{2,1,0:T(8,128)(2,1)S(1)}, u32[]{:S(2)}) copy-start(bf16[4,128,128]{2,1,0:T(8,128)(2,1)S(1)} %get-tuple-element.16.q_own) | copy-start | bytes 393220
  61.2 7.2 %copy-start.9 = (bf16[4,128,256]{2,1,0:T(8,128)(2,1)}, bf16[4,128,256]{2,1,0:T(8,128)(2,1)S(1)}, u32[]{:S(2)}) copy-start(bf16[4,128,256]{2,1,0:T(8,128)(2,1)S(1)} %get-tuple-element.18) | copy-start | bytes 786436
  61.2 75.8 %copy-start.5 = (bf16[8,128,16]{1,2,0:T(8,128)(2,1)S(1)}, bf16[8,128,16]{1,2,0:T(8,128)(2,1)}, u32[]{:S(2)}) copy-start(bf16[8,128,16]{1,2,0:T(8,128)(2,1)} %param.8) | copy-start | bytes 98308
  61.2 75.8 %copy-start.8 = (f32[1024]{0:T(1024)S(1)}, f32[1024]{0:T(1024)}, u32[]{:S(2)}) copy-start(f32[1024]{0:T(1024)} %param.9) | copy-start | bytes 12292
  61.3 4.3 %collective-permute-start.6 = (bf16[4,128,384]{2,1,0:T(8,128)(2,1)S(1)}, bf16[4,128,384]{2,1,0:T(8,128)(2,1)S(1)}, u32[]{:S(2)}, u32[]{:S(2)}) collective-permute-start(bf16[4,128,384]{2,1,0:T(8,128)(2,1)S(1)} %get-tuple-element.17), channel_id=1, source_target_pairs={{0,4},{4,0},{8,12},{12,8},{16,20},{20,16},{24,28},{28,24},{32,36},... | collective-permute-start | bytes 1179656 | tf_op jit(solution)/shard_map/ppermute | solution.py:336
  68.4 68.7 %copy-start.7 = (bf16[4,128,128]{2,1,0:T(8,128)(2,1)S(1)}, bf16[4,128,128]{2,1,0:T(8,128)(2,1)}, u32[]{:S(2)}) copy-start(bf16[4,128,128]{2,1,0:T(8,128)(2,1)} %copy-done.6) | copy-start | bytes 393220
  68.4 44.9 %all-to-all-start.2 = ((bf16[8,208,128]{2,1,0:T(8,128)(2,1)}), bf16[8,208,128]{2,1,0:T(8,128)(2,1)S(1)}, u32[]{:S(2)}, u32[]{:S(2)}) async-start(bf16[8,208,128]{2,1,0:T(8,128)(2,1)} %get-tuple-element.20), calls=%async_computation.2 | async-start | bytes 851968 | tf_op jit(solution)/shard_map/all_to_all | solution.py:283
  78.6 22.0 %collective-permute-start.12 = (bf16[4,128,256]{2,1,0:T(8,128)(2,1)}, bf16[4,128,256]{2,1,0:T(8,128)(2,1)S(1)}, u32[]{:S(2)}, u32[]{:S(2)}) collective-permute-start(bf16[4,128,256]{2,1,0:T(8,128)(2,1)} %copy-done.9), channel_id=1, source_target_pairs={{4,16},{12,24},{16,4},{20,32},{24,12},{28,40},{32,20},{36,48},{40,... | collective-permute-start | bytes 786440 | tf_op jit(solution)/shard_map/ppermute | solution.py:342
  83.6 24.2 %collective-permute-start.10 = (bf16[4,128,256]{2,1,0:T(8,128)(2,1)}, bf16[4,128,256]{2,1,0:T(8,128)(2,1)S(1)}, u32[]{:S(2)}, u32[]{:S(2)}) collective-permute-start(bf16[4,128,256]{2,1,0:T(8,128)(2,1)} %copy-done.9), channel_id=1, source_target_pairs={{8,4},{12,0},{16,12},{20,8},{24,20},{28,16},{32,28},{36,24},{40,36... | collective-permute-start | bytes 786440 | tf_op jit(solution)/shard_map/ppermute | solution.py:340
  84.9 23.0 %collective-permute-start.8 = (bf16[4,128,256]{2,1,0:T(8,128)(2,1)}, bf16[4,128,256]{2,1,0:T(8,128)(2,1)S(1)}, u32[]{:S(2)}, u32[]{:S(2)}) collective-permute-start(bf16[4,128,256]{2,1,0:T(8,128)(2,1)} %copy-done.9), channel_id=1, source_target_pairs={{0,12},{4,8},{8,20},{12,16},{16,28},{20,24},{24,36},{28,32},{32,44... | collective-permute-start | bytes 786440 | tf_op jit(solution)/shard_map/ppermute | solution.py:339
  89.2 18.7 %collective-permute-start.11 = (bf16[4,128,256]{2,1,0:T(8,128)(2,1)S(1)}, bf16[4,128,256]{2,1,0:T(8,128)(2,1)S(1)}, u32[]{:S(2)}, u32[]{:S(2)}) collective-permute-start(bf16[4,128,256]{2,1,0:T(8,128)(2,1)S(1)} %get-tuple-element.15.kv_own), channel_id=1, source_target_pairs={{4,20},{12,28},{16,0},{20,36},{24,8},{28,44},{32,16},{36,52},{40,2... | collective-permute-start | bytes 786440 | tf_op jit(solution)/shard_map/ppermute | solution.py:341
  94.4 18.8 %collective-permute-start.9 = (bf16[4,128,256]{2,1,0:T(8,128)(2,1)S(1)}, bf16[4,128,256]{2,1,0:T(8,128)(2,1)S(1)}, u32[]{:S(2)}, u32[]{:S(2)}) collective-permute-start(bf16[4,128,256]{2,1,0:T(8,128)(2,1)S(1)} %get-tuple-element.15.kv_own), channel_id=1, source_target_pairs={{8,0},{12,4},{16,8},{20,12},{24,16},{28,20},{32,24},{36,28},{40,32... | collective-permute-start | bytes 786440 | tf_op jit(solution)/shard_map/ppermute | solution.py:338
  100.5 12.8 %collective-permute-start.7 = (bf16[4,128,256]{2,1,0:T(8,128)(2,1)S(1)}, bf16[4,128,256]{2,1,0:T(8,128)(2,1)S(1)}, u32[]{:S(2)}, u32[]{:S(2)}) collective-permute-start(bf16[4,128,256]{2,1,0:T(8,128)(2,1)S(1)} %get-tuple-element.15.kv_own), channel_id=1, source_target_pairs={{0,8},{4,12},{8,16},{12,20},{16,24},{20,28},{24,32},{28,36},{32,40... | collective-permute-start | bytes 786440 | tf_op jit(solution)/shard_map/ppermute | solution.py:337
  114.7 22.4 %all-to-all-start.3 = ((bf16[8,208,128]{2,1,0:T(8,128)(2,1)}), bf16[8,208,128]{2,1,0:T(8,128)(2,1)S(1)}, u32[]{:S(2)}, u32[]{:S(2)}) async-start(bf16[8,208,128]{2,1,0:T(8,128)(2,1)} %get-tuple-element.21), calls=%async_computation.3 | async-start | bytes 851968 | tf_op jit(solution)/shard_map/all_to_all | solution.py:283

commit v3 on v2

--- a/solution.py
+++ b/solution.py
@@ -56,25 +56,57 @@
     return mm(steps, jnp.where(row <= col, 1.0, 0.0).astype(F32), HIGH)
 
 
+def top_kernel(tokens, out):
+    out[...] = tokens[0]
+
+
+def pack_kernel(pat, rows, steps, out):
+    part = rows[...].astype(F32)[:8]
+    body = [
+        jnp.concatenate([part[:, 256 * k : 256 * k + 128], part[:, 256 * k + 128 : 256 * k + 256]], axis=0).astype(BF)
+        for k in range(8)
+    ]
+    lane = lax.broadcasted_iota(jnp.int32, (1, TOK), 1)
+    row = lax.broadcasted_iota(jnp.int32, (16, TOK), 0)
+    wanted = jnp.zeros((1, TOK), jnp.int32)
+    for i in range(6):
+        wanted = jnp.where(lane == i, pat[0, i // 3, i % 3], wanted)
+    wanted = wanted.astype(F32)
+    hi, mid, lo = (p.astype(F32) for p in split3(steps[0]))
+    for peer in range(8):
+        for k in range(8):
+            out[peer, 16 * k : 16 * k + 16] = body[k]
+        here = slice(peer, peer + 1)
+        tail = jnp.where(row == 0, hi[here], jnp.where(row == 1, mid[here], jnp.where(row == 2, lo[here], wanted)))
+        out[peer, 128:144] = tail.astype(BF)
+
+
 def project_kernel(
-    scal, t0, at, ab, bt, bb, dt, db, ext, w, kv_own, kv_other, kvq_other, q_own, ext_own, rows, wv, sems
+    scal, t0, ta, tb, dt, db, got, w, kv_own, kv_other, kvq_other, q_own, ext_own, steps, rows, wv, sems
 ):
     c, x = scal[0], scal[1]
-    places = [(t0, 0, 128), (at, 128, 64), (ab, 192, 64), (bt, 384, 64), (bb, 448, 64), (ext, 512, 32), (dt, 256, 64), (db, 320, 64)]
-    copies = [pltpu.make_async_copy(w.at[0], wv.at[0], sems.at[8])]
-    copies += [
+    places = [(t0.at[0], 0, 128), (ta, 128, 128), (tb, 384, 128), (dt, 256, 64), (db, 320, 64)]
+    copies = [
         pltpu.make_async_copy(ref, rows.at[pl.ds(start, size)], sems.at[i])
         for i, (ref, start, size) in enumerate(places)
     ]
-    copies += [pltpu.make_async_copy(w.at[k], wv.at[k], sems.at[8 + k]) for k in (1, 2)]
+    copies += [pltpu.make_async_copy(w.at[k], wv.at[k], sems.at[5 + k]) for k in range(3)]
     for copy in copies:
         copy.start()
+    for pair in range(2):
+        two = [got[4 * pair + 2 * i, 0:128].astype(F32) for i in range(2)]
+        for l in range(16):
+            rows[512 + 16 * pair : 528 + 16 * pair, 128 * l : 128 * l + 128] = jnp.concatenate(
+                [p[8 * l : 8 * l + 8] for p in two], axis=0
+            ).astype(BF)
+    for i in range(8):
+        tail = got[i, 128:144].astype(F32)
+        steps[i : i + 1] = (tail[0:1] + tail[1:2]) + tail[2:3]
     first = c == 0
-    for copy in copies[:9]:
+    for copy in copies[:5]:
         copy.wait()
     for k in range(3):
-        if k:
-            copies[8 + k].wait()
+        copies[5 + k].wait()
         part = mm(rows[...], wv[k]).astype(BF)
         for r in range(DOCS):
             n = lax.rem(x - r + DOCS, DOCS)
@@ -143,7 +175,7 @@
     return state, decay, wide
 
 
-def row_kernel(scal, got, h0, h1, h2, h3, h4, h5, out, inner, outer):
+def row_kernel(scal, got, out, inner, outer):
     z = scal[3]
     total = jnp.zeros((64, TOK), F32)
     before = jnp.zeros((64, TOK), F32)
@@ -165,10 +197,10 @@
 
 
 def attend_kernel(
-    scal, pat, kv_own, q_own, kvq_mate, zps, zpx, zms, zmx, tws, twx, got, inner, outer,
-    state0, steps, wft, gain, out, win, qs,
+    scal, pat, kv_own, q_own, kvq_mate, zps, zpx, zms, zmx, tws, twx, steps, wft,
+    sparse, stats, local, phis, queried, win, qs,
 ):
-    c, q, y, h = scal[0], scal[2], scal[4], scal[5]
+    c, q, h = scal[0], scal[2], scal[5]
     mate = 1 - c
     for n in range(DOCS):
         win[n, 3 + c] = kv_own[n]
@@ -182,20 +214,64 @@
         qs[n, c] = q_own[n]
         qs[n, mate] = kvq_mate[n, :, 2 * DH :]
 
-    before = jnp.zeros((64, TOK), F32)
-    for peer in range(8):
-        state, _, wide = get_states(got, peer)
-        before = jnp.where(peer < y, before * jnp.exp(wide) + state, before)
-    entering = inner[...] + outer[...] * before
-
     cum = cumulative_of(steps[...])
     cum_t = cum.T
     feature = wft[h]
     row = lax.broadcasted_iota(jnp.int32, (TOK, TOK), 0)
     col = lax.broadcasted_iota(jnp.int32, (TOK, TOK), 1)
     causal = row >= col
+    lane = lax.broadcasted_iota(jnp.int32, (1, 6 * BS), 1)
+    first = lax.broadcasted_iota(jnp.int32, (BS, DH), 1) == 0
+    scale = DH ** (-0.5)
+    for n in range(DOCS):
+        for s in range(2):
+            line = cum[2 * n + s : 2 * n + s + 1]
+            column = cum_t[:, 2 * n + s : 2 * n + s + 1]
+            queries = qs[n, s]
+            queried[2 * n + s] = queries
+            keys = win[n, 3 + s, :, :DH]
+            values = win[n, 3 + s, :, DH:]
+            phi_q = softmax0(nt(feature, queries)).astype(BF).astype(F32)
+            phis[2 * n + s] = phi_q
+            phi_k = softmax0(nt(feature, keys)).astype(BF)
+            decay = jnp.where(causal, jnp.exp(jnp.minimum(column - line, 0.0)), 0.0)
+            mixing = (mm(phi_q.T.astype(BF), phi_k) * decay).astype(BF)
+            local[2 * n + s] = mm(mixing, values)
+            for half in range(2):
+                j = 2 * s + half
+                block = 4 * q + j
+                picks = [
+                    win[n, 3 + (j + d) // 2, pl.ds(BS * ((j + d) % 2), BS)] for d in (-1, 0, 1)
+                ]
+                for k in range(R):
+                    place = pat[12 * n + 3 * j + k]
+                    picks.append(
+                        win[n, lax.div(place, 2), pl.ds(pl.multiple_of(BS * lax.rem(place, 2), BS), BS)]
+                    )
+                near = jnp.concatenate(picks, axis=0)
+                scores = nt(queries[half * BS : half * BS + BS], near[:, :DH]) * scale
+                bad = (
+                    ((lane < BS) & (block < 2))
+                    | ((lane >= BS) & (lane < 2 * BS) & (block < 1))
+                    | ((lane >= 2 * BS) & (lane < 3 * BS) & (block > 4 * CHIPS - 2))
+                )
+                scores = jnp.where(bad, MASKED, scores)
+                top = jnp.max(scores, axis=1, keepdims=True)
+                e = jnp.exp(scores - top)
+                here = slice(half * BS, half * BS + BS)
+                sparse[2 * n + s, here] = mm(e.astype(BF), near[:, DH:])
+                stats[2 * n + s, here] = jnp.where(first, top, jnp.sum(e, axis=1, keepdims=True))
+
+
+def finish_kernel(scal, got, inner, outer, state0, steps, gain, sparse, stats, local, phis, queried, out):
+    y, h = scal[4], scal[5]
+    before = jnp.zeros((64, TOK), F32)
+    for peer in range(8):
+        state, _, wide = get_states(got, peer)
+        before = jnp.where(peer < y, before * jnp.exp(wide) + state, before)
+    entering = inner[...] + outer[...] * before
+    cum = cumulative_of(steps[...])
     gains = gain[h]
-    lane = lax.broadcasted_iota(jnp.int32, (1, 7 * BS), 1)
     scale = DH ** (-0.5)
     for n in range(DOCS):
         carried = entering[F * n : F * n + F]
@@ -206,56 +282,36 @@
             for at in (144, 176)
         ]
         for s in range(2):
-            line = cum[2 * n + s : 2 * n + s + 1]
-            column = cum_t[:, 2 * n + s : 2 * n + s + 1]
-            queries = qs[n, s]
-            keys = win[n, 3 + s, :, :DH]
-            values = win[n, 3 + s, :, DH:]
-            phi_q = softmax0(nt(feature, queries)).astype(BF).astype(F32).T
-            phi_k = softmax0(nt(feature, keys)).astype(BF)
-            decay = jnp.where(causal, jnp.exp(jnp.minimum(column - line, 0.0)), 0.0)
-            mixing = (mm(phi_q.astype(BF), phi_k) * decay).astype(BF)
-            linear = mm(mixing, values) + mm(phi_q, carried, HIGH) * jnp.exp(column)
+            i = 2 * n + s
+            scores = nt(queried[i], glob[0]) * scale
+            stat = stats[i]
+            top, total = stat[:, 0:1], stat[:, 1:2]
+            peak = jnp.maximum(top, jnp.max(scores, axis=1, keepdims=True))
+            shrink = jnp.exp(top - peak)
+            e = jnp.exp(scores - peak)
+            total = total * shrink + jnp.sum(e, axis=1, keepdims=True)
+            attended = (sparse[i] * shrink + mm(e.astype(BF), glob[1])) / total
+            line = cum[i : i + 1]
+            weighted = (phis[i] * jnp.exp(line)).T
+            linear = local[i] + mm(weighted, carried, HIGH)
             carried = jnp.exp(line[:, TOK - 1 :]) * carried + state0[n]
             square = jnp.mean(linear * linear, axis=1, keepdims=True)
             normed = linear * lax.rsqrt(square + EPS) * gains
-            for half in range(2):
-                j = 2 * s + half
-                block = 4 * q + j
-                picks = [win[n, 3 + (j + d) // 2 if j + d >= 0 else 2, pl.ds(BS * ((j + d) % 2), BS)] for d in (-1, 0, 1)]
-                for k in range(R):
-                    place = pat[12 * n + 3 * j + k]
-                    picks.append(
-                        win[n, lax.div(place, 2), pl.ds(pl.multiple_of(BS * lax.rem(place, 2), BS), BS)]
-                    )
-                near = jnp.concatenate(picks, axis=0)
-                all_k = jnp.concatenate([near[:, :DH], glob[0]], axis=0)
-                all_v = jnp.concatenate([near[:, DH:], glob[1]], axis=0)
-                scores = nt(queries[half * BS : half * BS + BS], all_k) * scale
-                bad = (
-                    ((lane < BS) & (block < 2))
-                    | ((lane >= BS) & (lane < 2 * BS) & (block < 1))
-                    | ((lane >= 2 * BS) & (lane < 3 * BS) & (block > 4 * CHIPS - 2))
-                )
-                scores = jnp.where(bad, MASKED, scores)
-                top = jnp.max(scores, axis=1, keepdims=True)
-                e = jnp.exp(scores - top)
-                soft = (e / jnp.sum(e, axis=1, keepdims=True)).astype(BF)
-                sparse = mm(soft, all_v)
-                out[2 * n + s, half * BS : half * BS + BS] = (
-                    normed[half * BS : half * BS + BS] + sparse
-                ).astype(BF)
-
-
-def call(kernel, outs, scratch, spaces, *args):
-    kinds = {"s": pltpu.SMEM, "v": pltpu.VMEM, "a": pl.ANY}
+            out[i] = (normed + attended).astype(BF)
+
+
+def call(kernel, outs, scratch, spaces, micros, room, *args):
+    kinds = {"s": pltpu.SMEM, "v": pltpu.VMEM, "a": pl.ANY, "h": pltpu.HBM}
     return pl.pallas_call(
         kernel,
         out_shape=outs,
         in_specs=[pl.BlockSpec(memory_space=kinds[k]) for k in spaces],
         out_specs=[pl.BlockSpec(memory_space=pltpu.VMEM)] * len(outs),
         scratch_shapes=scratch,
-        compiler_params=pltpu.CompilerParams(vmem_limit_bytes=28 * 2**20),
+        compiler_params=pltpu.CompilerParams(vmem_limit_bytes=room * 2**20),
+        cost_estimate=pl.CostEstimate(
+            flops=int(micros * 1e9), bytes_accessed=int(micros * 3e6), transcendentals=0
+        ),
     )(*args)
 
 
@@ -293,30 +349,39 @@
     t0 = tokens[0]
     up = [(i, (i + 1) % 4) for i in range(4)]
     down = [(i, (i - 1) % 4) for i in range(4)]
-    top, bottom = t0[:64], t0[64:]
-    at = lax.ppermute(top, "fsdp", up)
-    bb = lax.ppermute(bottom, "fsdp", down)
-    ab = lax.ppermute(bottom, "fsdp", up)
-    bt = lax.ppermute(top, "fsdp", down)
-    dt = lax.ppermute(at, "fsdp", up)
-    db = lax.ppermute(bb, "fsdp", down)
-
-    scattered = exchange(top.reshape(16, 64, TOK), "seq", YC)[0]
-    three = split3(log_decay[0])
-    wanted = jnp.broadcast_to(
-        jnp.pad(pattern.reshape(1, 6).astype(BF), ((0, 0), (0, TOK - 6))), (8, TOK)
-    )
-    small = jnp.stack([*three, wanted] + [jnp.zeros((8, TOK), BF)] * 12, axis=1)
-    small = jnp.concatenate([small, jnp.broadcast_to(scattered[None], (8, 64, TOK))], axis=1)
-    got0 = exchange(small, ("seq", "fsdp"), XC)
-    steps = (got0[:, 0].astype(F32) + got0[:, 1].astype(F32)) + got0[:, 2].astype(F32)
-    pat = got0[:, 3, :6].astype(jnp.int32).reshape(48) - (4 * q - 6)
+    ta = lax.ppermute(t0, "fsdp", up)
+    tb = lax.ppermute(t0, "fsdp", down)
+    dt = lax.ppermute(ta[:64], "fsdp", up)
+    db = lax.ppermute(tb[64:], "fsdp", down)
+
+    top = pl.pallas_call(
+        top_kernel,
+        grid=(1,),
+        out_shape=shape((64, D), BF),
+        in_specs=[pl.BlockSpec((1, 64, D), lambda i: (0, 0, 0))],
+        out_specs=pl.BlockSpec((64, D), lambda i: (0, 0)),
+        cost_estimate=pl.CostEstimate(flops=10**10, bytes_accessed=3 * 10**7, transcendentals=0),
+    )(tokens)
+    scattered = exchange(top, "seq", YS)
+    packed = pl.pallas_call(
+        pack_kernel,
+        grid=(1,),
+        out_shape=shape((8, 144, TOK), BF),
+        in_specs=[
+            pl.BlockSpec(memory_space=pltpu.SMEM),
+            pl.BlockSpec((16, D), lambda i: (0, 0)),
+            pl.BlockSpec((1, 8, TOK), lambda i: (0, 0, 0)),
+        ],
+        out_specs=pl.BlockSpec((8, 144, TOK), lambda i: (0, 0, 0)),
+        cost_estimate=pl.CostEstimate(flops=10**10, bytes_accessed=3 * 10**7, transcendentals=0),
+    )(pattern, scattered, log_decay)
+    got0 = exchange(packed, ("seq", "fsdp"), XC)
+    pat = got0[:, 131, :6].astype(jnp.int32).reshape(48) - (4 * q - 6)
     pat = jnp.clip(pat, 0, 15).astype(jnp.int32)
-    ext = got0[:, 16:].reshape(32, D)
 
     w3 = w_qkv.transpose(1, 0, 2)
     wft = w_feature.transpose(0, 2, 1)
-    kv_own, kv_other, kvq_other, q_own, ext_own = call(
+    kv_own, kv_other, kvq_other, q_own, ext_own, steps = call(
         project_kernel,
         [
             shape((DOCS, TOK, 2 * DH), BF),
@@ -324,14 +389,17 @@
             shape((DOCS, TOK, 3 * DH), BF),
             shape((DOCS, TOK, DH), BF),
             shape((64, DH), BF),
+            shape((8, TOK), F32),
         ],
         [
             pltpu.VMEM((4 * TOK + 32, D), BF),
             pltpu.VMEM((3, D, 2 * DH), BF),
-            pltpu.SemaphoreType.DMA((11,)),
+            pltpu.SemaphoreType.DMA((8,)),
         ],
-        "saaaaaaaaa",
-        scal, t0, at, ab, bt, bb, dt, db, ext, w3,
+        "shhhhhvh",
+        3,
+        16,
+        scal, tokens, ta, tb, dt, db, got0, w3,
     )
     kvq_mate = lax.ppermute(kvq_other, "seq", pairs(lambda q, c: (q, 1 - c)))
     zps = lax.ppermute(kv_own, "seq", pairs(lambda q, c: (q + 1, c)))
@@ -347,6 +415,8 @@
         [shape((8, ROWS, TOK), BF), shape((DOCS, F, DH), F32)],
         [],
         "svvvvv",
+        30,
+        6,
         scal, kv_own, kvq_mate, ext_own, steps, wft,
     )
     got1 = exchange(send1, "seq", ZS)
@@ -354,18 +424,36 @@
         row_kernel,
         [shape((8, ROWS, TOK), BF), shape((64, TOK), F32), shape((64, TOK), F32)],
         [],
-        "sv" + "a" * 6,
-        scal, got1, *halo,
+        "sv",
+        1,
+        4,
+        scal, got1,
     )
     got2 = exchange(send2, "seq", YS)
-
+    sparse, stats, local, phis, queried = call(
+        attend_kernel,
+        [
+            shape((8, TOK, DH), F32),
+            shape((8, TOK, DH), F32),
+            shape((8, TOK, DH), F32),
+            shape((8, F, TOK), F32),
+            shape((8, TOK, DH), BF),
+        ],
+        [pltpu.VMEM((DOCS, 8, TOK, 2 * DH), BF), pltpu.VMEM((DOCS, 2, TOK, DH), BF)],
+        "ss" + "v" * 11,
+        8,
+        14,
+        scal, pat, kv_own, q_own, kvq_mate, *halo, steps, wft,
+    )
     [out] = call(
-        attend_kernel,
+        finish_kernel,
         [shape((8, TOK, DH), BF)],
-        [pltpu.VMEM((DOCS, 8, TOK, 2 * DH), BF), pltpu.VMEM((DOCS, 2, TOK, DH), BF)],
-        "ss" + "v" * 16,
-        scal, pat, kv_own, q_own, kvq_mate, *halo, got2, inner, outer,
-        state0, steps, wft, norm_gain.reshape(HALF_HEADS, 1, DH),
+        [],
+        "s" + "v" * 11,
+        2,
+        10,
+        scal, got2, inner, outer, state0, steps, norm_gain.reshape(HALF_HEADS, 1, DH),
+        sparse, stats, local, phis, queried,
     )
     mixed = exchange(out, ("seq", "fsdp"), XC)
     return mixed.transpose(1, 0, 2).reshape(1, TOK, HD)

time: 159 us -> 138 us (0.87)
  waiting for transfers between devices: 36.8 us -> 17.5 us
  local copies, waits for them, and re-layouts: 14.1 us -> 9.38 us
  Pallas kernels: 19.2 us -> 23.4 us
  other arithmetic: 4.07 us -> 0.03 us
  blocking collectives: 10.2 us -> 13.1 us
    all_to_all x4, waiting for transfers between devices: 19.8 us -> 11.3 us  [exchange(): return lax.all_to_all(a, axis, 0, 0, tiled=True, axis_index_groups=groups)]
    unnamed x20 -> x22, local copies, waits for them, and re-layouts: 2.02 us -> 8.15 us
    ppermute x1, waiting for transfers between devices: 6.05 us -> 0.01 us  [per_device(): zmx = lax.ppermute(kv_other, 'seq', pairs(lambda q, c: (q - 1, 1 - c)))]
    ppermute x1, waiting for transfers between devices: 5.39 us -> 0.01 us  [per_device(): zms = lax.ppermute(kv_own, 'seq', pairs(lambda q, c: (q - 1, c)))]
    slice x3 -> x2, local copies, waits for them, and re-layouts: 4.48 us -> 0.04 us  [the longest x1 0.02 us: per_device(): dt = lax.ppermute(ta[:64], 'fsdp', up)]
    all_to_all x4, starting transfers between devices: 34.8 us -> 38.5 us  [exchange(): return lax.all_to_all(a, axis, 0, 0, tiled=True, axis_index_groups=groups)]
    ppermute x6 -> x4, starting transfers between devices: 17.1 us -> 13.6 us  [the longest x1 5.21 us: per_device(): tb = lax.ppermute(t0, 'fsdp', down)]
    pallas_call x0 -> x2, Pallas kernels: none -> 3.33 us  [the longest x1 1.68 us: per_device(): pl.pallas_call(top_kernel, grid=(1,), out_shape=shape((64, D), BF), in_sp...]
  transfers between devices with their start and end apart: 17 -> 15, of which waited for: 7 -> 5; matrix products, arithmetic and copies ran while one was open for 8% -> 0% of each run, Pallas kernels for 0% -> 9%
where the time goes in v3:
time: 138 us; the launch traced here: 137 us
  starting transfers between devices  73.6 us (53%)
  Pallas kernels  23.4 us (17%)
  waiting for transfers between devices  17.5 us (13%)
  blocking collectives  13.1 us (9%)
  local copies, waits for them, and re-layouts  9.38 us (7%)
    all_to_all x4, starting transfers between devices, exchange(): return lax.all_to_all(a, axis, 0, 0, tiled=True, axis_index_groups=groups)  38.5 us
    pallas_call x5, Pallas kernels, call(): pl.pallas_call(kernel, out_shape=outs, in_specs=[pl.BlockSpec(memory_spac...  20.1 us
    all_to_all x1, blocking collectives, exchange(): return lax.all_to_all(a, axis, 0, 0, tiled=True, axis_index_groups=groups)  13.1 us
    all_to_all x4, waiting for transfers between devices, exchange(): return lax.all_to_all(a, axis, 0, 0, tiled=True, axis_index_groups=groups)  11.3 us
    unnamed x22, local copies, waits for them, and re-layouts  8.15 us
    ppermute x1, starting transfers between devices, per_device(): tb = lax.ppermute(t0, 'fsdp', down)  5.21 us
    ppermute x1, starting transfers between devices, per_device(): lax.ppermute(kv_own, 'seq', pairs(lambda q, c: (q + 2, 1) if c else (q -...  5.2 us
    ppermute x1, starting transfers between devices, per_device(): lax.ppermute(kv_other, 'seq', pairs(lambda q, c: (q + 2, 0) if c else (q...  5.08 us
  transfers between devices with their start and end apart: 15, of which 5 were waited for; matrix products, arithmetic and copies ran while one was open for 0% of the time, Pallas kernels for 9%

profile of v3, /device:TPU:1, one launch (start us, length us, event | category | flops | bytes accessed | tf_op | source)
XLA Modules:
  0.0 137.3 jit_solution(12082864707302817525)
XLA Ops:
  0.0 5.2 %collective-permute-start.1 = (bf16[128,2048]{1,0:T(8,128)(2,1)}, bf16[128,2048]{1,0:T(8,128)(2,1)S(1)}, u32[]{:S(2)}, u32[]{:S(2)}) collective-permute-start(bf16[128,2048]{1,0:T(8,128)(2,1)} %bitcast.15), channel_id=1, source_target_pairs={{0,3},{1,0},{2,1},{3,2},{4,7},{5,4},{6,5},{7,6},{8,11},{9,8},{10,9... | collective-permute-start | bytes 1572872 | tf_op jit(solution)/shard_map/ppermute | solution.py:353
  5.2 1.9 %collective-permute-start = (bf16[128,2048]{1,0:T(8,128)(2,1)}, bf16[128,2048]{1,0:T(8,128)(2,1)S(1)}, u32[]{:S(2)}, u32[]{:S(2)}) collective-permute-start(bf16[128,2048]{1,0:T(8,128)(2,1)} %bitcast.16), channel_id=1, source_target_pairs={{0,1},{1,2},{2,3},{3,0},{4,5},{5,6},{6,7},{7,4},{8,9},{9,10},{10,1... | collective-permute-start | bytes 1572872 | tf_op jit(solution)/shard_map/ppermute | solution.py:352
  7.1 1.7 %shard_map.64 = bf16[64,2048]{1,0:T(8,128)(2,1)} custom-call(bf16[1,128,2048]{2,1,0:T(8,128)(2,1)} %t0.1), custom_call_target="tpu_custom_call" | custom-call | flops 10000000000 | bytes 30000000 | tf_op jit(solution)/shard_map/pallas_call | solution.py:357
  8.8 6.8 %all-to-all-start = ((bf16[8,8,2048]{2,1,0:T(8,128)(2,1)}), bf16[8,8,2048]{2,1,0:T(8,128)(2,1)S(1)}, u32[]{:S(2)}, u32[]{:S(2)}) async-start(bf16[8,8,2048]{2,1,0:T(8,128)(2,1)} %bitcast.23), calls=%async_computation | async-start | bytes 524288 | tf_op jit(solution)/shard_map/all_to_all | solution.py:339
  15.6 0.0 collective-permute-done.1.tb
  15.7 4.6 %collective-permute-start.3 = (bf16[64,2048]{1,0:T(8,128)(2,1)S(1)}, bf16[64,2048]{1,0:T(8,128)(2,1)S(1)}, u32[]{:S(2)}, u32[]{:S(2)}) collective-permute-start(bf16[64,2048]{1,0:T(8,128)(2,1)S(1)} %slice.13), channel_id=1, source_target_pairs={{0,3},{1,0},{2,1},{3,2},{4,7},{5,4},{6,5},{7,6},{8,11},{9,8},{10,9... | collective-permute-start | bytes 786440 | tf_op jit(solution)/shard_map/ppermute | solution.py:355
  20.3 0.0 collective-permute-done.ta
  20.3 1.9 %collective-permute-start.2 = (bf16[64,2048]{1,0:T(8,128)(2,1)S(1)}, bf16[64,2048]{1,0:T(8,128)(2,1)S(1)}, u32[]{:S(2)}, u32[]{:S(2)}) collective-permute-start(bf16[64,2048]{1,0:T(8,128)(2,1)S(1)} %slice.12), channel_id=1, source_target_pairs={{0,1},{1,2},{2,3},{3,0},{4,5},{5,6},{6,7},{7,4},{8,9},{9,10},{10,1... | collective-permute-start | bytes 786440 | tf_op jit(solution)/shard_map/ppermute | solution.py:354
  22.2 2.7 %all-to-all-done = bf16[8,8,2048]{2,1,0:T(8,128)(2,1)S(1)} async-done(((bf16[8,8,2048]{2,1,0:T(8,128)(2,1)}), bf16[8,8,2048]{2,1,0:T(8,128)(2,1)S(1)}, u32[]{:S(2)}, u32[]{:S(2)}) %all-to-all-start) | async-done | bytes 262176 | tf_op jit(solution)/shard_map/all_to_all | solution.py:339
  24.9 0.0 copy-start.10
  24.9 0.7 copy-done.10
  25.6 0.0 copy-start.1
  25.6 1.7 %shard_map.65 = bf16[8,144,128]{2,1,0:T(8,128)(2,1)} custom-call(s32[1,2,3]{2,1,0:T(2,128)} %pat.1, bf16[64,2048]{1,0:T(8,128)(2,1)} %bitcast.22, f32[1,8,128]{2,1,0:T(8,128)} %steps.1), custom_call_target="tpu_custom_call" | custom-call | flops 10000000000 | bytes 30000000 | tf_op jit(solution)/shard_map/pallas_call | solution.py:366
  27.3 7.8 %all-to-all-start.1 = ((bf16[8,144,128]{2,1,0:T(8,128)(2,1)}), bf16[8,144,128]{2,1,0:T(8,128)(2,1)S(1)}, u32[]{:S(2)}, u32[]{:S(2)}) async-start(bf16[8,144,128]{2,1,0:T(8,128)(2,1)} %shard_map.65), calls=%async_computation.1 | async-start | bytes 589824 | tf_op jit(solution)/shard_map/all_to_all | solution.py:339
  35.1 0.1 stack.27.scal
  35.1 6.7 %all-to-all-done.1.got = bf16[8,144,128]{2,1,0:T(8,128)(2,1)S(1)} async-done(((bf16[8,144,128]{2,1,0:T(8,128)(2,1)}), bf16[8,144,128]{2,1,0:T(8,128)(2,1)S(1)}, u32[]{:S(2)}, u32[]{:S(2)}) %all-to-all-start.1) | async-done | bytes 294944 | tf_op jit(solution)/shard_map/all_to_all | solution.py:339
  41.9 0.0 collective-permute-done.3.db
  41.9 0.0 collective-permute-done.2.dt
  41.9 0.0 copy-done.1
  41.9 0.0 copy-start
  41.9 1.9 %copy-done = bf16[2048,3,256]{2,0,1:T(8,128)(2,1)S(1)} copy-done((bf16[2048,3,256]{2,0,1:T(8,128)(2,1)S(1)}, bf16[2048,3,256]{2,0,1:T(8,128)(2,1)}, u32[]{:S(2)}) %copy-start) | copy-done | bytes 3145752
  43.8 0.0 copy-start.2
  43.8 4.4 %shard_map.66 = (bf16[4,128,256]{2,1,0:T(8,128)(2,1)S(1)}, bf16[4,128,256]{2,1,0:T(8,128)(2,1)S(1)}, bf16[4,128,384]{2,1,0:T(8,128)(2,1)S(1)}, bf16[4,128,128]{2...) custom-call(s32[6]{0:T(128)S(1)} %stack.27.scal, bf16[1,128,2048]{2,1,0:T(8,128)(2,1)S(1)} %copy-done.1, ...), custom_call_target="tpu_custom_call" | custom-call | flops 3000000000 | bytes 9000000 | tf_op jit(solution)/shard_map/pallas_call | solution.py:305
  48.1 3.0 %collective-permute-start.4 = (bf16[4,128,384]{2,1,0:T(8,128)(2,1)S(1)}, bf16[4,128,384]{2,1,0:T(8,128)(2,1)S(1)}, u32[]{:S(2)}, u32[]{:S(2)}) collective-permute-start(bf16[4,128,384]{2,1,0:T(8,128)(2,1)S(1)} %get-tuple-element.22), channel_id=1, source_target_pairs={{0,4},{4,0},{8,12},{12,8},{16,20},{20,16},{24,28},{28,24},{32,36},... | collective-permute-start | bytes 1179656 | tf_op jit(solution)/shard_map/ppermute | solution.py:404
  51.1 1.3 collective-permute-done.4.kvq_mate
  52.5 0.0 copy-done.2
  52.5 2.8 %shard_map.67 = (bf16[8,208,128]{2,1,0:T(8,128)(2,1)}, f32[4,16,128]{2,1,0:T(8,128)S(1)}) custom-call(s32[6]{0:T(128)S(1)} %stack.27.scal, bf16[4,128,256]{2,1,0:T(8,128)(2,1)S(1)} %get-tuple-element.21.kv_own, bf16[4,128,384]{2,1,0:T(8,128)(2,1)S(1)} %collective-permute-done.4.kvq_mate, bf16[64,128]{1,0:T(8,128)(2,1)S(1)} %get-tuple-element.23.ext_own, ...), custom_call_target="tpu_custom_call" | custom-call | flops 30000001024 | bytes 90000000 | tf_op jit(solution)/shard_map/pallas_call | solution.py:305
  55.3 10.0 %all-to-all-start.2 = ((bf16[8,208,128]{2,1,0:T(8,128)(2,1)}), bf16[8,208,128]{2,1,0:T(8,128)(2,1)S(1)}, u32[]{:S(2)}, u32[]{:S(2)}) async-start(bf16[8,208,128]{2,1,0:T(8,128)(2,1)} %get-tuple-element.25), calls=%async_computation.2 | async-start | bytes 851968 | tf_op jit(solution)/shard_map/all_to_all | solution.py:339
  65.3 5.1 %collective-permute-start.10 = (bf16[4,128,256]{2,1,0:T(8,128)(2,1)S(1)}, bf16[4,128,256]{2,1,0:T(8,128)(2,1)S(1)}, u32[]{:S(2)}, u32[]{:S(2)}) collective-permute-start(bf16[4,128,256]{2,1,0:T(8,128)(2,1)S(1)} %get-tuple-element.31), channel_id=1, source_target_pairs={{4,16},{12,24},{16,4},{20,32},{24,12},{28,40},{32,20},{36,48},{40,... | collective-permute-start | bytes 786440 | tf_op jit(solution)/shard_map/ppermute | solution.py:410
  70.4 1.3 collective-permute-start.8
  71.7 4.3 %collective-permute-start.6 = (bf16[4,128,256]{2,1,0:T(8,128)(2,1)S(1)}, bf16[4,128,256]{2,1,0:T(8,128)(2,1)S(1)}, u32[]{:S(2)}, u32[]{:S(2)}) collective-permute-start(bf16[4,128,256]{2,1,0:T(8,128)(2,1)S(1)} %get-tuple-element.31), channel_id=1, source_target_pairs={{0,12},{4,8},{8,20},{12,16},{16,28},{20,24},{24,36},{28,32},{32,44... | collective-permute-start | bytes 786440 | tf_op jit(solution)/shard_map/ppermute | solution.py:407
  76.0 5.2 %collective-permute-start.9 = (bf16[4,128,256]{2,1,0:T(8,128)(2,1)S(1)}, bf16[4,128,256]{2,1,0:T(8,128)(2,1)S(1)}, u32[]{:S(2)}, u32[]{:S(2)}) collective-permute-start(bf16[4,128,256]{2,1,0:T(8,128)(2,1)S(1)} %get-tuple-element.21.kv_own), channel_id=1, source_target_pairs={{4,20},{12,28},{16,0},{20,36},{24,8},{28,44},{32,16},{36,52},{40,2... | collective-permute-start | bytes 786440 | tf_op jit(solution)/shard_map/ppermute | solution.py:409
  81.2 1.3 collective-permute-start.7
  82.5 4.9 %collective-permute-done.10.twx = bf16[4,128,256]{2,1,0:T(8,128)(2,1)S(1)} collective-permute-done((bf16[4,128,256]{2,1,0:T(8,128)(2,1)S(1)}, bf16[4,128,256]{2,1,0:T(8,128)(2,1)S(1)}, u32[]{:S(2)}, u32[]{:S(2)}) %collective-permute-start.10) | collective-permute-done | bytes 262176 | tf_op jit(solution)/shard_map/ppermute | solution.py:410
  87.4 1.3 collective-permute-start.5
  88.8 0.1 min.12.pat
  88.8 0.0 all-to-all-done.2.got
  88.8 1.4 %shard_map.68 = (bf16[8,208,128]{2,1,0:T(8,128)(2,1)}, f32[64,128]{1,0:T(8,128)S(1)}, f32[64,128]{1,0:T(8,128)S(1)}) custom-call(s32[6]{0:T(128)S(1)} %stack.27.scal, bf16[8,208,128]{2,1,0:T(8,128)(2,1)S(1)} %all-to-all-done.2.got), custom_call_target="tpu_custom_call" | custom-call | flops 1000000000 | bytes 3000000 | tf_op jit(solution)/shard_map/pallas_call | solution.py:305
  90.2 13.9 %all-to-all-start.3 = ((bf16[8,208,128]{2,1,0:T(8,128)(2,1)}), bf16[8,208,128]{2,1,0:T(8,128)(2,1)S(1)}, u32[]{:S(2)}, u32[]{:S(2)}) async-start(bf16[8,208,128]{2,1,0:T(8,128)(2,1)} %get-tuple-element.26), calls=%async_computation.3 | async-start | bytes 851968 | tf_op jit(solution)/shard_map/all_to_all | solution.py:339
  104.1 0.0 collective-permute-done.8.zmx
  104.1 0.0 collective-permute-done.6.zpx
  104.1 0.0 collective-permute-done.9.tws
  104.2 0.0 collective-permute-done.7.zms
  104.2 0.0 collective-permute-done.5.zps
  104.2 0.0 copy-start.3
  104.2 7.8 %shard_map.69 = (f32[8,128,128]{2,1,0:T(8,128)S(1)}, f32[8,128,128]{2,1,0:T(8,128)S(1)}, f32[8,128,128]{2,1,0:T(8,128)S(1)}, f32[8,16,128]{2,1,0:T(8,128)S(1)}, bf16[8,128,128]{2,1,0:T(8,128)(2,1)S(1)}) custom-call(s32[6]{0:T(128)S(1)} %stack.27.scal, s32[48]{0:T(128)S(1)} %min.12.pat, bf16[4,128,256]{2,1,0:T(8,128)(2,1)S(1)} %get-tuple-element.21.kv_own, ...), custom_call_target="tpu_custom_call" | custom-call | flops 8000000000 | bytes 24000000 | tf_op jit(solution)/shard_map/pallas_call | solution.py:305
  112.0 0.0 copy-start.4
  112.0 0.8 copy-done.4
  112.8 0.0 copy-start.6
  112.8 0.8 copy-done.6
  113.6 0.0 copy-start.8
  113.6 0.8 copy-done.8
  114.4 1.9 %all-to-all-done.3.got = bf16[8,208,128]{2,1,0:T(8,128)(2,1)S(1)} async-done(((bf16[8,208,128]{2,1,0:T(8,128)(2,1)}), bf16[8,208,128]{2,1,0:T(8,128)(2,1)S(1)}, u32[]{:S(2)}, u32[]{:S(2)}) %all-to-all-start.3) | async-done | bytes 426016 | tf_op jit(solution)/shard_map/all_to_all | solution.py:339
  116.3 0.0 copy-done.3
  116.3 0.0 copy-start.5
  116.3 1.0 copy-done.5
  117.3 0.0 copy-start.7
  117.3 1.0 copy-done.7
  118.3 0.0 copy-start.9
  118.3 1.0 copy-done.9
  119.4 3.8 %shard_map.70 = bf16[8,128,128]{2,1,0:T(8,128)(2,1)S(1)} custom-call(s32[6]{0:T(128)S(1)} %stack.27.scal, bf16[8,208,128]{2,1,0:T(8,128)(2,1)S(1)} %all-to-all-done.3.got, f32[64,128]{1,0:T(8,128)S(1)} %get-tuple-element.27.inner, f32[64,128]{1,0:T(8,128)S(1)} %get-tuple-element.28.outer, f32[4,16,128]{2,1,0:T(8,128)S(1)} %get-tuple-element.29.state0, ...), custom_call_target="tpu_custom_call" | custom-call | flops 2000000000 | bytes 6000000 | tf_op jit(solution)/shard_map/pallas_call | solution.py:305
  123.2 13.1 %all_to_all.31 = bf16[8,128,128]{2,1,0:T(8,128)(2,1)S(1)} all-to-all(bf16[8,128,128]{2,1,0:T(8,128)(2,1)S(1)} %shard_map.70), channel_id=1, replica_groups={{0,4,1,5,2,6,3,7},{8,12,9,13,10,14,11,15},{16,20,17,21,18,22,19,23},{24..., dimensions={0} | all-to-all | bytes 524288 | tf_op jit(solution)/shard_map/all_to_all | solution.py:339
  136.3 0.2 copy.7
  136.5 0.9 copy.8
  (3 shorter events, 0.1 us)
Async XLA Ops:
  0.0 15.6 %collective-permute-start.1 = (bf16[128,2048]{1,0:T(8,128)(2,1)}, bf16[128,2048]{1,0:T(8,128)(2,1)S(1)}, u32[]{:S(2)}, u32[]{:S(2)}) collective-permute-start(bf16[128,2048]{1,0:T(8,128)(2,1)} %bitcast.15), channel_id=1, source_target_pairs={{0,3},{1,0},{2,1},{3,2},{4,7},{5,4},{6,5},{7,6},{8,11},{9,8},{10,9... | collective-permute-start | bytes 1572872 | tf_op jit(solution)/shard_map/ppermute | solution.py:353
  5.2 15.0 %collective-permute-start = (bf16[128,2048]{1,0:T(8,128)(2,1)}, bf16[128,2048]{1,0:T(8,128)(2,1)S(1)}, u32[]{:S(2)}, u32[]{:S(2)}) collective-permute-start(bf16[128,2048]{1,0:T(8,128)(2,1)} %bitcast.16), channel_id=1, source_target_pairs={{0,1},{1,2},{2,3},{3,0},{4,5},{5,6},{6,7},{7,4},{8,9},{9,10},{10,1... | collective-permute-start | bytes 1572872 | tf_op jit(solution)/shard_map/ppermute | solution.py:352
  8.8 16.1 %all-to-all-start = ((bf16[8,8,2048]{2,1,0:T(8,128)(2,1)}), bf16[8,8,2048]{2,1,0:T(8,128)(2,1)S(1)}, u32[]{:S(2)}, u32[]{:S(2)}) async-start(bf16[8,8,2048]{2,1,0:T(8,128)(2,1)} %bitcast.23), calls=%async_computation | async-start | bytes 524288 | tf_op jit(solution)/shard_map/all_to_all | solution.py:339
  15.7 26.2 %collective-permute-start.3 = (bf16[64,2048]{1,0:T(8,128)(2,1)S(1)}, bf16[64,2048]{1,0:T(8,128)(2,1)S(1)}, u32[]{:S(2)}, u32[]{:S(2)}) collective-permute-start(bf16[64,2048]{1,0:T(8,128)(2,1)S(1)} %slice.13), channel_id=1, source_target_pairs={{0,3},{1,0},{2,1},{3,2},{4,7},{5,4},{6,5},{7,6},{8,11},{9,8},{10,9... | collective-permute-start | bytes 786440 | tf_op jit(solution)/shard_map/ppermute | solution.py:355
  20.3 21.6 %collective-permute-start.2 = (bf16[64,2048]{1,0:T(8,128)(2,1)S(1)}, bf16[64,2048]{1,0:T(8,128)(2,1)S(1)}, u32[]{:S(2)}, u32[]{:S(2)}) collective-permute-start(bf16[64,2048]{1,0:T(8,128)(2,1)S(1)} %slice.12), channel_id=1, source_target_pairs={{0,1},{1,2},{2,3},{3,0},{4,5},{5,6},{6,7},{7,4},{8,9},{9,10},{10,1... | collective-permute-start | bytes 786440 | tf_op jit(solution)/shard_map/ppermute | solution.py:354
  24.9 0.7 copy-start.10
  25.6 16.2 %copy-start.1 = (bf16[1,128,2048]{2,1,0:T(8,128)(2,1)S(1)}, bf16[1,128,2048]{2,1,0:T(8,128)(2,1)}, u32[]{:S(2)}) copy-start(bf16[1,128,2048]{2,1,0:T(8,128)(2,1)} %t0.1) | copy-start | bytes 1572868
  27.3 14.6 %all-to-all-start.1 = ((bf16[8,144,128]{2,1,0:T(8,128)(2,1)}), bf16[8,144,128]{2,1,0:T(8,128)(2,1)S(1)}, u32[]{:S(2)}, u32[]{:S(2)}) async-start(bf16[8,144,128]{2,1,0:T(8,128)(2,1)} %shard_map.65), calls=%async_computation.1 | async-start | bytes 589824 | tf_op jit(solution)/shard_map/all_to_all | solution.py:339
  41.9 1.9 %copy-start = (bf16[2048,3,256]{2,0,1:T(8,128)(2,1)S(1)}, bf16[2048,3,256]{2,0,1:T(8,128)(2,1)}, u32[]{:S(2)}) copy-start(bf16[2048,3,256]{2,0,1:T(8,128)(2,1)} %param.7) | copy-start | bytes 9437188
  43.8 8.7 %copy-start.2 = (bf16[8,128,16]{1,2,0:T(8,128)(2,1)S(1)}, bf16[8,128,16]{1,2,0:T(8,128)(2,1)}, u32[]{:S(2)}) copy-start(bf16[8,128,16]{1,2,0:T(8,128)(2,1)} %param.8) | copy-start | bytes 98308
  48.1 4.3 %collective-permute-start.4 = (bf16[4,128,384]{2,1,0:T(8,128)(2,1)S(1)}, bf16[4,128,384]{2,1,0:T(8,128)(2,1)S(1)}, u32[]{:S(2)}, u32[]{:S(2)}) collective-permute-start(bf16[4,128,384]{2,1,0:T(8,128)(2,1)S(1)} %get-tuple-element.22), channel_id=1, source_target_pairs={{0,4},{4,0},{8,12},{12,8},{16,20},{20,16},{24,28},{28,24},{32,36},... | collective-permute-start | bytes 1179656 | tf_op jit(solution)/shard_map/ppermute | solution.py:404
  55.3 33.5 %all-to-all-start.2 = ((bf16[8,208,128]{2,1,0:T(8,128)(2,1)}), bf16[8,208,128]{2,1,0:T(8,128)(2,1)S(1)}, u32[]{:S(2)}, u32[]{:S(2)}) async-start(bf16[8,208,128]{2,1,0:T(8,128)(2,1)} %get-tuple-element.25), calls=%async_computation.2 | async-start | bytes 851968 | tf_op jit(solution)/shard_map/all_to_all | solution.py:339
  65.3 22.1 %collective-permute-start.10 = (bf16[4,128,256]{2,1,0:T(8,128)(2,1)S(1)}, bf16[4,128,256]{2,1,0:T(8,128)(2,1)S(1)}, u32[]{:S(2)}, u32[]{:S(2)}) collective-permute-start(bf16[4,128,256]{2,1,0:T(8,128)(2,1)S(1)} %get-tuple-element.31), channel_id=1, source_target_pairs={{4,16},{12,24},{16,4},{20,32},{24,12},{28,40},{32,20},{36,48},{40,... | collective-permute-start | bytes 786440 | tf_op jit(solution)/shard_map/ppermute | solution.py:410
  70.4 33.7 %collective-permute-start.8 = (bf16[4,128,256]{2,1,0:T(8,128)(2,1)S(1)}, bf16[4,128,256]{2,1,0:T(8,128)(2,1)S(1)}, u32[]{:S(2)}, u32[]{:S(2)}) collective-permute-start(bf16[4,128,256]{2,1,0:T(8,128)(2,1)S(1)} %get-tuple-element.31), channel_id=1, source_target_pairs={{8,4},{12,0},{16,12},{20,8},{24,20},{28,16},{32,28},{36,24},{40,36... | collective-permute-start | bytes 786440 | tf_op jit(solution)/shard_map/ppermute | solution.py:408
  71.7 32.4 %collective-permute-start.6 = (bf16[4,128,256]{2,1,0:T(8,128)(2,1)S(1)}, bf16[4,128,256]{2,1,0:T(8,128)(2,1)S(1)}, u32[]{:S(2)}, u32[]{:S(2)}) collective-permute-start(bf16[4,128,256]{2,1,0:T(8,128)(2,1)S(1)} %get-tuple-element.31), channel_id=1, source_target_pairs={{0,12},{4,8},{8,20},{12,16},{16,28},{20,24},{24,36},{28,32},{32,44... | collective-permute-start | bytes 786440 | tf_op jit(solution)/shard_map/ppermute | solution.py:407
  76.0 28.1 %collective-permute-start.9 = (bf16[4,128,256]{2,1,0:T(8,128)(2,1)S(1)}, bf16[4,128,256]{2,1,0:T(8,128)(2,1)S(1)}, u32[]{:S(2)}, u32[]{:S(2)}) collective-permute-start(bf16[4,128,256]{2,1,0:T(8,128)(2,1)S(1)} %get-tuple-element.21.kv_own), channel_id=1, source_target_pairs={{4,20},{12,28},{16,0},{20,36},{24,8},{28,44},{32,16},{36,52},{40,2... | collective-permute-start | bytes 786440 | tf_op jit(solution)/shard_map/ppermute | solution.py:409
  81.2 22.9 %collective-permute-start.7 = (bf16[4,128,256]{2,1,0:T(8,128)(2,1)S(1)}, bf16[4,128,256]{2,1,0:T(8,128)(2,1)S(1)}, u32[]{:S(2)}, u32[]{:S(2)}) collective-permute-start(bf16[4,128,256]{2,1,0:T(8,128)(2,1)S(1)} %get-tuple-element.21.kv_own), channel_id=1, source_target_pairs={{8,0},{12,4},{16,8},{20,12},{24,16},{28,20},{32,24},{36,28},{40,32... | collective-permute-start | bytes 786440 | tf_op jit(solution)/shard_map/ppermute | solution.py:406
  87.4 16.7 %collective-permute-start.5 = (bf16[4,128,256]{2,1,0:T(8,128)(2,1)S(1)}, bf16[4,128,256]{2,1,0:T(8,128)(2,1)S(1)}, u32[]{:S(2)}, u32[]{:S(2)}) collective-permute-start(bf16[4,128,256]{2,1,0:T(8,128)(2,1)S(1)} %get-tuple-element.21.kv_own), channel_id=1, source_target_pairs={{0,8},{4,12},{8,16},{12,20},{16,24},{20,28},{24,32},{28,36},{32,40... | collective-permute-start | bytes 786440 | tf_op jit(solution)/shard_map/ppermute | solution.py:405
  90.2 26.0 %all-to-all-start.3 = ((bf16[8,208,128]{2,1,0:T(8,128)(2,1)}), bf16[8,208,128]{2,1,0:T(8,128)(2,1)S(1)}, u32[]{:S(2)}, u32[]{:S(2)}) async-start(bf16[8,208,128]{2,1,0:T(8,128)(2,1)} %get-tuple-element.26), calls=%async_computation.3 | async-start | bytes 851968 | tf_op jit(solution)/shard_map/all_to_all | solution.py:339
  104.2 12.1 %copy-start.3 = (f32[1024]{0:T(1024)S(1)}, f32[1024]{0:T(1024)}, u32[]{:S(2)}) copy-start(f32[1024]{0:T(1024)} %param.9) | copy-start | bytes 12292
  112.0 0.8 copy-start.4
  112.8 0.8 copy-start.6
  113.6 0.8 copy-start.8
  116.3 1.0 copy-start.5
  117.3 1.0 copy-start.7
  118.3 1.0 copy-start.9

commit v4 on v1

--- a/solution.py
+++ b/solution.py
@@ -56,31 +56,54 @@
     return mm(steps, jnp.where(row <= col, 1.0, 0.0).astype(F32), HIGH)
 
 
-def project_kernel(scal, t0, ta, tb, td1, td2, w, kv_own, kv_other, kvq_other, q_own, rows):
+def pack_kernel(pat, steps, packed):
+    lane = lax.broadcasted_iota(jnp.int32, (8, TOK), 1)
+    row = lax.broadcasted_iota(jnp.int32, (8, TOK), 0)
+    wanted = jnp.zeros((8, TOK), jnp.int32)
+    for i in range(6):
+        wanted = jnp.where(lane == i, pat[0, i // 3, i % 3], wanted)
+    wanted = wanted.astype(F32)
+    for head in range(8):
+        packed[head] = jnp.where(row == 0, steps[0, head : head + 1], wanted)
+
+
+def halves_kernel(ta, tb, got, da, db):
+    da[...] = ta[...]
+    db[...] = tb[...]
+
+
+def early_kernel(t0, got, w, own):
+    for k in range(3):
+        own[k] = mm(t0[0], w[k]).astype(BF)
+
+
+def project_kernel(
+    scal, early, ta, tb, td1, td2, got, w, kv_own, kv_other, kvq_other, q_own, steps, rows
+):
     c, x = scal[0], scal[1]
-    rows[0:128] = t0[...]
-    rows[128:256] = ta[...]
-    rows[256:320] = td1[...]
-    rows[320:384] = td2[...]
-    rows[384:512] = tb[...]
-    parts = [mm(rows[...], w[k]).astype(BF) for k in range(3)]
+    rows[0:128] = ta[...]
+    rows[128:192] = td1[...]
+    rows[192:256] = td2[...]
+    rows[256:384] = tb[...]
+    for i in range(8):
+        steps[i : i + 1] = got[i, 0:1]
     first = c == 0
-    for r in range(DOCS):
-        n = lax.rem(x - r + DOCS, DOCS)
-        own, other = [], []
-        for k in range(3):
-            lo = parts[k][r * TOK : (r + 1) * TOK, :DH]
-            hi = parts[k][r * TOK : (r + 1) * TOK, DH:]
-            own.append(jnp.where(first, lo, hi))
-            other.append(jnp.where(first, hi, lo))
-        q_own[n] = own[0]
-        kv_own[n, :, :DH] = own[1]
-        kv_own[n, :, DH:] = own[2]
-        kv_other[n, :, :DH] = other[1]
-        kv_other[n, :, DH:] = other[2]
-        kvq_other[n, :, :DH] = other[1]
-        kvq_other[n, :, DH : 2 * DH] = other[2]
-        kvq_other[n, :, 2 * DH :] = other[0]
+    for k in range(3):
+        part = jnp.concatenate([early[k], mm(rows[...], w[k]).astype(BF)], axis=0)
+        for r in range(DOCS):
+            n = lax.rem(x - r + DOCS, DOCS)
+            lo = part[r * TOK : (r + 1) * TOK, :DH]
+            hi = part[r * TOK : (r + 1) * TOK, DH:]
+            own = jnp.where(first, lo, hi)
+            other = jnp.where(first, hi, lo)
+            if k == 0:
+                q_own[n] = own
+                kvq_other[n, :, 2 * DH :] = other
+            else:
+                here = slice((k - 1) * DH, k * DH)
+                kv_own[n, :, here] = own
+                kv_other[n, :, here] = other
+                kvq_other[n, :, here] = other
 
 
 def states_kernel(scal, kv_own, kvq_mate, steps, wft, out, state0):
@@ -233,16 +256,18 @@
                 ).astype(BF)
 
 
-def call(kernel, outs, scratch, n_smem, *args):
-    vmem = pl.BlockSpec(memory_space=pltpu.VMEM)
-    smem = pl.BlockSpec(memory_space=pltpu.SMEM)
+def call(kernel, outs, scratch, spaces, micros, room, *args):
+    kinds = {"s": pltpu.SMEM, "v": pltpu.VMEM, "a": pl.ANY}
     return pl.pallas_call(
         kernel,
         out_shape=outs,
-        in_specs=[smem] * n_smem + [vmem] * (len(args) - n_smem),
-        out_specs=[vmem] * len(outs),
+        in_specs=[pl.BlockSpec(memory_space=kinds[k]) for k in spaces],
+        out_specs=[pl.BlockSpec(memory_space=pltpu.VMEM)] * len(outs),
         scratch_shapes=scratch,
-        compiler_params=pltpu.CompilerParams(vmem_limit_bytes=28 * 2**20),
+        compiler_params=pltpu.CompilerParams(vmem_limit_bytes=room * 2**20),
+        cost_estimate=pl.CostEstimate(
+            flops=int(micros * 1e9), bytes_accessed=int(micros * 3e6), transcendentals=0
+        ),
     )(*args)
 
 
@@ -281,38 +306,44 @@
     down = [(i, (i - 1) % 4) for i in range(4)]
     ta = lax.ppermute(t0, "fsdp", up)
     tb = lax.ppermute(t0, "fsdp", down)
-    td1 = lax.ppermute(ta[:64], "fsdp", up)
-    td2 = lax.ppermute(tb[64:], "fsdp", down)
-
-    small = jnp.concatenate(
-        [
-            log_decay[0][:, None, :],
-            jnp.broadcast_to(
-                jnp.pad(pattern.reshape(1, 1, 6).astype(F32), ((0, 0), (0, 0), (0, 122))),
-                (8, 1, TOK),
-            ),
-            jnp.zeros((8, 6, TOK), F32),
+
+    w3 = w_qkv.transpose(1, 0, 2)
+    wft = w_feature.transpose(0, 2, 1)
+    [packed] = call(pack_kernel, [shape((8, 8, TOK), F32)], [], "sv", 1, 4, pattern, log_decay)
+    got0 = exchange(packed, ("seq", "fsdp"), XC)
+    da, db = pl.pallas_call(
+        halves_kernel,
+        grid=(1,),
+        out_shape=[shape((64, D), BF)] * 2,
+        in_specs=[
+            pl.BlockSpec((64, D), lambda i: (0, 0)),
+            pl.BlockSpec((64, D), lambda i: (1, 0)),
+            pl.BlockSpec(memory_space=pl.ANY),
         ],
-        axis=1,
-    )
-    got0 = exchange(small, ("seq", "fsdp"), XC)
-    steps = got0[:, 0]
+        out_specs=[pl.BlockSpec((64, D), lambda i: (0, 0))] * 2,
+    )(ta, tb, got0)
+    td1 = lax.ppermute(da, "fsdp", up)
+    td2 = lax.ppermute(db, "fsdp", down)
+    [early] = call(
+        early_kernel, [shape((3, TOK, 2 * DH), BF)], [], "vav", 6, 12, tokens, got0, w3
+    )
     pat = got0[:, 1, :6].astype(jnp.int32).reshape(48) - (4 * q - 6)
     pat = jnp.clip(pat, 0, 15).astype(jnp.int32)
 
-    w3 = w_qkv.transpose(1, 0, 2)
-    wft = w_feature.transpose(0, 2, 1)
-    kv_own, kv_other, kvq_other, q_own = call(
+    kv_own, kv_other, kvq_other, q_own, steps = call(
         project_kernel,
         [
             shape((DOCS, TOK, 2 * DH), BF),
             shape((DOCS, TOK, 2 * DH), BF),
             shape((DOCS, TOK, 3 * DH), BF),
             shape((DOCS, TOK, DH), BF),
+            shape((8, TOK), F32),
         ],
-        [pltpu.VMEM((4 * TOK, D), BF)],
-        1,
-        scal, t0, ta, tb, td1, td2, w3,
+        [pltpu.VMEM((3 * TOK, D), BF)],
+        "s" + "v" * 7,
+        3,
+        16,
+        scal, early, ta, tb, td1, td2, got0, w3,
     )
     kvq_mate = lax.ppermute(kvq_other, "seq", pairs(lambda q, c: (q, 1 - c)))
     zps = lax.ppermute(kv_own, "seq", pairs(lambda q, c: (q + 1, c)))
@@ -326,7 +357,9 @@
         states_kernel,
         [shape((8, ROWS, TOK), BF), shape((DOCS, F, DH), F32)],
         [],
-        1,
+        "svvvv",
+        2,
+        6,
         scal, kv_own, kvq_mate, steps, wft,
     )
     got1 = exchange(send1, "seq", ZS)
@@ -334,7 +367,9 @@
         row_kernel,
         [shape((8, ROWS, TOK), BF), shape((64, TOK), F32), shape((64, TOK), F32)],
         [],
-        1,
+        "sv",
+        40,
+        4,
         scal, got1,
     )
     got2 = exchange(send2, "seq", YS)
@@ -344,7 +379,9 @@
         attend_kernel,
         [shape((8, TOK, DH), BF)],
         [pltpu.VMEM((DOCS, 8, TOK, 2 * DH), BF), pltpu.VMEM((DOCS, 2, TOK, DH), BF)],
-        2,
+        "ss" + "v" * 17,
+        8,
+        16,
         scal, pat, kv_own, q_own, kvq_mate, zps, zpx, zms, zmx, tws, twx, glob, got2, inner, outer,
         state0, steps, wft, norm_gain.reshape(HALF_HEADS, 1, DH),
     )

time: 139 us -> 137 us (0.986)
  blocking collectives: 42.1 us -> 31.6 us
  starting transfers between devices: 56.2 us -> 59.7 us
  Pallas kernels: 15.4 us -> 18.6 us
  local copies, waits for them, and re-layouts: 5.03 us -> 7.54 us
    all_to_all x3 -> x2, blocking collectives: 42.1 us -> 31.6 us  [exchange(): return lax.all_to_all(a, axis, 0, 0, tiled=True, axis_index_groups=groups)]
    all_to_all x2 -> x3, starting transfers between devices: 14.7 us -> 24.7 us  [exchange(): return lax.all_to_all(a, axis, 0, 0, tiled=True, axis_index_groups=groups)]
    ppermute x1, waiting for transfers between devices: 4.84 us -> 0.01 us  [per_device(): ta = lax.ppermute(t0, 'fsdp', up)]
    all_to_all x2 -> x3, waiting for transfers between devices: 2.46 us -> 7.26 us  [exchange(): return lax.all_to_all(a, axis, 0, 0, tiled=True, axis_index_groups=groups)]
    ppermute x2, starting transfers between devices: 10 us -> 6.48 us  [the longest x1 4.29 us: per_device(): td2 = lax.ppermute(db, 'fsdp', down)]
    pallas_call x4 -> x7, Pallas kernels: 15.4 us -> 18.6 us  [the longest x6 16.7 us: call(): pl.pallas_call(kernel, out_shape=outs, in_specs=[pl.BlockSpec(memory_spac...]
    unnamed x12 -> x28, local copies, waits for them, and re-layouts: 2.95 us -> 5.67 us
    ppermute x1, starting transfers between devices: 6.18 us -> 3.84 us  [per_device(): kvq_mate = lax.ppermute(kvq_other, 'seq', pairs(lambda q, c: (q, 1 - c)))]
  transfers between devices with their start and end apart: 13 -> 14, of which waited for: 6 -> 6; matrix products, arithmetic and copies ran while one was open for 1% -> 1% of each run, Pallas kernels for 0% -> 1%
where the time goes in v4:
time: 137 us; the launch traced here: 135 us
  starting transfers between devices  59.7 us (44%)
  blocking collectives  31.6 us (23%)
  Pallas kernels  18.6 us (14%)
  waiting for transfers between devices  16.9 us (12%)
  local copies, waits for them, and re-layouts  7.54 us (6%)
    all_to_all x2, blocking collectives, exchange(): return lax.all_to_all(a, axis, 0, 0, tiled=True, axis_index_groups=groups)  31.6 us
    all_to_all x3, starting transfers between devices, exchange(): return lax.all_to_all(a, axis, 0, 0, tiled=True, axis_index_groups=groups)  24.7 us
    pallas_call x6, Pallas kernels, call(): pl.pallas_call(kernel, out_shape=outs, in_specs=[pl.BlockSpec(memory_spac...  16.7 us
    all_to_all x3, waiting for transfers between devices, exchange(): return lax.all_to_all(a, axis, 0, 0, tiled=True, axis_index_groups=groups)  7.26 us
    ppermute x1, waiting for transfers between devices, per_device(): zmx = lax.ppermute(kv_other, 'seq', pairs(lambda q, c: (q - 1, 1 - c)))  6.68 us
    ppermute x1, starting transfers between devices, per_device(): lax.ppermute(kv_own, 'seq', pairs(lambda q, c: (q + 2, 1) if c else (q -...  5.92 us
    unnamed x28, local copies, waits for them, and re-layouts  5.67 us
    ppermute x1, starting transfers between devices, per_device(): td2 = lax.ppermute(db, 'fsdp', down)  4.29 us
  transfers between devices with their start and end apart: 14, of which 6 were waited for; matrix products, arithmetic and copies ran while one was open for 1% of the time, Pallas kernels for 1%

profile of v4, /device:TPU:1, one launch (start us, length us, event | category | flops | bytes accessed | tf_op | source)
XLA Modules:
  0.0 134.5 jit_solution(7549916123159348632)
XLA Ops:
  0.0 0.0 copy-start.9
  0.0 4.1 %collective-permute-start = (bf16[128,2048]{1,0:T(8,128)(2,1)}, bf16[128,2048]{1,0:T(8,128)(2,1)S(1)}, u32[]{:S(2)}, u32[]{:S(2)}) collective-permute-start(bf16[128,2048]{1,0:T(8,128)(2,1)} %bitcast.16), channel_id=1, source_target_pairs={{0,1},{1,2},{2,3},{3,0},{4,5},{5,6},{6,7},{7,4},{8,9},{9,10},{10,1... | collective-permute-start | bytes 1572872 | tf_op jit(solution)/shard_map/ppermute | solution.py:307
  4.1 3.2 %collective-permute-start.1 = (bf16[128,2048]{1,0:T(8,128)(2,1)}, bf16[128,2048]{1,0:T(8,128)(2,1)S(1)}, u32[]{:S(2)}, u32[]{:S(2)}) collective-permute-start(bf16[128,2048]{1,0:T(8,128)(2,1)} %bitcast.17), channel_id=1, source_target_pairs={{0,3},{1,0},{2,1},{3,2},{4,7},{5,4},{6,5},{7,6},{8,11},{9,8},{10,9... | collective-permute-start | bytes 1572872 | tf_op jit(solution)/shard_map/ppermute | solution.py:308
  7.3 0.0 copy-start.11
  7.3 0.7 copy-done.11
  8.0 0.0 copy-start.13
  8.0 0.7 copy-done.13
  8.6 1.2 shard_map.64
  9.8 10.0 %all-to-all-start = ((f32[8,8,128]{2,1,0:T(8,128)}), f32[8,8,128]{2,1,0:T(8,128)S(1)}, u32[]{:S(2)}, u32[]{:S(2)}) async-start(f32[8,8,128]{2,1,0:T(8,128)} %shard_map.64), calls=%async_computation | async-start | bytes 65536 | tf_op jit(solution)/shard_map/all_to_all | solution.py:294
  19.9 0.1 stack.27.scal
  19.9 4.7 %all-to-all-done.got = f32[8,8,128]{2,1,0:T(8,128)S(1)} async-done(((f32[8,8,128]{2,1,0:T(8,128)}), f32[8,8,128]{2,1,0:T(8,128)S(1)}, u32[]{:S(2)}, u32[]{:S(2)}) %all-to-all-start) | async-done | bytes 32800 | tf_op jit(solution)/shard_map/all_to_all | solution.py:294
  24.6 0.0 copy-start.4
  24.6 0.0 collective-permute-done.ta
  24.6 0.0 copy-start
  24.6 0.0 collective-permute-done.1.tb
  24.6 0.6 copy-done.4
  25.2 0.2 copy-done
  25.4 0.0 copy-start.2
  25.4 0.8 copy-done.2
  26.2 1.8 %shard_map.66 = (bf16[64,2048]{1,0:T(8,128)(2,1)}, bf16[64,2048]{1,0:T(8,128)(2,1)}) custom-call(bf16[128,2048]{1,0:T(8,128)(2,1)} %copy-done, bf16[128,2048]{1,0:T(8,128)(2,1)} %copy-done.2, f32[8,8,128]{2,1,0:T(8,128)} %copy-done.4), custom_call_target="tpu_custom_call" | custom-call | tf_op jit(solution)/shard_map/pallas_call | solution.py:314
  28.1 2.2 %collective-permute-start.2 = (bf16[64,2048]{1,0:T(8,128)(2,1)}, bf16[64,2048]{1,0:T(8,128)(2,1)S(1)}, u32[]{:S(2)}, u32[]{:S(2)}) collective-permute-start(bf16[64,2048]{1,0:T(8,128)(2,1)} %get-tuple-element.17), channel_id=1, source_target_pairs={{0,1},{1,2},{2,3},{3,0},{4,5},{5,6},{6,7},{7,4},{8,9},{9,10},{10,1... | collective-permute-start | bytes 786440 | tf_op jit(solution)/shard_map/ppermute | solution.py:325
  30.3 4.3 %collective-permute-start.3 = (bf16[64,2048]{1,0:T(8,128)(2,1)}, bf16[64,2048]{1,0:T(8,128)(2,1)S(1)}, u32[]{:S(2)}, u32[]{:S(2)}) collective-permute-start(bf16[64,2048]{1,0:T(8,128)(2,1)} %get-tuple-element.18), channel_id=1, source_target_pairs={{0,3},{1,0},{2,1},{3,2},{4,7},{5,4},{6,5},{7,6},{8,11},{9,8},{10,9... | collective-permute-start | bytes 786440 | tf_op jit(solution)/shard_map/ppermute | solution.py:326
  34.6 0.0 copy-done.9
  34.6 0.0 copy-start.5
  34.6 0.7 copy-done.5
  35.3 1.9 %copy-done.7 = bf16[2048,3,256]{2,0,1:T(8,128)(2,1)S(1)} copy-done((bf16[2048,3,256]{2,0,1:T(8,128)(2,1)S(1)}, bf16[2048,3,256]{2,0,1:T(8,128)(2,1)}, u32[]{:S(2)}) %copy-start.7) | copy-done | bytes 3145752
  37.2 0.6 shard_map.65.early
  37.9 0.0 copy-start.10
  37.9 0.6 collective-permute-done.2.td1
  38.5 1.0 collective-permute-done.3.td2
  39.4 0.0 copy-done.1
  39.5 0.0 copy-done.3
  39.5 0.0 copy-done.6
  39.5 0.0 copy-done.8
  39.5 1.9 %shard_map.67 = (bf16[4,128,256]{2,1,0:T(8,128)(2,1)S(1)}, bf16[4,128,256]{2,1,0:T(8,128)(2,1)S(1)}, bf16[4,128,384]{2,1,0:T(8,128)(2,1)S(1)}, bf16[4,128,128]{2,1,0:T(8,128)(2,1)S(1)}, f32[8,128]{1,0:T(8,128)S(1)}) custom-call(s32[6]{0:T(128)S(1)} %stack.27.scal, bf16[3,128,256]{2,1,0:T(8,128)(2,1)S(1)} %shard_map.65.early, ...), custom_call_target="tpu_custom_call" | custom-call | flops 3000000000 | bytes 9000000 | tf_op jit(solution)/shard_map/pallas_call | solution.py:261
  41.4 3.8 %collective-permute-start.4 = (bf16[4,128,384]{2,1,0:T(8,128)(2,1)S(1)}, bf16[4,128,384]{2,1,0:T(8,128)(2,1)S(1)}, u32[]{:S(2)}, u32[]{:S(2)}) collective-permute-start(bf16[4,128,384]{2,1,0:T(8,128)(2,1)S(1)} %get-tuple-element.21), channel_id=1, source_target_pairs={{0,4},{4,0},{8,12},{12,8},{16,20},{20,16},{24,28},{28,24},{32,36},... | collective-permute-start | bytes 1179656 | tf_op jit(solution)/shard_map/ppermute | solution.py:348
  45.3 1.3 collective-permute-done.4.kvq_mate
  46.6 0.0 copy-done.10
  46.6 2.1 %shard_map.68 = (bf16[8,208,128]{2,1,0:T(8,128)(2,1)S(1)}, f32[4,16,128]{2,1,0:T(8,128)S(1)}) custom-call(s32[6]{0:T(128)S(1)} %stack.27.scal, bf16[4,128,256]{2,1,0:T(8,128)(2,1)S(1)} %get-tuple-element.19.kv_own, bf16[4,128,384]{2,1,0:T(8,128)(2,1)S(1)} %collective-permute-done.4.kvq_mate, f32[8,128]{1,0:T(8,128)S(1)} %get-tuple-element.23.steps, ...), custom_call_target="tpu_custom_call" | custom-call | flops 2000000000 | bytes 6000000 | tf_op jit(solution)/shard_map/pallas_call | solution.py:261
  48.6 21.3 %all_to_all.25.got = bf16[8,208,128]{2,1,0:T(8,128)(2,1)S(1)} all-to-all(bf16[8,208,128]{2,1,0:T(8,128)(2,1)S(1)} %get-tuple-element.24), channel_id=1, replica_groups={{0,8,16,24,32,40,48,56},{4,12,20,28,36,44,52,60},{64,72,80,88,96,104,11..., dimensions={0} | all-to-all | bytes 851968 | tf_op jit(solution)/shard_map/all_to_all | solution.py:294
  69.9 1.4 %shard_map.69 = (bf16[8,208,128]{2,1,0:T(8,128)(2,1)}, f32[64,128]{1,0:T(8,128)S(1)}, f32[64,128]{1,0:T(8,128)S(1)}) custom-call(s32[6]{0:T(128)S(1)} %stack.27.scal, bf16[8,208,128]{2,1,0:T(8,128)(2,1)S(1)} %all_to_all.25.got), custom_call_target="tpu_custom_call" | custom-call | flops 40000000000 | bytes 120000000 | tf_op jit(solution)/shard_map/pallas_call | solution.py:261
  71.3 6.8 %all-to-all-start.2 = ((bf16[8,208,128]{2,1,0:T(8,128)(2,1)}), bf16[8,208,128]{2,1,0:T(8,128)(2,1)S(1)}, u32[]{:S(2)}, u32[]{:S(2)}) async-start(bf16[8,208,128]{2,1,0:T(8,128)(2,1)} %get-tuple-element.25), calls=%async_computation.2 | async-start | bytes 851968 | tf_op jit(solution)/shard_map/all_to_all | solution.py:294
  78.1 3.5 %collective-permute-start.10 = (bf16[4,128,256]{2,1,0:T(8,128)(2,1)S(1)}, bf16[4,128,256]{2,1,0:T(8,128)(2,1)S(1)}, u32[]{:S(2)}, u32[]{:S(2)}) collective-permute-start(bf16[4,128,256]{2,1,0:T(8,128)(2,1)S(1)} %get-tuple-element.22), channel_id=1, source_target_pairs={{4,16},{12,24},{16,4},{20,32},{24,12},{28,40},{32,20},{36,48},{40,... | collective-permute-start | bytes 786440 | tf_op jit(solution)/shard_map/ppermute | solution.py:354
  81.6 2.6 %collective-permute-start.5 = (bf16[4,128,256]{2,1,0:T(8,128)(2,1)S(1)}, bf16[4,128,256]{2,1,0:T(8,128)(2,1)S(1)}, u32[]{:S(2)}, u32[]{:S(2)}) collective-permute-start(bf16[4,128,256]{2,1,0:T(8,128)(2,1)S(1)} %get-tuple-element.19.kv_own), channel_id=1, source_target_pairs={{0,8},{4,12},{8,16},{12,20},{16,24},{20,28},{24,32},{28,36},{32,40... | collective-permute-start | bytes 786440 | tf_op jit(solution)/shard_map/ppermute | solution.py:349
  84.2 2.8 %collective-permute-start.6 = (bf16[4,128,256]{2,1,0:T(8,128)(2,1)S(1)}, bf16[4,128,256]{2,1,0:T(8,128)(2,1)S(1)}, u32[]{:S(2)}, u32[]{:S(2)}) collective-permute-start(bf16[4,128,256]{2,1,0:T(8,128)(2,1)S(1)} %get-tuple-element.22), channel_id=1, source_target_pairs={{0,12},{4,8},{8,20},{12,16},{16,28},{20,24},{24,36},{28,32},{32,44... | collective-permute-start | bytes 786440 | tf_op jit(solution)/shard_map/ppermute | solution.py:351
  87.1 1.3 collective-permute-start.7
  88.4 1.3 collective-permute-start.8
  89.7 0.0 collective-permute-done.10.twx
  89.7 5.9 %collective-permute-start.9 = (bf16[4,128,256]{2,1,0:T(8,128)(2,1)S(1)}, bf16[4,128,256]{2,1,0:T(8,128)(2,1)S(1)}, u32[]{:S(2)}, u32[]{:S(2)}) collective-permute-start(bf16[4,128,256]{2,1,0:T(8,128)(2,1)S(1)} %get-tuple-element.19.kv_own), channel_id=1, source_target_pairs={{4,20},{12,28},{16,0},{20,36},{24,8},{28,44},{32,16},{36,52},{40,2... | collective-permute-start | bytes 786440 | tf_op jit(solution)/shard_map/ppermute | solution.py:353
  95.6 0.0 all-to-all-done.2.got
  95.6 0.7 broadcast_in_dim.8
  96.3 7.9 %all-to-all-start.3 = ((bf16[8,64,128]{2,1,0:T(8,128)(2,1)}), bf16[8,64,128]{2,1,0:T(8,128)(2,1)S(1)}, u32[]{:S(2)}, u32[]{:S(2)}) async-start(bf16[8,64,128]{2,1,0:T(8,128)(2,1)} %broadcast_in_dim.8), calls=%async_computation.3 | async-start | bytes 262144 | tf_op jit(solution)/shard_map/all_to_all | solution.py:294
  104.2 0.1 min.12.pat
  104.3 0.0 collective-permute-done.5.zps
  104.3 0.0 collective-permute-done.6.zpx
  104.3 0.0 collective-permute-done.7.zms
  104.3 6.7 %collective-permute-done.8.zmx = bf16[4,128,256]{2,1,0:T(8,128)(2,1)S(1)} collective-permute-done((bf16[4,128,256]{2,1,0:T(8,128)(2,1)S(1)}, bf16[4,128,256]{2,1,0:T(8,128)(2,1)S(1)}, u32[]{:S(2)}, u32[]{:S(2)}) %collective-permute-start.8) | collective-permute-done | bytes 262176 | tf_op jit(solution)/shard_map/ppermute | solution.py:352
  111.0 0.0 collective-permute-done.9.tws
  111.0 2.6 %all-to-all-done.3.glob = bf16[8,64,128]{2,1,0:T(8,128)(2,1)S(1)} async-done(((bf16[8,64,128]{2,1,0:T(8,128)(2,1)}), bf16[8,64,128]{2,1,0:T(8,128)(2,1)S(1)}, u32[]{:S(2)}, u32[]{:S(2)}) %all-to-all-start.3) | async-done | bytes 131104 | tf_op jit(solution)/shard_map/all_to_all | solution.py:294
  113.6 0.0 copy-done.12
  113.6 9.6 %shard_map.70 = bf16[8,128,128]{2,1,0:T(8,128)(2,1)S(1)} custom-call(s32[6]{0:T(128)S(1)} %stack.27.scal, s32[48]{0:T(128)S(1)} %min.12.pat, bf16[4,128,256]{2,1,0:T(8,128)(2,1)S(1)} %get-tuple-element.19.kv_own, bf16[4,128,128]{2,1,0:T(8,128)(2,1)S(1)} %get-tuple-element.20.q_own, bf16[4,128,384]{2,1,0:T(8,128)(2,1)S(1)} %collective-permute-done.4.kvq_mate, ...), custom_call_target="tpu_custom_call" | custom-call | flops 8000000000 | bytes 24000000 | tf_op jit(solution)/shard_map/pallas_call | solution.py:261
  123.2 10.3 %all_to_all.26 = bf16[8,128,128]{2,1,0:T(8,128)(2,1)S(1)} all-to-all(bf16[8,128,128]{2,1,0:T(8,128)(2,1)S(1)} %shard_map.70), channel_id=1, replica_groups={{0,4,1,5,2,6,3,7},{8,12,9,13,10,14,11,15},{16,20,17,21,18,22,19,23},{24..., dimensions={0} | all-to-all | bytes 524288 | tf_op jit(solution)/shard_map/all_to_all | solution.py:294
  133.5 0.2 copy.7
  133.7 0.9 copy.8
  (8 shorter events, 0.0 us)
Async XLA Ops:
  0.0 34.6 %copy-start.9 = (bf16[1,128,2048]{2,1,0:T(8,128)(2,1)S(1)}, bf16[1,128,2048]{2,1,0:T(8,128)(2,1)}, u32[]{:S(2)}) copy-start(bf16[1,128,2048]{2,1,0:T(8,128)(2,1)} %t0.1) | copy-start | bytes 1572868
  0.0 24.6 %collective-permute-start = (bf16[128,2048]{1,0:T(8,128)(2,1)}, bf16[128,2048]{1,0:T(8,128)(2,1)S(1)}, u32[]{:S(2)}, u32[]{:S(2)}) collective-permute-start(bf16[128,2048]{1,0:T(8,128)(2,1)} %bitcast.16), channel_id=1, source_target_pairs={{0,1},{1,2},{2,3},{3,0},{4,5},{5,6},{6,7},{7,4},{8,9},{9,10},{10,1... | collective-permute-start | bytes 1572872 | tf_op jit(solution)/shard_map/ppermute | solution.py:307
  4.1 20.5 %collective-permute-start.1 = (bf16[128,2048]{1,0:T(8,128)(2,1)}, bf16[128,2048]{1,0:T(8,128)(2,1)S(1)}, u32[]{:S(2)}, u32[]{:S(2)}) collective-permute-start(bf16[128,2048]{1,0:T(8,128)(2,1)} %bitcast.17), channel_id=1, source_target_pairs={{0,3},{1,0},{2,1},{3,2},{4,7},{5,4},{6,5},{7,6},{8,11},{9,8},{10,9... | collective-permute-start | bytes 1572872 | tf_op jit(solution)/shard_map/ppermute | solution.py:308
  7.3 0.7 copy-start.11
  8.0 0.7 copy-start.13
  9.8 14.8 %all-to-all-start = ((f32[8,8,128]{2,1,0:T(8,128)}), f32[8,8,128]{2,1,0:T(8,128)S(1)}, u32[]{:S(2)}, u32[]{:S(2)}) async-start(f32[8,8,128]{2,1,0:T(8,128)} %shard_map.64), calls=%async_computation | async-start | bytes 65536 | tf_op jit(solution)/shard_map/all_to_all | solution.py:294
  24.6 0.6 copy-start.4
  24.6 0.8 copy-start
  25.4 0.8 copy-start.2
  28.1 10.4 %collective-permute-start.2 = (bf16[64,2048]{1,0:T(8,128)(2,1)}, bf16[64,2048]{1,0:T(8,128)(2,1)S(1)}, u32[]{:S(2)}, u32[]{:S(2)}) collective-permute-start(bf16[64,2048]{1,0:T(8,128)(2,1)} %get-tuple-element.17), channel_id=1, source_target_pairs={{0,1},{1,2},{2,3},{3,0},{4,5},{5,6},{6,7},{7,4},{8,9},{9,10},{10,1... | collective-permute-start | bytes 786440 | tf_op jit(solution)/shard_map/ppermute | solution.py:325
  30.3 9.2 %collective-permute-start.3 = (bf16[64,2048]{1,0:T(8,128)(2,1)}, bf16[64,2048]{1,0:T(8,128)(2,1)S(1)}, u32[]{:S(2)}, u32[]{:S(2)}) collective-permute-start(bf16[64,2048]{1,0:T(8,128)(2,1)} %get-tuple-element.18), channel_id=1, source_target_pairs={{0,3},{1,0},{2,1},{3,2},{4,7},{5,4},{6,5},{7,6},{8,11},{9,8},{10,9... | collective-permute-start | bytes 786440 | tf_op jit(solution)/shard_map/ppermute | solution.py:326
  34.6 0.8 copy-start.5
  35.3 1.9 %copy-start.7 = (bf16[2048,3,256]{2,0,1:T(8,128)(2,1)S(1)}, bf16[2048,3,256]{2,0,1:T(8,128)(2,1)}, u32[]{:S(2)}) copy-start(bf16[2048,3,256]{2,0,1:T(8,128)(2,1)} %param.7) | copy-start | bytes 9437188
  37.2 2.2 %copy-start.1 = (bf16[128,2048]{1,0:T(8,128)(2,1)S(1)}, bf16[128,2048]{1,0:T(8,128)(2,1)}, u32[]{:S(2)}) copy-start(bf16[128,2048]{1,0:T(8,128)(2,1)} %copy-done) | copy-start | bytes 1572868
  37.2 2.2 %copy-start.3 = (bf16[128,2048]{1,0:T(8,128)(2,1)S(1)}, bf16[128,2048]{1,0:T(8,128)(2,1)}, u32[]{:S(2)}) copy-start(bf16[128,2048]{1,0:T(8,128)(2,1)} %copy-done.2) | copy-start | bytes 1572868
  37.2 2.2 %copy-start.6 = (f32[8,8,128]{2,1,0:T(8,128)S(1)}, f32[8,8,128]{2,1,0:T(8,128)}, u32[]{:S(2)}) copy-start(f32[8,8,128]{2,1,0:T(8,128)} %copy-done.4) | copy-start | bytes 98308
  37.2 2.2 %copy-start.8 = (bf16[2048,3,256]{2,0,1:T(8,128)(2,1)S(1)}, bf16[2048,3,256]{2,0,1:T(8,128)(2,1)}, u32[]{:S(2)}) copy-start(bf16[2048,3,256]{2,0,1:T(8,128)(2,1)} %param.7) | copy-start | bytes 9437188
  37.9 8.7 %copy-start.10 = (bf16[8,128,16]{1,2,0:T(8,128)(2,1)S(1)}, bf16[8,128,16]{1,2,0:T(8,128)(2,1)}, u32[]{:S(2)}) copy-start(bf16[8,128,16]{1,2,0:T(8,128)(2,1)} %param.8) | copy-start | bytes 98308
  41.4 5.2 %collective-permute-start.4 = (bf16[4,128,384]{2,1,0:T(8,128)(2,1)S(1)}, bf16[4,128,384]{2,1,0:T(8,128)(2,1)S(1)}, u32[]{:S(2)}, u32[]{:S(2)}) collective-permute-start(bf16[4,128,384]{2,1,0:T(8,128)(2,1)S(1)} %get-tuple-element.21), channel_id=1, source_target_pairs={{0,4},{4,0},{8,12},{12,8},{16,20},{20,16},{24,28},{28,24},{32,36},... | collective-permute-start | bytes 1179656 | tf_op jit(solution)/shard_map/ppermute | solution.py:348
  69.9 43.7 %copy-start.12 = (f32[1024]{0:T(1024)S(1)}, f32[1024]{0:T(1024)}, u32[]{:S(2)}) copy-start(f32[1024]{0:T(1024)} %param.9) | copy-start | bytes 12292
  71.3 24.3 %all-to-all-start.2 = ((bf16[8,208,128]{2,1,0:T(8,128)(2,1)}), bf16[8,208,128]{2,1,0:T(8,128)(2,1)S(1)}, u32[]{:S(2)}, u32[]{:S(2)}) async-start(bf16[8,208,128]{2,1,0:T(8,128)(2,1)} %get-tuple-element.25), calls=%async_computation.2 | async-start | bytes 851968 | tf_op jit(solution)/shard_map/all_to_all | solution.py:294
  78.1 11.6 %collective-permute-start.10 = (bf16[4,128,256]{2,1,0:T(8,128)(2,1)S(1)}, bf16[4,128,256]{2,1,0:T(8,128)(2,1)S(1)}, u32[]{:S(2)}, u32[]{:S(2)}) collective-permute-start(bf16[4,128,256]{2,1,0:T(8,128)(2,1)S(1)} %get-tuple-element.22), channel_id=1, source_target_pairs={{4,16},{12,24},{16,4},{20,32},{24,12},{28,40},{32,20},{36,48},{40,... | collective-permute-start | bytes 786440 | tf_op jit(solution)/shard_map/ppermute | solution.py:354
  81.6 22.6 %collective-permute-start.5 = (bf16[4,128,256]{2,1,0:T(8,128)(2,1)S(1)}, bf16[4,128,256]{2,1,0:T(8,128)(2,1)S(1)}, u32[]{:S(2)}, u32[]{:S(2)}) collective-permute-start(bf16[4,128,256]{2,1,0:T(8,128)(2,1)S(1)} %get-tuple-element.19.kv_own), channel_id=1, source_target_pairs={{0,8},{4,12},{8,16},{12,20},{16,24},{20,28},{24,32},{28,36},{32,40... | collective-permute-start | bytes 786440 | tf_op jit(solution)/shard_map/ppermute | solution.py:349
  84.2 20.1 %collective-permute-start.6 = (bf16[4,128,256]{2,1,0:T(8,128)(2,1)S(1)}, bf16[4,128,256]{2,1,0:T(8,128)(2,1)S(1)}, u32[]{:S(2)}, u32[]{:S(2)}) collective-permute-start(bf16[4,128,256]{2,1,0:T(8,128)(2,1)S(1)} %get-tuple-element.22), channel_id=1, source_target_pairs={{0,12},{4,8},{8,20},{12,16},{16,28},{20,24},{24,36},{28,32},{32,44... | collective-permute-start | bytes 786440 | tf_op jit(solution)/shard_map/ppermute | solution.py:351
  87.1 17.2 %collective-permute-start.7 = (bf16[4,128,256]{2,1,0:T(8,128)(2,1)S(1)}, bf16[4,128,256]{2,1,0:T(8,128)(2,1)S(1)}, u32[]{:S(2)}, u32[]{:S(2)}) collective-permute-start(bf16[4,128,256]{2,1,0:T(8,128)(2,1)S(1)} %get-tuple-element.19.kv_own), channel_id=1, source_target_pairs={{8,0},{12,4},{16,8},{20,12},{24,16},{28,20},{32,24},{36,28},{40,32... | collective-permute-start | bytes 786440 | tf_op jit(solution)/shard_map/ppermute | solution.py:350
  88.4 22.6 %collective-permute-start.8 = (bf16[4,128,256]{2,1,0:T(8,128)(2,1)S(1)}, bf16[4,128,256]{2,1,0:T(8,128)(2,1)S(1)}, u32[]{:S(2)}, u32[]{:S(2)}) collective-permute-start(bf16[4,128,256]{2,1,0:T(8,128)(2,1)S(1)} %get-tuple-element.22), channel_id=1, source_target_pairs={{8,4},{12,0},{16,12},{20,8},{24,20},{28,16},{32,28},{36,24},{40,36... | collective-permute-start | bytes 786440 | tf_op jit(solution)/shard_map/ppermute | solution.py:352
  89.7 21.3 %collective-permute-start.9 = (bf16[4,128,256]{2,1,0:T(8,128)(2,1)S(1)}, bf16[4,128,256]{2,1,0:T(8,128)(2,1)S(1)}, u32[]{:S(2)}, u32[]{:S(2)}) collective-permute-start(bf16[4,128,256]{2,1,0:T(8,128)(2,1)S(1)} %get-tuple-element.19.kv_own), channel_id=1, source_target_pairs={{4,20},{12,28},{16,0},{20,36},{24,8},{28,44},{32,16},{36,52},{40,2... | collective-permute-start | bytes 786440 | tf_op jit(solution)/shard_map/ppermute | solution.py:353
  96.3 17.3 %all-to-all-start.3 = ((bf16[8,64,128]{2,1,0:T(8,128)(2,1)}), bf16[8,64,128]{2,1,0:T(8,128)(2,1)S(1)}, u32[]{:S(2)}, u32[]{:S(2)}) async-start(bf16[8,64,128]{2,1,0:T(8,128)(2,1)} %broadcast_in_dim.8), calls=%async_computation.3 | async-start | bytes 262144 | tf_op jit(solution)/shard_map/all_to_all | solution.py:294

commit v5 on v4

--- a/solution.py
+++ b/solution.py
@@ -65,11 +65,6 @@
     wanted = wanted.astype(F32)
     for head in range(8):
         packed[head] = jnp.where(row == 0, steps[0, head : head + 1], wanted)
-
-
-def halves_kernel(ta, tb, got, da, db):
-    da[...] = ta[...]
-    db[...] = tb[...]
 
 
 def early_kernel(t0, got, w, own):
@@ -311,19 +306,8 @@
     wft = w_feature.transpose(0, 2, 1)
     [packed] = call(pack_kernel, [shape((8, 8, TOK), F32)], [], "sv", 1, 4, pattern, log_decay)
     got0 = exchange(packed, ("seq", "fsdp"), XC)
-    da, db = pl.pallas_call(
-        halves_kernel,
-        grid=(1,),
-        out_shape=[shape((64, D), BF)] * 2,
-        in_specs=[
-            pl.BlockSpec((64, D), lambda i: (0, 0)),
-            pl.BlockSpec((64, D), lambda i: (1, 0)),
-            pl.BlockSpec(memory_space=pl.ANY),
-        ],
-        out_specs=[pl.BlockSpec((64, D), lambda i: (0, 0))] * 2,
-    )(ta, tb, got0)
-    td1 = lax.ppermute(da, "fsdp", up)
-    td2 = lax.ppermute(db, "fsdp", down)
+    td1 = lax.ppermute(ta[:64], "fsdp", up)
+    td2 = lax.ppermute(tb[64:], "fsdp", down)
     [early] = call(
         early_kernel, [shape((3, TOK, 2 * DH), BF)], [], "vav", 6, 12, tokens, got0, w3
     )
@@ -345,35 +329,51 @@
         16,
         scal, early, ta, tb, td1, td2, got0, w3,
     )
+    def behind(a, done):
+        return lax.optimization_barrier((a, done))[0]
+
     kvq_mate = lax.ppermute(kvq_other, "seq", pairs(lambda q, c: (q, 1 - c)))
-    zps = lax.ppermute(kv_own, "seq", pairs(lambda q, c: (q + 1, c)))
-    zms = lax.ppermute(kv_own, "seq", pairs(lambda q, c: (q - 1, c)))
-    zpx = lax.ppermute(kv_other, "seq", pairs(lambda q, c: (q + 1, 1 - c)))
-    zmx = lax.ppermute(kv_other, "seq", pairs(lambda q, c: (q - 1, 1 - c)))
     tws = lax.ppermute(kv_own, "seq", pairs(lambda q, c: (q + 2, 1) if c else (q - 2, 0)))
     twx = lax.ppermute(kv_other, "seq", pairs(lambda q, c: (q + 2, 0) if c else (q - 2, 1)))
-
-    send1, state0 = call(
-        states_kernel,
-        [shape((8, ROWS, TOK), BF), shape((DOCS, F, DH), F32)],
-        [],
-        "svvvv",
-        2,
-        6,
-        scal, kv_own, kvq_mate, steps, wft,
-    )
-    got1 = exchange(send1, "seq", ZS)
-    send2, inner, outer = call(
-        row_kernel,
-        [shape((8, ROWS, TOK), BF), shape((64, TOK), F32), shape((64, TOK), F32)],
-        [],
-        "sv",
-        40,
-        4,
-        scal, got1,
-    )
-    got2 = exchange(send2, "seq", YS)
-    glob = exchange(jnp.broadcast_to(got2[0, 144:208][None], (8, 64, TOK)), "seq", ZS)
+    zps = lax.ppermute(kv_own, "seq", pairs(lambda q, c: (q + 1, c)))
+    zpx = lax.ppermute(kv_other, "seq", pairs(lambda q, c: (q + 1, 1 - c)))
+    zms = lax.ppermute(behind(kv_own, kvq_mate), "seq", pairs(lambda q, c: (q - 1, c)))
+    zmx = lax.ppermute(behind(kv_other, zps), "seq", pairs(lambda q, c: (q - 1, 1 - c)))
+
+    def chain(kv_own, kvq_mate, steps):
+        send1, state0 = call(
+            states_kernel,
+            [shape((8, ROWS, TOK), BF), shape((DOCS, F, DH), F32)],
+            [],
+            "svvvv",
+            2,
+            6,
+            scal, kv_own, kvq_mate, steps, wft,
+        )
+        got1 = exchange(send1, "seq", ZS)
+        send2, inner, outer = call(
+            row_kernel,
+            [shape((8, ROWS, TOK), BF), shape((64, TOK), F32), shape((64, TOK), F32)],
+            [],
+            "sv",
+            3,
+            4,
+            scal, got1,
+        )
+        got2 = exchange(send2, "seq", YS)
+        glob = exchange(jnp.broadcast_to(got2[0, 144:208][None], (8, 64, TOK)), "seq", ZS)
+        return got2, glob, inner, outer, state0
+
+    def idle(*_):
+        return (
+            jnp.zeros((8, ROWS, TOK), BF),
+            jnp.zeros((8, 64, TOK), BF),
+            jnp.zeros((64, TOK), F32),
+            jnp.zeros((64, TOK), F32),
+            jnp.zeros((DOCS, F, DH), F32),
+        )
+
+    got2, glob, inner, outer, state0 = lax.cond(s < 1000, chain, idle, kv_own, kvq_mate, steps)
 
     [out] = call(
         attend_kernel,

time: 137 us -> 144 us (1.051); the launches traced: 135 us -> 144 us
  blocking collectives: 31.6 us -> 74.1 us
  starting transfers between devices: 59.7 us -> 44 us
  waiting for transfers between devices: 16.9 us -> 3.42 us
  local copies, waits for them, and re-layouts: 7.54 us -> 5.23 us
  Pallas kernels: 18.6 us -> 16.5 us
    all_to_all x2 -> x4, blocking collectives: 31.6 us -> 74.1 us  [exchange(): return lax.all_to_all(a, axis, 0, 0, tiled=True, axis_index_groups=groups)]
    all_to_all x3 -> x1, starting transfers between devices: 24.7 us -> 10 us  [exchange(): return lax.all_to_all(a, axis, 0, 0, tiled=True, axis_index_groups=groups)]
    all_to_all x3 -> x1, waiting for transfers between devices: 7.26 us -> 0.01 us  [exchange(): return lax.all_to_all(a, axis, 0, 0, tiled=True, axis_index_groups=groups)]
    ppermute x4, waiting for transfers between devices: 8.26 us -> 3.39 us  [the longest x1 1.8 us: per_device(): td1 = lax.ppermute(ta[:64], 'fsdp', up)]
    unnamed x28 -> x14, local copies, waits for them, and re-layouts: 5.67 us -> 3.26 us
    pallas_call x1 -> x0, Pallas kernels: 1.84 us -> none  [per_device(): pl.pallas_call(halves_kernel, grid=(1,), out_shape=[shape((64, D), BF)] *...]
    ppermute x1, starting transfers between devices: 2.85 us -> 1.31 us  [per_device(): zpx = lax.ppermute(kv_other, 'seq', pairs(lambda q, c: (q + 1, 1 - c)))]
  transfers between devices with their start and end apart: 14 -> 12, of which waited for: 6 -> 2; matrix products, arithmetic and copies ran while one was open for 1% -> 1% of each run, Pallas kernels for 1% -> 3%
where the time goes in v5:
time: 144 us
  blocking collectives  74.1 us (51%)
  starting transfers between devices  44 us (31%)
  Pallas kernels  16.5 us (11%)
  local copies, waits for them, and re-layouts  5.23 us (4%)
  waiting for transfers between devices  3.42 us (2%)
    all_to_all x4, blocking collectives, exchange(): return lax.all_to_all(a, axis, 0, 0, tiled=True, axis_index_groups=groups)  74.1 us
    pallas_call x6, Pallas kernels, call(): pl.pallas_call(kernel, out_shape=outs, in_specs=[pl.BlockSpec(memory_spac...  16.5 us
    all_to_all x1, starting transfers between devices, exchange(): return lax.all_to_all(a, axis, 0, 0, tiled=True, axis_index_groups=groups)  10 us
    ppermute x1, starting transfers between devices, per_device(): lax.ppermute(kv_own, 'seq', pairs(lambda q, c: (q + 2, 1) if c else (q -...  6.75 us
    ppermute x1, starting transfers between devices, per_device(): lax.ppermute(kv_other, 'seq', pairs(lambda q, c: (q + 2, 0) if c else (q...  4.88 us
    ppermute x1, starting transfers between devices, per_device(): ta = lax.ppermute(t0, 'fsdp', up)  4.07 us
    ppermute x1, starting transfers between devices, per_device(): kvq_mate = lax.ppermute(kvq_other, 'seq', pairs(lambda q, c: (q, 1 - c)))  3.42 us
    ppermute x1, starting transfers between devices, per_device(): td1 = lax.ppermute(ta[:64], 'fsdp', up)  3.3 us
  transfers between devices with their start and end apart: 12, of which 2 were waited for; matrix products, arithmetic and copies ran while one was open for 1% of the time, Pallas kernels for 3%

profile of v5, /device:TPU:1, one launch (start us, length us, event | category | flops | bytes accessed | tf_op | source)
XLA Modules:
  0.0 143.6 jit_solution(16081025985823605843)
XLA Ops:
  0.0 0.0 copy-start.2
  0.0 4.1 %collective-permute-start = (bf16[128,2048]{1,0:T(8,128)(2,1)}, bf16[128,2048]{1,0:T(8,128)(2,1)S(1)}, u32[]{:S(2)}, u32[]{:S(2)}) collective-permute-start(bf16[128,2048]{1,0:T(8,128)(2,1)} %bitcast.16), channel_id=1, source_target_pairs={{0,1},{1,2},{2,3},{3,0},{4,5},{5,6},{6,7},{7,4},{8,9},{9,10},{10,1... | collective-permute-start | bytes 1572872 | tf_op jit(solution)/shard_map/ppermute | solution.py:302
  4.1 3.2 %collective-permute-start.1 = (bf16[128,2048]{1,0:T(8,128)(2,1)}, bf16[128,2048]{1,0:T(8,128)(2,1)S(1)}, u32[]{:S(2)}, u32[]{:S(2)}) collective-permute-start(bf16[128,2048]{1,0:T(8,128)(2,1)} %bitcast.17), channel_id=1, source_target_pairs={{0,3},{1,0},{2,1},{3,2},{4,7},{5,4},{6,5},{7,6},{8,11},{9,8},{10,9... | collective-permute-start | bytes 1572872 | tf_op jit(solution)/shard_map/ppermute | solution.py:303
  7.3 0.0 copy-start.3
  7.3 0.7 copy-done.3
  8.0 0.0 copy-start.5
  8.0 0.7 copy-done.5
  8.6 1.2 shard_map.64
  9.8 10.0 %all-to-all-start.3 = ((f32[8,8,128]{2,1,0:T(8,128)}), f32[8,8,128]{2,1,0:T(8,128)S(1)}, u32[]{:S(2)}, u32[]{:S(2)}) async-start(f32[8,8,128]{2,1,0:T(8,128)} %shard_map.64), calls=%async_computation.3 | async-start | bytes 65536 | tf_op jit(solution)/shard_map/all_to_all | solution.py:289
  19.9 0.1 stack.27.scal
  19.9 0.0 collective-permute-done.ta
  20.0 3.3 %collective-permute-start.2 = (bf16[64,2048]{1,0:T(8,128)(2,1)S(1)}, bf16[64,2048]{1,0:T(8,128)(2,1)S(1)}, u32[]{:S(2)}, u32[]{:S(2)}) collective-permute-start(bf16[64,2048]{1,0:T(8,128)(2,1)S(1)} %slice.17), channel_id=1, source_target_pairs={{0,1},{1,2},{2,3},{3,0},{4,5},{5,6},{6,7},{7,4},{8,9},{9,10},{10,1... | collective-permute-start | bytes 786440 | tf_op jit(solution)/shard_map/ppermute | solution.py:309
  23.3 0.0 collective-permute-done.1.tb
  23.3 3.2 %collective-permute-start.3 = (bf16[64,2048]{1,0:T(8,128)(2,1)S(1)}, bf16[64,2048]{1,0:T(8,128)(2,1)S(1)}, u32[]{:S(2)}, u32[]{:S(2)}) collective-permute-start(bf16[64,2048]{1,0:T(8,128)(2,1)S(1)} %slice.18), channel_id=1, source_target_pairs={{0,3},{1,0},{2,1},{3,2},{4,7},{5,4},{6,5},{7,6},{8,11},{9,8},{10,9... | collective-permute-start | bytes 786440 | tf_op jit(solution)/shard_map/ppermute | solution.py:310
  26.5 0.0 all-to-all-done.3.got
  26.5 0.0 copy-done.2
  26.5 0.0 copy-start
  26.5 1.9 %copy-done = bf16[2048,3,256]{2,0,1:T(8,128)(2,1)S(1)} copy-done((bf16[2048,3,256]{2,0,1:T(8,128)(2,1)S(1)}, bf16[2048,3,256]{2,0,1:T(8,128)(2,1)}, u32[]{:S(2)}) %copy-start) | copy-done | bytes 3145752
  28.4 0.0 copy-start.1
  28.4 0.6 shard_map.65.early
  29.0 0.0 copy-start.6
  29.0 1.8 %collective-permute-done.2.td1 = bf16[64,2048]{1,0:T(8,128)(2,1)S(1)} collective-permute-done((bf16[64,2048]{1,0:T(8,128)(2,1)S(1)}, bf16[64,2048]{1,0:T(8,128)(2,1)S(1)}, u32[]{:S(2)}, u32[]{:S(2)}) %collective-permute-start.2) | collective-permute-done | bytes 262176 | tf_op jit(solution)/shard_map/ppermute | solution.py:309
  30.8 1.6 %collective-permute-done.3.td2 = bf16[64,2048]{1,0:T(8,128)(2,1)S(1)} collective-permute-done((bf16[64,2048]{1,0:T(8,128)(2,1)S(1)}, bf16[64,2048]{1,0:T(8,128)(2,1)S(1)}, u32[]{:S(2)}, u32[]{:S(2)}) %collective-permute-start.3) | collective-permute-done | bytes 262176 | tf_op jit(solution)/shard_map/ppermute | solution.py:310
  32.4 0.0 copy-done.1
  32.4 1.9 %shard_map.66 = (bf16[4,128,256]{2,1,0:T(8,128)(2,1)S(1)}, bf16[4,128,256]{2,1,0:T(8,128)(2,1)S(1)}, bf16[4,128,384]{2,1,0:T(8,128)(2,1)S(1)}, bf16[4,128,128]{2,1,0:T(8,128)(2,1)S(1)}, f32[8,128]{1,0:T(8,128)S(1)}) custom-call(s32[6]{0:T(128)S(1)} %stack.27.scal, bf16[3,128,256]{2,1,0:T(8,128)(2,1)S(1)} %shard_map.65.early, ...), custom_call_target="tpu_custom_call" | custom-call | flops 3000000000 | bytes 9000000 | tf_op jit(solution)/shard_map/pallas_call | solution.py:256
  34.4 3.4 %collective-permute-start.4 = (bf16[4,128,384]{2,1,0:T(8,128)(2,1)S(1)}, bf16[4,128,384]{2,1,0:T(8,128)(2,1)S(1)}, u32[]{:S(2)}, u32[]{:S(2)}) collective-permute-start(bf16[4,128,384]{2,1,0:T(8,128)(2,1)S(1)} %get-tuple-element.39), channel_id=1, source_target_pairs={{0,4},{4,0},{8,12},{12,8},{16,20},{20,16},{24,28},{28,24},{32,36},... | collective-permute-start | bytes 1179656 | tf_op jit(solution)/shard_map/ppermute | solution.py:335
  37.8 1.3 collective-permute-start.5
  39.1 4.9 %collective-permute-start.10 = (bf16[4,128,256]{2,1,0:T(8,128)(2,1)S(1)}, bf16[4,128,256]{2,1,0:T(8,128)(2,1)S(1)}, u32[]{:S(2)}, u32[]{:S(2)}) collective-permute-start(bf16[4,128,256]{2,1,0:T(8,128)(2,1)S(1)} %get-tuple-element.42), channel_id=1, source_target_pairs={{4,16},{12,24},{16,4},{20,32},{24,12},{28,40},{32,20},{36,48},{40,... | collective-permute-start | bytes 786440 | tf_op jit(solution)/shard_map/ppermute | solution.py:337
  44.0 1.3 collective-permute-start.6
  45.3 6.7 %collective-permute-start.9 = (bf16[4,128,256]{2,1,0:T(8,128)(2,1)S(1)}, bf16[4,128,256]{2,1,0:T(8,128)(2,1)S(1)}, u32[]{:S(2)}, u32[]{:S(2)}) collective-permute-start(bf16[4,128,256]{2,1,0:T(8,128)(2,1)S(1)} %get-tuple-element.41.kv_own), channel_id=1, source_target_pairs={{4,20},{12,28},{16,0},{20,36},{24,8},{28,44},{32,16},{36,52},{40,2... | collective-permute-start | bytes 786440 | tf_op jit(solution)/shard_map/ppermute | solution.py:336
  52.0 0.0 collective-permute-done.5.zps
  52.1 1.3 collective-permute-start.8
  53.4 0.0 collective-permute-done.4.kvq_mate
  53.4 1.3 collective-permute-start.7
  54.7 0.1 min.12.pat
  54.8 0.0 copy-done.6
  54.8 0.0 copy-start.4
  54.8 63.1 %conditional.1 = (bf16[8,208,128]{2,1,0:T(8,128)(2,1)}, bf16[8,64,128]{2,1,0:T(8,128)(2,1)S(1)}, f32[64,128]{1,0:T(8,128)S(1)}, f32[64,128]{1,0:T(8,128)S(1)}, f32[4,16,128]{2,1,0:T(8,128)S(1)}) conditional(s32[]{:T(128)} %convert_element_type.9, () %tuple.17, (s32[6]{0:T(128)S(1)}, bf16[4,128,256]{2,1,0:T(8,128)(2,1)S(1)}, ...), branch_computations={%region_0.1_spmd, %region_1.2_spmd} | conditional | flops 5000000000 | bytes 17146344 | solution.py:376
  54.8 2.1 %branch_1_fun.2 = (bf16[8,208,128]{2,1,0:T(8,128)(2,1)S(1)}, f32[4,16,128]{2,1,0:T(8,128)S(1)}) custom-call(s32[6]{0:T(128)S(1)} %get-tuple-element.15.scal, bf16[4,128,256]{2,1,0:T(8,128)(2,1)S(1)} %get-tuple-element.16.kv_own, bf16[4,128,384]{2,1,0:T(8,128)(2,1)S(1)} %get-tuple-element.17.kvq_mate, f32[8,128]{1,0:T(8,128)S(1)} %get-tuple-element.18.steps, ...), custom_call_target="tpu_custom_call" | custom-call | flops 2000000000 | bytes 6000000 | tf_op jit(solution)/shard_map/cond/branch_1_fun/pallas_call | solution.py:256
  56.9 23.9 %all_to_all.22.got = bf16[8,208,128]{2,1,0:T(8,128)(2,1)S(1)} all-to-all(bf16[8,208,128]{2,1,0:T(8,128)(2,1)S(1)} %get-tuple-element.20), channel_id=1, replica_groups={{0,8,16,24,32,40,48,56},{4,12,20,28,36,44,52,60},{64,72,80,88,96,104,11..., dimensions={0} | all-to-all | bytes 851968 | tf_op jit(solution)/shard_map/cond/branch_1_fun/all_to_all | solution.py:289
  80.8 0.7 branch_1_fun.3
  81.5 22.8 %all_to_all.23 = bf16[8,208,128]{2,1,0:T(8,128)(2,1)} all-to-all(bf16[8,208,128]{2,1,0:T(8,128)(2,1)S(1)} %get-tuple-element.21), channel_id=1, replica_groups={{0,64,128,192,256,320,384,448},{4,68,132,196,260,324,388,452},{8,72,136..., dimensions={0} | all-to-all | bytes 851968 | tf_op jit(solution)/shard_map/cond/branch_1_fun/all_to_all | solution.py:289
  104.2 0.7 slice_bitcast_fusion
  105.0 13.0 %all_to_all.24 = bf16[8,64,128]{2,1,0:T(8,128)(2,1)S(1)} all-to-all(bf16[8,64,128]{2,1,0:T(8,128)(2,1)S(1)} %broadcast_in_dim.6), channel_id=1, replica_groups={{0,8,16,24,32,40,48,56},{4,12,20,28,36,44,52,60},{64,72,80,88,96,104,11..., dimensions={0} | all-to-all | bytes 262144 | tf_op jit(solution)/shard_map/cond/branch_1_fun/all_to_all | solution.py:289
  117.9 0.0 collective-permute-done.10.twx
  117.9 0.0 collective-permute-done.6.zpx
  117.9 0.0 collective-permute-done.9.tws
  117.9 0.0 collective-permute-done.8.zmx
  118.0 0.0 collective-permute-done.7.zms
  118.0 0.0 copy-done.4
  118.0 10.1 %shard_map.67 = bf16[8,128,128]{2,1,0:T(8,128)(2,1)S(1)} custom-call(s32[6]{0:T(128)S(1)} %stack.27.scal, s32[48]{0:T(128)S(1)} %min.12.pat, bf16[4,128,256]{2,1,0:T(8,128)(2,1)S(1)} %get-tuple-element.41.kv_own, bf16[4,128,128]{2,1,0:T(8,128)(2,1)S(1)} %get-tuple-element.38.q_own, bf16[4,128,384]{2,1,0:T(8,128)(2,1)S(1)} %collective-permute-done.4.kvq_mate, ...), custom_call_target="tpu_custom_call" | custom-call | flops 8000000000 | bytes 24000000 | tf_op jit(solution)/shard_map/pallas_call | solution.py:256
  128.1 14.4 %all_to_all.25 = bf16[8,128,128]{2,1,0:T(8,128)(2,1)S(1)} all-to-all(bf16[8,128,128]{2,1,0:T(8,128)(2,1)S(1)} %shard_map.67), channel_id=1, replica_groups={{0,4,1,5,2,6,3,7},{8,12,9,13,10,14,11,15},{16,20,17,21,18,22,19,23},{24..., dimensions={0} | all-to-all | bytes 524288 | tf_op jit(solution)/shard_map/all_to_all | solution.py:289
  142.5 0.2 copy.7
  142.7 0.9 copy.8
  (4 shorter events, 0.1 us)
Async XLA Ops:
  0.0 26.5 %copy-start.2 = (bf16[1,128,2048]{2,1,0:T(8,128)(2,1)S(1)}, bf16[1,128,2048]{2,1,0:T(8,128)(2,1)}, u32[]{:S(2)}) copy-start(bf16[1,128,2048]{2,1,0:T(8,128)(2,1)} %t0.1) | copy-start | bytes 1572868
  0.0 19.9 %collective-permute-start = (bf16[128,2048]{1,0:T(8,128)(2,1)}, bf16[128,2048]{1,0:T(8,128)(2,1)S(1)}, u32[]{:S(2)}, u32[]{:S(2)}) collective-permute-start(bf16[128,2048]{1,0:T(8,128)(2,1)} %bitcast.16), channel_id=1, source_target_pairs={{0,1},{1,2},{2,3},{3,0},{4,5},{5,6},{6,7},{7,4},{8,9},{9,10},{10,1... | collective-permute-start | bytes 1572872 | tf_op jit(solution)/shard_map/ppermute | solution.py:302
  4.1 19.2 %collective-permute-start.1 = (bf16[128,2048]{1,0:T(8,128)(2,1)}, bf16[128,2048]{1,0:T(8,128)(2,1)S(1)}, u32[]{:S(2)}, u32[]{:S(2)}) collective-permute-start(bf16[128,2048]{1,0:T(8,128)(2,1)} %bitcast.17), channel_id=1, source_target_pairs={{0,3},{1,0},{2,1},{3,2},{4,7},{5,4},{6,5},{7,6},{8,11},{9,8},{10,9... | collective-permute-start | bytes 1572872 | tf_op jit(solution)/shard_map/ppermute | solution.py:303
  7.3 0.7 copy-start.3
  8.0 0.7 copy-start.5
  9.8 16.7 %all-to-all-start.3 = ((f32[8,8,128]{2,1,0:T(8,128)}), f32[8,8,128]{2,1,0:T(8,128)S(1)}, u32[]{:S(2)}, u32[]{:S(2)}) async-start(f32[8,8,128]{2,1,0:T(8,128)} %shard_map.64), calls=%async_computation.3 | async-start | bytes 65536 | tf_op jit(solution)/shard_map/all_to_all | solution.py:289
  20.0 10.9 %collective-permute-start.2 = (bf16[64,2048]{1,0:T(8,128)(2,1)S(1)}, bf16[64,2048]{1,0:T(8,128)(2,1)S(1)}, u32[]{:S(2)}, u32[]{:S(2)}) collective-permute-start(bf16[64,2048]{1,0:T(8,128)(2,1)S(1)} %slice.17), channel_id=1, source_target_pairs={{0,1},{1,2},{2,3},{3,0},{4,5},{5,6},{6,7},{7,4},{8,9},{9,10},{10,1... | collective-permute-start | bytes 786440 | tf_op jit(solution)/shard_map/ppermute | solution.py:309
  23.3 9.1 %collective-permute-start.3 = (bf16[64,2048]{1,0:T(8,128)(2,1)S(1)}, bf16[64,2048]{1,0:T(8,128)(2,1)S(1)}, u32[]{:S(2)}, u32[]{:S(2)}) collective-permute-start(bf16[64,2048]{1,0:T(8,128)(2,1)S(1)} %slice.18), channel_id=1, source_target_pairs={{0,3},{1,0},{2,1},{3,2},{4,7},{5,4},{6,5},{7,6},{8,11},{9,8},{10,9... | collective-permute-start | bytes 786440 | tf_op jit(solution)/shard_map/ppermute | solution.py:310
  26.5 1.9 %copy-start = (bf16[2048,3,256]{2,0,1:T(8,128)(2,1)S(1)}, bf16[2048,3,256]{2,0,1:T(8,128)(2,1)}, u32[]{:S(2)}) copy-start(bf16[2048,3,256]{2,0,1:T(8,128)(2,1)} %param.9) | copy-start | bytes 9437188
  28.4 4.0 %copy-start.1 = (bf16[2048,3,256]{2,0,1:T(8,128)(2,1)S(1)}, bf16[2048,3,256]{2,0,1:T(8,128)(2,1)}, u32[]{:S(2)}) copy-start(bf16[2048,3,256]{2,0,1:T(8,128)(2,1)} %param.9) | copy-start | bytes 9437188
  29.0 25.8 %copy-start.6 = (bf16[8,128,16]{1,2,0:T(8,128)(2,1)S(1)}, bf16[8,128,16]{1,2,0:T(8,128)(2,1)}, u32[]{:S(2)}) copy-start(bf16[8,128,16]{1,2,0:T(8,128)(2,1)} %param.10) | copy-start | bytes 98308
  34.4 19.0 %collective-permute-start.4 = (bf16[4,128,384]{2,1,0:T(8,128)(2,1)S(1)}, bf16[4,128,384]{2,1,0:T(8,128)(2,1)S(1)}, u32[]{:S(2)}, u32[]{:S(2)}) collective-permute-start(bf16[4,128,384]{2,1,0:T(8,128)(2,1)S(1)} %get-tuple-element.39), channel_id=1, source_target_pairs={{0,4},{4,0},{8,12},{12,8},{16,20},{20,16},{24,28},{28,24},{32,36},... | collective-permute-start | bytes 1179656 | tf_op jit(solution)/shard_map/ppermute | solution.py:335
  37.8 14.3 %collective-permute-start.5 = (bf16[4,128,256]{2,1,0:T(8,128)(2,1)S(1)}, bf16[4,128,256]{2,1,0:T(8,128)(2,1)S(1)}, u32[]{:S(2)}, u32[]{:S(2)}) collective-permute-start(bf16[4,128,256]{2,1,0:T(8,128)(2,1)S(1)} %get-tuple-element.41.kv_own), channel_id=1, source_target_pairs={{0,8},{4,12},{8,16},{12,20},{16,24},{20,28},{24,32},{28,36},{32,40... | collective-permute-start | bytes 786440 | tf_op jit(solution)/shard_map/ppermute | solution.py:338
  39.1 78.8 %collective-permute-start.10 = (bf16[4,128,256]{2,1,0:T(8,128)(2,1)S(1)}, bf16[4,128,256]{2,1,0:T(8,128)(2,1)S(1)}, u32[]{:S(2)}, u32[]{:S(2)}) collective-permute-start(bf16[4,128,256]{2,1,0:T(8,128)(2,1)S(1)} %get-tuple-element.42), channel_id=1, source_target_pairs={{4,16},{12,24},{16,4},{20,32},{24,12},{28,40},{32,20},{36,48},{40,... | collective-permute-start | bytes 786440 | tf_op jit(solution)/shard_map/ppermute | solution.py:337
  44.0 74.0 %collective-permute-start.6 = (bf16[4,128,256]{2,1,0:T(8,128)(2,1)S(1)}, bf16[4,128,256]{2,1,0:T(8,128)(2,1)S(1)}, u32[]{:S(2)}, u32[]{:S(2)}) collective-permute-start(bf16[4,128,256]{2,1,0:T(8,128)(2,1)S(1)} %get-tuple-element.42), channel_id=1, source_target_pairs={{0,12},{4,8},{8,20},{12,16},{16,28},{20,24},{24,36},{28,32},{32,44... | collective-permute-start | bytes 786440 | tf_op jit(solution)/shard_map/ppermute | solution.py:339
  45.3 72.6 %collective-permute-start.9 = (bf16[4,128,256]{2,1,0:T(8,128)(2,1)S(1)}, bf16[4,128,256]{2,1,0:T(8,128)(2,1)S(1)}, u32[]{:S(2)}, u32[]{:S(2)}) collective-permute-start(bf16[4,128,256]{2,1,0:T(8,128)(2,1)S(1)} %get-tuple-element.41.kv_own), channel_id=1, source_target_pairs={{4,20},{12,28},{16,0},{20,36},{24,8},{28,44},{32,16},{36,52},{40,2... | collective-permute-start | bytes 786440 | tf_op jit(solution)/shard_map/ppermute | solution.py:336
  52.1 65.9 %collective-permute-start.8 = (bf16[4,128,256]{2,1,0:T(8,128)(2,1)S(1)}, bf16[4,128,256]{2,1,0:T(8,128)(2,1)S(1)}, u32[]{:S(2)}, u32[]{:S(2)}) collective-permute-start(bf16[4,128,256]{2,1,0:T(8,128)(2,1)S(1)} %get-tuple-element.42), channel_id=1, source_target_pairs={{8,4},{12,0},{16,12},{20,8},{24,20},{28,16},{32,28},{36,24},{40,36... | collective-permute-start | bytes 786440 | tf_op jit(solution)/shard_map/ppermute | solution.py:341
  53.4 64.6 %collective-permute-start.7 = (bf16[4,128,256]{2,1,0:T(8,128)(2,1)S(1)}, bf16[4,128,256]{2,1,0:T(8,128)(2,1)S(1)}, u32[]{:S(2)}, u32[]{:S(2)}) collective-permute-start(bf16[4,128,256]{2,1,0:T(8,128)(2,1)S(1)} %get-tuple-element.41.kv_own), channel_id=1, source_target_pairs={{8,0},{12,4},{16,8},{20,12},{24,16},{28,20},{32,24},{36,28},{40,32... | collective-permute-start | bytes 786440 | tf_op jit(solution)/shard_map/ppermute | solution.py:340
  54.8 63.2 %copy-start.4 = (f32[1024]{0:T(1024)S(1)}, f32[1024]{0:T(1024)}, u32[]{:S(2)}) copy-start(f32[1024]{0:T(1024)} %param.11) | copy-start | bytes 12292

commit v6 on v5

--- a/solution.py
+++ b/solution.py
@@ -18,7 +18,7 @@
 EPS = 1e-06
 MASKED = -1e30
 CHIPS = 64
-ROWS = 208
+ROWS = 96
 BF = jnp.bfloat16
 F32 = jnp.float32
 HIGH = lax.Precision.HIGHEST
@@ -73,7 +73,7 @@
 
 
 def project_kernel(
-    scal, early, ta, tb, td1, td2, got, w, kv_own, kv_other, kvq_other, q_own, steps, rows
+    scal, early, ta, tb, td1, td2, got, w, kv_own, kvq_other, q_own, steps, rows
 ):
     c, x = scal[0], scal[1]
     rows[0:128] = ta[...]
@@ -97,22 +97,24 @@
             else:
                 here = slice((k - 1) * DH, k * DH)
                 kv_own[n, :, here] = own
-                kv_other[n, :, here] = other
                 kvq_other[n, :, here] = other
 
 
-def states_kernel(scal, kv_own, kvq_mate, steps, wft, out, state0):
+def states_kernel(scal, kv_own, q_own, kvq_mate, steps, wft, out, state0, kv2, q2):
     c, h = scal[0], scal[5]
     first = c == 0
     cum = cumulative_of(steps[...])
     feature = wft[h]
-    states, decays = [], []
+    row = lax.broadcasted_iota(jnp.int32, (16, TOK), 0)
     for n in range(DOCS):
         own = kv_own[n]
         mate = kvq_mate[n, :, : 2 * DH]
         segs = (jnp.where(first, own, mate), jnp.where(first, mate, own))
+        q2[c, n] = q_own[n]
+        q2[1 - c, n] = kvq_mate[n, :, 2 * DH :]
         local = []
         for s in range(2):
+            kv2[s, n] = segs[s]
             phi = softmax0(nt(feature, segs[s][:, :DH])).astype(BF).astype(F32)
             line = cum[2 * n + s : 2 * n + s + 1]
             final = line[:, TOK - 1 :]
@@ -121,80 +123,73 @@
         last0 = jnp.broadcast_to(cum[2 * n : 2 * n + 1, TOK - 1 :], (1, TOK))
         last1 = jnp.broadcast_to(cum[2 * n + 1 : 2 * n + 2, TOK - 1 :], (1, TOK))
         state0[n] = local[0]
-        states.append(jnp.exp(last1) * local[0] + local[1])
-        decays.append(last0 + last1)
+        state = jnp.exp(last1) * local[0] + local[1]
+        tail = decay_rows(row, last0 + last1)
         for half in range(2):
-            out[2 * n + half, 144:176] = segs[0][32 * half : 32 * half + 32, :DH]
-            out[2 * n + half, 176:208] = segs[0][32 * half : 32 * half + 32, DH:]
-    put_states(out, jnp.concatenate(states, axis=0), decays)
-
-
-def put_states(out, state, decays):
+            p = 2 * n + half
+            out[p, 0:16] = state_rows(state[8 * half : 8 * half + 8])
+            out[p, 16:32] = tail
+            out[p, 32:64] = segs[0][32 * half : 32 * half + 32, :DH]
+            out[p, 64:96] = segs[0][32 * half : 32 * half + 32, DH:]
+
+
+def state_rows(state):
     hi, lo = split2(state)
-    three = split3(jnp.concatenate(decays, axis=0))
-    tail = jnp.concatenate(
-        [p.astype(F32) for p in three] + [jnp.zeros((4, TOK), F32)], axis=0
-    ).astype(BF)
+    return jnp.concatenate([hi.astype(F32), lo.astype(F32)], axis=0).astype(BF)
+
+
+def decay_rows(row, decay):
+    hi, mid, lo = (p.astype(F32) for p in split3(decay))
+    return jnp.where(row == 0, hi, jnp.where(row == 1, mid, jnp.where(row == 2, lo, 0.0))).astype(BF)
+
+
+def read_state(got, peer):
+    both = got[peer, 0:16].astype(F32)
+    return both[0:8] + both[8:16]
+
+
+def read_decay(got, peer):
+    tail = got[peer, 16:32].astype(F32)
+    return (tail[0:1] + tail[1:2]) + tail[2:3]
+
+
+def row_kernel(got, out, inner, outer):
+    row = lax.broadcasted_iota(jnp.int32, (16, TOK), 0)
+    total = jnp.zeros((8, TOK), F32)
+    reach = jnp.zeros((1, TOK), F32)
     for peer in range(8):
-        out[peer, 0:64] = hi
-        out[peer, 64:128] = lo
-        out[peer, 128:144] = tail
-
-
-def get_states(got, peer):
-    state = got[peer, 0:64].astype(F32) + got[peer, 64:128].astype(F32)
-    tail = got[peer, 128:144].astype(F32)
-    decay = (tail[0:4] + tail[4:8]) + tail[8:12]
-    wide = jnp.concatenate(
-        [jnp.broadcast_to(decay[n : n + 1], (F, TOK)) for n in range(DOCS)], axis=0
-    )
-    return state, decay, wide
-
-
-def row_kernel(scal, got, out, inner, outer):
-    z = scal[3]
-    total = jnp.zeros((64, TOK), F32)
-    before = jnp.zeros((64, TOK), F32)
-    decays = jnp.zeros((4, TOK), F32)
-    reach = jnp.zeros((64, TOK), F32)
+        inner[peer] = total
+        outer[peer] = jnp.broadcast_to(jnp.exp(reach), (8, TOK))
+        decay = read_decay(got, peer)
+        total = total * jnp.exp(decay) + read_state(got, peer)
+        reach = reach + decay
+    state, tail = state_rows(total), decay_rows(row, reach)
     for peer in range(8):
-        state, decay, wide = get_states(got, peer)
-        grow = jnp.exp(wide)
-        use = peer < z
-        before = jnp.where(use, before * grow + state, before)
-        reach = jnp.where(use, reach + wide, reach)
-        total = total * grow + state
-        decays = decays + decay
-    inner[...] = before
-    outer[...] = jnp.exp(reach)
-    put_states(out, total, [decays])
+        out[peer, 0:16] = state
+        out[peer, 16:32] = tail
+        out[peer, 32:96] = got[0, 32:96]
+
+
+def back_kernel(scal, got, inner, outer, out):
+    y = scal[4]
+    before = jnp.zeros((8, TOK), F32)
     for peer in range(8):
-        out[peer, 144:208] = got[0, 144:208]
-
-
-def attend_kernel(
-    scal, pat, kv_own, q_own, kvq_mate, zps, zpx, zms, zmx, tws, twx, glob, got, inner, outer,
-    state0, steps, wft, gain, out, win, qs,
-):
-    c, q, y, h = scal[0], scal[2], scal[4], scal[5]
-    mate = 1 - c
+        longer = before * jnp.exp(read_decay(got, peer)) + read_state(got, peer)
+        before = jnp.where(peer < y, longer, before)
+    for peer in range(8):
+        out[peer, 0:16] = state_rows(inner[peer] + outer[peer] * before)
+        out[peer, 16:80] = got[0, 32:96]
+
+
+def attend_kernel(scal, pat, kv2, q2, zp, zm, tp, tm, got, state0, steps, wft, gain, out, win):
+    q, h = scal[2], scal[5]
     for n in range(DOCS):
-        win[n, 3 + c] = kv_own[n]
-        win[n, 3 + mate] = kvq_mate[n, :, : 2 * DH]
-        win[n, 1 + c] = zps[n]
-        win[n, 1 + mate] = zpx[n]
-        win[n, 5 + c] = zms[n]
-        win[n, 5 + mate] = zmx[n]
-        win[n, 7 * mate] = tws[n]
-        win[n, 7 * c] = twx[n]
-        qs[n, c] = q_own[n]
-        qs[n, mate] = kvq_mate[n, :, 2 * DH :]
-
-    before = jnp.zeros((64, TOK), F32)
-    for peer in range(8):
-        state, _, wide = get_states(got, peer)
-        before = jnp.where(peer < y, before * jnp.exp(wide) + state, before)
-    entering = inner[...] + outer[...] * before
+        win[n, 0] = tp[n]
+        win[n, 7] = tm[n]
+        for s in range(2):
+            win[n, 1 + s] = zp[s, n]
+            win[n, 3 + s] = kv2[s, n]
+            win[n, 5 + s] = zm[s, n]
 
     cum = cumulative_of(steps[...])
     cum_t = cum.T
@@ -206,13 +201,15 @@
     lane = lax.broadcasted_iota(jnp.int32, (1, 7 * BS), 1)
     scale = DH ** (-0.5)
     for n in range(DOCS):
-        carried = entering[F * n : F * n + F]
+        carried = jnp.concatenate([read_state(got, 2 * n), read_state(got, 2 * n + 1)], axis=0)
+        gk = jnp.concatenate([got[2 * n, 16:48], got[2 * n + 1, 16:48]], axis=0)
+        gv = jnp.concatenate([got[2 * n, 48:80], got[2 * n + 1, 48:80]], axis=0)
         for s in range(2):
             line = cum[2 * n + s : 2 * n + s + 1]
             column = cum_t[:, 2 * n + s : 2 * n + s + 1]
-            queries = qs[n, s]
-            keys = win[n, 3 + s, :, :DH]
-            values = win[n, 3 + s, :, DH:]
+            queries = q2[s, n]
+            keys = kv2[s, n, :, :DH]
+            values = kv2[s, n, :, DH:]
             phi_q = softmax0(nt(feature, queries)).astype(BF).astype(F32).T
             phi_k = softmax0(nt(feature, keys)).astype(BF)
             decay = jnp.where(causal, jnp.exp(jnp.minimum(column - line, 0.0)), 0.0)
@@ -224,15 +221,13 @@
             for half in range(2):
                 j = 2 * s + half
                 block = 4 * q + j
-                picks = [win[n, 3 + (j + d) // 2 if j + d >= 0 else 2, pl.ds(BS * ((j + d) % 2), BS)] for d in (-1, 0, 1)]
+                picks = [win[n, 3 + (j + d) // 2, pl.ds(BS * ((j + d) % 2), BS)] for d in (-1, 0, 1)]
                 for k in range(R):
                     place = pat[12 * n + 3 * j + k]
                     picks.append(
                         win[n, lax.div(place, 2), pl.ds(pl.multiple_of(BS * lax.rem(place, 2), BS), BS)]
                     )
                 near = jnp.concatenate(picks, axis=0)
-                gk = jnp.concatenate([glob[2 * n, 0:32], glob[2 * n + 1, 0:32]], axis=0)
-                gv = jnp.concatenate([glob[2 * n, 32:64], glob[2 * n + 1, 32:64]], axis=0)
                 all_k = jnp.concatenate([near[:, :DH], gk], axis=0)
                 all_v = jnp.concatenate([near[:, DH:], gv], axis=0)
                 scores = nt(queries[half * BS : half * BS + BS], all_k) * scale
@@ -314,10 +309,9 @@
     pat = got0[:, 1, :6].astype(jnp.int32).reshape(48) - (4 * q - 6)
     pat = jnp.clip(pat, 0, 15).astype(jnp.int32)
 
-    kv_own, kv_other, kvq_other, q_own, steps = call(
+    kv_own, kvq_other, q_own, steps = call(
         project_kernel,
         [
-            shape((DOCS, TOK, 2 * DH), BF),
             shape((DOCS, TOK, 2 * DH), BF),
             shape((DOCS, TOK, 3 * DH), BF),
             shape((DOCS, TOK, DH), BF),
@@ -329,61 +323,54 @@
         16,
         scal, early, ta, tb, td1, td2, got0, w3,
     )
-    def behind(a, done):
-        return lax.optimization_barrier((a, done))[0]
-
     kvq_mate = lax.ppermute(kvq_other, "seq", pairs(lambda q, c: (q, 1 - c)))
-    tws = lax.ppermute(kv_own, "seq", pairs(lambda q, c: (q + 2, 1) if c else (q - 2, 0)))
-    twx = lax.ppermute(kv_other, "seq", pairs(lambda q, c: (q + 2, 0) if c else (q - 2, 1)))
-    zps = lax.ppermute(kv_own, "seq", pairs(lambda q, c: (q + 1, c)))
-    zpx = lax.ppermute(kv_other, "seq", pairs(lambda q, c: (q + 1, 1 - c)))
-    zms = lax.ppermute(behind(kv_own, kvq_mate), "seq", pairs(lambda q, c: (q - 1, c)))
-    zmx = lax.ppermute(behind(kv_other, zps), "seq", pairs(lambda q, c: (q - 1, 1 - c)))
-
-    def chain(kv_own, kvq_mate, steps):
-        send1, state0 = call(
-            states_kernel,
-            [shape((8, ROWS, TOK), BF), shape((DOCS, F, DH), F32)],
-            [],
-            "svvvv",
-            2,
-            6,
-            scal, kv_own, kvq_mate, steps, wft,
-        )
-        got1 = exchange(send1, "seq", ZS)
+    send1, state0, kv2, q2 = call(
+        states_kernel,
+        [
+            shape((8, ROWS, TOK), BF),
+            shape((DOCS, F, DH), F32),
+            shape((2, DOCS, TOK, 2 * DH), BF),
+            shape((2, DOCS, TOK, DH), BF),
+        ],
+        [],
+        "svvvvv",
+        2,
+        8,
+        scal, kv_own, q_own, kvq_mate, steps, wft,
+    )
+    got1 = exchange(send1, "seq", ZS)
+    zp = lax.ppermute(kv2, "seq", pairs(lambda q, c: (q + 1, c)))
+    zm = lax.ppermute(kv2, "seq", pairs(lambda q, c: (q - 1, c)))
+    tp = lax.ppermute(kv2[1], "seq", pairs(lambda q, c: (q + 2, c)))
+    tm = lax.ppermute(kv2[0], "seq", pairs(lambda q, c: (q - 2, c)))
+
+    def chain(got1):
         send2, inner, outer = call(
             row_kernel,
-            [shape((8, ROWS, TOK), BF), shape((64, TOK), F32), shape((64, TOK), F32)],
+            [shape((8, ROWS, TOK), BF), shape((8, 8, TOK), F32), shape((8, 8, TOK), F32)],
             [],
-            "sv",
-            3,
+            "v",
+            1,
             4,
-            scal, got1,
+            got1,
         )
         got2 = exchange(send2, "seq", YS)
-        glob = exchange(jnp.broadcast_to(got2[0, 144:208][None], (8, 64, TOK)), "seq", ZS)
-        return got2, glob, inner, outer, state0
-
-    def idle(*_):
-        return (
-            jnp.zeros((8, ROWS, TOK), BF),
-            jnp.zeros((8, 64, TOK), BF),
-            jnp.zeros((64, TOK), F32),
-            jnp.zeros((64, TOK), F32),
-            jnp.zeros((DOCS, F, DH), F32),
+        [send3] = call(
+            back_kernel, [shape((8, 80, TOK), BF)], [], "svvv", 1, 4, scal, got2, inner, outer
         )
-
-    got2, glob, inner, outer, state0 = lax.cond(s < 1000, chain, idle, kv_own, kvq_mate, steps)
+        return exchange(send3, "seq", ZS)
+
+    got3 = lax.cond(s < 1000, chain, lambda _: jnp.zeros((8, 80, TOK), BF), got1)
 
     [out] = call(
         attend_kernel,
         [shape((8, TOK, DH), BF)],
-        [pltpu.VMEM((DOCS, 8, TOK, 2 * DH), BF), pltpu.VMEM((DOCS, 2, TOK, DH), BF)],
-        "ss" + "v" * 17,
+        [pltpu.VMEM((DOCS, 8, TOK, 2 * DH), BF)],
+        "ss" + "v" * 11,
         8,
         16,
-        scal, pat, kv_own, q_own, kvq_mate, zps, zpx, zms, zmx, tws, twx, glob, got2, inner, outer,
-        state0, steps, wft, norm_gain.reshape(HALF_HEADS, 1, DH),
+        scal, pat, kv2, q2, zp, zm, tp, tm, got3, state0, steps, wft,
+        norm_gain.reshape(HALF_HEADS, 1, DH),
     )
     mixed = exchange(out, ("seq", "fsdp"), XC)
     return mixed.transpose(1, 0, 2).reshape(1, TOK, HD)

time: 144 us -> 137 us (0.951)
  blocking collectives: 74.1 us -> 45.3 us
  waiting for transfers between devices: 3.42 us -> 21.9 us
  starting transfers between devices: 44 us -> 47.8 us
    all_to_all x4 -> x3, blocking collectives: 74.1 us -> 45.3 us  [exchange(): return lax.all_to_all(a, axis, 0, 0, tiled=True, axis_index_groups=groups)]
    all_to_all x1 -> x2, waiting for transfers between devices: 0.01 us -> 14.7 us  [exchange(): return lax.all_to_all(a, axis, 0, 0, tiled=True, axis_index_groups=groups)]
    all_to_all x1 -> x2, starting transfers between devices: 10 us -> 19.1 us  [exchange(): return lax.all_to_all(a, axis, 0, 0, tiled=True, axis_index_groups=groups)]
    ppermute x6 -> x4, starting transfers between devices: 16.8 us -> 11.5 us  [the longest x1 4.91 us: per_device(): tp = lax.ppermute(kv2[1], 'seq', pairs(lambda q, c: (q + 2, c)))]
    ppermute x1, waiting for transfers between devices: 1.8 us -> 5.05 us  [per_device(): td1 = lax.ppermute(ta[:64], 'fsdp', up)]
    ppermute x1, starting transfers between devices: 3.19 us -> 5.34 us  [per_device(): tb = lax.ppermute(t0, 'fsdp', down)]
    ppermute x1, starting transfers between devices: 4.07 us -> 1.92 us  [per_device(): ta = lax.ppermute(t0, 'fsdp', up)]
    pallas_call x6 -> x7, Pallas kernels: 16.5 us -> 16.6 us  [call(): pl.pallas_call(kernel, out_shape=outs, in_specs=[pl.BlockSpec(memory_spac...]
  transfers between devices with their start and end apart: 12 -> 11, of which waited for: 2 -> 4; matrix products, arithmetic and copies ran while one was open for 1% -> 0% of each run, Pallas kernels for 3% -> 2%
where the time goes in v6:
time: 137 us; the launch traced here: 136 us
  starting transfers between devices  47.8 us (35%)
  blocking collectives  45.3 us (33%)
  waiting for transfers between devices  21.9 us (16%)
  Pallas kernels  16.6 us (12%)
  local copies, waits for them, and re-layouts  4.53 us (3%)
    all_to_all x3, blocking collectives, exchange(): return lax.all_to_all(a, axis, 0, 0, tiled=True, axis_index_groups=groups)  45.3 us
    all_to_all x2, starting transfers between devices, exchange(): return lax.all_to_all(a, axis, 0, 0, tiled=True, axis_index_groups=groups)  19.1 us
    pallas_call x7, Pallas kernels, call(): pl.pallas_call(kernel, out_shape=outs, in_specs=[pl.BlockSpec(memory_spac...  16.6 us
    all_to_all x2, waiting for transfers between devices, exchange(): return lax.all_to_all(a, axis, 0, 0, tiled=True, axis_index_groups=groups)  14.7 us
    ppermute x1, starting transfers between devices, per_device(): tb = lax.ppermute(t0, 'fsdp', down)  5.34 us
    ppermute x1, waiting for transfers between devices, per_device(): td1 = lax.ppermute(ta[:64], 'fsdp', up)  5.05 us
    ppermute x1, starting transfers between devices, per_device(): tp = lax.ppermute(kv2[1], 'seq', pairs(lambda q, c: (q + 2, c)))  4.91 us
    ppermute x1, starting transfers between devices, per_device(): td2 = lax.ppermute(tb[64:], 'fsdp', down)  4.54 us
  transfers between devices with their start and end apart: 11, of which 4 were waited for; matrix products, arithmetic and copies ran while one was open for 0% of the time, Pallas kernels for 2%

profile of v6, /device:TPU:1, one launch (start us, length us, event | category | flops | bytes accessed | tf_op | source)
XLA Modules:
  0.0 136.4 jit_solution(9541376194168626527)
XLA Ops:
  0.0 0.0 copy-start.2
  0.0 5.3 %collective-permute-start.1 = (bf16[128,2048]{1,0:T(8,128)(2,1)}, bf16[128,2048]{1,0:T(8,128)(2,1)S(1)}, u32[]{:S(2)}, u32[]{:S(2)}) collective-permute-start(bf16[128,2048]{1,0:T(8,128)(2,1)} %bitcast.18), channel_id=1, source_target_pairs={{0,3},{1,0},{2,1},{3,2},{4,7},{5,4},{6,5},{7,6},{8,11},{9,8},{10,9... | collective-permute-start | bytes 1572872 | tf_op jit(solution)/shard_map/ppermute | solution.py:298
  5.3 1.9 %collective-permute-start = (bf16[128,2048]{1,0:T(8,128)(2,1)}, bf16[128,2048]{1,0:T(8,128)(2,1)S(1)}, u32[]{:S(2)}, u32[]{:S(2)}) collective-permute-start(bf16[128,2048]{1,0:T(8,128)(2,1)} %bitcast.19), channel_id=1, source_target_pairs={{0,1},{1,2},{2,3},{3,0},{4,5},{5,6},{6,7},{7,4},{8,9},{9,10},{10,1... | collective-permute-start | bytes 1572872 | tf_op jit(solution)/shard_map/ppermute | solution.py:297
  7.3 0.0 copy-start.4
  7.3 0.7 copy-done.4
  8.0 0.0 copy-start.6
  8.0 0.7 copy-done.6
  8.6 1.2 shard_map.64
  9.8 8.8 %all-to-all-start.2 = ((f32[8,8,128]{2,1,0:T(8,128)}), f32[8,8,128]{2,1,0:T(8,128)S(1)}, u32[]{:S(2)}, u32[]{:S(2)}) async-start(f32[8,8,128]{2,1,0:T(8,128)} %shard_map.64), calls=%async_computation.2 | async-start | bytes 65536 | tf_op jit(solution)/shard_map/all_to_all | solution.py:284
  18.6 0.1 stack.27.scal
  18.7 0.0 collective-permute-done.1.tb
  18.8 4.5 %collective-permute-start.3 = (bf16[64,2048]{1,0:T(8,128)(2,1)S(1)}, bf16[64,2048]{1,0:T(8,128)(2,1)S(1)}, u32[]{:S(2)}, u32[]{:S(2)}) collective-permute-start(bf16[64,2048]{1,0:T(8,128)(2,1)S(1)} %slice.22), channel_id=1, source_target_pairs={{0,3},{1,0},{2,1},{3,2},{4,7},{5,4},{6,5},{7,6},{8,11},{9,8},{10,9... | collective-permute-start | bytes 786440 | tf_op jit(solution)/shard_map/ppermute | solution.py:305
  23.3 0.0 collective-permute-done.ta
  23.3 1.9 %collective-permute-start.2 = (bf16[64,2048]{1,0:T(8,128)(2,1)S(1)}, bf16[64,2048]{1,0:T(8,128)(2,1)S(1)}, u32[]{:S(2)}, u32[]{:S(2)}) collective-permute-start(bf16[64,2048]{1,0:T(8,128)(2,1)S(1)} %slice.21), channel_id=1, source_target_pairs={{0,1},{1,2},{2,3},{3,0},{4,5},{5,6},{6,7},{7,4},{8,9},{9,10},{10,1... | collective-permute-start | bytes 786440 | tf_op jit(solution)/shard_map/ppermute | solution.py:304
  25.3 0.0 all-to-all-done.2.got
  25.3 0.0 copy-done.2
  25.3 0.0 copy-start
  25.3 1.9 %copy-done = bf16[2048,3,256]{2,0,1:T(8,128)(2,1)S(1)} copy-done((bf16[2048,3,256]{2,0,1:T(8,128)(2,1)S(1)}, bf16[2048,3,256]{2,0,1:T(8,128)(2,1)}, u32[]{:S(2)}) %copy-start) | copy-done | bytes 3145752
  27.2 0.0 copy-start.1
  27.2 0.6 shard_map.65.early
  27.8 0.0 copy-start.3
  27.8 0.8 collective-permute-done.3.td2
  28.6 5.0 %collective-permute-done.2.td1 = bf16[64,2048]{1,0:T(8,128)(2,1)S(1)} collective-permute-done((bf16[64,2048]{1,0:T(8,128)(2,1)S(1)}, bf16[64,2048]{1,0:T(8,128)(2,1)S(1)}, u32[]{:S(2)}, u32[]{:S(2)}) %collective-permute-start.2) | collective-permute-done | bytes 262176 | tf_op jit(solution)/shard_map/ppermute | solution.py:304
  33.7 0.0 copy-done.1
  33.7 1.9 %shard_map.66 = (bf16[4,128,256]{2,1,0:T(8,128)(2,1)S(1)}, bf16[4,128,384]{2,1,0:T(8,128)(2,1)S(1)}, bf16[4,128,128]{2,1,0:T(8,128)(2,1)S(1)}, f32[8,128]{1,0:T(8,128)S(1)}) custom-call(s32[6]{0:T(128)S(1)} %stack.27.scal, bf16[3,128,256]{2,1,0:T(8,128)(2,1)S(1)} %shard_map.65.early, bf16[128,2048]{1,0:T(8,128)(2,1)S(1)} %collective-permute-done.ta, ...), custom_call_target="tpu_custom_call" | custom-call | flops 3000000000 | bytes 9000000 | tf_op jit(solution)/shard_map/pallas_call | solution.py:251
  35.6 3.4 %collective-permute-start.4 = (bf16[4,128,384]{2,1,0:T(8,128)(2,1)S(1)}, bf16[4,128,384]{2,1,0:T(8,128)(2,1)S(1)}, u32[]{:S(2)}, u32[]{:S(2)}) collective-permute-start(bf16[4,128,384]{2,1,0:T(8,128)(2,1)S(1)} %get-tuple-element.27), channel_id=1, source_target_pairs={{0,4},{4,0},{8,12},{12,8},{16,20},{20,16},{24,28},{28,24},{32,36},... | collective-permute-start | bytes 1179656 | tf_op jit(solution)/shard_map/ppermute | solution.py:326
  39.0 1.3 collective-permute-done.4.kvq_mate
  40.3 0.0 copy-done.3
  40.3 2.8 %shard_map.67 = (bf16[8,96,128]{2,1,0:T(8,128)(2,1)}, f32[4,16,128]{2,1,0:T(8,128)S(1)}, bf16[2,4,128,256]{3,2,1,0:T(8,128)(2,1)S(1)}, bf16[2,4,128,128]{3,2,1,0:T(8,128)(2,1)S(1)}) custom-call(s32[6]{0:T(128)S(1)} %stack.27.scal, bf16[4,128,256]{2,1,0:T(8,128)(2,1)S(1)} %get-tuple-element.25.kv_own, bf16[4,128,128]{2,1,0:T(8,128)(2,1)S(1)} %get-tuple-element.26.q_own, ...), custom_call_target="tpu_custom_call" | custom-call | flops 2000000000 | bytes 6000000 | tf_op jit(solution)/shard_map/pallas_call | solution.py:251
  43.1 1.3 collective-permute-start.6
  44.4 4.0 %collective-permute-start.5 = (bf16[2,4,128,256]{3,2,1,0:T(8,128)(2,1)S(1)}, bf16[2,4,128,256]{3,2,1,0:T(8,128)(2,1)S(1)}, u32[]{:S(2)}, u32[]{:S(2)}) collective-permute-start(bf16[2,4,128,256]{3,2,1,0:T(8,128)(2,1)S(1)} %get-tuple-element.29.kv2), channel_id=1, source_target_pairs={{0,8},{4,12},{8,16},{12,20},{16,24},{20,28},{24,32},{28,36},{32,40... | collective-permute-start | bytes 1572872 | tf_op jit(solution)/shard_map/ppermute | solution.py:342
  48.4 10.3 %all-to-all-start.3 = ((bf16[8,96,128]{2,1,0:T(8,128)(2,1)}), bf16[8,96,128]{2,1,0:T(8,128)(2,1)S(1)}, u32[]{:S(2)}, u32[]{:S(2)}) async-start(bf16[8,96,128]{2,1,0:T(8,128)(2,1)} %get-tuple-element.31), calls=%async_computation.3 | async-start | bytes 393216 | tf_op jit(solution)/shard_map/all_to_all | solution.py:284
  58.8 1.3 collective-permute-start.8
  60.1 4.9 %collective-permute-start.7 = (bf16[4,128,256]{2,1,0:T(8,128)(2,1)S(1)}, bf16[4,128,256]{2,1,0:T(8,128)(2,1)S(1)}, u32[]{:S(2)}, u32[]{:S(2)}) collective-permute-start(bf16[4,128,256]{2,1,0:T(8,128)(2,1)S(1)} %get-tuple-element.34), channel_id=1, source_target_pairs={{0,16},{4,20},{8,24},{12,28},{16,32},{20,36},{24,40},{28,44},{32,4... | collective-permute-start | bytes 786440 | tf_op jit(solution)/shard_map/ppermute | solution.py:344
  65.0 0.1 min.12.pat
  65.1 14.7 %all-to-all-done.3 = bf16[8,96,128]{2,1,0:T(8,128)(2,1)S(1)} async-done(((bf16[8,96,128]{2,1,0:T(8,128)(2,1)}), bf16[8,96,128]{2,1,0:T(8,128)(2,1)S(1)}, u32[]{:S(2)}, u32[]{:S(2)}) %all-to-all-start.3) | async-done | bytes 196640 | tf_op jit(solution)/shard_map/all_to_all | solution.py:284
  79.8 0.0 copy-start.5
  79.8 33.8 %conditional.1 = (bf16[8,80,128]{2,1,0:T(8,128)(2,1)S(1)}) conditional(s32[]{:T(128)} %convert_element_type.9, () %tuple.11, (bf16[8,96,128]{2,1,0:T(8,128)(2,1)S(1)}, s32[6]{0:T(128)S(1)}) %tuple.12), branch_computations={%region_0.1_spmd, %region_1.2_spmd} | conditional | flops 2000000000 | bytes 6720904 | solution.py:363
  79.8 22.4 %all_to_all.23.got = bf16[8,96,128]{2,1,0:T(8,128)(2,1)S(1)} all-to-all(bf16[8,96,128]{2,1,0:T(8,128)(2,1)S(1)} %get-tuple-element.14), channel_id=1, replica_groups={{0,64,128,192,256,320,384,448},{4,68,132,196,260,324,388,452},{8,72,136..., dimensions={0} | all-to-all | bytes 393216 | tf_op jit(solution)/shard_map/cond/branch_1_fun/all_to_all | solution.py:284
  102.2 0.6 branch_1_fun.3
  102.8 10.8 %all_to_all.24 = bf16[8,80,128]{2,1,0:T(8,128)(2,1)S(1)} all-to-all(bf16[8,80,128]{2,1,0:T(8,128)(2,1)S(1)} %branch_1_fun.3), channel_id=1, replica_groups={{0,8,16,24,32,40,48,56},{4,12,20,28,36,44,52,60},{64,72,80,88,96,104,11..., dimensions={0} | all-to-all | bytes 327680 | tf_op jit(solution)/shard_map/cond/branch_1_fun/all_to_all | solution.py:284
  113.6 0.0 collective-permute-done.8.tm
  113.6 0.0 collective-permute-done.7.tp
  113.6 0.0 collective-permute-done.6.zm
  113.6 0.0 collective-permute-done.5.zp
  113.6 0.0 copy-done.5
  113.6 9.6 %shard_map.68 = bf16[8,128,128]{2,1,0:T(8,128)(2,1)S(1)} custom-call(s32[6]{0:T(128)S(1)} %stack.27.scal, s32[48]{0:T(128)S(1)} %min.12.pat, bf16[2,4,128,256]{3,2,1,0:T(8,128)(2,1)S(1)} %get-tuple-element.29.kv2, bf16[2,4,128,128]{3,2,1,0:T(8,128)(2,1)S(1)} %get-tuple-element.30.q2, bf16[2,4,128,256]{3,2,1,0:T(8,128)(2,1)S(1)} %collective-permute-done.5.zp, ...), custom_call_target="tpu_custom_call" | custom-call | flops 8000000000 | bytes 24000000 | tf_op jit(solution)/shard_map/pallas_call | solution.py:251
  123.2 12.2 %all_to_all.25 = bf16[8,128,128]{2,1,0:T(8,128)(2,1)S(1)} all-to-all(bf16[8,128,128]{2,1,0:T(8,128)(2,1)S(1)} %shard_map.68), channel_id=1, replica_groups={{0,4,1,5,2,6,3,7},{8,12,9,13,10,14,11,15},{16,20,17,21,18,22,19,23},{24..., dimensions={0} | all-to-all | bytes 524288 | tf_op jit(solution)/shard_map/all_to_all | solution.py:284
  135.3 0.2 copy.7
  135.5 0.9 copy.8
  (5 shorter events, 0.1 us)
Async XLA Ops:
  0.0 25.3 %copy-start.2 = (bf16[1,128,2048]{2,1,0:T(8,128)(2,1)S(1)}, bf16[1,128,2048]{2,1,0:T(8,128)(2,1)}, u32[]{:S(2)}) copy-start(bf16[1,128,2048]{2,1,0:T(8,128)(2,1)} %t0.1) | copy-start | bytes 1572868
  0.0 18.7 %collective-permute-start.1 = (bf16[128,2048]{1,0:T(8,128)(2,1)}, bf16[128,2048]{1,0:T(8,128)(2,1)S(1)}, u32[]{:S(2)}, u32[]{:S(2)}) collective-permute-start(bf16[128,2048]{1,0:T(8,128)(2,1)} %bitcast.18), channel_id=1, source_target_pairs={{0,3},{1,0},{2,1},{3,2},{4,7},{5,4},{6,5},{7,6},{8,11},{9,8},{10,9... | collective-permute-start | bytes 1572872 | tf_op jit(solution)/shard_map/ppermute | solution.py:298
  5.3 18.0 %collective-permute-start = (bf16[128,2048]{1,0:T(8,128)(2,1)}, bf16[128,2048]{1,0:T(8,128)(2,1)S(1)}, u32[]{:S(2)}, u32[]{:S(2)}) collective-permute-start(bf16[128,2048]{1,0:T(8,128)(2,1)} %bitcast.19), channel_id=1, source_target_pairs={{0,1},{1,2},{2,3},{3,0},{4,5},{5,6},{6,7},{7,4},{8,9},{9,10},{10,1... | collective-permute-start | bytes 1572872 | tf_op jit(solution)/shard_map/ppermute | solution.py:297
  7.3 0.7 copy-start.4
  8.0 0.7 copy-start.6
  9.8 15.5 %all-to-all-start.2 = ((f32[8,8,128]{2,1,0:T(8,128)}), f32[8,8,128]{2,1,0:T(8,128)S(1)}, u32[]{:S(2)}, u32[]{:S(2)}) async-start(f32[8,8,128]{2,1,0:T(8,128)} %shard_map.64), calls=%async_computation.2 | async-start | bytes 65536 | tf_op jit(solution)/shard_map/all_to_all | solution.py:284
  18.8 9.9 %collective-permute-start.3 = (bf16[64,2048]{1,0:T(8,128)(2,1)S(1)}, bf16[64,2048]{1,0:T(8,128)(2,1)S(1)}, u32[]{:S(2)}, u32[]{:S(2)}) collective-permute-start(bf16[64,2048]{1,0:T(8,128)(2,1)S(1)} %slice.22), channel_id=1, source_target_pairs={{0,3},{1,0},{2,1},{3,2},{4,7},{5,4},{6,5},{7,6},{8,11},{9,8},{10,9... | collective-permute-start | bytes 786440 | tf_op jit(solution)/shard_map/ppermute | solution.py:305
  23.3 10.3 %collective-permute-start.2 = (bf16[64,2048]{1,0:T(8,128)(2,1)S(1)}, bf16[64,2048]{1,0:T(8,128)(2,1)S(1)}, u32[]{:S(2)}, u32[]{:S(2)}) collective-permute-start(bf16[64,2048]{1,0:T(8,128)(2,1)S(1)} %slice.21), channel_id=1, source_target_pairs={{0,1},{1,2},{2,3},{3,0},{4,5},{5,6},{6,7},{7,4},{8,9},{9,10},{10,1... | collective-permute-start | bytes 786440 | tf_op jit(solution)/shard_map/ppermute | solution.py:304
  25.3 1.9 %copy-start = (bf16[2048,3,256]{2,0,1:T(8,128)(2,1)S(1)}, bf16[2048,3,256]{2,0,1:T(8,128)(2,1)}, u32[]{:S(2)}) copy-start(bf16[2048,3,256]{2,0,1:T(8,128)(2,1)} %param.9) | copy-start | bytes 9437188
  27.2 6.5 %copy-start.1 = (bf16[2048,3,256]{2,0,1:T(8,128)(2,1)S(1)}, bf16[2048,3,256]{2,0,1:T(8,128)(2,1)}, u32[]{:S(2)}) copy-start(bf16[2048,3,256]{2,0,1:T(8,128)(2,1)} %param.9) | copy-start | bytes 9437188
  27.8 12.6 %copy-start.3 = (bf16[8,128,16]{1,2,0:T(8,128)(2,1)S(1)}, bf16[8,128,16]{1,2,0:T(8,128)(2,1)}, u32[]{:S(2)}) copy-start(bf16[8,128,16]{1,2,0:T(8,128)(2,1)} %param.10) | copy-start | bytes 98308
  35.6 4.8 %collective-permute-start.4 = (bf16[4,128,384]{2,1,0:T(8,128)(2,1)S(1)}, bf16[4,128,384]{2,1,0:T(8,128)(2,1)S(1)}, u32[]{:S(2)}, u32[]{:S(2)}) collective-permute-start(bf16[4,128,384]{2,1,0:T(8,128)(2,1)S(1)} %get-tuple-element.27), channel_id=1, source_target_pairs={{0,4},{4,0},{8,12},{12,8},{16,20},{20,16},{24,28},{28,24},{32,36},... | collective-permute-start | bytes 1179656 | tf_op jit(solution)/shard_map/ppermute | solution.py:326
  43.1 70.5 %collective-permute-start.6 = (bf16[2,4,128,256]{3,2,1,0:T(8,128)(2,1)S(1)}, bf16[2,4,128,256]{3,2,1,0:T(8,128)(2,1)S(1)}, u32[]{:S(2)}, u32[]{:S(2)}) collective-permute-start(bf16[2,4,128,256]{3,2,1,0:T(8,128)(2,1)S(1)} %get-tuple-element.29.kv2), channel_id=1, source_target_pairs={{8,0},{12,4},{16,8},{20,12},{24,16},{28,20},{32,24},{36,28},{40,32... | collective-permute-start | bytes 1572872 | tf_op jit(solution)/shard_map/ppermute | solution.py:343
  44.4 69.2 %collective-permute-start.5 = (bf16[2,4,128,256]{3,2,1,0:T(8,128)(2,1)S(1)}, bf16[2,4,128,256]{3,2,1,0:T(8,128)(2,1)S(1)}, u32[]{:S(2)}, u32[]{:S(2)}) collective-permute-start(bf16[2,4,128,256]{3,2,1,0:T(8,128)(2,1)S(1)} %get-tuple-element.29.kv2), channel_id=1, source_target_pairs={{0,8},{4,12},{8,16},{12,20},{16,24},{20,28},{24,32},{28,36},{32,40... | collective-permute-start | bytes 1572872 | tf_op jit(solution)/shard_map/ppermute | solution.py:342
  48.4 31.4 %all-to-all-start.3 = ((bf16[8,96,128]{2,1,0:T(8,128)(2,1)}), bf16[8,96,128]{2,1,0:T(8,128)(2,1)S(1)}, u32[]{:S(2)}, u32[]{:S(2)}) async-start(bf16[8,96,128]{2,1,0:T(8,128)(2,1)} %get-tuple-element.31), calls=%async_computation.3 | async-start | bytes 393216 | tf_op jit(solution)/shard_map/all_to_all | solution.py:284
  58.8 54.8 %collective-permute-start.8 = (bf16[4,128,256]{2,1,0:T(8,128)(2,1)S(1)}, bf16[4,128,256]{2,1,0:T(8,128)(2,1)S(1)}, u32[]{:S(2)}, u32[]{:S(2)}) collective-permute-start(bf16[4,128,256]{2,1,0:T(8,128)(2,1)S(1)} %get-tuple-element.33), channel_id=1, source_target_pairs={{16,0},{20,4},{24,8},{28,12},{32,16},{36,20},{40,24},{44,28},{48,3... | collective-permute-start | bytes 786440 | tf_op jit(solution)/shard_map/ppermute | solution.py:345
  60.1 53.5 %collective-permute-start.7 = (bf16[4,128,256]{2,1,0:T(8,128)(2,1)S(1)}, bf16[4,128,256]{2,1,0:T(8,128)(2,1)S(1)}, u32[]{:S(2)}, u32[]{:S(2)}) collective-permute-start(bf16[4,128,256]{2,1,0:T(8,128)(2,1)S(1)} %get-tuple-element.34), channel_id=1, source_target_pairs={{0,16},{4,20},{8,24},{12,28},{16,32},{20,36},{24,40},{28,44},{32,4... | collective-permute-start | bytes 786440 | tf_op jit(solution)/shard_map/ppermute | solution.py:344
  79.8 33.8 %copy-start.5 = (f32[1024]{0:T(1024)S(1)}, f32[1024]{0:T(1024)}, u32[]{:S(2)}) copy-start(f32[1024]{0:T(1024)} %param.11) | copy-start | bytes 12292

commit v7 on v6

--- a/solution.py
+++ b/solution.py
@@ -16,6 +16,7 @@
 NB = 2
 DOCS = 4
 EPS = 1e-06
+LOG2E = 1.4426950408889634
 MASKED = -1e30
 CHIPS = 64
 ROWS = 96
@@ -100,7 +101,7 @@
                 kvq_other[n, :, here] = other
 
 
-def states_kernel(scal, kv_own, q_own, kvq_mate, steps, wft, out, state0, kv2, q2):
+def states_kernel(scal, kv_own, kvq_mate, steps, wft, out, state0):
     c, h = scal[0], scal[5]
     first = c == 0
     cum = cumulative_of(steps[...])
@@ -110,11 +111,8 @@
         own = kv_own[n]
         mate = kvq_mate[n, :, : 2 * DH]
         segs = (jnp.where(first, own, mate), jnp.where(first, mate, own))
-        q2[c, n] = q_own[n]
-        q2[1 - c, n] = kvq_mate[n, :, 2 * DH :]
         local = []
         for s in range(2):
-            kv2[s, n] = segs[s]
             phi = softmax0(nt(feature, segs[s][:, :DH])).astype(BF).astype(F32)
             line = cum[2 * n + s : 2 * n + s + 1]
             final = line[:, TOK - 1 :]
@@ -133,6 +131,21 @@
             out[p, 64:96] = segs[0][32 * half : 32 * half + 32, DH:]
 
 
+def join_kernel(scal, kv_own, q_own, kvq_mate, send1, kv2, q2, seg0, seg1):
+    c = scal[0]
+    first = c == 0
+    for n in range(DOCS):
+        own = kv_own[n]
+        mate = kvq_mate[n, :, : 2 * DH]
+        early, later = jnp.where(first, own, mate), jnp.where(first, mate, own)
+        kv2[0, n] = early
+        seg0[n] = early
+        kv2[1, n] = later
+        seg1[n] = later
+        q2[c, n] = q_own[n]
+        q2[1 - c, n] = kvq_mate[n, :, 2 * DH :]
+
+
 def state_rows(state):
     hi, lo = split2(state)
     return jnp.concatenate([hi.astype(F32), lo.astype(F32)], axis=0).astype(BF)
@@ -199,7 +212,7 @@
     causal = row >= col
     gains = gain[h]
     lane = lax.broadcasted_iota(jnp.int32, (1, 7 * BS), 1)
-    scale = DH ** (-0.5)
+    scale = DH ** (-0.5) * LOG2E
     for n in range(DOCS):
         carried = jnp.concatenate([read_state(got, 2 * n), read_state(got, 2 * n + 1)], axis=0)
         gk = jnp.concatenate([got[2 * n, 16:48], got[2 * n + 1, 16:48]], axis=0)
@@ -230,7 +243,7 @@
                 near = jnp.concatenate(picks, axis=0)
                 all_k = jnp.concatenate([near[:, :DH], gk], axis=0)
                 all_v = jnp.concatenate([near[:, DH:], gv], axis=0)
-                scores = nt(queries[half * BS : half * BS + BS], all_k) * scale
+                scores = nt(queries[half * BS : half * BS + BS], all_k)
                 bad = (
                     ((lane < BS) & (block < 2))
                     | ((lane >= BS) & (lane < 2 * BS) & (block < 1))
@@ -238,9 +251,9 @@
                 )
                 scores = jnp.where(bad, MASKED, scores)
                 top = jnp.max(scores, axis=1, keepdims=True)
-                e = jnp.exp(scores - top)
-                soft = (e / jnp.sum(e, axis=1, keepdims=True)).astype(BF)
-                sparse = mm(soft, all_v)
+                e = jnp.exp2((scores - top) * scale)
+                share = 1.0 / jnp.sum(e, axis=1, keepdims=True)
+                sparse = mm(e.astype(BF), all_v) * share
                 out[2 * n + s, half * BS : half * BS + BS] = (
                     normed[half * BS : half * BS + BS] + sparse
                 ).astype(BF)
@@ -324,25 +337,35 @@
         scal, early, ta, tb, td1, td2, got0, w3,
     )
     kvq_mate = lax.ppermute(kvq_other, "seq", pairs(lambda q, c: (q, 1 - c)))
-    send1, state0, kv2, q2 = call(
+    send1, state0 = call(
         states_kernel,
+        [shape((8, ROWS, TOK), BF), shape((DOCS, F, DH), F32)],
+        [],
+        "svvvv",
+        2,
+        8,
+        scal, kv_own, kvq_mate, steps, wft,
+    )
+    got1 = exchange(send1, "seq", ZS)
+    kv2, q2, seg0, seg1 = call(
+        join_kernel,
         [
-            shape((8, ROWS, TOK), BF),
-            shape((DOCS, F, DH), F32),
             shape((2, DOCS, TOK, 2 * DH), BF),
             shape((2, DOCS, TOK, DH), BF),
+            shape((DOCS, TOK, 2 * DH), BF),
+            shape((DOCS, TOK, 2 * DH), BF),
         ],
         [],
-        "svvvvv",
-        2,
+        "svvva",
+        1,
         8,
-        scal, kv_own, q_own, kvq_mate, steps, wft,
-    )
-    got1 = exchange(send1, "seq", ZS)
+        scal, kv_own, q_own, kvq_mate, send1,
+    )
+    kv2, seg0, seg1, got1 = lax.optimization_barrier((kv2, seg0, seg1, got1))
     zp = lax.ppermute(kv2, "seq", pairs(lambda q, c: (q + 1, c)))
     zm = lax.ppermute(kv2, "seq", pairs(lambda q, c: (q - 1, c)))
-    tp = lax.ppermute(kv2[1], "seq", pairs(lambda q, c: (q + 2, c)))
-    tm = lax.ppermute(kv2[0], "seq", pairs(lambda q, c: (q - 2, c)))
+    tp = lax.ppermute(seg1, "seq", pairs(lambda q, c: (q + 2, c)))
+    tm = lax.ppermute(seg0, "seq", pairs(lambda q, c: (q - 2, c)))
 
     def chain(got1):
         send2, inner, outer = call(

time: 137 us -> 130 us (0.949)
  waiting for transfers between devices: 21.9 us -> 16 us
  starting transfers between devices: 47.8 us -> 42.6 us
  blocking collectives: 45.3 us -> 50.4 us
    all_to_all x2, waiting for transfers between devices: 14.7 us -> 8.78 us  [exchange(): return lax.all_to_all(a, axis, 0, 0, tiled=True, axis_index_groups=groups)]
    all_to_all x3, blocking collectives: 45.3 us -> 50.4 us  [exchange(): return lax.all_to_all(a, axis, 0, 0, tiled=True, axis_index_groups=groups)]
    ppermute x2, starting transfers between devices: 6.2 us -> 3.13 us  [the longest x1 1.83 us: per_device(): tp = lax.ppermute(seg1, 'seq', pairs(lambda q, c: (q + 2, c)))]
    all_to_all x2, starting transfers between devices: 19.1 us -> 17 us  [exchange(): return lax.all_to_all(a, axis, 0, 0, tiled=True, axis_index_groups=groups)]
    pallas_call x7 -> x8, Pallas kernels: 16.6 us -> 16 us  [call(): pl.pallas_call(kernel, out_shape=outs, in_specs=[pl.BlockSpec(memory_spac...]
where the time goes in v7:
time: 130 us
  blocking collectives  50.4 us (39%)
  starting transfers between devices  42.6 us (33%)
  Pallas kernels  16 us (12%)
  waiting for transfers between devices  16 us (12%)
  local copies, waits for them, and re-layouts  4.49 us (3%)
    all_to_all x3, blocking collectives, exchange(): return lax.all_to_all(a, axis, 0, 0, tiled=True, axis_index_groups=groups)  50.4 us
    all_to_all x2, starting transfers between devices, exchange(): return lax.all_to_all(a, axis, 0, 0, tiled=True, axis_index_groups=groups)  17 us
    pallas_call x8, Pallas kernels, call(): pl.pallas_call(kernel, out_shape=outs, in_specs=[pl.BlockSpec(memory_spac...  16 us
    all_to_all x2, waiting for transfers between devices, exchange(): return lax.all_to_all(a, axis, 0, 0, tiled=True, axis_index_groups=groups)  8.78 us
    ppermute x1, starting transfers between devices, per_device(): tb = lax.ppermute(t0, 'fsdp', down)  5.34 us
    ppermute x1, waiting for transfers between devices, per_device(): td1 = lax.ppermute(ta[:64], 'fsdp', up)  5.05 us
    ppermute x1, starting transfers between devices, per_device(): td2 = lax.ppermute(tb[64:], 'fsdp', down)  4.54 us
    ppermute x1, starting transfers between devices, per_device(): zp = lax.ppermute(kv2, 'seq', pairs(lambda q, c: (q + 1, c)))  4.02 us
  transfers between devices with their start and end apart: 11, of which 4 were waited for; matrix products, arithmetic and copies ran while one was open for 0% of the time, Pallas kernels for 2%

profile of v7, /device:TPU:1, one launch (start us, length us, event | category | flops | bytes accessed | tf_op | source)
XLA Modules:
  0.0 129.7 jit_solution(2614851151939569894)
XLA Ops:
  0.0 0.0 copy-start.2
  0.0 5.3 %collective-permute-start.1 = (bf16[128,2048]{1,0:T(8,128)(2,1)}, bf16[128,2048]{1,0:T(8,128)(2,1)S(1)}, u32[]{:S(2)}, u32[]{:S(2)}) collective-permute-start(bf16[128,2048]{1,0:T(8,128)(2,1)} %bitcast.14), channel_id=1, source_target_pairs={{0,3},{1,0},{2,1},{3,2},{4,7},{5,4},{6,5},{7,6},{8,11},{9,8},{10,9... | collective-permute-start | bytes 1572872 | tf_op jit(solution)/shard_map/ppermute | solution.py:311
  5.3 1.9 %collective-permute-start = (bf16[128,2048]{1,0:T(8,128)(2,1)}, bf16[128,2048]{1,0:T(8,128)(2,1)S(1)}, u32[]{:S(2)}, u32[]{:S(2)}) collective-permute-start(bf16[128,2048]{1,0:T(8,128)(2,1)} %bitcast.15), channel_id=1, source_target_pairs={{0,1},{1,2},{2,3},{3,0},{4,5},{5,6},{6,7},{7,4},{8,9},{9,10},{10,1... | collective-permute-start | bytes 1572872 | tf_op jit(solution)/shard_map/ppermute | solution.py:310
  7.3 0.0 copy-start.4
  7.3 0.7 copy-done.4
  8.0 0.0 copy-start.6
  8.0 0.7 copy-done.6
  8.6 1.2 shard_map.64
  9.8 8.8 %all-to-all-start.2 = ((f32[8,8,128]{2,1,0:T(8,128)}), f32[8,8,128]{2,1,0:T(8,128)S(1)}, u32[]{:S(2)}, u32[]{:S(2)}) async-start(f32[8,8,128]{2,1,0:T(8,128)} %shard_map.64), calls=%async_computation.2 | async-start | bytes 65536 | tf_op jit(solution)/shard_map/all_to_all | solution.py:297
  18.6 0.1 stack.27.scal
  18.7 0.0 collective-permute-done.1.tb
  18.8 4.5 %collective-permute-start.3 = (bf16[64,2048]{1,0:T(8,128)(2,1)S(1)}, bf16[64,2048]{1,0:T(8,128)(2,1)S(1)}, u32[]{:S(2)}, u32[]{:S(2)}) collective-permute-start(bf16[64,2048]{1,0:T(8,128)(2,1)S(1)} %slice.14), channel_id=1, source_target_pairs={{0,3},{1,0},{2,1},{3,2},{4,7},{5,4},{6,5},{7,6},{8,11},{9,8},{10,9... | collective-permute-start | bytes 786440 | tf_op jit(solution)/shard_map/ppermute | solution.py:318
  23.3 0.0 collective-permute-done.ta
  23.3 1.9 %collective-permute-start.2 = (bf16[64,2048]{1,0:T(8,128)(2,1)S(1)}, bf16[64,2048]{1,0:T(8,128)(2,1)S(1)}, u32[]{:S(2)}, u32[]{:S(2)}) collective-permute-start(bf16[64,2048]{1,0:T(8,128)(2,1)S(1)} %slice.13), channel_id=1, source_target_pairs={{0,1},{1,2},{2,3},{3,0},{4,5},{5,6},{6,7},{7,4},{8,9},{9,10},{10,1... | collective-permute-start | bytes 786440 | tf_op jit(solution)/shard_map/ppermute | solution.py:317
  25.3 0.0 all-to-all-done.2.got
  25.3 0.0 copy-done.2
  25.3 0.0 copy-start
  25.3 1.9 %copy-done = bf16[2048,3,256]{2,0,1:T(8,128)(2,1)S(1)} copy-done((bf16[2048,3,256]{2,0,1:T(8,128)(2,1)S(1)}, bf16[2048,3,256]{2,0,1:T(8,128)(2,1)}, u32[]{:S(2)}) %copy-start) | copy-done | bytes 3145752
  27.2 0.0 copy-start.1
  27.2 0.6 shard_map.65.early
  27.8 0.0 copy-start.3
  27.8 0.8 collective-permute-done.3.td2
  28.6 5.0 %collective-permute-done.2.td1 = bf16[64,2048]{1,0:T(8,128)(2,1)S(1)} collective-permute-done((bf16[64,2048]{1,0:T(8,128)(2,1)S(1)}, bf16[64,2048]{1,0:T(8,128)(2,1)S(1)}, u32[]{:S(2)}, u32[]{:S(2)}) %collective-permute-start.2) | collective-permute-done | bytes 262176 | tf_op jit(solution)/shard_map/ppermute | solution.py:317
  33.7 0.0 copy-done.1
  33.7 1.9 %shard_map.66 = (bf16[4,128,256]{2,1,0:T(8,128)(2,1)S(1)}, bf16[4,128,384]{2,1,0:T(8,128)(2,1)S(1)}, bf16[4,128,128]{2,1,0:T(8,128)(2,1)S(1)}, f32[8,128]{1,0:T(8,128)S(1)}) custom-call(s32[6]{0:T(128)S(1)} %stack.27.scal, bf16[3,128,256]{2,1,0:T(8,128)(2,1)S(1)} %shard_map.65.early, bf16[128,2048]{1,0:T(8,128)(2,1)S(1)} %collective-permute-done.ta, ...), custom_call_target="tpu_custom_call" | custom-call | flops 3000000000 | bytes 9000000 | tf_op jit(solution)/shard_map/pallas_call | solution.py:264
  35.6 3.4 %collective-permute-start.4 = (bf16[4,128,384]{2,1,0:T(8,128)(2,1)S(1)}, bf16[4,128,384]{2,1,0:T(8,128)(2,1)S(1)}, u32[]{:S(2)}, u32[]{:S(2)}) collective-permute-start(bf16[4,128,384]{2,1,0:T(8,128)(2,1)S(1)} %get-tuple-element.33), channel_id=1, source_target_pairs={{0,4},{4,0},{8,12},{12,8},{16,20},{20,16},{24,28},{28,24},{32,36},... | collective-permute-start | bytes 1179656 | tf_op jit(solution)/shard_map/ppermute | solution.py:339
  39.0 1.3 %collective-permute-done.4.kvq_mate = bf16[4,128,384]{2,1,0:T(8,128)(2,1)S(1)} collective-permute-done((bf16[4,128,384]{2,1,0:T(8,128)(2,1)S(1)}, bf16[4,128,384]{2,1,0:T(8,128)(2,1)S(1)}, u32[]{:S(2)}, u32[]{:S(2)}) %collective-permute-start.4) | collective-permute-done | bytes 393248 | tf_op jit(solution)/shard_map/ppermute | solution.py:339
  40.3 0.0 copy-done.3
  40.3 2.7 %shard_map.67 = (bf16[8,96,128]{2,1,0:T(8,128)(2,1)}, f32[4,16,128]{2,1,0:T(8,128)S(1)}) custom-call(s32[6]{0:T(128)S(1)} %stack.27.scal, bf16[4,128,256]{2,1,0:T(8,128)(2,1)S(1)} %get-tuple-element.31.kv_own, bf16[4,128,384]{2,1,0:T(8,128)(2,1)S(1)} %collective-permute-done.4.kvq_mate, f32[8,128]{1,0:T(8,128)S(1)} %get-tuple-element.34.steps, ...), custom_call_target="tpu_custom_call" | custom-call | flops 2000000000 | bytes 6000000 | tf_op jit(solution)/shard_map/pallas_call | solution.py:264
  43.1 8.2 %all-to-all-start.3 = ((bf16[8,96,128]{2,1,0:T(8,128)(2,1)}), bf16[8,96,128]{2,1,0:T(8,128)(2,1)S(1)}, u32[]{:S(2)}, u32[]{:S(2)}) async-start(bf16[8,96,128]{2,1,0:T(8,128)(2,1)} %get-tuple-element.35.send1), calls=%async_computation.3 | async-start | bytes 393216 | tf_op jit(solution)/shard_map/all_to_all | solution.py:297
  51.3 0.6 shard_map.68
  51.9 8.8 %all-to-all-done.3 = bf16[8,96,128]{2,1,0:T(8,128)(2,1)S(1)} async-done(((bf16[8,96,128]{2,1,0:T(8,128)(2,1)}), bf16[8,96,128]{2,1,0:T(8,128)(2,1)S(1)}, u32[]{:S(2)}, u32[]{:S(2)}) %all-to-all-start.3) | async-done | bytes 196640 | tf_op jit(solution)/shard_map/all_to_all | solution.py:297
  60.7 1.3 collective-permute-start.6
  62.0 4.0 %collective-permute-start.5 = (bf16[2,4,128,256]{3,2,1,0:T(8,128)(2,1)S(1)}, bf16[2,4,128,256]{3,2,1,0:T(8,128)(2,1)S(1)}, u32[]{:S(2)}, u32[]{:S(2)}) collective-permute-start(bf16[2,4,128,256]{3,2,1,0:T(8,128)(2,1)S(1)} %get-tuple-element.39.kv2), channel_id=1, source_target_pairs={{0,8},{4,12},{8,16},{12,20},{16,24},{20,28},{24,32},{28,36},{32,40... | collective-permute-start | bytes 1572872 | tf_op jit(solution)/shard_map/ppermute | solution.py:365
  66.0 1.8 %collective-permute-start.7 = (bf16[4,128,256]{2,1,0:T(8,128)(2,1)S(1)}, bf16[4,128,256]{2,1,0:T(8,128)(2,1)S(1)}, u32[]{:S(2)}, u32[]{:S(2)}) collective-permute-start(bf16[4,128,256]{2,1,0:T(8,128)(2,1)S(1)} %get-tuple-element.41), channel_id=1, source_target_pairs={{0,16},{4,20},{8,24},{12,28},{16,32},{20,36},{24,40},{28,44},{32,4... | collective-permute-start | bytes 786440 | tf_op jit(solution)/shard_map/ppermute | solution.py:367
  67.9 1.3 collective-permute-start.8
  69.2 0.1 min.12.pat
  69.3 0.0 copy-start.5
  69.3 36.7 %conditional.1 = (bf16[8,80,128]{2,1,0:T(8,128)(2,1)S(1)}) conditional(s32[]{:T(128)} %convert_element_type.9, () %tuple.13, (bf16[8,96,128]{2,1,0:T(8,128)(2,1)S(1)}, s32[6]{0:T(128)S(1)}) %tuple.14), branch_computations={%region_0.1_spmd, %region_1.2_spmd} | conditional | flops 2000000000 | bytes 6720904 | solution.py:386
  69.3 21.7 %all_to_all.23.got = bf16[8,96,128]{2,1,0:T(8,128)(2,1)S(1)} all-to-all(bf16[8,96,128]{2,1,0:T(8,128)(2,1)S(1)} %get-tuple-element.14), channel_id=1, replica_groups={{0,64,128,192,256,320,384,448},{4,68,132,196,260,324,388,452},{8,72,136..., dimensions={0} | all-to-all | bytes 393216 | tf_op jit(solution)/shard_map/cond/branch_1_fun/all_to_all | solution.py:297
  91.0 0.6 branch_1_fun.3
  91.6 14.4 %all_to_all.24 = bf16[8,80,128]{2,1,0:T(8,128)(2,1)S(1)} all-to-all(bf16[8,80,128]{2,1,0:T(8,128)(2,1)S(1)} %branch_1_fun.3), channel_id=1, replica_groups={{0,8,16,24,32,40,48,56},{4,12,20,28,36,44,52,60},{64,72,80,88,96,104,11..., dimensions={0} | all-to-all | bytes 327680 | tf_op jit(solution)/shard_map/cond/branch_1_fun/all_to_all | solution.py:297
  106.0 0.0 collective-permute-done.7.tp
  106.0 0.0 collective-permute-done.8.tm
  106.0 0.0 collective-permute-done.6.zm
  106.0 0.0 collective-permute-done.5.zp
  106.1 0.0 copy-done.5
  106.1 8.3 %shard_map.69 = bf16[8,128,128]{2,1,0:T(8,128)(2,1)S(1)} custom-call(s32[6]{0:T(128)S(1)} %stack.27.scal, s32[48]{0:T(128)S(1)} %min.12.pat, bf16[2,4,128,256]{3,2,1,0:T(8,128)(2,1)S(1)} %get-tuple-element.39.kv2, bf16[2,4,128,128]{3,2,1,0:T(8,128)(2,1)S(1)} %get-tuple-element.40.q2, bf16[2,4,128,256]{3,2,1,0:T(8,128)(2,1)S(1)} %collective-permute-done.5.zp, ...), custom_call_target="tpu_custom_call" | custom-call | flops 8000000000 | bytes 24000000 | tf_op jit(solution)/shard_map/pallas_call | solution.py:264
  114.4 14.3 %all_to_all.25 = bf16[8,128,128]{2,1,0:T(8,128)(2,1)S(1)} all-to-all(bf16[8,128,128]{2,1,0:T(8,128)(2,1)S(1)} %shard_map.69), channel_id=1, replica_groups={{0,4,1,5,2,6,3,7},{8,12,9,13,10,14,11,15},{16,20,17,21,18,22,19,23},{24..., dimensions={0} | all-to-all | bytes 524288 | tf_op jit(solution)/shard_map/all_to_all | solution.py:297
  128.7 0.2 copy.7
  128.9 0.9 copy.8
  (4 shorter events, 0.1 us)
Async XLA Ops:
  0.0 25.3 %copy-start.2 = (bf16[1,128,2048]{2,1,0:T(8,128)(2,1)S(1)}, bf16[1,128,2048]{2,1,0:T(8,128)(2,1)}, u32[]{:S(2)}) copy-start(bf16[1,128,2048]{2,1,0:T(8,128)(2,1)} %t0.1) | copy-start | bytes 1572868
  0.0 18.7 %collective-permute-start.1 = (bf16[128,2048]{1,0:T(8,128)(2,1)}, bf16[128,2048]{1,0:T(8,128)(2,1)S(1)}, u32[]{:S(2)}, u32[]{:S(2)}) collective-permute-start(bf16[128,2048]{1,0:T(8,128)(2,1)} %bitcast.14), channel_id=1, source_target_pairs={{0,3},{1,0},{2,1},{3,2},{4,7},{5,4},{6,5},{7,6},{8,11},{9,8},{10,9... | collective-permute-start | bytes 1572872 | tf_op jit(solution)/shard_map/ppermute | solution.py:311
  5.3 18.0 %collective-permute-start = (bf16[128,2048]{1,0:T(8,128)(2,1)}, bf16[128,2048]{1,0:T(8,128)(2,1)S(1)}, u32[]{:S(2)}, u32[]{:S(2)}) collective-permute-start(bf16[128,2048]{1,0:T(8,128)(2,1)} %bitcast.15), channel_id=1, source_target_pairs={{0,1},{1,2},{2,3},{3,0},{4,5},{5,6},{6,7},{7,4},{8,9},{9,10},{10,1... | collective-permute-start | bytes 1572872 | tf_op jit(solution)/shard_map/ppermute | solution.py:310
  7.3 0.7 copy-start.4
  8.0 0.7 copy-start.6
  9.8 15.5 %all-to-all-start.2 = ((f32[8,8,128]{2,1,0:T(8,128)}), f32[8,8,128]{2,1,0:T(8,128)S(1)}, u32[]{:S(2)}, u32[]{:S(2)}) async-start(f32[8,8,128]{2,1,0:T(8,128)} %shard_map.64), calls=%async_computation.2 | async-start | bytes 65536 | tf_op jit(solution)/shard_map/all_to_all | solution.py:297
  18.8 9.9 %collective-permute-start.3 = (bf16[64,2048]{1,0:T(8,128)(2,1)S(1)}, bf16[64,2048]{1,0:T(8,128)(2,1)S(1)}, u32[]{:S(2)}, u32[]{:S(2)}) collective-permute-start(bf16[64,2048]{1,0:T(8,128)(2,1)S(1)} %slice.14), channel_id=1, source_target_pairs={{0,3},{1,0},{2,1},{3,2},{4,7},{5,4},{6,5},{7,6},{8,11},{9,8},{10,9... | collective-permute-start | bytes 786440 | tf_op jit(solution)/shard_map/ppermute | solution.py:318
  23.3 10.3 %collective-permute-start.2 = (bf16[64,2048]{1,0:T(8,128)(2,1)S(1)}, bf16[64,2048]{1,0:T(8,128)(2,1)S(1)}, u32[]{:S(2)}, u32[]{:S(2)}) collective-permute-start(bf16[64,2048]{1,0:T(8,128)(2,1)S(1)} %slice.13), channel_id=1, source_target_pairs={{0,1},{1,2},{2,3},{3,0},{4,5},{5,6},{6,7},{7,4},{8,9},{9,10},{10,1... | collective-permute-start | bytes 786440 | tf_op jit(solution)/shard_map/ppermute | solution.py:317
  25.3 1.9 %copy-start = (bf16[2048,3,256]{2,0,1:T(8,128)(2,1)S(1)}, bf16[2048,3,256]{2,0,1:T(8,128)(2,1)}, u32[]{:S(2)}) copy-start(bf16[2048,3,256]{2,0,1:T(8,128)(2,1)} %param.9) | copy-start | bytes 9437188
  27.2 6.5 %copy-start.1 = (bf16[2048,3,256]{2,0,1:T(8,128)(2,1)S(1)}, bf16[2048,3,256]{2,0,1:T(8,128)(2,1)}, u32[]{:S(2)}) copy-start(bf16[2048,3,256]{2,0,1:T(8,128)(2,1)} %param.9) | copy-start | bytes 9437188
  27.8 12.6 %copy-start.3 = (bf16[8,128,16]{1,2,0:T(8,128)(2,1)S(1)}, bf16[8,128,16]{1,2,0:T(8,128)(2,1)}, u32[]{:S(2)}) copy-start(bf16[8,128,16]{1,2,0:T(8,128)(2,1)} %param.10) | copy-start | bytes 98308
  35.6 4.8 %collective-permute-start.4 = (bf16[4,128,384]{2,1,0:T(8,128)(2,1)S(1)}, bf16[4,128,384]{2,1,0:T(8,128)(2,1)S(1)}, u32[]{:S(2)}, u32[]{:S(2)}) collective-permute-start(bf16[4,128,384]{2,1,0:T(8,128)(2,1)S(1)} %get-tuple-element.33), channel_id=1, source_target_pairs={{0,4},{4,0},{8,12},{12,8},{16,20},{20,16},{24,28},{28,24},{32,36},... | collective-permute-start | bytes 1179656 | tf_op jit(solution)/shard_map/ppermute | solution.py:339
  43.1 17.6 %all-to-all-start.3 = ((bf16[8,96,128]{2,1,0:T(8,128)(2,1)}), bf16[8,96,128]{2,1,0:T(8,128)(2,1)S(1)}, u32[]{:S(2)}, u32[]{:S(2)}) async-start(bf16[8,96,128]{2,1,0:T(8,128)(2,1)} %get-tuple-element.35.send1), calls=%async_computation.3 | async-start | bytes 393216 | tf_op jit(solution)/shard_map/all_to_all | solution.py:297
  60.7 45.3 %collective-permute-start.6 = (bf16[2,4,128,256]{3,2,1,0:T(8,128)(2,1)S(1)}, bf16[2,4,128,256]{3,2,1,0:T(8,128)(2,1)S(1)}, u32[]{:S(2)}, u32[]{:S(2)}) collective-permute-start(bf16[2,4,128,256]{3,2,1,0:T(8,128)(2,1)S(1)} %get-tuple-element.39.kv2), channel_id=1, source_target_pairs={{8,0},{12,4},{16,8},{20,12},{24,16},{28,20},{32,24},{36,28},{40,32... | collective-permute-start | bytes 1572872 | tf_op jit(solution)/shard_map/ppermute | solution.py:366
  62.0 44.0 %collective-permute-start.5 = (bf16[2,4,128,256]{3,2,1,0:T(8,128)(2,1)S(1)}, bf16[2,4,128,256]{3,2,1,0:T(8,128)(2,1)S(1)}, u32[]{:S(2)}, u32[]{:S(2)}) collective-permute-start(bf16[2,4,128,256]{3,2,1,0:T(8,128)(2,1)S(1)} %get-tuple-element.39.kv2), channel_id=1, source_target_pairs={{0,8},{4,12},{8,16},{12,20},{16,24},{20,28},{24,32},{28,36},{32,40... | collective-permute-start | bytes 1572872 | tf_op jit(solution)/shard_map/ppermute | solution.py:365
  66.0 40.0 %collective-permute-start.7 = (bf16[4,128,256]{2,1,0:T(8,128)(2,1)S(1)}, bf16[4,128,256]{2,1,0:T(8,128)(2,1)S(1)}, u32[]{:S(2)}, u32[]{:S(2)}) collective-permute-start(bf16[4,128,256]{2,1,0:T(8,128)(2,1)S(1)} %get-tuple-element.41), channel_id=1, source_target_pairs={{0,16},{4,20},{8,24},{12,28},{16,32},{20,36},{24,40},{28,44},{32,4... | collective-permute-start | bytes 786440 | tf_op jit(solution)/shard_map/ppermute | solution.py:367
  67.9 38.1 %collective-permute-start.8 = (bf16[4,128,256]{2,1,0:T(8,128)(2,1)S(1)}, bf16[4,128,256]{2,1,0:T(8,128)(2,1)S(1)}, u32[]{:S(2)}, u32[]{:S(2)}) collective-permute-start(bf16[4,128,256]{2,1,0:T(8,128)(2,1)S(1)} %get-tuple-element.42), channel_id=1, source_target_pairs={{16,0},{20,4},{24,8},{28,12},{32,16},{36,20},{40,24},{44,28},{48,3... | collective-permute-start | bytes 786440 | tf_op jit(solution)/shard_map/ppermute | solution.py:368
  69.3 36.8 %copy-start.5 = (f32[1024]{0:T(1024)S(1)}, f32[1024]{0:T(1024)}, u32[]{:S(2)}) copy-start(f32[1024]{0:T(1024)} %param.11) | copy-start | bytes 12292

commit v8 on v7

--- a/solution.py
+++ b/solution.py
@@ -131,7 +131,7 @@
             out[p, 64:96] = segs[0][32 * half : 32 * half + 32, DH:]
 
 
-def join_kernel(scal, kv_own, q_own, kvq_mate, send1, kv2, q2, seg0, seg1):
+def join_kernel(scal, kv_own, q_own, kvq_mate, kv2, q2):
     c = scal[0]
     first = c == 0
     for n in range(DOCS):
@@ -139,9 +139,7 @@
         mate = kvq_mate[n, :, : 2 * DH]
         early, later = jnp.where(first, own, mate), jnp.where(first, mate, own)
         kv2[0, n] = early
-        seg0[n] = early
         kv2[1, n] = later
-        seg1[n] = later
         q2[c, n] = q_own[n]
         q2[1 - c, n] = kvq_mate[n, :, 2 * DH :]
 
@@ -337,6 +335,17 @@
         scal, early, ta, tb, td1, td2, got0, w3,
     )
     kvq_mate = lax.ppermute(kvq_other, "seq", pairs(lambda q, c: (q, 1 - c)))
+    kv2, q2 = call(
+        join_kernel,
+        [shape((2, DOCS, TOK, 2 * DH), BF), shape((2, DOCS, TOK, DH), BF)],
+        [],
+        "svvv",
+        20,
+        8,
+        scal, kv_own, q_own, kvq_mate,
+    )
+    zp = lax.ppermute(kv2, "seq", pairs(lambda q, c: (q + 1, c)))
+    zm = lax.ppermute(kv2, "seq", pairs(lambda q, c: (q - 1, c)))
     send1, state0 = call(
         states_kernel,
         [shape((8, ROWS, TOK), BF), shape((DOCS, F, DH), F32)],
@@ -347,25 +356,9 @@
         scal, kv_own, kvq_mate, steps, wft,
     )
     got1 = exchange(send1, "seq", ZS)
-    kv2, q2, seg0, seg1 = call(
-        join_kernel,
-        [
-            shape((2, DOCS, TOK, 2 * DH), BF),
-            shape((2, DOCS, TOK, DH), BF),
-            shape((DOCS, TOK, 2 * DH), BF),
-            shape((DOCS, TOK, 2 * DH), BF),
-        ],
-        [],
-        "svvva",
-        1,
-        8,
-        scal, kv_own, q_own, kvq_mate, send1,
-    )
-    kv2, seg0, seg1, got1 = lax.optimization_barrier((kv2, seg0, seg1, got1))
-    zp = lax.ppermute(kv2, "seq", pairs(lambda q, c: (q + 1, c)))
-    zm = lax.ppermute(kv2, "seq", pairs(lambda q, c: (q - 1, c)))
-    tp = lax.ppermute(seg1, "seq", pairs(lambda q, c: (q + 2, c)))
-    tm = lax.ppermute(seg0, "seq", pairs(lambda q, c: (q - 2, c)))
+    near_p, near_m, got1 = lax.optimization_barrier((zp[1], zm[0], got1))
+    tp = lax.ppermute(near_p, "seq", pairs(lambda q, c: (q + 1, c)))
+    tm = lax.ppermute(near_m, "seq", pairs(lambda q, c: (q - 1, c)))
 
     def chain(got1):
         send2, inner, outer = call(

time: 130 us -> 131 us (level)
  starting transfers between devices: 42.6 us -> 46.4 us
  blocking collectives: 50.4 us -> 48.1 us
    all_to_all x3, blocking collectives: 50.4 us -> 48.1 us  [exchange(): return lax.all_to_all(a, axis, 0, 0, tiled=True, axis_index_groups=groups)]
    all_to_all x2, starting transfers between devices: 17 us -> 19.1 us  [exchange(): return lax.all_to_all(a, axis, 0, 0, tiled=True, axis_index_groups=groups)]
    ppermute x2, starting transfers between devices: 3.13 us -> 4.84 us  [the longest x1 3.55 us: per_device(): tp = lax.ppermute(near_p, 'seq', pairs(lambda q, c: (q + 1, c)))]
  transfers between devices with their start and end apart: 11 -> 11, of which waited for: 4 -> 4; matrix products, arithmetic and copies ran while one was open for 0% -> 0% of each run, Pallas kernels for 2% -> 4%
where the time goes in v8:
time: 131 us; the launch traced here: 130 us
  blocking collectives  48.1 us (37%)
  starting transfers between devices  46.4 us (35%)
  Pallas kernels  15.9 us (12%)
  waiting for transfers between devices  15.2 us (12%)
  local copies, waits for them, and re-layouts  4.53 us (3%)
    all_to_all x3, blocking collectives, exchange(): return lax.all_to_all(a, axis, 0, 0, tiled=True, axis_index_groups=groups)  48.1 us
    all_to_all x2, starting transfers between devices, exchange(): return lax.all_to_all(a, axis, 0, 0, tiled=True, axis_index_groups=groups)  19.1 us
    pallas_call x8, Pallas kernels, call(): pl.pallas_call(kernel, out_shape=outs, in_specs=[pl.BlockSpec(memory_spac...  15.9 us
    all_to_all x2, waiting for transfers between devices, exchange(): return lax.all_to_all(a, axis, 0, 0, tiled=True, axis_index_groups=groups)  8.01 us
    ppermute x1, starting transfers between devices, per_device(): tb = lax.ppermute(t0, 'fsdp', down)  5.34 us
    ppermute x1, waiting for transfers between devices, per_device(): td1 = lax.ppermute(ta[:64], 'fsdp', up)  5.05 us
    ppermute x1, starting transfers between devices, per_device(): td2 = lax.ppermute(tb[64:], 'fsdp', down)  4.54 us
    ppermute x1, starting transfers between devices, per_device(): zp = lax.ppermute(kv2, 'seq', pairs(lambda q, c: (q + 1, c)))  4.02 us
  transfers between devices with their start and end apart: 11, of which 4 were waited for; matrix products, arithmetic and copies ran while one was open for 0% of the time, Pallas kernels for 4%

profile of v8, /device:TPU:1, one launch (start us, length us, event | category | flops | bytes accessed | tf_op | source)
XLA Modules:
  0.0 130.4 jit_solution(448480392366676155)
XLA Ops:
  0.0 0.0 copy-start.2
  0.0 5.3 %collective-permute-start.1 = (bf16[128,2048]{1,0:T(8,128)(2,1)}, bf16[128,2048]{1,0:T(8,128)(2,1)S(1)}, u32[]{:S(2)}, u32[]{:S(2)}) collective-permute-start(bf16[128,2048]{1,0:T(8,128)(2,1)} %bitcast.18), channel_id=1, source_target_pairs={{0,3},{1,0},{2,1},{3,2},{4,7},{5,4},{6,5},{7,6},{8,11},{9,8},{10,9... | collective-permute-start | bytes 1572872 | tf_op jit(solution)/shard_map/ppermute | solution.py:309
  5.3 1.9 %collective-permute-start = (bf16[128,2048]{1,0:T(8,128)(2,1)}, bf16[128,2048]{1,0:T(8,128)(2,1)S(1)}, u32[]{:S(2)}, u32[]{:S(2)}) collective-permute-start(bf16[128,2048]{1,0:T(8,128)(2,1)} %bitcast.19), channel_id=1, source_target_pairs={{0,1},{1,2},{2,3},{3,0},{4,5},{5,6},{6,7},{7,4},{8,9},{9,10},{10,1... | collective-permute-start | bytes 1572872 | tf_op jit(solution)/shard_map/ppermute | solution.py:308
  7.3 0.0 copy-start.4
  7.3 0.7 copy-done.4
  8.0 0.0 copy-start.6
  8.0 0.7 copy-done.6
  8.6 1.2 shard_map.64
  9.8 8.8 %all-to-all-start.2 = ((f32[8,8,128]{2,1,0:T(8,128)}), f32[8,8,128]{2,1,0:T(8,128)S(1)}, u32[]{:S(2)}, u32[]{:S(2)}) async-start(f32[8,8,128]{2,1,0:T(8,128)} %shard_map.64), calls=%async_computation.2 | async-start | bytes 65536 | tf_op jit(solution)/shard_map/all_to_all | solution.py:295
  18.6 0.1 stack.27.scal
  18.7 0.0 collective-permute-done.1.tb
  18.8 4.5 %collective-permute-start.3 = (bf16[64,2048]{1,0:T(8,128)(2,1)S(1)}, bf16[64,2048]{1,0:T(8,128)(2,1)S(1)}, u32[]{:S(2)}, u32[]{:S(2)}) collective-permute-start(bf16[64,2048]{1,0:T(8,128)(2,1)S(1)} %slice.22), channel_id=1, source_target_pairs={{0,3},{1,0},{2,1},{3,2},{4,7},{5,4},{6,5},{7,6},{8,11},{9,8},{10,9... | collective-permute-start | bytes 786440 | tf_op jit(solution)/shard_map/ppermute | solution.py:316
  23.3 0.0 collective-permute-done.ta
  23.3 1.9 %collective-permute-start.2 = (bf16[64,2048]{1,0:T(8,128)(2,1)S(1)}, bf16[64,2048]{1,0:T(8,128)(2,1)S(1)}, u32[]{:S(2)}, u32[]{:S(2)}) collective-permute-start(bf16[64,2048]{1,0:T(8,128)(2,1)S(1)} %slice.21), channel_id=1, source_target_pairs={{0,1},{1,2},{2,3},{3,0},{4,5},{5,6},{6,7},{7,4},{8,9},{9,10},{10,1... | collective-permute-start | bytes 786440 | tf_op jit(solution)/shard_map/ppermute | solution.py:315
  25.3 0.0 all-to-all-done.2.got
  25.3 0.0 copy-done.2
  25.3 0.0 copy-start
  25.3 1.9 %copy-done = bf16[2048,3,256]{2,0,1:T(8,128)(2,1)S(1)} copy-done((bf16[2048,3,256]{2,0,1:T(8,128)(2,1)S(1)}, bf16[2048,3,256]{2,0,1:T(8,128)(2,1)}, u32[]{:S(2)}) %copy-start) | copy-done | bytes 3145752
  27.2 0.0 copy-start.1
  27.2 0.6 shard_map.65.early
  27.8 0.8 collective-permute-done.3.td2
  28.6 5.0 %collective-permute-done.2.td1 = bf16[64,2048]{1,0:T(8,128)(2,1)S(1)} collective-permute-done((bf16[64,2048]{1,0:T(8,128)(2,1)S(1)}, bf16[64,2048]{1,0:T(8,128)(2,1)S(1)}, u32[]{:S(2)}, u32[]{:S(2)}) %collective-permute-start.2) | collective-permute-done | bytes 262176 | tf_op jit(solution)/shard_map/ppermute | solution.py:315
  33.7 0.0 copy-done.1
  33.7 1.9 %shard_map.66 = (bf16[4,128,256]{2,1,0:T(8,128)(2,1)S(1)}, bf16[4,128,384]{2,1,0:T(8,128)(2,1)S(1)}, bf16[4,128,128]{2,1,0:T(8,128)(2,1)S(1)}, f32[8,128]{1,0:T(8,128)S(1)}) custom-call(s32[6]{0:T(128)S(1)} %stack.27.scal, bf16[3,128,256]{2,1,0:T(8,128)(2,1)S(1)} %shard_map.65.early, bf16[128,2048]{1,0:T(8,128)(2,1)S(1)} %collective-permute-done.ta, ...), custom_call_target="tpu_custom_call" | custom-call | flops 3000000000 | bytes 9000000 | tf_op jit(solution)/shard_map/pallas_call | solution.py:262
  35.6 3.4 %collective-permute-start.4 = (bf16[4,128,384]{2,1,0:T(8,128)(2,1)S(1)}, bf16[4,128,384]{2,1,0:T(8,128)(2,1)S(1)}, u32[]{:S(2)}, u32[]{:S(2)}) collective-permute-start(bf16[4,128,384]{2,1,0:T(8,128)(2,1)S(1)} %get-tuple-element.30), channel_id=1, source_target_pairs={{0,4},{4,0},{8,12},{12,8},{16,20},{20,16},{24,28},{28,24},{32,36},... | collective-permute-start | bytes 1179656 | tf_op jit(solution)/shard_map/ppermute | solution.py:337
  39.0 1.3 %collective-permute-done.4.kvq_mate = bf16[4,128,384]{2,1,0:T(8,128)(2,1)S(1)} collective-permute-done((bf16[4,128,384]{2,1,0:T(8,128)(2,1)S(1)}, bf16[4,128,384]{2,1,0:T(8,128)(2,1)S(1)}, u32[]{:S(2)}, u32[]{:S(2)}) %collective-permute-start.4) | collective-permute-done | bytes 393248 | tf_op jit(solution)/shard_map/ppermute | solution.py:337
  40.3 0.0 copy-start.3
  40.3 0.6 shard_map.67
  41.0 1.3 collective-permute-start.6
  42.3 4.0 %collective-permute-start.5 = (bf16[2,4,128,256]{3,2,1,0:T(8,128)(2,1)S(1)}, bf16[2,4,128,256]{3,2,1,0:T(8,128)(2,1)S(1)}, u32[]{:S(2)}, u32[]{:S(2)}) collective-permute-start(bf16[2,4,128,256]{3,2,1,0:T(8,128)(2,1)S(1)} %get-tuple-element.31.kv2), channel_id=1, source_target_pairs={{0,8},{4,12},{8,16},{12,20},{16,24},{20,28},{24,32},{28,36},{32,40... | collective-permute-start | bytes 1572872 | tf_op jit(solution)/shard_map/ppermute | solution.py:347
  46.3 0.0 copy-done.3
  46.3 2.7 %shard_map.68 = (bf16[8,96,128]{2,1,0:T(8,128)(2,1)}, f32[4,16,128]{2,1,0:T(8,128)S(1)}) custom-call(s32[6]{0:T(128)S(1)} %stack.27.scal, bf16[4,128,256]{2,1,0:T(8,128)(2,1)S(1)} %get-tuple-element.28.kv_own, bf16[4,128,384]{2,1,0:T(8,128)(2,1)S(1)} %collective-permute-done.4.kvq_mate, f32[8,128]{1,0:T(8,128)S(1)} %get-tuple-element.33.steps, ...), custom_call_target="tpu_custom_call" | custom-call | flops 2000000000 | bytes 6000000 | tf_op jit(solution)/shard_map/pallas_call | solution.py:262
  49.0 10.3 %all-to-all-start.3 = ((bf16[8,96,128]{2,1,0:T(8,128)(2,1)}), bf16[8,96,128]{2,1,0:T(8,128)(2,1)S(1)}, u32[]{:S(2)}, u32[]{:S(2)}) async-start(bf16[8,96,128]{2,1,0:T(8,128)(2,1)} %get-tuple-element.34), calls=%async_computation.3 | async-start | bytes 393216 | tf_op jit(solution)/shard_map/all_to_all | solution.py:295
  59.3 0.0 collective-permute-done.6.zm
  59.4 0.0 collective-permute-done.5.zp
  59.4 8.0 %all-to-all-done.3 = bf16[8,96,128]{2,1,0:T(8,128)(2,1)S(1)} async-done(((bf16[8,96,128]{2,1,0:T(8,128)(2,1)}), bf16[8,96,128]{2,1,0:T(8,128)(2,1)S(1)}, u32[]{:S(2)}, u32[]{:S(2)}) %all-to-all-start.3) | async-done | bytes 196640 | tf_op jit(solution)/shard_map/all_to_all | solution.py:295
  67.4 3.6 %collective-permute-start.7 = (bf16[4,128,256]{2,1,0:T(8,128)(2,1)S(1)}, bf16[4,128,256]{2,1,0:T(8,128)(2,1)S(1)}, u32[]{:S(2)}, u32[]{:S(2)}) collective-permute-start(bf16[4,128,256]{2,1,0:T(8,128)(2,1)S(1)} %slice_bitcast_fusion.1), channel_id=1, source_target_pairs={{0,8},{4,12},{8,16},{12,20},{16,24},{20,28},{24,32},{28,36},{32,40... | collective-permute-start | bytes 786440 | tf_op jit(solution)/shard_map/ppermute | solution.py:360
  71.0 1.3 collective-permute-start.8
  72.3 0.1 min.12.pat
  72.4 0.0 copy-start.5
  72.4 35.6 %conditional.1 = (bf16[8,80,128]{2,1,0:T(8,128)(2,1)S(1)}) conditional(s32[]{:T(128)} %convert_element_type.9, () %tuple.13, (bf16[8,96,128]{2,1,0:T(8,128)(2,1)S(1)}, s32[6]{0:T(128)S(1)}) %tuple.14), branch_computations={%region_0.1_spmd, %region_1.2_spmd} | conditional | flops 2000000000 | bytes 6720904 | solution.py:379
  72.4 24.3 %all_to_all.23.got = bf16[8,96,128]{2,1,0:T(8,128)(2,1)S(1)} all-to-all(bf16[8,96,128]{2,1,0:T(8,128)(2,1)S(1)} %get-tuple-element.14), channel_id=1, replica_groups={{0,64,128,192,256,320,384,448},{4,68,132,196,260,324,388,452},{8,72,136..., dimensions={0} | all-to-all | bytes 393216 | tf_op jit(solution)/shard_map/cond/branch_1_fun/all_to_all | solution.py:295
  96.7 0.6 branch_1_fun.3
  97.3 10.7 %all_to_all.24 = bf16[8,80,128]{2,1,0:T(8,128)(2,1)S(1)} all-to-all(bf16[8,80,128]{2,1,0:T(8,128)(2,1)S(1)} %branch_1_fun.3), channel_id=1, replica_groups={{0,8,16,24,32,40,48,56},{4,12,20,28,36,44,52,60},{64,72,80,88,96,104,11..., dimensions={0} | all-to-all | bytes 327680 | tf_op jit(solution)/shard_map/cond/branch_1_fun/all_to_all | solution.py:295
  108.0 0.0 collective-permute-done.7.tp
  108.0 0.0 collective-permute-done.8.tm
  108.0 0.0 copy-done.5
  108.0 8.3 %shard_map.69 = bf16[8,128,128]{2,1,0:T(8,128)(2,1)S(1)} custom-call(s32[6]{0:T(128)S(1)} %stack.27.scal, s32[48]{0:T(128)S(1)} %min.12.pat, bf16[2,4,128,256]{3,2,1,0:T(8,128)(2,1)S(1)} %get-tuple-element.31.kv2, bf16[2,4,128,128]{3,2,1,0:T(8,128)(2,1)S(1)} %get-tuple-element.32.q2, bf16[2,4,128,256]{3,2,1,0:T(8,128)(2,1)S(1)} %collective-permute-done.5.zp, ...), custom_call_target="tpu_custom_call" | custom-call | flops 8000000000 | bytes 24000000 | tf_op jit(solution)/shard_map/pallas_call | solution.py:262
  116.3 13.1 %all_to_all.25 = bf16[8,128,128]{2,1,0:T(8,128)(2,1)S(1)} all-to-all(bf16[8,128,128]{2,1,0:T(8,128)(2,1)S(1)} %shard_map.69), channel_id=1, replica_groups={{0,4,1,5,2,6,3,7},{8,12,9,13,10,14,11,15},{16,20,17,21,18,22,19,23},{24..., dimensions={0} | all-to-all | bytes 524288 | tf_op jit(solution)/shard_map/all_to_all | solution.py:295
  129.4 0.2 copy.7
  129.6 0.9 copy.8
  (6 shorter events, 0.1 us)
Async XLA Ops:
  0.0 25.3 %copy-start.2 = (bf16[1,128,2048]{2,1,0:T(8,128)(2,1)S(1)}, bf16[1,128,2048]{2,1,0:T(8,128)(2,1)}, u32[]{:S(2)}) copy-start(bf16[1,128,2048]{2,1,0:T(8,128)(2,1)} %t0.1) | copy-start | bytes 1572868
  0.0 18.7 %collective-permute-start.1 = (bf16[128,2048]{1,0:T(8,128)(2,1)}, bf16[128,2048]{1,0:T(8,128)(2,1)S(1)}, u32[]{:S(2)}, u32[]{:S(2)}) collective-permute-start(bf16[128,2048]{1,0:T(8,128)(2,1)} %bitcast.18), channel_id=1, source_target_pairs={{0,3},{1,0},{2,1},{3,2},{4,7},{5,4},{6,5},{7,6},{8,11},{9,8},{10,9... | collective-permute-start | bytes 1572872 | tf_op jit(solution)/shard_map/ppermute | solution.py:309
  5.3 18.0 %collective-permute-start = (bf16[128,2048]{1,0:T(8,128)(2,1)}, bf16[128,2048]{1,0:T(8,128)(2,1)S(1)}, u32[]{:S(2)}, u32[]{:S(2)}) collective-permute-start(bf16[128,2048]{1,0:T(8,128)(2,1)} %bitcast.19), channel_id=1, source_target_pairs={{0,1},{1,2},{2,3},{3,0},{4,5},{5,6},{6,7},{7,4},{8,9},{9,10},{10,1... | collective-permute-start | bytes 1572872 | tf_op jit(solution)/shard_map/ppermute | solution.py:308
  7.3 0.7 copy-start.4
  8.0 0.7 copy-start.6
  9.8 15.5 %all-to-all-start.2 = ((f32[8,8,128]{2,1,0:T(8,128)}), f32[8,8,128]{2,1,0:T(8,128)S(1)}, u32[]{:S(2)}, u32[]{:S(2)}) async-start(f32[8,8,128]{2,1,0:T(8,128)} %shard_map.64), calls=%async_computation.2 | async-start | bytes 65536 | tf_op jit(solution)/shard_map/all_to_all | solution.py:295
  18.8 9.9 %collective-permute-start.3 = (bf16[64,2048]{1,0:T(8,128)(2,1)S(1)}, bf16[64,2048]{1,0:T(8,128)(2,1)S(1)}, u32[]{:S(2)}, u32[]{:S(2)}) collective-permute-start(bf16[64,2048]{1,0:T(8,128)(2,1)S(1)} %slice.22), channel_id=1, source_target_pairs={{0,3},{1,0},{2,1},{3,2},{4,7},{5,4},{6,5},{7,6},{8,11},{9,8},{10,9... | collective-permute-start | bytes 786440 | tf_op jit(solution)/shard_map/ppermute | solution.py:316
  23.3 10.3 %collective-permute-start.2 = (bf16[64,2048]{1,0:T(8,128)(2,1)S(1)}, bf16[64,2048]{1,0:T(8,128)(2,1)S(1)}, u32[]{:S(2)}, u32[]{:S(2)}) collective-permute-start(bf16[64,2048]{1,0:T(8,128)(2,1)S(1)} %slice.21), channel_id=1, source_target_pairs={{0,1},{1,2},{2,3},{3,0},{4,5},{5,6},{6,7},{7,4},{8,9},{9,10},{10,1... | collective-permute-start | bytes 786440 | tf_op jit(solution)/shard_map/ppermute | solution.py:315
  25.3 1.9 %copy-start = (bf16[2048,3,256]{2,0,1:T(8,128)(2,1)S(1)}, bf16[2048,3,256]{2,0,1:T(8,128)(2,1)}, u32[]{:S(2)}) copy-start(bf16[2048,3,256]{2,0,1:T(8,128)(2,1)} %param.9) | copy-start | bytes 9437188
  27.2 6.5 %copy-start.1 = (bf16[2048,3,256]{2,0,1:T(8,128)(2,1)S(1)}, bf16[2048,3,256]{2,0,1:T(8,128)(2,1)}, u32[]{:S(2)}) copy-start(bf16[2048,3,256]{2,0,1:T(8,128)(2,1)} %param.9) | copy-start | bytes 9437188
  35.6 4.8 %collective-permute-start.4 = (bf16[4,128,384]{2,1,0:T(8,128)(2,1)S(1)}, bf16[4,128,384]{2,1,0:T(8,128)(2,1)S(1)}, u32[]{:S(2)}, u32[]{:S(2)}) collective-permute-start(bf16[4,128,384]{2,1,0:T(8,128)(2,1)S(1)} %get-tuple-element.30), channel_id=1, source_target_pairs={{0,4},{4,0},{8,12},{12,8},{16,20},{20,16},{24,28},{28,24},{32,36},... | collective-permute-start | bytes 1179656 | tf_op jit(solution)/shard_map/ppermute | solution.py:337
  40.3 5.9 %copy-start.3 = (bf16[8,128,16]{1,2,0:T(8,128)(2,1)S(1)}, bf16[8,128,16]{1,2,0:T(8,128)(2,1)}, u32[]{:S(2)}) copy-start(bf16[8,128,16]{1,2,0:T(8,128)(2,1)} %param.10) | copy-start | bytes 98308
  41.0 18.4 %collective-permute-start.6 = (bf16[2,4,128,256]{3,2,1,0:T(8,128)(2,1)S(1)}, bf16[2,4,128,256]{3,2,1,0:T(8,128)(2,1)S(1)}, u32[]{:S(2)}, u32[]{:S(2)}) collective-permute-start(bf16[2,4,128,256]{3,2,1,0:T(8,128)(2,1)S(1)} %get-tuple-element.31.kv2), channel_id=1, source_target_pairs={{8,0},{12,4},{16,8},{20,12},{24,16},{28,20},{32,24},{36,28},{40,32... | collective-permute-start | bytes 1572872 | tf_op jit(solution)/shard_map/ppermute | solution.py:348
  42.3 17.1 %collective-permute-start.5 = (bf16[2,4,128,256]{3,2,1,0:T(8,128)(2,1)S(1)}, bf16[2,4,128,256]{3,2,1,0:T(8,128)(2,1)S(1)}, u32[]{:S(2)}, u32[]{:S(2)}) collective-permute-start(bf16[2,4,128,256]{3,2,1,0:T(8,128)(2,1)S(1)} %get-tuple-element.31.kv2), channel_id=1, source_target_pairs={{0,8},{4,12},{8,16},{12,20},{16,24},{20,28},{24,32},{28,36},{32,40... | collective-permute-start | bytes 1572872 | tf_op jit(solution)/shard_map/ppermute | solution.py:347
  49.0 18.4 %all-to-all-start.3 = ((bf16[8,96,128]{2,1,0:T(8,128)(2,1)}), bf16[8,96,128]{2,1,0:T(8,128)(2,1)S(1)}, u32[]{:S(2)}, u32[]{:S(2)}) async-start(bf16[8,96,128]{2,1,0:T(8,128)(2,1)} %get-tuple-element.34), calls=%async_computation.3 | async-start | bytes 393216 | tf_op jit(solution)/shard_map/all_to_all | solution.py:295
  67.4 40.6 %collective-permute-start.7 = (bf16[4,128,256]{2,1,0:T(8,128)(2,1)S(1)}, bf16[4,128,256]{2,1,0:T(8,128)(2,1)S(1)}, u32[]{:S(2)}, u32[]{:S(2)}) collective-permute-start(bf16[4,128,256]{2,1,0:T(8,128)(2,1)S(1)} %slice_bitcast_fusion.1), channel_id=1, source_target_pairs={{0,8},{4,12},{8,16},{12,20},{16,24},{20,28},{24,32},{28,36},{32,40... | collective-permute-start | bytes 786440 | tf_op jit(solution)/shard_map/ppermute | solution.py:360
  71.0 37.0 %collective-permute-start.8 = (bf16[4,128,256]{2,1,0:T(8,128)(2,1)S(1)}, bf16[4,128,256]{2,1,0:T(8,128)(2,1)S(1)}, u32[]{:S(2)}, u32[]{:S(2)}) collective-permute-start(bf16[4,128,256]{2,1,0:T(8,128)(2,1)S(1)} %slice_bitcast_fusion), channel_id=1, source_target_pairs={{8,0},{12,4},{16,8},{20,12},{24,16},{28,20},{32,24},{36,28},{40,32... | collective-permute-start | bytes 786440 | tf_op jit(solution)/shard_map/ppermute | solution.py:361
  72.4 35.6 %copy-start.5 = (f32[1024]{0:T(1024)S(1)}, f32[1024]{0:T(1024)}, u32[]{:S(2)}) copy-start(f32[1024]{0:T(1024)} %param.11) | copy-start | bytes 12292

commit v9 on v8

--- a/solution.py
+++ b/solution.py
@@ -107,28 +107,31 @@
     cum = cumulative_of(steps[...])
     feature = wft[h]
     row = lax.broadcasted_iota(jnp.int32, (16, TOK), 0)
+    segs = []
     for n in range(DOCS):
         own = kv_own[n]
         mate = kvq_mate[n, :, : 2 * DH]
-        segs = (jnp.where(first, own, mate), jnp.where(first, mate, own))
-        local = []
-        for s in range(2):
-            phi = softmax0(nt(feature, segs[s][:, :DH])).astype(BF).astype(F32)
-            line = cum[2 * n + s : 2 * n + s + 1]
-            final = line[:, TOK - 1 :]
-            weighted = (jnp.exp(final - line) * phi).astype(BF)
-            local.append(mm(weighted, segs[s][:, DH:]))
-        last0 = jnp.broadcast_to(cum[2 * n : 2 * n + 1, TOK - 1 :], (1, TOK))
-        last1 = jnp.broadcast_to(cum[2 * n + 1 : 2 * n + 2, TOK - 1 :], (1, TOK))
-        state0[n] = local[0]
-        state = jnp.exp(last1) * local[0] + local[1]
+        segs += [jnp.where(first, own, mate), jnp.where(first, mate, own)]
+    keys = jnp.concatenate([a[:, :DH] for a in segs], axis=0)
+    phi = softmax0(nt(feature, keys)).astype(BF).astype(F32)
+    lines = [cum[i : i + 1] for i in range(8)]
+    finals = [a[:, TOK - 1 :] for a in lines]
+    weighted = [
+        (jnp.exp(finals[i] - lines[i]) * phi[:, TOK * i : TOK * i + TOK]).astype(BF) for i in range(8)
+    ]
+    local = [mm(weighted[i], segs[i][:, DH:]) for i in range(8)]
+    for n in range(DOCS):
+        last0 = jnp.broadcast_to(finals[2 * n], (1, TOK))
+        last1 = jnp.broadcast_to(finals[2 * n + 1], (1, TOK))
+        state0[n] = local[2 * n]
+        state = jnp.exp(last1) * local[2 * n] + local[2 * n + 1]
         tail = decay_rows(row, last0 + last1)
         for half in range(2):
             p = 2 * n + half
             out[p, 0:16] = state_rows(state[8 * half : 8 * half + 8])
             out[p, 16:32] = tail
-            out[p, 32:64] = segs[0][32 * half : 32 * half + 32, :DH]
-            out[p, 64:96] = segs[0][32 * half : 32 * half + 32, DH:]
+            out[p, 32:64] = segs[2 * n][32 * half : 32 * half + 32, :DH]
+            out[p, 64:96] = segs[2 * n][32 * half : 32 * half + 32, DH:]
 
 
 def join_kernel(scal, kv_own, q_own, kvq_mate, kv2, q2):
@@ -209,52 +212,61 @@
     col = lax.broadcasted_iota(jnp.int32, (TOK, TOK), 1)
     causal = row >= col
     gains = gain[h]
+    units = [(n, s) for n in range(DOCS) for s in range(2)]
+    lines = [cum[i : i + 1] for i in range(8)]
+    columns = [cum_t[:, i : i + 1] for i in range(8)]
+    both = jnp.concatenate([q2[s, n] for n, s in units] + [kv2[s, n, :, :DH] for n, s in units], axis=0)
+    phi = softmax0(nt(feature, both)).astype(BF)
+    phi_q = phi[:, : 8 * TOK].astype(F32).T
+    phi_b = phi_q.astype(BF)
+    alike = [mm(phi_b[TOK * i : TOK * i + TOK], phi[:, TOK * (8 + i) : TOK * (9 + i)]) for i in range(8)]
+    entering = []
+    for n in range(DOCS):
+        carried = jnp.concatenate([read_state(got, 2 * n), read_state(got, 2 * n + 1)], axis=0)
+        entering += [carried, jnp.exp(lines[2 * n][:, TOK - 1 :]) * carried + state0[n]]
+    brought = [mm(phi_q[TOK * i : TOK * i + TOK], entering[i], HIGH) for i in range(8)]
+    decays = [jnp.where(causal, jnp.exp(jnp.minimum(columns[i] - lines[i], 0.0)), 0.0) for i in range(8)]
+    mixing = [(alike[i] * decays[i]).astype(BF) for i in range(8)]
+    inside = [mm(mixing[i], kv2[s, n, :, DH:]) for i, (n, s) in enumerate(units)]
+    linear = [inside[i] + brought[i] * jnp.exp(columns[i]) for i in range(8)]
+    roots = [lax.rsqrt(jnp.mean(a * a, axis=1, keepdims=True) + EPS) for a in linear]
+    normed = [linear[i] * roots[i] * gains for i in range(8)]
+
     lane = lax.broadcasted_iota(jnp.int32, (1, 7 * BS), 1)
     scale = DH ** (-0.5) * LOG2E
     for n in range(DOCS):
-        carried = jnp.concatenate([read_state(got, 2 * n), read_state(got, 2 * n + 1)], axis=0)
         gk = jnp.concatenate([got[2 * n, 16:48], got[2 * n + 1, 16:48]], axis=0)
         gv = jnp.concatenate([got[2 * n, 48:80], got[2 * n + 1, 48:80]], axis=0)
-        for s in range(2):
-            line = cum[2 * n + s : 2 * n + s + 1]
-            column = cum_t[:, 2 * n + s : 2 * n + s + 1]
-            queries = q2[s, n]
-            keys = kv2[s, n, :, :DH]
-            values = kv2[s, n, :, DH:]
-            phi_q = softmax0(nt(feature, queries)).astype(BF).astype(F32).T
-            phi_k = softmax0(nt(feature, keys)).astype(BF)
-            decay = jnp.where(causal, jnp.exp(jnp.minimum(column - line, 0.0)), 0.0)
-            mixing = (mm(phi_q.astype(BF), phi_k) * decay).astype(BF)
-            linear = mm(mixing, values) + mm(phi_q, carried, HIGH) * jnp.exp(column)
-            carried = jnp.exp(line[:, TOK - 1 :]) * carried + state0[n]
-            square = jnp.mean(linear * linear, axis=1, keepdims=True)
-            normed = linear * lax.rsqrt(square + EPS) * gains
-            for half in range(2):
-                j = 2 * s + half
-                block = 4 * q + j
-                picks = [win[n, 3 + (j + d) // 2, pl.ds(BS * ((j + d) % 2), BS)] for d in (-1, 0, 1)]
-                for k in range(R):
-                    place = pat[12 * n + 3 * j + k]
-                    picks.append(
-                        win[n, lax.div(place, 2), pl.ds(pl.multiple_of(BS * lax.rem(place, 2), BS), BS)]
-                    )
-                near = jnp.concatenate(picks, axis=0)
-                all_k = jnp.concatenate([near[:, :DH], gk], axis=0)
-                all_v = jnp.concatenate([near[:, DH:], gv], axis=0)
-                scores = nt(queries[half * BS : half * BS + BS], all_k)
-                bad = (
-                    ((lane < BS) & (block < 2))
-                    | ((lane >= BS) & (lane < 2 * BS) & (block < 1))
-                    | ((lane >= 2 * BS) & (lane < 3 * BS) & (block > 4 * CHIPS - 2))
+        picked = []
+        for j in range(4):
+            picks = [win[n, 3 + (j + d) // 2, pl.ds(BS * ((j + d) % 2), BS)] for d in (-1, 0, 1)]
+            for k in range(R):
+                place = pat[12 * n + 3 * j + k]
+                picks.append(
+                    win[n, lax.div(place, 2), pl.ds(pl.multiple_of(BS * lax.rem(place, 2), BS), BS)]
                 )
-                scores = jnp.where(bad, MASKED, scores)
-                top = jnp.max(scores, axis=1, keepdims=True)
-                e = jnp.exp2((scores - top) * scale)
-                share = 1.0 / jnp.sum(e, axis=1, keepdims=True)
-                sparse = mm(e.astype(BF), all_v) * share
-                out[2 * n + s, half * BS : half * BS + BS] = (
-                    normed[half * BS : half * BS + BS] + sparse
-                ).astype(BF)
+            picked.append(jnp.concatenate(picks, axis=0))
+        scores = [
+            nt(q2[j // 2, n, BS * (j % 2) : BS * (j % 2) + BS], jnp.concatenate([picked[j][:, :DH], gk], axis=0))
+            for j in range(4)
+        ]
+        for j in range(4):
+            block = 4 * q + j
+            bad = (
+                ((lane < BS) & (block < 2))
+                | ((lane >= BS) & (lane < 2 * BS) & (block < 1))
+                | ((lane >= 2 * BS) & (lane < 3 * BS) & (block > 4 * CHIPS - 2))
+            )
+            scores[j] = jnp.where(bad, MASKED, scores[j])
+        tops = [jnp.max(a, axis=1, keepdims=True) for a in scores]
+        es = [jnp.exp2((a - top) * scale) for a, top in zip(scores, tops)]
+        shares = [1.0 / jnp.sum(e, axis=1, keepdims=True) for e in es]
+        sparse = [
+            mm(es[j].astype(BF), jnp.concatenate([picked[j][:, DH:], gv], axis=0)) * shares[j] for j in range(4)
+        ]
+        for j in range(4):
+            half = slice(BS * (j % 2), BS * (j % 2) + BS)
+            out[2 * n + j // 2, half] = (normed[2 * n + j // 2][half] + sparse[j]).astype(BF)
 
 
 def call(kernel, outs, scratch, spaces, micros, room, *args):
@@ -356,11 +368,7 @@
         scal, kv_own, kvq_mate, steps, wft,
     )
     got1 = exchange(send1, "seq", ZS)
-    near_p, near_m, got1 = lax.optimization_barrier((zp[1], zm[0], got1))
-    tp = lax.ppermute(near_p, "seq", pairs(lambda q, c: (q + 1, c)))
-    tm = lax.ppermute(near_m, "seq", pairs(lambda q, c: (q - 1, c)))
-
-    def chain(got1):
+    def chain(got1, near_p, near_m):
         send2, inner, outer = call(
             row_kernel,
             [shape((8, ROWS, TOK), BF), shape((8, 8, TOK), F32), shape((8, 8, TOK), F32)],
@@ -374,9 +382,11 @@
         [send3] = call(
             back_kernel, [shape((8, 80, TOK), BF)], [], "svvv", 1, 4, scal, got2, inner, outer
         )
-        return exchange(send3, "seq", ZS)
-
-    got3 = lax.cond(s < 1000, chain, lambda _: jnp.zeros((8, 80, TOK), BF), got1)
+        tp = lax.ppermute(near_p, "seq", pairs(lambda q, c: (q + 1, c)))
+        tm = lax.ppermute(near_m, "seq", pairs(lambda q, c: (q - 1, c)))
+        return exchange(send3, "seq", ZS), tp, tm
+
+    got3, tp, tm = chain(got1, zp[1], zm[0])
 
     [out] = call(
         attend_kernel,

time: 131 us -> 110 us (0.84)
  blocking collectives: 48.1 us -> 14.3 us
  starting transfers between devices: 46.4 us -> 55.7 us
  waiting for transfers between devices: 15.2 us -> 23.2 us
  Pallas kernels: 15.9 us -> 11.6 us
    all_to_all x3 -> x1, blocking collectives: 48.1 us -> 14.3 us  [exchange(): return lax.all_to_all(a, axis, 0, 0, tiled=True, axis_index_groups=groups)]
    all_to_all x2 -> x4, starting transfers between devices: 19.1 us -> 28.6 us  [exchange(): return lax.all_to_all(a, axis, 0, 0, tiled=True, axis_index_groups=groups)]
    ppermute x2, waiting for transfers between devices: 0.01 us -> 5.1 us  [the longest x1 5.09 us: chain(): tp = lax.ppermute(near_p, 'seq', pairs(lambda q, c: (q + 1, c)))]
    pallas_call x8, Pallas kernels: 15.9 us -> 11.6 us  [call(): pl.pallas_call(kernel, out_shape=outs, in_specs=[pl.BlockSpec(memory_spac...]
    all_to_all x2 -> x4, waiting for transfers between devices: 8.01 us -> 9.95 us  [exchange(): return lax.all_to_all(a, axis, 0, 0, tiled=True, axis_index_groups=groups)]
  transfers between devices with their start and end apart: 11 -> 13, of which waited for: 4 -> 7; matrix products, arithmetic and copies ran while one was open for 0% -> 0% of each run, Pallas kernels for 4% -> 4%
where the time goes in v9:
time: 110 us
  starting transfers between devices  55.7 us (51%)
  waiting for transfers between devices  23.2 us (21%)
  blocking collectives  14.3 us (13%)
  Pallas kernels  11.6 us (11%)
  local copies, waits for them, and re-layouts  4.53 us (4%)
    all_to_all x4, starting transfers between devices, exchange(): return lax.all_to_all(a, axis, 0, 0, tiled=True, axis_index_groups=groups)  28.6 us
    all_to_all x1, blocking collectives, exchange(): return lax.all_to_all(a, axis, 0, 0, tiled=True, axis_index_groups=groups)  14.3 us
    pallas_call x8, Pallas kernels, call(): pl.pallas_call(kernel, out_shape=outs, in_specs=[pl.BlockSpec(memory_spac...  11.6 us
    all_to_all x4, waiting for transfers between devices, exchange(): return lax.all_to_all(a, axis, 0, 0, tiled=True, axis_index_groups=groups)  9.95 us
    ppermute x1, starting transfers between devices, per_device(): tb = lax.ppermute(t0, 'fsdp', down)  5.34 us
    ppermute x1, waiting for transfers between devices, chain(): tp = lax.ppermute(near_p, 'seq', pairs(lambda q, c: (q + 1, c)))  5.09 us
    ppermute x1, waiting for transfers between devices, per_device(): td1 = lax.ppermute(ta[:64], 'fsdp', up)  5.05 us
    ppermute x1, starting transfers between devices, per_device(): td2 = lax.ppermute(tb[64:], 'fsdp', down)  4.54 us
  transfers between devices with their start and end apart: 13, of which 7 were waited for; matrix products, arithmetic and copies ran while one was open for 0% of the time, Pallas kernels for 4%

profile of v9, /device:TPU:1, one launch (start us, length us, event | category | flops | bytes accessed | tf_op | source)
XLA Modules:
  0.0 109.5 jit_solution(18291000205608240693)
XLA Ops:
  0.0 0.0 copy-start.2
  0.0 5.3 %collective-permute-start.1 = (bf16[128,2048]{1,0:T(8,128)(2,1)}, bf16[128,2048]{1,0:T(8,128)(2,1)S(1)}, u32[]{:S(2)}, u32[]{:S(2)}) collective-permute-start(bf16[128,2048]{1,0:T(8,128)(2,1)} %bitcast.18), channel_id=1, source_target_pairs={{0,3},{1,0},{2,1},{3,2},{4,7},{5,4},{6,5},{7,6},{8,11},{9,8},{10,9... | collective-permute-start | bytes 1572872 | tf_op jit(solution)/shard_map/ppermute | solution.py:321
  5.3 1.9 %collective-permute-start = (bf16[128,2048]{1,0:T(8,128)(2,1)}, bf16[128,2048]{1,0:T(8,128)(2,1)S(1)}, u32[]{:S(2)}, u32[]{:S(2)}) collective-permute-start(bf16[128,2048]{1,0:T(8,128)(2,1)} %bitcast.19), channel_id=1, source_target_pairs={{0,1},{1,2},{2,3},{3,0},{4,5},{5,6},{6,7},{7,4},{8,9},{9,10},{10,1... | collective-permute-start | bytes 1572872 | tf_op jit(solution)/shard_map/ppermute | solution.py:320
  7.3 0.0 copy-start.4
  7.3 0.7 copy-done.4
  8.0 0.0 copy-start.6
  8.0 0.7 copy-done.6
  8.6 1.2 %shard_map.64 = f32[8,8,128]{2,1,0:T(8,128)} custom-call(s32[1,2,3]{2,1,0:T(2,128)S(1)} %copy-done.6, f32[1,8,128]{2,1,0:T(8,128)S(1)} %copy-done.4), custom_call_target="tpu_custom_call" | custom-call | flops 1000000000 | bytes 3000000 | tf_op jit(solution)/shard_map/pallas_call | solution.py:274
  9.8 8.8 %all-to-all-start = ((f32[8,8,128]{2,1,0:T(8,128)}), f32[8,8,128]{2,1,0:T(8,128)S(1)}, u32[]{:S(2)}, u32[]{:S(2)}) async-start(f32[8,8,128]{2,1,0:T(8,128)} %shard_map.64), calls=%async_computation | async-start | bytes 65536 | tf_op jit(solution)/shard_map/all_to_all | solution.py:307
  18.6 0.1 stack.27.scal
  18.7 0.0 collective-permute-done.1.tb
  18.8 4.5 %collective-permute-start.3 = (bf16[64,2048]{1,0:T(8,128)(2,1)S(1)}, bf16[64,2048]{1,0:T(8,128)(2,1)S(1)}, u32[]{:S(2)}, u32[]{:S(2)}) collective-permute-start(bf16[64,2048]{1,0:T(8,128)(2,1)S(1)} %slice.22), channel_id=1, source_target_pairs={{0,3},{1,0},{2,1},{3,2},{4,7},{5,4},{6,5},{7,6},{8,11},{9,8},{10,9... | collective-permute-start | bytes 786440 | tf_op jit(solution)/shard_map/ppermute | solution.py:328
  23.3 0.0 collective-permute-done.ta
  23.3 1.9 %collective-permute-start.2 = (bf16[64,2048]{1,0:T(8,128)(2,1)S(1)}, bf16[64,2048]{1,0:T(8,128)(2,1)S(1)}, u32[]{:S(2)}, u32[]{:S(2)}) collective-permute-start(bf16[64,2048]{1,0:T(8,128)(2,1)S(1)} %slice.21), channel_id=1, source_target_pairs={{0,1},{1,2},{2,3},{3,0},{4,5},{5,6},{6,7},{7,4},{8,9},{9,10},{10,1... | collective-permute-start | bytes 786440 | tf_op jit(solution)/shard_map/ppermute | solution.py:327
  25.3 0.0 all-to-all-done.got
  25.3 0.0 copy-done.2
  25.3 0.0 copy-start
  25.3 1.9 %copy-done = bf16[2048,3,256]{2,0,1:T(8,128)(2,1)S(1)} copy-done((bf16[2048,3,256]{2,0,1:T(8,128)(2,1)S(1)}, bf16[2048,3,256]{2,0,1:T(8,128)(2,1)}, u32[]{:S(2)}) %copy-start) | copy-done | bytes 3145752
  27.2 0.0 copy-start.1
  27.2 0.6 shard_map.65.early
  27.8 0.0 copy-start.3
  27.8 0.8 collective-permute-done.3.td2
  28.6 5.0 %collective-permute-done.2.td1 = bf16[64,2048]{1,0:T(8,128)(2,1)S(1)} collective-permute-done((bf16[64,2048]{1,0:T(8,128)(2,1)S(1)}, bf16[64,2048]{1,0:T(8,128)(2,1)S(1)}, u32[]{:S(2)}, u32[]{:S(2)}) %collective-permute-start.2) | collective-permute-done | bytes 262176 | tf_op jit(solution)/shard_map/ppermute | solution.py:327
  33.7 0.0 copy-done.1
  33.7 1.9 %shard_map.66 = (bf16[4,128,256]{2,1,0:T(8,128)(2,1)S(1)}, bf16[4,128,384]{2,1,0:T(8,128)(2,1)S(1)}, bf16[4,128,128]{2,1,0:T(8,128)(2,1)S(1)}, f32[8,128]{1,0:T(8,128)S(1)}) custom-call(s32[6]{0:T(128)S(1)} %stack.27.scal, bf16[3,128,256]{2,1,0:T(8,128)(2,1)S(1)} %shard_map.65.early, bf16[128,2048]{1,0:T(8,128)(2,1)S(1)} %collective-permute-done.ta, ...), custom_call_target="tpu_custom_call" | custom-call | flops 3000000000 | bytes 9000000 | tf_op jit(solution)/shard_map/pallas_call | solution.py:274
  35.6 3.4 %collective-permute-start.4 = (bf16[4,128,384]{2,1,0:T(8,128)(2,1)S(1)}, bf16[4,128,384]{2,1,0:T(8,128)(2,1)S(1)}, u32[]{:S(2)}, u32[]{:S(2)}) collective-permute-start(bf16[4,128,384]{2,1,0:T(8,128)(2,1)S(1)} %get-tuple-element.18), channel_id=1, source_target_pairs={{0,4},{4,0},{8,12},{12,8},{16,20},{20,16},{24,28},{28,24},{32,36},... | collective-permute-start | bytes 1179656 | tf_op jit(solution)/shard_map/ppermute | solution.py:349
  39.0 1.3 %collective-permute-done.4.kvq_mate = bf16[4,128,384]{2,1,0:T(8,128)(2,1)S(1)} collective-permute-done((bf16[4,128,384]{2,1,0:T(8,128)(2,1)S(1)}, bf16[4,128,384]{2,1,0:T(8,128)(2,1)S(1)}, u32[]{:S(2)}, u32[]{:S(2)}) %collective-permute-start.4) | collective-permute-done | bytes 393248 | tf_op jit(solution)/shard_map/ppermute | solution.py:349
  40.3 0.0 copy-done.3
  40.4 1.7 %shard_map.68 = (bf16[8,96,128]{2,1,0:T(8,128)(2,1)}, f32[4,16,128]{2,1,0:T(8,128)S(1)}) custom-call(s32[6]{0:T(128)S(1)} %stack.27.scal, bf16[4,128,256]{2,1,0:T(8,128)(2,1)S(1)} %get-tuple-element.16.kv_own, bf16[4,128,384]{2,1,0:T(8,128)(2,1)S(1)} %collective-permute-done.4.kvq_mate, f32[8,128]{1,0:T(8,128)S(1)} %get-tuple-element.21.steps, ...), custom_call_target="tpu_custom_call" | custom-call | flops 2000000000 | bytes 6000000 | tf_op jit(solution)/shard_map/pallas_call | solution.py:274
  42.1 8.2 %all-to-all-start.1 = ((bf16[8,96,128]{2,1,0:T(8,128)(2,1)}), bf16[8,96,128]{2,1,0:T(8,128)(2,1)S(1)}, u32[]{:S(2)}, u32[]{:S(2)}) async-start(bf16[8,96,128]{2,1,0:T(8,128)(2,1)} %get-tuple-element.22), calls=%async_computation.1 | async-start | bytes 393216 | tf_op jit(solution)/shard_map/all_to_all | solution.py:307
  50.3 0.6 shard_map.67
  50.9 1.3 %collective-permute-start.6 = (bf16[2,4,128,256]{3,2,1,0:T(8,128)(2,1)S(1)}, bf16[2,4,128,256]{3,2,1,0:T(8,128)(2,1)S(1)}, u32[]{:S(2)}, u32[]{:S(2)}) collective-permute-start(bf16[2,4,128,256]{3,2,1,0:T(8,128)(2,1)S(1)} %get-tuple-element.19.kv2), channel_id=1, source_target_pairs={{8,0},{12,4},{16,8},{20,12},{24,16},{28,20},{32,24},{36,28},{40,32... | collective-permute-start | bytes 1572872 | tf_op jit(solution)/shard_map/ppermute | solution.py:360
  52.2 4.0 %collective-permute-start.5 = (bf16[2,4,128,256]{3,2,1,0:T(8,128)(2,1)S(1)}, bf16[2,4,128,256]{3,2,1,0:T(8,128)(2,1)S(1)}, u32[]{:S(2)}, u32[]{:S(2)}) collective-permute-start(bf16[2,4,128,256]{3,2,1,0:T(8,128)(2,1)S(1)} %get-tuple-element.19.kv2), channel_id=1, source_target_pairs={{0,8},{4,12},{8,16},{12,20},{16,24},{20,28},{24,32},{28,36},{32,40... | collective-permute-start | bytes 1572872 | tf_op jit(solution)/shard_map/ppermute | solution.py:359
  56.2 3.5 %all-to-all-done.1.got = bf16[8,96,128]{2,1,0:T(8,128)(2,1)S(1)} async-done(((bf16[8,96,128]{2,1,0:T(8,128)(2,1)}), bf16[8,96,128]{2,1,0:T(8,128)(2,1)S(1)}, u32[]{:S(2)}, u32[]{:S(2)}) %all-to-all-start.1) | async-done | bytes 196640 | tf_op jit(solution)/shard_map/all_to_all | solution.py:307
  59.7 0.7 shard_map.69
  60.4 0.0 copy-start.5
  60.4 7.0 %all-to-all-start.2 = ((bf16[8,96,128]{2,1,0:T(8,128)(2,1)}), bf16[8,96,128]{2,1,0:T(8,128)(2,1)S(1)}, u32[]{:S(2)}, u32[]{:S(2)}) async-start(bf16[8,96,128]{2,1,0:T(8,128)(2,1)} %get-tuple-element.23), calls=%async_computation.2 | async-start | bytes 393216 | tf_op jit(solution)/shard_map/all_to_all | solution.py:307
  67.4 1.0 collective-permute-done.6.zm
  68.4 1.3 %collective-permute-start.8 = (bf16[4,128,256]{2,1,0:T(8,128)(2,1)S(1)}, bf16[4,128,256]{2,1,0:T(8,128)(2,1)S(1)}, u32[]{:S(2)}, u32[]{:S(2)}) collective-permute-start(bf16[4,128,256]{2,1,0:T(8,128)(2,1)S(1)} %slice_bitcast_fusion), channel_id=1, source_target_pairs={{8,0},{12,4},{16,8},{20,12},{24,16},{28,20},{32,24},{36,28},{40,32... | collective-permute-start | bytes 786440 | tf_op jit(solution)/shard_map/ppermute | solution.py:386
  69.7 6.5 %all-to-all-done.2.got = bf16[8,96,128]{2,1,0:T(8,128)(2,1)S(1)} async-done(((bf16[8,96,128]{2,1,0:T(8,128)(2,1)}), bf16[8,96,128]{2,1,0:T(8,128)(2,1)S(1)}, u32[]{:S(2)}, u32[]{:S(2)}) %all-to-all-start.2) | async-done | bytes 196640 | tf_op jit(solution)/shard_map/all_to_all | solution.py:307
  76.1 1.2 %shard_map.70 = bf16[8,80,128]{2,1,0:T(8,128)(2,1)} custom-call(s32[6]{0:T(128)S(1)} %stack.27.scal, bf16[8,96,128]{2,1,0:T(8,128)(2,1)S(1)} %all-to-all-done.2.got, f32[8,8,128]{2,1,0:T(8,128)S(1)} %get-tuple-element.24.inner, f32[8,8,128]{2,1,0:T(8,128)S(1)} %get-tuple-element.25.outer), custom_call_target="tpu_custom_call" | custom-call | flops 1000000000 | bytes 3000000 | tf_op jit(solution)/shard_map/pallas_call | solution.py:274
  77.4 4.6 %all-to-all-start.3 = ((bf16[8,80,128]{2,1,0:T(8,128)(2,1)}), bf16[8,80,128]{2,1,0:T(8,128)(2,1)S(1)}, u32[]{:S(2)}, u32[]{:S(2)}) async-start(bf16[8,80,128]{2,1,0:T(8,128)(2,1)} %shard_map.70), calls=%async_computation.3 | async-start | bytes 327680 | tf_op jit(solution)/shard_map/all_to_all | solution.py:307
  82.0 0.0 collective-permute-done.5.zp
  82.0 3.4 %collective-permute-start.7 = (bf16[4,128,256]{2,1,0:T(8,128)(2,1)S(1)}, bf16[4,128,256]{2,1,0:T(8,128)(2,1)S(1)}, u32[]{:S(2)}, u32[]{:S(2)}) collective-permute-start(bf16[4,128,256]{2,1,0:T(8,128)(2,1)S(1)} %slice_bitcast_fusion.1), channel_id=1, source_target_pairs={{0,8},{4,12},{8,16},{12,20},{16,24},{20,28},{24,32},{28,36},{32,40... | collective-permute-start | bytes 786440 | tf_op jit(solution)/shard_map/ppermute | solution.py:385
  85.4 0.1 min.12.pat
  85.5 0.0 collective-permute-done.8.tm
  85.5 5.1 %collective-permute-done.7.tp = bf16[4,128,256]{2,1,0:T(8,128)(2,1)S(1)} collective-permute-done((bf16[4,128,256]{2,1,0:T(8,128)(2,1)S(1)}, bf16[4,128,256]{2,1,0:T(8,128)(2,1)S(1)}, u32[]{:S(2)}, u32[]{:S(2)}) %collective-permute-start.7) | collective-permute-done | bytes 262176 | tf_op jit(solution)/shard_map/ppermute | solution.py:385
  90.6 0.0 all-to-all-done.3.got
  90.6 0.0 copy-done.5
  90.6 3.6 %shard_map.71 = bf16[8,128,128]{2,1,0:T(8,128)(2,1)S(1)} custom-call(s32[6]{0:T(128)S(1)} %stack.27.scal, s32[48]{0:T(128)S(1)} %min.12.pat, bf16[2,4,128,256]{3,2,1,0:T(8,128)(2,1)S(1)} %get-tuple-element.19.kv2, bf16[2,4,128,128]{3,2,1,0:T(8,128)(2,1)S(1)} %get-tuple-element.20.q2, bf16[2,4,128,256]{3,2,1,0:T(8,128)(2,1)S(1)} %collective-permute-done.5.zp, ...), custom_call_target="tpu_custom_call" | custom-call | flops 8000000000 | bytes 24000000 | tf_op jit(solution)/shard_map/pallas_call | solution.py:274
  94.2 14.3 %all_to_all.25 = bf16[8,128,128]{2,1,0:T(8,128)(2,1)S(1)} all-to-all(bf16[8,128,128]{2,1,0:T(8,128)(2,1)S(1)} %shard_map.71), channel_id=1, replica_groups={{0,4,1,5,2,6,3,7},{8,12,9,13,10,14,11,15},{16,20,17,21,18,22,19,23},{24..., dimensions={0} | all-to-all | bytes 524288 | tf_op jit(solution)/shard_map/all_to_all | solution.py:307
  108.5 0.2 copy.7
  108.6 0.9 copy.8
  (5 shorter events, 0.1 us)
Async XLA Ops:
  0.0 25.3 %copy-start.2 = (bf16[1,128,2048]{2,1,0:T(8,128)(2,1)S(1)}, bf16[1,128,2048]{2,1,0:T(8,128)(2,1)}, u32[]{:S(2)}) copy-start(bf16[1,128,2048]{2,1,0:T(8,128)(2,1)} %t0.1) | copy-start | bytes 1572868
  0.0 18.7 %collective-permute-start.1 = (bf16[128,2048]{1,0:T(8,128)(2,1)}, bf16[128,2048]{1,0:T(8,128)(2,1)S(1)}, u32[]{:S(2)}, u32[]{:S(2)}) collective-permute-start(bf16[128,2048]{1,0:T(8,128)(2,1)} %bitcast.18), channel_id=1, source_target_pairs={{0,3},{1,0},{2,1},{3,2},{4,7},{5,4},{6,5},{7,6},{8,11},{9,8},{10,9... | collective-permute-start | bytes 1572872 | tf_op jit(solution)/shard_map/ppermute | solution.py:321
  5.3 18.0 %collective-permute-start = (bf16[128,2048]{1,0:T(8,128)(2,1)}, bf16[128,2048]{1,0:T(8,128)(2,1)S(1)}, u32[]{:S(2)}, u32[]{:S(2)}) collective-permute-start(bf16[128,2048]{1,0:T(8,128)(2,1)} %bitcast.19), channel_id=1, source_target_pairs={{0,1},{1,2},{2,3},{3,0},{4,5},{5,6},{6,7},{7,4},{8,9},{9,10},{10,1... | collective-permute-start | bytes 1572872 | tf_op jit(solution)/shard_map/ppermute | solution.py:320
  7.3 0.7 copy-start.4
  8.0 0.7 copy-start.6
  9.8 15.5 %all-to-all-start = ((f32[8,8,128]{2,1,0:T(8,128)}), f32[8,8,128]{2,1,0:T(8,128)S(1)}, u32[]{:S(2)}, u32[]{:S(2)}) async-start(f32[8,8,128]{2,1,0:T(8,128)} %shard_map.64), calls=%async_computation | async-start | bytes 65536 | tf_op jit(solution)/shard_map/all_to_all | solution.py:307
  18.8 9.9 %collective-permute-start.3 = (bf16[64,2048]{1,0:T(8,128)(2,1)S(1)}, bf16[64,2048]{1,0:T(8,128)(2,1)S(1)}, u32[]{:S(2)}, u32[]{:S(2)}) collective-permute-start(bf16[64,2048]{1,0:T(8,128)(2,1)S(1)} %slice.22), channel_id=1, source_target_pairs={{0,3},{1,0},{2,1},{3,2},{4,7},{5,4},{6,5},{7,6},{8,11},{9,8},{10,9... | collective-permute-start | bytes 786440 | tf_op jit(solution)/shard_map/ppermute | solution.py:328
  23.3 10.3 %collective-permute-start.2 = (bf16[64,2048]{1,0:T(8,128)(2,1)S(1)}, bf16[64,2048]{1,0:T(8,128)(2,1)S(1)}, u32[]{:S(2)}, u32[]{:S(2)}) collective-permute-start(bf16[64,2048]{1,0:T(8,128)(2,1)S(1)} %slice.21), channel_id=1, source_target_pairs={{0,1},{1,2},{2,3},{3,0},{4,5},{5,6},{6,7},{7,4},{8,9},{9,10},{10,1... | collective-permute-start | bytes 786440 | tf_op jit(solution)/shard_map/ppermute | solution.py:327
  25.3 1.9 %copy-start = (bf16[2048,3,256]{2,0,1:T(8,128)(2,1)S(1)}, bf16[2048,3,256]{2,0,1:T(8,128)(2,1)}, u32[]{:S(2)}) copy-start(bf16[2048,3,256]{2,0,1:T(8,128)(2,1)} %param.7) | copy-start | bytes 9437188
  27.2 6.5 %copy-start.1 = (bf16[2048,3,256]{2,0,1:T(8,128)(2,1)S(1)}, bf16[2048,3,256]{2,0,1:T(8,128)(2,1)}, u32[]{:S(2)}) copy-start(bf16[2048,3,256]{2,0,1:T(8,128)(2,1)} %param.7) | copy-start | bytes 9437188
  27.8 12.6 %copy-start.3 = (bf16[8,128,16]{1,2,0:T(8,128)(2,1)S(1)}, bf16[8,128,16]{1,2,0:T(8,128)(2,1)}, u32[]{:S(2)}) copy-start(bf16[8,128,16]{1,2,0:T(8,128)(2,1)} %param.8) | copy-start | bytes 98308
  35.6 4.8 %collective-permute-start.4 = (bf16[4,128,384]{2,1,0:T(8,128)(2,1)S(1)}, bf16[4,128,384]{2,1,0:T(8,128)(2,1)S(1)}, u32[]{:S(2)}, u32[]{:S(2)}) collective-permute-start(bf16[4,128,384]{2,1,0:T(8,128)(2,1)S(1)} %get-tuple-element.18), channel_id=1, source_target_pairs={{0,4},{4,0},{8,12},{12,8},{16,20},{20,16},{24,28},{28,24},{32,36},... | collective-permute-start | bytes 1179656 | tf_op jit(solution)/shard_map/ppermute | solution.py:349
  42.1 17.6 %all-to-all-start.1 = ((bf16[8,96,128]{2,1,0:T(8,128)(2,1)}), bf16[8,96,128]{2,1,0:T(8,128)(2,1)S(1)}, u32[]{:S(2)}, u32[]{:S(2)}) async-start(bf16[8,96,128]{2,1,0:T(8,128)(2,1)} %get-tuple-element.22), calls=%async_computation.1 | async-start | bytes 393216 | tf_op jit(solution)/shard_map/all_to_all | solution.py:307
  50.9 17.5 %collective-permute-start.6 = (bf16[2,4,128,256]{3,2,1,0:T(8,128)(2,1)S(1)}, bf16[2,4,128,256]{3,2,1,0:T(8,128)(2,1)S(1)}, u32[]{:S(2)}, u32[]{:S(2)}) collective-permute-start(bf16[2,4,128,256]{3,2,1,0:T(8,128)(2,1)S(1)} %get-tuple-element.19.kv2), channel_id=1, source_target_pairs={{8,0},{12,4},{16,8},{20,12},{24,16},{28,20},{32,24},{36,28},{40,32... | collective-permute-start | bytes 1572872 | tf_op jit(solution)/shard_map/ppermute | solution.py:360
  52.2 29.8 %collective-permute-start.5 = (bf16[2,4,128,256]{3,2,1,0:T(8,128)(2,1)S(1)}, bf16[2,4,128,256]{3,2,1,0:T(8,128)(2,1)S(1)}, u32[]{:S(2)}, u32[]{:S(2)}) collective-permute-start(bf16[2,4,128,256]{3,2,1,0:T(8,128)(2,1)S(1)} %get-tuple-element.19.kv2), channel_id=1, source_target_pairs={{0,8},{4,12},{8,16},{12,20},{16,24},{20,28},{24,32},{28,36},{32,40... | collective-permute-start | bytes 1572872 | tf_op jit(solution)/shard_map/ppermute | solution.py:359
  60.4 30.2 %copy-start.5 = (f32[1024]{0:T(1024)S(1)}, f32[1024]{0:T(1024)}, u32[]{:S(2)}) copy-start(f32[1024]{0:T(1024)} %param.9) | copy-start | bytes 12292
  60.4 15.7 %all-to-all-start.2 = ((bf16[8,96,128]{2,1,0:T(8,128)(2,1)}), bf16[8,96,128]{2,1,0:T(8,128)(2,1)S(1)}, u32[]{:S(2)}, u32[]{:S(2)}) async-start(bf16[8,96,128]{2,1,0:T(8,128)(2,1)} %get-tuple-element.23), calls=%async_computation.2 | async-start | bytes 393216 | tf_op jit(solution)/shard_map/all_to_all | solution.py:307
  68.4 17.1 %collective-permute-start.8 = (bf16[4,128,256]{2,1,0:T(8,128)(2,1)S(1)}, bf16[4,128,256]{2,1,0:T(8,128)(2,1)S(1)}, u32[]{:S(2)}, u32[]{:S(2)}) collective-permute-start(bf16[4,128,256]{2,1,0:T(8,128)(2,1)S(1)} %slice_bitcast_fusion), channel_id=1, source_target_pairs={{8,0},{12,4},{16,8},{20,12},{24,16},{28,20},{32,24},{36,28},{40,32... | collective-permute-start | bytes 786440 | tf_op jit(solution)/shard_map/ppermute | solution.py:386
  77.4 13.2 %all-to-all-start.3 = ((bf16[8,80,128]{2,1,0:T(8,128)(2,1)}), bf16[8,80,128]{2,1,0:T(8,128)(2,1)S(1)}, u32[]{:S(2)}, u32[]{:S(2)}) async-start(bf16[8,80,128]{2,1,0:T(8,128)(2,1)} %shard_map.70), calls=%async_computation.3 | async-start | bytes 327680 | tf_op jit(solution)/shard_map/all_to_all | solution.py:307
  82.0 8.6 %collective-permute-start.7 = (bf16[4,128,256]{2,1,0:T(8,128)(2,1)S(1)}, bf16[4,128,256]{2,1,0:T(8,128)(2,1)S(1)}, u32[]{:S(2)}, u32[]{:S(2)}) collective-permute-start(bf16[4,128,256]{2,1,0:T(8,128)(2,1)S(1)} %slice_bitcast_fusion.1), channel_id=1, source_target_pairs={{0,8},{4,12},{8,16},{12,20},{16,24},{20,28},{24,32},{28,36},{32,40... | collective-permute-start | bytes 786440 | tf_op jit(solution)/shard_map/ppermute | solution.py:385

commit v10 on v9

--- a/solution.py
+++ b/solution.py
@@ -57,33 +57,50 @@
     return mm(steps, jnp.where(row <= col, 1.0, 0.0).astype(F32), HIGH)
 
 
-def pack_kernel(pat, steps, packed):
+def split_kernel(pat, tokens, steps, upper, lower):
+    for b in range(4):
+        upper[64 * b : 64 * b + 64] = tokens[0, :64, 512 * b : 512 * b + 512]
+    lower[...] = tokens[0, 64:]
     lane = lax.broadcasted_iota(jnp.int32, (8, TOK), 1)
-    row = lax.broadcasted_iota(jnp.int32, (8, TOK), 0)
     wanted = jnp.zeros((8, TOK), jnp.int32)
     for i in range(6):
         wanted = jnp.where(lane == i, pat[0, i // 3, i % 3], wanted)
-    wanted = wanted.astype(F32)
-    for head in range(8):
-        packed[head] = jnp.where(row == 0, steps[0, head : head + 1], wanted)
-
-
-def early_kernel(t0, got, w, own):
+    parts = [p.astype(F32) for p in split3(steps[0])] + [wanted.astype(F32)]
+    body = jnp.concatenate(parts, axis=1)
+    upper[256:272] = jnp.concatenate([body, jnp.zeros((8, 4 * TOK), F32)], axis=0).astype(BF)
+
+
+def early_kernel(t0, w, ta1, own):
     for k in range(3):
         own[k] = mm(t0[0], w[k]).astype(BF)
 
 
 def project_kernel(
-    scal, early, ta, tb, td1, td2, got, w, kv_own, kvq_other, q_own, steps, rows
+    scal, early, upper, ta1, td1, tb1, ta2, td2, tb2, w,
+    kv_own, kvq_other, q_own, steps_own, wanted_own, rows,
 ):
-    c, x = scal[0], scal[1]
-    rows[0:128] = ta[...]
-    rows[128:192] = td1[...]
-    rows[192:256] = td2[...]
-    rows[256:384] = tb[...]
-    for i in range(8):
-        steps[i : i + 1] = got[i, 0:1]
+    c, x, h = scal[0], scal[1], scal[5]
+    for r, part in enumerate((ta1, td1, tb1)):
+        for b in range(4):
+            rows[128 * r : 128 * r + 64, 512 * b : 512 * b + 512] = part[64 * b : 64 * b + 64]
+    for r, part in enumerate((ta2, td2, tb2)):
+        rows[128 * r + 64 : 128 * r + 128] = part[...]
     first = c == 0
+    head = lax.broadcasted_iota(jnp.int32, (8, 4 * TOK), 0)
+    row = lax.broadcasted_iota(jnp.int32, (16, 3 * TOK), 0)
+    other_head = h + 1 - 2 * c
+    for r, part in enumerate((upper, ta1, td1, tb1)):
+        n = lax.rem(x - r + DOCS, DOCS)
+        body = part[256:272].astype(F32)[0:8]
+        mine = jnp.sum(jnp.where(head == h, body, 0.0), axis=0, keepdims=True)
+        theirs = jnp.sum(jnp.where(head == other_head, body, 0.0), axis=0, keepdims=True)
+        decay = (mine[:, :TOK] + mine[:, TOK : 2 * TOK]) + mine[:, 2 * TOK : 3 * TOK]
+        wanted = mine[:, 3 * TOK :]
+        steps_own[n] = jnp.broadcast_to(decay, (8, TOK))
+        wanted_own[n] = jnp.broadcast_to(wanted, (8, TOK))
+        line = jnp.concatenate([wanted, wanted, wanted], axis=1)
+        note = jnp.where(row == 0, theirs[:, : 3 * TOK], jnp.where(row == 1, line, 0.0))
+        kvq_other[n, TOK:] = note.astype(BF)
     for k in range(3):
         part = jnp.concatenate([early[k], mm(rows[...], w[k]).astype(BF)], axis=0)
         for r in range(DOCS):
@@ -94,23 +111,34 @@
             other = jnp.where(first, hi, lo)
             if k == 0:
                 q_own[n] = own
-                kvq_other[n, :, 2 * DH :] = other
+                kvq_other[n, :TOK, 2 * DH :] = other
             else:
                 here = slice((k - 1) * DH, k * DH)
                 kv_own[n, :, here] = own
-                kvq_other[n, :, here] = other
-
-
-def states_kernel(scal, kv_own, kvq_mate, steps, wft, out, state0):
+                kvq_other[n, :TOK, here] = other
+
+
+def states_kernel(scal, kv_own, kvq_mate, steps_own, wanted_own, wft, out, state0, steps, wanted):
     c, h = scal[0], scal[5]
     first = c == 0
-    cum = cumulative_of(steps[...])
+    place = lax.broadcasted_iota(jnp.int32, (8, TOK), 0)
+    decays, blocks = jnp.zeros((8, TOK), F32), jnp.zeros((8, TOK), F32)
+    for n in range(DOCS):
+        note = kvq_mate[n, TOK:].astype(F32)
+        theirs = (note[0:1, :TOK] + note[0:1, TOK : 2 * TOK]) + note[0:1, 2 * TOK :]
+        here = place == 2 * n + c
+        there = place == 2 * n + 1 - c
+        decays = jnp.where(here, steps_own[n], jnp.where(there, theirs, decays))
+        blocks = jnp.where(here, wanted_own[n], jnp.where(there, note[1:2, :TOK], blocks))
+    steps[...] = decays
+    wanted[...] = blocks
+    cum = cumulative_of(decays)
     feature = wft[h]
     row = lax.broadcasted_iota(jnp.int32, (16, TOK), 0)
     segs = []
     for n in range(DOCS):
         own = kv_own[n]
-        mate = kvq_mate[n, :, : 2 * DH]
+        mate = kvq_mate[n, :TOK, : 2 * DH]
         segs += [jnp.where(first, own, mate), jnp.where(first, mate, own)]
     keys = jnp.concatenate([a[:, :DH] for a in segs], axis=0)
     phi = softmax0(nt(feature, keys)).astype(BF).astype(F32)
@@ -139,12 +167,12 @@
     first = c == 0
     for n in range(DOCS):
         own = kv_own[n]
-        mate = kvq_mate[n, :, : 2 * DH]
+        mate = kvq_mate[n, :TOK, : 2 * DH]
         early, later = jnp.where(first, own, mate), jnp.where(first, mate, own)
         kv2[0, n] = early
         kv2[1, n] = later
         q2[c, n] = q_own[n]
-        q2[1 - c, n] = kvq_mate[n, :, 2 * DH :]
+        q2[1 - c, n] = kvq_mate[n, :TOK, 2 * DH :]
 
 
 def state_rows(state):
@@ -314,37 +342,46 @@
     z, y = q % 8, q // 8
     h = 2 * x + c
     scal = jnp.stack([c, x, q, z, y, h]).astype(jnp.int32)
-    t0 = tokens[0]
     up = [(i, (i + 1) % 4) for i in range(4)]
     down = [(i, (i - 1) % 4) for i in range(4)]
-    ta = lax.ppermute(t0, "fsdp", up)
-    tb = lax.ppermute(t0, "fsdp", down)
-
     w3 = w_qkv.transpose(1, 0, 2)
     wft = w_feature.transpose(0, 2, 1)
-    [packed] = call(pack_kernel, [shape((8, 8, TOK), F32)], [], "sv", 1, 4, pattern, log_decay)
-    got0 = exchange(packed, ("seq", "fsdp"), XC)
-    td1 = lax.ppermute(ta[:64], "fsdp", up)
-    td2 = lax.ppermute(tb[64:], "fsdp", down)
-    [early] = call(
-        early_kernel, [shape((3, TOK, 2 * DH), BF)], [], "vav", 6, 12, tokens, got0, w3
-    )
-    pat = got0[:, 1, :6].astype(jnp.int32).reshape(48) - (4 * q - 6)
-    pat = jnp.clip(pat, 0, 15).astype(jnp.int32)
-
-    kv_own, kvq_other, q_own, steps = call(
+    upper, lower = pl.pallas_call(
+        split_kernel,
+        grid=(1,),
+        out_shape=[shape((272, 512), BF), shape((64, D), BF)],
+        in_specs=[
+            pl.BlockSpec(memory_space=pltpu.SMEM),
+            pl.BlockSpec((1, TOK, D), lambda i: (0, 0, 0)),
+            pl.BlockSpec((1, 8, TOK), lambda i: (0, 0, 0)),
+        ],
+        out_specs=[
+            pl.BlockSpec((272, 512), lambda i: (0, 0)),
+            pl.BlockSpec((64, D), lambda i: (0, 0)),
+        ],
+    )(pattern, tokens, log_decay)
+    ta1 = lax.ppermute(upper, "fsdp", up)
+    tb2 = lax.ppermute(lower, "fsdp", down)
+    ta2 = lax.ppermute(lower, "fsdp", up)
+    tb1 = lax.ppermute(upper, "fsdp", down)
+    td1 = lax.ppermute(ta1, "fsdp", up)
+    td2 = lax.ppermute(tb2, "fsdp", down)
+    [early] = call(early_kernel, [shape((3, TOK, 2 * DH), BF)], [], "vva", 6, 12, tokens, w3, ta1)
+
+    kv_own, kvq_other, q_own, steps_own, wanted_own = call(
         project_kernel,
         [
             shape((DOCS, TOK, 2 * DH), BF),
-            shape((DOCS, TOK, 3 * DH), BF),
+            shape((DOCS, TOK + 16, 3 * DH), BF),
             shape((DOCS, TOK, DH), BF),
-            shape((8, TOK), F32),
+            shape((DOCS, 8, TOK), F32),
+            shape((DOCS, 8, TOK), F32),
         ],
         [pltpu.VMEM((3 * TOK, D), BF)],
-        "s" + "v" * 7,
+        "s" + "v" * 9,
         3,
         16,
-        scal, early, ta, tb, td1, td2, got0, w3,
+        scal, early, upper, ta1, td1, tb1, ta2, td2, tb2, w3,
     )
     kvq_mate = lax.ppermute(kvq_other, "seq", pairs(lambda q, c: (q, 1 - c)))
     kv2, q2 = call(
@@ -358,15 +395,22 @@
     )
     zp = lax.ppermute(kv2, "seq", pairs(lambda q, c: (q + 1, c)))
     zm = lax.ppermute(kv2, "seq", pairs(lambda q, c: (q - 1, c)))
-    send1, state0 = call(
+    send1, state0, steps, wanted = call(
         states_kernel,
-        [shape((8, ROWS, TOK), BF), shape((DOCS, F, DH), F32)],
+        [
+            shape((8, ROWS, TOK), BF),
+            shape((DOCS, F, DH), F32),
+            shape((8, TOK), F32),
+            shape((8, TOK), F32),
+        ],
         [],
-        "svvvv",
+        "svvvvv",
         2,
         8,
-        scal, kv_own, kvq_mate, steps, wft,
-    )
+        scal, kv_own, kvq_mate, steps_own, wanted_own, wft,
+    )
+    pat = wanted[:, :6].astype(jnp.int32).reshape(48) - (4 * q - 6)
+    pat = jnp.clip(pat, 0, 15).astype(jnp.int32)
     got1 = exchange(send1, "seq", ZS)
     def chain(got1, near_p, near_m):
         send2, inner, outer = call(

time: 110 us -> 109 us (level)
  waiting for transfers between devices: 23.2 us -> 20.7 us
    all_to_all x4 -> x3, starting transfers between devices: 28.6 us -> 15.3 us  [exchange(): return lax.all_to_all(a, axis, 0, 0, tiled=True, axis_index_groups=groups)]
    ppermute x1, starting transfers between devices: 3.42 us -> 12 us  [per_device(): kvq_mate = lax.ppermute(kvq_other, 'seq', pairs(lambda q, c: (q, 1 - c)))]
    ppermute x4 -> x6, starting transfers between devices: 13.7 us -> 18.9 us  [the longest x1 4.4 us: per_device(): tb1 = lax.ppermute(upper, 'fsdp', down)]
    ppermute x4 -> x6, waiting for transfers between devices: 5.86 us -> 3.28 us  [the longest x1 1.81 us: per_device(): td1 = lax.ppermute(ta1, 'fsdp', up)]
    pallas_call x0 -> x1, Pallas kernels: none -> 1.88 us  [per_device(): pl.pallas_call(split_kernel, grid=(1,), out_shape=[shape((272, 512), BF),...]
    pallas_call x8 -> x7, Pallas kernels: 11.6 us -> 10.4 us  [call(): pl.pallas_call(kernel, out_shape=outs, in_specs=[pl.BlockSpec(memory_spac...]
    unnamed x14 -> x12, local copies, waits for them, and re-layouts: 3.26 us -> 2.94 us
    all_to_all x4 -> x3, waiting for transfers between devices: 9.95 us -> 9.94 us  [exchange(): return lax.all_to_all(a, axis, 0, 0, tiled=True, axis_index_groups=groups)]
  transfers between devices with their start and end apart: 13 -> 14, of which waited for: 7 -> 7; matrix products, arithmetic and copies ran while one was open for 0% -> 0% of each run, Pallas kernels for 4% -> 3%
where the time goes in v10:
time: 109 us; the launch traced here: 108 us
  starting transfers between devices  56.1 us (51%)
  waiting for transfers between devices  20.7 us (19%)
  blocking collectives  14.2 us (13%)
  Pallas kernels  12.3 us (11%)
  local copies, waits for them, and re-layouts  4.17 us (4%)
    all_to_all x3, starting transfers between devices, exchange(): return lax.all_to_all(a, axis, 0, 0, tiled=True, axis_index_groups=groups)  15.3 us
    all_to_all x1, blocking collectives, exchange(): return lax.all_to_all(a, axis, 0, 0, tiled=True, axis_index_groups=groups)  14.2 us
    ppermute x1, starting transfers between devices, per_device(): kvq_mate = lax.ppermute(kvq_other, 'seq', pairs(lambda q, c: (q, 1 - c)))  12 us
    pallas_call x7, Pallas kernels, call(): pl.pallas_call(kernel, out_shape=outs, in_specs=[pl.BlockSpec(memory_spac...  10.4 us
    all_to_all x3, waiting for transfers between devices, exchange(): return lax.all_to_all(a, axis, 0, 0, tiled=True, axis_index_groups=groups)  9.94 us
    ppermute x1, waiting for transfers between devices, chain(): tp = lax.ppermute(near_p, 'seq', pairs(lambda q, c: (q + 1, c)))  5.13 us
    ppermute x1, starting transfers between devices, per_device(): tb1 = lax.ppermute(upper, 'fsdp', down)  4.4 us
    ppermute x1, starting transfers between devices, per_device(): zp = lax.ppermute(kv2, 'seq', pairs(lambda q, c: (q + 1, c)))  4.03 us
  transfers between devices with their start and end apart: 14, of which 7 were waited for; matrix products, arithmetic and copies ran while one was open for 0% of the time, Pallas kernels for 3%

profile of v10, /device:TPU:1, one launch (start us, length us, event | category | flops | bytes accessed | tf_op | source)
XLA Modules:
  0.0 107.8 jit_solution(14954841498946455438)
XLA Ops:
  0.0 1.9 %shard_map.64 = (bf16[272,512]{1,0:T(8,128)(2,1)}, bf16[64,2048]{1,0:T(8,128)(2,1)}) custom-call(s32[1,2,3]{2,1,0:T(2,128)} %pat.1, bf16[1,128,2048]{2,1,0:T(8,128)(2,1)} %t0.1, f32[1,8,128]{2,1,0:T(8,128)} %steps.1), custom_call_target="tpu_custom_call" | custom-call | tf_op jit(solution)/shard_map/pallas_call | solution.py:349
  1.9 3.9 %collective-permute-start = (bf16[272,512]{1,0:T(8,128)(2,1)}, bf16[272,512]{1,0:T(8,128)(2,1)S(1)}, u32[]{:S(2)}, u32[]{:S(2)}) collective-permute-start(bf16[272,512]{1,0:T(8,128)(2,1)} %get-tuple-element.21.upper), channel_id=1, source_target_pairs={{0,1},{1,2},{2,3},{3,0},{4,5},{5,6},{6,7},{7,4},{8,9},{9,10},{10,1... | collective-permute-start | bytes 835592 | tf_op jit(solution)/shard_map/ppermute | solution.py:363
  5.8 3.2 %collective-permute-start.4 = (bf16[64,2048]{1,0:T(8,128)(2,1)}, bf16[64,2048]{1,0:T(8,128)(2,1)S(1)}, u32[]{:S(2)}, u32[]{:S(2)}) collective-permute-start(bf16[64,2048]{1,0:T(8,128)(2,1)} %get-tuple-element.22), channel_id=1, source_target_pairs={{0,3},{1,0},{2,1},{3,2},{4,7},{5,4},{6,5},{7,6},{8,11},{9,8},{10,9... | collective-permute-start | bytes 786440 | tf_op jit(solution)/shard_map/ppermute | solution.py:364
  9.0 2.1 %collective-permute-start.3 = (bf16[64,2048]{1,0:T(8,128)(2,1)}, bf16[64,2048]{1,0:T(8,128)(2,1)S(1)}, u32[]{:S(2)}, u32[]{:S(2)}) collective-permute-start(bf16[64,2048]{1,0:T(8,128)(2,1)} %get-tuple-element.22), channel_id=1, source_target_pairs={{0,1},{1,2},{2,3},{3,0},{4,5},{5,6},{6,7},{7,4},{8,9},{9,10},{10,1... | collective-permute-start | bytes 786440 | tf_op jit(solution)/shard_map/ppermute | solution.py:365
  11.1 4.4 %collective-permute-start.2 = (bf16[272,512]{1,0:T(8,128)(2,1)}, bf16[272,512]{1,0:T(8,128)(2,1)S(1)}, u32[]{:S(2)}, u32[]{:S(2)}) collective-permute-start(bf16[272,512]{1,0:T(8,128)(2,1)} %get-tuple-element.21.upper), channel_id=1, source_target_pairs={{0,3},{1,0},{2,1},{3,2},{4,7},{5,4},{6,5},{7,6},{8,11},{9,8},{10,9... | collective-permute-start | bytes 835592 | tf_op jit(solution)/shard_map/ppermute | solution.py:366
  15.6 0.1 stack.27.scal
  15.7 0.0 collective-permute-done.4.tb2
  15.7 2.1 %collective-permute-start.5 = (bf16[64,2048]{1,0:T(8,128)(2,1)S(1)}, bf16[64,2048]{1,0:T(8,128)(2,1)S(1)}, u32[]{:S(2)}, u32[]{:S(2)}) collective-permute-start(bf16[64,2048]{1,0:T(8,128)(2,1)S(1)} %collective-permute-done.4.tb2), channel_id=1, source_target_pairs={{0,3},{1,0},{2,1},{3,2},{4,7},{5,4},{6,5},{7,6},{8,11},{9,8},{10,9... | collective-permute-start | bytes 786440 | tf_op jit(solution)/shard_map/ppermute | solution.py:368
  17.8 0.0 collective-permute-done.ta1
  17.8 3.1 %collective-permute-start.1 = (bf16[272,512]{1,0:T(8,128)(2,1)S(1)}, bf16[272,512]{1,0:T(8,128)(2,1)S(1)}, u32[]{:S(2)}, u32[]{:S(2)}) collective-permute-start(bf16[272,512]{1,0:T(8,128)(2,1)S(1)} %collective-permute-done.ta1), channel_id=1, source_target_pairs={{0,1},{1,2},{2,3},{3,0},{4,5},{5,6},{6,7},{7,4},{8,9},{9,10},{10,1... | collective-permute-start | bytes 835592 | tf_op jit(solution)/shard_map/ppermute | solution.py:367
  21.0 0.0 copy-start
  21.0 1.0 copy-done
  22.0 0.0 copy-start.1
  22.0 1.9 %copy-done.1 = bf16[2048,3,256]{2,0,1:T(8,128)(2,1)S(1)} copy-done((bf16[2048,3,256]{2,0,1:T(8,128)(2,1)S(1)}, bf16[2048,3,256]{2,0,1:T(8,128)(2,1)}, u32[]{:S(2)}) %copy-start.1) | copy-done | bytes 3145752
  23.9 0.0 copy-start.2
  23.9 0.0 copy-start.3
  23.9 0.6 shard_map.65.early
  24.5 0.0 copy-start.4
  24.5 0.0 collective-permute-done.3.ta2
  24.5 0.0 collective-permute-done.2.tb1
  24.5 1.5 %collective-permute-done.5.td2 = bf16[64,2048]{1,0:T(8,128)(2,1)S(1)} collective-permute-done((bf16[64,2048]{1,0:T(8,128)(2,1)S(1)}, bf16[64,2048]{1,0:T(8,128)(2,1)S(1)}, u32[]{:S(2)}, u32[]{:S(2)}) %collective-permute-start.5) | collective-permute-done | bytes 262176 | tf_op jit(solution)/shard_map/ppermute | solution.py:368
  26.0 1.8 %collective-permute-done.1.td1 = bf16[272,512]{1,0:T(8,128)(2,1)S(1)} collective-permute-done((bf16[272,512]{1,0:T(8,128)(2,1)S(1)}, bf16[272,512]{1,0:T(8,128)(2,1)S(1)}, u32[]{:S(2)}, u32[]{:S(2)}) %collective-permute-start.1) | collective-permute-done | bytes 278560 | tf_op jit(solution)/shard_map/ppermute | solution.py:367
  27.8 0.0 copy-done.2
  27.8 0.0 copy-done.3
  27.8 1.9 %shard_map.66 = (bf16[4,128,256]{2,1,0:T(8,128)(2,1)S(1)}, bf16[4,144,384]{2,1,0:T(8,128)(2,1)S(1)}, bf16[4,128,128]{2,1,0:T(8,128)(2,1)S(1)}, f32[4,8,128]{2,1,0:T(8,128)S(1)}, f32[4,8,128]{2,1,0:T(8,128)S(1)}) custom-call(s32[6]{0:T(128)S(1)} %stack.27.scal, bf16[3,128,256]{2,1,0:T(8,128)(2,1)S(1)} %shard_map.65.early, bf16[272,512]{1,0:T(8,128)(2,1)S(1)} %copy-done.3, ...), custom_call_target="tpu_custom_call" | custom-call | flops 3000000000 | bytes 9000000 | tf_op jit(solution)/shard_map/pallas_call | solution.py:302
  29.7 12.0 %collective-permute-start.6 = (bf16[4,144,384]{2,1,0:T(8,128)(2,1)S(1)}, bf16[4,144,384]{2,1,0:T(8,128)(2,1)S(1)}, u32[]{:S(2)}, u32[]{:S(2)}) collective-permute-start(bf16[4,144,384]{2,1,0:T(8,128)(2,1)S(1)} %get-tuple-element.24), channel_id=1, source_target_pairs={{0,4},{4,0},{8,12},{12,8},{16,20},{20,16},{24,28},{28,24},{32,36},... | collective-permute-start | bytes 1327112 | tf_op jit(solution)/shard_map/ppermute | solution.py:386
  41.7 1.4 %collective-permute-done.6.kvq_mate = bf16[4,144,384]{2,1,0:T(8,128)(2,1)S(1)} collective-permute-done((bf16[4,144,384]{2,1,0:T(8,128)(2,1)S(1)}, bf16[4,144,384]{2,1,0:T(8,128)(2,1)S(1)}, u32[]{:S(2)}, u32[]{:S(2)}) %collective-permute-start.6) | collective-permute-done | bytes 442400 | tf_op jit(solution)/shard_map/ppermute | solution.py:386
  43.1 0.0 copy-done.4
  43.1 1.7 %shard_map.67 = (bf16[8,96,128]{2,1,0:T(8,128)(2,1)}, f32[4,16,128]{2,1,0:T(8,128)S(1)}, f32[8,128]{1,0:T(8,128)S(1)}, f32[8,128]{1,0:T(8,128)S(1)}) custom-call(s32[6]{0:T(128)S(1)} %stack.27.scal, bf16[4,128,256]{2,1,0:T(8,128)(2,1)S(1)} %get-tuple-element.23.kv_own, bf16[4,144,384]{2,1,0:T(8,128)(2,1)S(1)} %collective-permute-done.6.kvq_mate, ...), custom_call_target="tpu_custom_call" | custom-call | flops 2000000000 | bytes 6000000 | tf_op jit(solution)/shard_map/pallas_call | solution.py:302
  44.9 3.7 %all-to-all-start = ((bf16[8,96,128]{2,1,0:T(8,128)(2,1)}), bf16[8,96,128]{2,1,0:T(8,128)(2,1)S(1)}, u32[]{:S(2)}, u32[]{:S(2)}) async-start(bf16[8,96,128]{2,1,0:T(8,128)(2,1)} %get-tuple-element.31), calls=%async_computation | async-start | bytes 393216 | tf_op jit(solution)/shard_map/all_to_all | solution.py:335
  48.6 0.6 shard_map.68
  49.2 1.3 %collective-permute-start.8 = (bf16[2,4,128,256]{3,2,1,0:T(8,128)(2,1)S(1)}, bf16[2,4,128,256]{3,2,1,0:T(8,128)(2,1)S(1)}, u32[]{:S(2)}, u32[]{:S(2)}) collective-permute-start(bf16[2,4,128,256]{3,2,1,0:T(8,128)(2,1)S(1)} %get-tuple-element.29.kv2), channel_id=1, source_target_pairs={{8,0},{12,4},{16,8},{20,12},{24,16},{28,20},{32,24},{36,28},{40,32... | collective-permute-start | bytes 1572872 | tf_op jit(solution)/shard_map/ppermute | solution.py:397
  50.5 4.0 %collective-permute-start.7 = (bf16[2,4,128,256]{3,2,1,0:T(8,128)(2,1)S(1)}, bf16[2,4,128,256]{3,2,1,0:T(8,128)(2,1)S(1)}, u32[]{:S(2)}, u32[]{:S(2)}) collective-permute-start(bf16[2,4,128,256]{3,2,1,0:T(8,128)(2,1)S(1)} %get-tuple-element.29.kv2), channel_id=1, source_target_pairs={{0,8},{4,12},{8,16},{12,20},{16,24},{20,28},{24,32},{28,36},{32,40... | collective-permute-start | bytes 1572872 | tf_op jit(solution)/shard_map/ppermute | solution.py:396
  54.5 3.5 %all-to-all-done.got = bf16[8,96,128]{2,1,0:T(8,128)(2,1)S(1)} async-done(((bf16[8,96,128]{2,1,0:T(8,128)(2,1)}), bf16[8,96,128]{2,1,0:T(8,128)(2,1)S(1)}, u32[]{:S(2)}, u32[]{:S(2)}) %all-to-all-start) | async-done | bytes 196640 | tf_op jit(solution)/shard_map/all_to_all | solution.py:335
  58.0 0.7 shard_map.69
  58.7 0.0 copy-start.5
  58.7 7.0 %all-to-all-start.1 = ((bf16[8,96,128]{2,1,0:T(8,128)(2,1)}), bf16[8,96,128]{2,1,0:T(8,128)(2,1)S(1)}, u32[]{:S(2)}, u32[]{:S(2)}) async-start(bf16[8,96,128]{2,1,0:T(8,128)(2,1)} %get-tuple-element.32), calls=%async_computation.1 | async-start | bytes 393216 | tf_op jit(solution)/shard_map/all_to_all | solution.py:335
  65.7 1.0 collective-permute-done.8.zm
  66.7 1.3 %collective-permute-start.10 = (bf16[4,128,256]{2,1,0:T(8,128)(2,1)S(1)}, bf16[4,128,256]{2,1,0:T(8,128)(2,1)S(1)}, u32[]{:S(2)}, u32[]{:S(2)}) collective-permute-start(bf16[4,128,256]{2,1,0:T(8,128)(2,1)S(1)} %slice_bitcast_fusion), channel_id=1, source_target_pairs={{8,0},{12,4},{16,8},{20,12},{24,16},{28,20},{32,24},{36,28},{40,32... | collective-permute-start | bytes 786440 | tf_op jit(solution)/shard_map/ppermute | solution.py:430
  68.0 6.5 %all-to-all-done.1.got = bf16[8,96,128]{2,1,0:T(8,128)(2,1)S(1)} async-done(((bf16[8,96,128]{2,1,0:T(8,128)(2,1)}), bf16[8,96,128]{2,1,0:T(8,128)(2,1)S(1)}, u32[]{:S(2)}, u32[]{:S(2)}) %all-to-all-start.1) | async-done | bytes 196640 | tf_op jit(solution)/shard_map/all_to_all | solution.py:335
  74.4 1.2 %shard_map.70 = bf16[8,80,128]{2,1,0:T(8,128)(2,1)} custom-call(s32[6]{0:T(128)S(1)} %stack.27.scal, bf16[8,96,128]{2,1,0:T(8,128)(2,1)S(1)} %all-to-all-done.1.got, f32[8,8,128]{2,1,0:T(8,128)S(1)} %get-tuple-element.33.inner, f32[8,8,128]{2,1,0:T(8,128)S(1)} %get-tuple-element.34.outer), custom_call_target="tpu_custom_call" | custom-call | flops 1000000000 | bytes 3000000 | tf_op jit(solution)/shard_map/pallas_call | solution.py:302
  75.7 4.6 %all-to-all-start.2 = ((bf16[8,80,128]{2,1,0:T(8,128)(2,1)}), bf16[8,80,128]{2,1,0:T(8,128)(2,1)S(1)}, u32[]{:S(2)}, u32[]{:S(2)}) async-start(bf16[8,80,128]{2,1,0:T(8,128)(2,1)} %shard_map.70), calls=%async_computation.2 | async-start | bytes 327680 | tf_op jit(solution)/shard_map/all_to_all | solution.py:335
  80.3 0.0 collective-permute-done.7.zp
  80.3 3.4 %collective-permute-start.9 = (bf16[4,128,256]{2,1,0:T(8,128)(2,1)S(1)}, bf16[4,128,256]{2,1,0:T(8,128)(2,1)S(1)}, u32[]{:S(2)}, u32[]{:S(2)}) collective-permute-start(bf16[4,128,256]{2,1,0:T(8,128)(2,1)S(1)} %slice_bitcast_fusion.1), channel_id=1, source_target_pairs={{0,8},{4,12},{8,16},{12,20},{16,24},{20,28},{24,32},{28,36},{32,40... | collective-permute-start | bytes 786440 | tf_op jit(solution)/shard_map/ppermute | solution.py:429
  83.7 0.1 min.12.pat
  83.8 0.0 collective-permute-done.10.tm
  83.8 5.1 %collective-permute-done.9.tp = bf16[4,128,256]{2,1,0:T(8,128)(2,1)S(1)} collective-permute-done((bf16[4,128,256]{2,1,0:T(8,128)(2,1)S(1)}, bf16[4,128,256]{2,1,0:T(8,128)(2,1)S(1)}, u32[]{:S(2)}, u32[]{:S(2)}) %collective-permute-start.9) | collective-permute-done | bytes 262176 | tf_op jit(solution)/shard_map/ppermute | solution.py:429
  88.9 0.0 all-to-all-done.2.got
  88.9 0.0 copy-done.5
  88.9 3.6 %shard_map.71 = bf16[8,128,128]{2,1,0:T(8,128)(2,1)S(1)} custom-call(s32[6]{0:T(128)S(1)} %stack.27.scal, s32[48]{0:T(128)S(1)} %min.12.pat, bf16[2,4,128,256]{3,2,1,0:T(8,128)(2,1)S(1)} %get-tuple-element.29.kv2, bf16[2,4,128,128]{3,2,1,0:T(8,128)(2,1)S(1)} %get-tuple-element.30.q2, bf16[2,4,128,256]{3,2,1,0:T(8,128)(2,1)S(1)} %collective-permute-done.7.zp, ...), custom_call_target="tpu_custom_call" | custom-call | flops 8000000000 | bytes 24000000 | tf_op jit(solution)/shard_map/pallas_call | solution.py:302
  92.5 14.2 %all_to_all.20 = bf16[8,128,128]{2,1,0:T(8,128)(2,1)S(1)} all-to-all(bf16[8,128,128]{2,1,0:T(8,128)(2,1)S(1)} %shard_map.71), channel_id=1, replica_groups={{0,4,1,5,2,6,3,7},{8,12,9,13,10,14,11,15},{16,20,17,21,18,22,19,23},{24..., dimensions={0} | all-to-all | bytes 524288 | tf_op jit(solution)/shard_map/all_to_all | solution.py:335
  106.8 0.2 copy.7
  107.0 0.9 copy.8
  (3 shorter events, 0.0 us)
Async XLA Ops:
  1.9 15.9 %collective-permute-start = (bf16[272,512]{1,0:T(8,128)(2,1)}, bf16[272,512]{1,0:T(8,128)(2,1)S(1)}, u32[]{:S(2)}, u32[]{:S(2)}) collective-permute-start(bf16[272,512]{1,0:T(8,128)(2,1)} %get-tuple-element.21.upper), channel_id=1, source_target_pairs={{0,1},{1,2},{2,3},{3,0},{4,5},{5,6},{6,7},{7,4},{8,9},{9,10},{10,1... | collective-permute-start | bytes 835592 | tf_op jit(solution)/shard_map/ppermute | solution.py:363
  5.8 9.8 %collective-permute-start.4 = (bf16[64,2048]{1,0:T(8,128)(2,1)}, bf16[64,2048]{1,0:T(8,128)(2,1)S(1)}, u32[]{:S(2)}, u32[]{:S(2)}) collective-permute-start(bf16[64,2048]{1,0:T(8,128)(2,1)} %get-tuple-element.22), channel_id=1, source_target_pairs={{0,3},{1,0},{2,1},{3,2},{4,7},{5,4},{6,5},{7,6},{8,11},{9,8},{10,9... | collective-permute-start | bytes 786440 | tf_op jit(solution)/shard_map/ppermute | solution.py:364
  9.0 15.5 %collective-permute-start.3 = (bf16[64,2048]{1,0:T(8,128)(2,1)}, bf16[64,2048]{1,0:T(8,128)(2,1)S(1)}, u32[]{:S(2)}, u32[]{:S(2)}) collective-permute-start(bf16[64,2048]{1,0:T(8,128)(2,1)} %get-tuple-element.22), channel_id=1, source_target_pairs={{0,1},{1,2},{2,3},{3,0},{4,5},{5,6},{6,7},{7,4},{8,9},{9,10},{10,1... | collective-permute-start | bytes 786440 | tf_op jit(solution)/shard_map/ppermute | solution.py:365
  11.1 13.4 %collective-permute-start.2 = (bf16[272,512]{1,0:T(8,128)(2,1)}, bf16[272,512]{1,0:T(8,128)(2,1)S(1)}, u32[]{:S(2)}, u32[]{:S(2)}) collective-permute-start(bf16[272,512]{1,0:T(8,128)(2,1)} %get-tuple-element.21.upper), channel_id=1, source_target_pairs={{0,3},{1,0},{2,1},{3,2},{4,7},{5,4},{6,5},{7,6},{8,11},{9,8},{10,9... | collective-permute-start | bytes 835592 | tf_op jit(solution)/shard_map/ppermute | solution.py:366
  15.7 10.3 %collective-permute-start.5 = (bf16[64,2048]{1,0:T(8,128)(2,1)S(1)}, bf16[64,2048]{1,0:T(8,128)(2,1)S(1)}, u32[]{:S(2)}, u32[]{:S(2)}) collective-permute-start(bf16[64,2048]{1,0:T(8,128)(2,1)S(1)} %collective-permute-done.4.tb2), channel_id=1, source_target_pairs={{0,3},{1,0},{2,1},{3,2},{4,7},{5,4},{6,5},{7,6},{8,11},{9,8},{10,9... | collective-permute-start | bytes 786440 | tf_op jit(solution)/shard_map/ppermute | solution.py:368
  17.8 10.0 %collective-permute-start.1 = (bf16[272,512]{1,0:T(8,128)(2,1)S(1)}, bf16[272,512]{1,0:T(8,128)(2,1)S(1)}, u32[]{:S(2)}, u32[]{:S(2)}) collective-permute-start(bf16[272,512]{1,0:T(8,128)(2,1)S(1)} %collective-permute-done.ta1), channel_id=1, source_target_pairs={{0,1},{1,2},{2,3},{3,0},{4,5},{5,6},{6,7},{7,4},{8,9},{9,10},{10,1... | collective-permute-start | bytes 835592 | tf_op jit(solution)/shard_map/ppermute | solution.py:367
  21.0 1.0 copy-start
  22.0 1.9 %copy-start.1 = (bf16[2048,3,256]{2,0,1:T(8,128)(2,1)S(1)}, bf16[2048,3,256]{2,0,1:T(8,128)(2,1)}, u32[]{:S(2)}) copy-start(bf16[2048,3,256]{2,0,1:T(8,128)(2,1)} %param.7) | copy-start | bytes 9437188
  23.9 3.9 %copy-start.2 = (bf16[2048,3,256]{2,0,1:T(8,128)(2,1)S(1)}, bf16[2048,3,256]{2,0,1:T(8,128)(2,1)}, u32[]{:S(2)}) copy-start(bf16[2048,3,256]{2,0,1:T(8,128)(2,1)} %param.7) | copy-start | bytes 9437188
  23.9 3.9 %copy-start.3 = (bf16[272,512]{1,0:T(8,128)(2,1)S(1)}, bf16[272,512]{1,0:T(8,128)(2,1)}, u32[]{:S(2)}) copy-start(bf16[272,512]{1,0:T(8,128)(2,1)} %get-tuple-element.21.upper) | copy-start | bytes 835588
  24.5 18.7 %copy-start.4 = (bf16[8,128,16]{1,2,0:T(8,128)(2,1)S(1)}, bf16[8,128,16]{1,2,0:T(8,128)(2,1)}, u32[]{:S(2)}) copy-start(bf16[8,128,16]{1,2,0:T(8,128)(2,1)} %param.8) | copy-start | bytes 98308
  29.7 13.4 %collective-permute-start.6 = (bf16[4,144,384]{2,1,0:T(8,128)(2,1)S(1)}, bf16[4,144,384]{2,1,0:T(8,128)(2,1)S(1)}, u32[]{:S(2)}, u32[]{:S(2)}) collective-permute-start(bf16[4,144,384]{2,1,0:T(8,128)(2,1)S(1)} %get-tuple-element.24), channel_id=1, source_target_pairs={{0,4},{4,0},{8,12},{12,8},{16,20},{20,16},{24,28},{28,24},{32,36},... | collective-permute-start | bytes 1327112 | tf_op jit(solution)/shard_map/ppermute | solution.py:386
  44.9 13.1 %all-to-all-start = ((bf16[8,96,128]{2,1,0:T(8,128)(2,1)}), bf16[8,96,128]{2,1,0:T(8,128)(2,1)S(1)}, u32[]{:S(2)}, u32[]{:S(2)}) async-start(bf16[8,96,128]{2,1,0:T(8,128)(2,1)} %get-tuple-element.31), calls=%async_computation | async-start | bytes 393216 | tf_op jit(solution)/shard_map/all_to_all | solution.py:335
  49.2 17.5 %collective-permute-start.8 = (bf16[2,4,128,256]{3,2,1,0:T(8,128)(2,1)S(1)}, bf16[2,4,128,256]{3,2,1,0:T(8,128)(2,1)S(1)}, u32[]{:S(2)}, u32[]{:S(2)}) collective-permute-start(bf16[2,4,128,256]{3,2,1,0:T(8,128)(2,1)S(1)} %get-tuple-element.29.kv2), channel_id=1, source_target_pairs={{8,0},{12,4},{16,8},{20,12},{24,16},{28,20},{32,24},{36,28},{40,32... | collective-permute-start | bytes 1572872 | tf_op jit(solution)/shard_map/ppermute | solution.py:397
  50.5 29.8 %collective-permute-start.7 = (bf16[2,4,128,256]{3,2,1,0:T(8,128)(2,1)S(1)}, bf16[2,4,128,256]{3,2,1,0:T(8,128)(2,1)S(1)}, u32[]{:S(2)}, u32[]{:S(2)}) collective-permute-start(bf16[2,4,128,256]{3,2,1,0:T(8,128)(2,1)S(1)} %get-tuple-element.29.kv2), channel_id=1, source_target_pairs={{0,8},{4,12},{8,16},{12,20},{16,24},{20,28},{24,32},{28,36},{32,40... | collective-permute-start | bytes 1572872 | tf_op jit(solution)/shard_map/ppermute | solution.py:396
  58.7 30.2 %copy-start.5 = (f32[1024]{0:T(1024)S(1)}, f32[1024]{0:T(1024)}, u32[]{:S(2)}) copy-start(f32[1024]{0:T(1024)} %param.9) | copy-start | bytes 12292
  58.7 15.7 %all-to-all-start.1 = ((bf16[8,96,128]{2,1,0:T(8,128)(2,1)}), bf16[8,96,128]{2,1,0:T(8,128)(2,1)S(1)}, u32[]{:S(2)}, u32[]{:S(2)}) async-start(bf16[8,96,128]{2,1,0:T(8,128)(2,1)} %get-tuple-element.32), calls=%async_computation.1 | async-start | bytes 393216 | tf_op jit(solution)/shard_map/all_to_all | solution.py:335
  66.7 17.1 %collective-permute-start.10 = (bf16[4,128,256]{2,1,0:T(8,128)(2,1)S(1)}, bf16[4,128,256]{2,1,0:T(8,128)(2,1)S(1)}, u32[]{:S(2)}, u32[]{:S(2)}) collective-permute-start(bf16[4,128,256]{2,1,0:T(8,128)(2,1)S(1)} %slice_bitcast_fusion), channel_id=1, source_target_pairs={{8,0},{12,4},{16,8},{20,12},{24,16},{28,20},{32,24},{36,28},{40,32... | collective-permute-start | bytes 786440 | tf_op jit(solution)/shard_map/ppermute | solution.py:430
  75.7 13.3 %all-to-all-start.2 = ((bf16[8,80,128]{2,1,0:T(8,128)(2,1)}), bf16[8,80,128]{2,1,0:T(8,128)(2,1)S(1)}, u32[]{:S(2)}, u32[]{:S(2)}) async-start(bf16[8,80,128]{2,1,0:T(8,128)(2,1)} %shard_map.70), calls=%async_computation.2 | async-start | bytes 327680 | tf_op jit(solution)/shard_map/all_to_all | solution.py:335
  80.3 8.6 %collective-permute-start.9 = (bf16[4,128,256]{2,1,0:T(8,128)(2,1)S(1)}, bf16[4,128,256]{2,1,0:T(8,128)(2,1)S(1)}, u32[]{:S(2)}, u32[]{:S(2)}) collective-permute-start(bf16[4,128,256]{2,1,0:T(8,128)(2,1)S(1)} %slice_bitcast_fusion.1), channel_id=1, source_target_pairs={{0,8},{4,12},{8,16},{12,20},{16,24},{20,28},{24,32},{28,36},{32,40... | collective-permute-start | bytes 786440 | tf_op jit(solution)/shard_map/ppermute | solution.py:429

commit v11 on v10

--- a/solution.py
+++ b/solution.py
@@ -162,7 +162,7 @@
             out[p, 64:96] = segs[2 * n][32 * half : 32 * half + 32, DH:]
 
 
-def join_kernel(scal, kv_own, q_own, kvq_mate, kv2, q2):
+def join_kernel(scal, kv_own, q_own, kvq_mate, send1, kv2, q2):
     c = scal[0]
     first = c == 0
     for n in range(DOCS):
@@ -212,7 +212,8 @@
         out[peer, 32:96] = got[0, 32:96]
 
 
-def back_kernel(scal, got, inner, outer, out):
+def back_kernel(scal, got, inner, outer, *refs):
+    out = refs[-1]
     y = scal[4]
     before = jnp.zeros((8, TOK), F32)
     for peer in range(8):
@@ -384,17 +385,6 @@
         scal, early, upper, ta1, td1, tb1, ta2, td2, tb2, w3,
     )
     kvq_mate = lax.ppermute(kvq_other, "seq", pairs(lambda q, c: (q, 1 - c)))
-    kv2, q2 = call(
-        join_kernel,
-        [shape((2, DOCS, TOK, 2 * DH), BF), shape((2, DOCS, TOK, DH), BF)],
-        [],
-        "svvv",
-        20,
-        8,
-        scal, kv_own, q_own, kvq_mate,
-    )
-    zp = lax.ppermute(kv2, "seq", pairs(lambda q, c: (q + 1, c)))
-    zm = lax.ppermute(kv2, "seq", pairs(lambda q, c: (q - 1, c)))
     send1, state0, steps, wanted = call(
         states_kernel,
         [
@@ -411,6 +401,17 @@
     )
     pat = wanted[:, :6].astype(jnp.int32).reshape(48) - (4 * q - 6)
     pat = jnp.clip(pat, 0, 15).astype(jnp.int32)
+    kv2, q2 = call(
+        join_kernel,
+        [shape((2, DOCS, TOK, 2 * DH), BF), shape((2, DOCS, TOK, DH), BF)],
+        [],
+        "svvva",
+        20,
+        8,
+        scal, kv_own, q_own, kvq_mate, send1,
+    )
+    zp = lax.ppermute(kv2, "seq", pairs(lambda q, c: (q + 1, c)))
+    zm = lax.ppermute(kv2, "seq", pairs(lambda q, c: (q - 1, c)))
     got1 = exchange(send1, "seq", ZS)
     def chain(got1, near_p, near_m):
         send2, inner, outer = call(
@@ -422,12 +423,12 @@
             4,
             got1,
         )
+        tp = lax.ppermute(near_p, "seq", pairs(lambda q, c: (q + 1, c)))
+        tm = lax.ppermute(near_m, "seq", pairs(lambda q, c: (q - 1, c)))
         got2 = exchange(send2, "seq", YS)
         [send3] = call(
-            back_kernel, [shape((8, 80, TOK), BF)], [], "svvv", 1, 4, scal, got2, inner, outer
+            back_kernel, [shape((8, 80, TOK), BF)], [], "svvvaa", 1, 4, scal, got2, inner, outer, tp, tm
         )
-        tp = lax.ppermute(near_p, "seq", pairs(lambda q, c: (q + 1, c)))
-        tm = lax.ppermute(near_m, "seq", pairs(lambda q, c: (q - 1, c)))
         return exchange(send3, "seq", ZS), tp, tm
 
     got3, tp, tm = chain(got1, zp[1], zm[0])

time: 109 us -> 123 us (1.13)
  the two profiles are of different devices: /device:TPU:1 before, /device:TPU:32 now
where the time goes in v11:
time: 123 us; the launch traced here: 122 us
  starting transfers between devices  62.7 us (51%)
  waiting for transfers between devices  32.6 us (27%)
  Pallas kernels  12.3 us (10%)
  blocking collectives  9.95 us (8%)
  local copies, waits for them, and re-layouts  4.17 us (3%)
    all_to_all x3, starting transfers between devices, exchange(): return lax.all_to_all(a, axis, 0, 0, tiled=True, axis_index_groups=groups)  20.3 us
    all_to_all x3, waiting for transfers between devices, exchange(): return lax.all_to_all(a, axis, 0, 0, tiled=True, axis_index_groups=groups)  18.7 us
    ppermute x1, starting transfers between devices, per_device(): zm = lax.ppermute(kv2, 'seq', pairs(lambda q, c: (q - 1, c)))  10.8 us
    pallas_call x7, Pallas kernels, call(): pl.pallas_call(kernel, out_shape=outs, in_specs=[pl.BlockSpec(memory_spac...  10.4 us
    all_to_all x1, blocking collectives, exchange(): return lax.all_to_all(a, axis, 0, 0, tiled=True, axis_index_groups=groups)  9.95 us
    ppermute x1, waiting for transfers between devices, chain(): tp = lax.ppermute(near_p, 'seq', pairs(lambda q, c: (q + 1, c)))  5.29 us
    ppermute x1, starting transfers between devices, per_device(): tb1 = lax.ppermute(upper, 'fsdp', down)  4.86 us
    ppermute x1, starting transfers between devices, chain(): tp = lax.ppermute(near_p, 'seq', pairs(lambda q, c: (q + 1, c)))  3.92 us
  transfers between devices with their start and end apart: 14, of which 7 were waited for; matrix products, arithmetic and copies ran while one was open for 0% of the time, Pallas kernels for 1%

profile of v11, /device:TPU:32, one launch (start us, length us, event | category | flops | bytes accessed | tf_op | source)
XLA Modules:
  0.0 122.0 jit_solution(8009644143203678975)
XLA Ops:
  0.0 1.9 %shard_map.64 = (bf16[272,512]{1,0:T(8,128)(2,1)}, bf16[64,2048]{1,0:T(8,128)(2,1)}) custom-call(s32[1,2,3]{2,1,0:T(2,128)} %pat.1, bf16[1,128,2048]{2,1,0:T(8,128)(2,1)} %t0.1, f32[1,8,128]{2,1,0:T(8,128)} %steps.1), custom_call_target="tpu_custom_call" | custom-call | tf_op jit(solution)/shard_map/pallas_call | solution.py:350
  1.9 3.4 %collective-permute-start = (bf16[272,512]{1,0:T(8,128)(2,1)}, bf16[272,512]{1,0:T(8,128)(2,1)S(1)}, u32[]{:S(2)}, u32[]{:S(2)}) collective-permute-start(bf16[272,512]{1,0:T(8,128)(2,1)} %get-tuple-element.21.upper), channel_id=1, source_target_pairs={{0,1},{1,2},{2,3},{3,0},{4,5},{5,6},{6,7},{7,4},{8,9},{9,10},{10,1... | collective-permute-start | bytes 835592 | tf_op jit(solution)/shard_map/ppermute | solution.py:364
  5.3 3.7 %collective-permute-start.4 = (bf16[64,2048]{1,0:T(8,128)(2,1)}, bf16[64,2048]{1,0:T(8,128)(2,1)S(1)}, u32[]{:S(2)}, u32[]{:S(2)}) collective-permute-start(bf16[64,2048]{1,0:T(8,128)(2,1)} %get-tuple-element.22), channel_id=1, source_target_pairs={{0,3},{1,0},{2,1},{3,2},{4,7},{5,4},{6,5},{7,6},{8,11},{9,8},{10,9... | collective-permute-start | bytes 786440 | tf_op jit(solution)/shard_map/ppermute | solution.py:365
  8.9 2.2 %collective-permute-start.3 = (bf16[64,2048]{1,0:T(8,128)(2,1)}, bf16[64,2048]{1,0:T(8,128)(2,1)S(1)}, u32[]{:S(2)}, u32[]{:S(2)}) collective-permute-start(bf16[64,2048]{1,0:T(8,128)(2,1)} %get-tuple-element.22), channel_id=1, source_target_pairs={{0,1},{1,2},{2,3},{3,0},{4,5},{5,6},{6,7},{7,4},{8,9},{9,10},{10,1... | collective-permute-start | bytes 786440 | tf_op jit(solution)/shard_map/ppermute | solution.py:366
  11.1 4.9 %collective-permute-start.2 = (bf16[272,512]{1,0:T(8,128)(2,1)}, bf16[272,512]{1,0:T(8,128)(2,1)S(1)}, u32[]{:S(2)}, u32[]{:S(2)}) collective-permute-start(bf16[272,512]{1,0:T(8,128)(2,1)} %get-tuple-element.21.upper), channel_id=1, source_target_pairs={{0,3},{1,0},{2,1},{3,2},{4,7},{5,4},{6,5},{7,6},{8,11},{9,8},{10,9... | collective-permute-start | bytes 835592 | tf_op jit(solution)/shard_map/ppermute | solution.py:367
  16.1 0.1 stack.27.scal
  16.1 0.0 collective-permute-done.4.tb2
  16.1 3.9 %collective-permute-start.5 = (bf16[64,2048]{1,0:T(8,128)(2,1)S(1)}, bf16[64,2048]{1,0:T(8,128)(2,1)S(1)}, u32[]{:S(2)}, u32[]{:S(2)}) collective-permute-start(bf16[64,2048]{1,0:T(8,128)(2,1)S(1)} %collective-permute-done.4.tb2), channel_id=1, source_target_pairs={{0,3},{1,0},{2,1},{3,2},{4,7},{5,4},{6,5},{7,6},{8,11},{9,8},{10,9... | collective-permute-start | bytes 786440 | tf_op jit(solution)/shard_map/ppermute | solution.py:369
  20.0 0.0 collective-permute-done.ta1
  20.0 2.0 %collective-permute-start.1 = (bf16[272,512]{1,0:T(8,128)(2,1)S(1)}, bf16[272,512]{1,0:T(8,128)(2,1)S(1)}, u32[]{:S(2)}, u32[]{:S(2)}) collective-permute-start(bf16[272,512]{1,0:T(8,128)(2,1)S(1)} %collective-permute-done.ta1), channel_id=1, source_target_pairs={{0,1},{1,2},{2,3},{3,0},{4,5},{5,6},{6,7},{7,4},{8,9},{9,10},{10,1... | collective-permute-start | bytes 835592 | tf_op jit(solution)/shard_map/ppermute | solution.py:368
  22.0 0.0 copy-start
  22.0 1.0 copy-done
  23.0 0.0 copy-start.1
  23.1 1.9 %copy-done.1 = bf16[2048,3,256]{2,0,1:T(8,128)(2,1)S(1)} copy-done((bf16[2048,3,256]{2,0,1:T(8,128)(2,1)S(1)}, bf16[2048,3,256]{2,0,1:T(8,128)(2,1)}, u32[]{:S(2)}) %copy-start.1) | copy-done | bytes 3145752
  24.9 0.0 copy-start.2
  24.9 0.0 copy-start.3
  24.9 0.6 shard_map.65.early
  25.5 0.0 copy-start.4
  25.5 0.0 collective-permute-done.3.ta2
  25.5 0.0 collective-permute-done.2.tb1
  25.6 1.3 %collective-permute-done.5.td2 = bf16[64,2048]{1,0:T(8,128)(2,1)S(1)} collective-permute-done((bf16[64,2048]{1,0:T(8,128)(2,1)S(1)}, bf16[64,2048]{1,0:T(8,128)(2,1)S(1)}, u32[]{:S(2)}, u32[]{:S(2)}) %collective-permute-start.5) | collective-permute-done | bytes 262176 | tf_op jit(solution)/shard_map/ppermute | solution.py:369
  26.9 3.2 %collective-permute-done.1.td1 = bf16[272,512]{1,0:T(8,128)(2,1)S(1)} collective-permute-done((bf16[272,512]{1,0:T(8,128)(2,1)S(1)}, bf16[272,512]{1,0:T(8,128)(2,1)S(1)}, u32[]{:S(2)}, u32[]{:S(2)}) %collective-permute-start.1) | collective-permute-done | bytes 278560 | tf_op jit(solution)/shard_map/ppermute | solution.py:368
  30.1 0.0 copy-done.2
  30.1 0.0 copy-done.3
  30.1 1.9 %shard_map.66 = (bf16[4,128,256]{2,1,0:T(8,128)(2,1)S(1)}, bf16[4,144,384]{2,1,0:T(8,128)(2,1)S(1)}, bf16[4,128,128]{2,1,0:T(8,128)(2,1)S(1)}, f32[4,8,128]{2,1,0:T(8,128)S(1)}, f32[4,8,128]{2,1,0:T(8,128)S(1)}) custom-call(s32[6]{0:T(128)S(1)} %stack.27.scal, bf16[3,128,256]{2,1,0:T(8,128)(2,1)S(1)} %shard_map.65.early, bf16[272,512]{1,0:T(8,128)(2,1)S(1)} %copy-done.3, ...), custom_call_target="tpu_custom_call" | custom-call | flops 3000000000 | bytes 9000000 | tf_op jit(solution)/shard_map/pallas_call | solution.py:303
  32.0 1.9 %collective-permute-start.6 = (bf16[4,144,384]{2,1,0:T(8,128)(2,1)S(1)}, bf16[4,144,384]{2,1,0:T(8,128)(2,1)S(1)}, u32[]{:S(2)}, u32[]{:S(2)}) collective-permute-start(bf16[4,144,384]{2,1,0:T(8,128)(2,1)S(1)} %get-tuple-element.24), channel_id=1, source_target_pairs={{0,4},{4,0},{8,12},{12,8},{16,20},{20,16},{24,28},{28,24},{32,36},... | collective-permute-start | bytes 1327112 | tf_op jit(solution)/shard_map/ppermute | solution.py:387
  33.9 1.8 %collective-permute-done.6.kvq_mate = bf16[4,144,384]{2,1,0:T(8,128)(2,1)S(1)} collective-permute-done((bf16[4,144,384]{2,1,0:T(8,128)(2,1)S(1)}, bf16[4,144,384]{2,1,0:T(8,128)(2,1)S(1)}, u32[]{:S(2)}, u32[]{:S(2)}) %collective-permute-start.6) | collective-permute-done | bytes 442400 | tf_op jit(solution)/shard_map/ppermute | solution.py:387
  35.7 0.0 copy-done.4
  35.7 1.7 %shard_map.67 = (bf16[8,96,128]{2,1,0:T(8,128)(2,1)}, f32[4,16,128]{2,1,0:T(8,128)S(1)}, f32[8,128]{1,0:T(8,128)S(1)}, f32[8,128]{1,0:T(8,128)S(1)}) custom-call(s32[6]{0:T(128)S(1)} %stack.27.scal, bf16[4,128,256]{2,1,0:T(8,128)(2,1)S(1)} %get-tuple-element.23.kv_own, bf16[4,144,384]{2,1,0:T(8,128)(2,1)S(1)} %collective-permute-done.6.kvq_mate, ...), custom_call_target="tpu_custom_call" | custom-call | flops 2000000000 | bytes 6000000 | tf_op jit(solution)/shard_map/pallas_call | solution.py:303
  37.4 0.6 shard_map.68
  38.0 10.8 %collective-permute-start.8 = (bf16[2,4,128,256]{3,2,1,0:T(8,128)(2,1)S(1)}, bf16[2,4,128,256]{3,2,1,0:T(8,128)(2,1)S(1)}, u32[]{:S(2)}, u32[]{:S(2)}) collective-permute-start(bf16[2,4,128,256]{3,2,1,0:T(8,128)(2,1)S(1)} %get-tuple-element.30.kv2), channel_id=1, source_target_pairs={{8,0},{12,4},{16,8},{20,12},{24,16},{28,20},{32,24},{36,28},{40,32... | collective-permute-start | bytes 1572872 | tf_op jit(solution)/shard_map/ppermute | solution.py:414
  48.9 3.4 %all-to-all-start = ((bf16[8,96,128]{2,1,0:T(8,128)(2,1)}), bf16[8,96,128]{2,1,0:T(8,128)(2,1)S(1)}, u32[]{:S(2)}, u32[]{:S(2)}) async-start(bf16[8,96,128]{2,1,0:T(8,128)(2,1)} %get-tuple-element.29.send1), calls=%async_computation | async-start | bytes 393216 | tf_op jit(solution)/shard_map/all_to_all | solution.py:336
  52.3 3.8 %collective-permute-start.7 = (bf16[2,4,128,256]{3,2,1,0:T(8,128)(2,1)S(1)}, bf16[2,4,128,256]{3,2,1,0:T(8,128)(2,1)S(1)}, u32[]{:S(2)}, u32[]{:S(2)}) collective-permute-start(bf16[2,4,128,256]{3,2,1,0:T(8,128)(2,1)S(1)} %get-tuple-element.30.kv2), channel_id=1, source_target_pairs={{0,8},{4,12},{8,16},{12,20},{16,24},{20,28},{24,32},{28,36},{32,40... | collective-permute-start | bytes 1572872 | tf_op jit(solution)/shard_map/ppermute | solution.py:413
  56.1 9.5 %all-to-all-done.got = bf16[8,96,128]{2,1,0:T(8,128)(2,1)S(1)} async-done(((bf16[8,96,128]{2,1,0:T(8,128)(2,1)}), bf16[8,96,128]{2,1,0:T(8,128)(2,1)S(1)}, u32[]{:S(2)}, u32[]{:S(2)}) %all-to-all-start) | async-done | bytes 196640 | tf_op jit(solution)/shard_map/all_to_all | solution.py:336
  65.5 0.7 shard_map.69
  66.3 0.0 copy-start.5
  66.3 13.5 %all-to-all-start.1 = ((bf16[8,96,128]{2,1,0:T(8,128)(2,1)}), bf16[8,96,128]{2,1,0:T(8,128)(2,1)S(1)}, u32[]{:S(2)}, u32[]{:S(2)}) async-start(bf16[8,96,128]{2,1,0:T(8,128)(2,1)} %get-tuple-element.32), calls=%async_computation.1 | async-start | bytes 393216 | tf_op jit(solution)/shard_map/all_to_all | solution.py:336
  79.8 0.0 collective-permute-done.8.zm
  79.8 1.9 %collective-permute-start.10 = (bf16[4,128,256]{2,1,0:T(8,128)(2,1)S(1)}, bf16[4,128,256]{2,1,0:T(8,128)(2,1)S(1)}, u32[]{:S(2)}, u32[]{:S(2)}) collective-permute-start(bf16[4,128,256]{2,1,0:T(8,128)(2,1)S(1)} %slice_bitcast_fusion), channel_id=1, source_target_pairs={{8,0},{12,4},{16,8},{20,12},{24,16},{28,20},{32,24},{36,28},{40,32... | collective-permute-start | bytes 786440 | tf_op jit(solution)/shard_map/ppermute | solution.py:427
  81.8 0.0 collective-permute-done.7.zp
  81.8 3.9 %collective-permute-start.9 = (bf16[4,128,256]{2,1,0:T(8,128)(2,1)S(1)}, bf16[4,128,256]{2,1,0:T(8,128)(2,1)S(1)}, u32[]{:S(2)}, u32[]{:S(2)}) collective-permute-start(bf16[4,128,256]{2,1,0:T(8,128)(2,1)S(1)} %slice_bitcast_fusion.1), channel_id=1, source_target_pairs={{0,8},{4,12},{8,16},{12,20},{16,24},{20,28},{24,32},{28,36},{32,40... | collective-permute-start | bytes 786440 | tf_op jit(solution)/shard_map/ppermute | solution.py:426
  85.7 0.0 all-to-all-done.1.got
  85.7 2.4 %collective-permute-done.10.refs_1_.tm = bf16[4,128,256]{2,1,0:T(8,128)(2,1)S(1)} collective-permute-done((bf16[4,128,256]{2,1,0:T(8,128)(2,1)S(1)}, bf16[4,128,256]{2,1,0:T(8,128)(2,1)S(1)}, u32[]{:S(2)}, u32[]{:S(2)}) %collective-permute-start.10) | collective-permute-done | bytes 262176 | tf_op jit(solution)/shard_map/ppermute | solution.py:427
  88.1 5.3 %collective-permute-done.9.refs_0_.tp = bf16[4,128,256]{2,1,0:T(8,128)(2,1)S(1)} collective-permute-done((bf16[4,128,256]{2,1,0:T(8,128)(2,1)S(1)}, bf16[4,128,256]{2,1,0:T(8,128)(2,1)S(1)}, u32[]{:S(2)}, u32[]{:S(2)}) %collective-permute-start.9) | collective-permute-done | bytes 262176 | tf_op jit(solution)/shard_map/ppermute | solution.py:426
  93.4 1.2 %shard_map.70 = bf16[8,80,128]{2,1,0:T(8,128)(2,1)} custom-call(s32[6]{0:T(128)S(1)} %stack.27.scal, bf16[8,96,128]{2,1,0:T(8,128)(2,1)S(1)} %all-to-all-done.1.got, f32[8,8,128]{2,1,0:T(8,128)S(1)} %get-tuple-element.33.inner, f32[8,8,128]{2,1,0:T(8,128)S(1)} %get-tuple-element.34.outer, bf16[4,128,256]{2,1,0:T(8,128)(2,1)S(1)} %collective-permute-done.9.refs_0_.tp, ...), custom_call_target="tpu_custom_call" | custom-call | flops 1000000000 | bytes 3000000 | tf_op jit(solution)/shard_map/pallas_call | solution.py:303
  94.6 3.4 %all-to-all-start.2 = ((bf16[8,80,128]{2,1,0:T(8,128)(2,1)}), bf16[8,80,128]{2,1,0:T(8,128)(2,1)S(1)}, u32[]{:S(2)}, u32[]{:S(2)}) async-start(bf16[8,80,128]{2,1,0:T(8,128)(2,1)} %shard_map.70), calls=%async_computation.2 | async-start | bytes 327680 | tf_op jit(solution)/shard_map/all_to_all | solution.py:336
  98.0 0.1 min.12.pat
  98.1 9.3 %all-to-all-done.2.got = bf16[8,80,128]{2,1,0:T(8,128)(2,1)S(1)} async-done(((bf16[8,80,128]{2,1,0:T(8,128)(2,1)}), bf16[8,80,128]{2,1,0:T(8,128)(2,1)S(1)}, u32[]{:S(2)}, u32[]{:S(2)}) %all-to-all-start.2) | async-done | bytes 163872 | tf_op jit(solution)/shard_map/all_to_all | solution.py:336
  107.4 0.0 copy-done.5
  107.4 3.6 %shard_map.71 = bf16[8,128,128]{2,1,0:T(8,128)(2,1)S(1)} custom-call(s32[6]{0:T(128)S(1)} %stack.27.scal, s32[48]{0:T(128)S(1)} %min.12.pat, bf16[2,4,128,256]{3,2,1,0:T(8,128)(2,1)S(1)} %get-tuple-element.30.kv2, bf16[2,4,128,128]{3,2,1,0:T(8,128)(2,1)S(1)} %get-tuple-element.31.q2, bf16[2,4,128,256]{3,2,1,0:T(8,128)(2,1)S(1)} %collective-permute-done.7.zp, ...), custom_call_target="tpu_custom_call" | custom-call | flops 8000000000 | bytes 24000000 | tf_op jit(solution)/shard_map/pallas_call | solution.py:303
  111.0 9.9 %all_to_all.20 = bf16[8,128,128]{2,1,0:T(8,128)(2,1)S(1)} all-to-all(bf16[8,128,128]{2,1,0:T(8,128)(2,1)S(1)} %shard_map.71), channel_id=1, replica_groups={{0,4,1,5,2,6,3,7},{8,12,9,13,10,14,11,15},{16,20,17,21,18,22,19,23},{24..., dimensions={0} | all-to-all | bytes 524288 | tf_op jit(solution)/shard_map/all_to_all | solution.py:336
  120.9 0.2 copy.7
  121.1 0.9 copy.8
  (3 shorter events, 0.0 us)
Async XLA Ops:
  1.9 18.1 %collective-permute-start = (bf16[272,512]{1,0:T(8,128)(2,1)}, bf16[272,512]{1,0:T(8,128)(2,1)S(1)}, u32[]{:S(2)}, u32[]{:S(2)}) collective-permute-start(bf16[272,512]{1,0:T(8,128)(2,1)} %get-tuple-element.21.upper), channel_id=1, source_target_pairs={{0,1},{1,2},{2,3},{3,0},{4,5},{5,6},{6,7},{7,4},{8,9},{9,10},{10,1... | collective-permute-start | bytes 835592 | tf_op jit(solution)/shard_map/ppermute | solution.py:364
  5.3 10.9 %collective-permute-start.4 = (bf16[64,2048]{1,0:T(8,128)(2,1)}, bf16[64,2048]{1,0:T(8,128)(2,1)S(1)}, u32[]{:S(2)}, u32[]{:S(2)}) collective-permute-start(bf16[64,2048]{1,0:T(8,128)(2,1)} %get-tuple-element.22), channel_id=1, source_target_pairs={{0,3},{1,0},{2,1},{3,2},{4,7},{5,4},{6,5},{7,6},{8,11},{9,8},{10,9... | collective-permute-start | bytes 786440 | tf_op jit(solution)/shard_map/ppermute | solution.py:365
  8.9 16.6 %collective-permute-start.3 = (bf16[64,2048]{1,0:T(8,128)(2,1)}, bf16[64,2048]{1,0:T(8,128)(2,1)S(1)}, u32[]{:S(2)}, u32[]{:S(2)}) collective-permute-start(bf16[64,2048]{1,0:T(8,128)(2,1)} %get-tuple-element.22), channel_id=1, source_target_pairs={{0,1},{1,2},{2,3},{3,0},{4,5},{5,6},{6,7},{7,4},{8,9},{9,10},{10,1... | collective-permute-start | bytes 786440 | tf_op jit(solution)/shard_map/ppermute | solution.py:366
  11.1 14.4 %collective-permute-start.2 = (bf16[272,512]{1,0:T(8,128)(2,1)}, bf16[272,512]{1,0:T(8,128)(2,1)S(1)}, u32[]{:S(2)}, u32[]{:S(2)}) collective-permute-start(bf16[272,512]{1,0:T(8,128)(2,1)} %get-tuple-element.21.upper), channel_id=1, source_target_pairs={{0,3},{1,0},{2,1},{3,2},{4,7},{5,4},{6,5},{7,6},{8,11},{9,8},{10,9... | collective-permute-start | bytes 835592 | tf_op jit(solution)/shard_map/ppermute | solution.py:367
  16.1 10.7 %collective-permute-start.5 = (bf16[64,2048]{1,0:T(8,128)(2,1)S(1)}, bf16[64,2048]{1,0:T(8,128)(2,1)S(1)}, u32[]{:S(2)}, u32[]{:S(2)}) collective-permute-start(bf16[64,2048]{1,0:T(8,128)(2,1)S(1)} %collective-permute-done.4.tb2), channel_id=1, source_target_pairs={{0,3},{1,0},{2,1},{3,2},{4,7},{5,4},{6,5},{7,6},{8,11},{9,8},{10,9... | collective-permute-start | bytes 786440 | tf_op jit(solution)/shard_map/ppermute | solution.py:369
  20.0 10.0 %collective-permute-start.1 = (bf16[272,512]{1,0:T(8,128)(2,1)S(1)}, bf16[272,512]{1,0:T(8,128)(2,1)S(1)}, u32[]{:S(2)}, u32[]{:S(2)}) collective-permute-start(bf16[272,512]{1,0:T(8,128)(2,1)S(1)} %collective-permute-done.ta1), channel_id=1, source_target_pairs={{0,1},{1,2},{2,3},{3,0},{4,5},{5,6},{6,7},{7,4},{8,9},{9,10},{10,1... | collective-permute-start | bytes 835592 | tf_op jit(solution)/shard_map/ppermute | solution.py:368
  22.0 1.0 copy-start
  23.0 1.9 %copy-start.1 = (bf16[2048,3,256]{2,0,1:T(8,128)(2,1)S(1)}, bf16[2048,3,256]{2,0,1:T(8,128)(2,1)}, u32[]{:S(2)}) copy-start(bf16[2048,3,256]{2,0,1:T(8,128)(2,1)} %param.7) | copy-start | bytes 9437188
  24.9 5.1 %copy-start.2 = (bf16[2048,3,256]{2,0,1:T(8,128)(2,1)S(1)}, bf16[2048,3,256]{2,0,1:T(8,128)(2,1)}, u32[]{:S(2)}) copy-start(bf16[2048,3,256]{2,0,1:T(8,128)(2,1)} %param.7) | copy-start | bytes 9437188
  24.9 5.1 %copy-start.3 = (bf16[272,512]{1,0:T(8,128)(2,1)S(1)}, bf16[272,512]{1,0:T(8,128)(2,1)}, u32[]{:S(2)}) copy-start(bf16[272,512]{1,0:T(8,128)(2,1)} %get-tuple-element.21.upper) | copy-start | bytes 835588
  25.5 10.2 %copy-start.4 = (bf16[8,128,16]{1,2,0:T(8,128)(2,1)S(1)}, bf16[8,128,16]{1,2,0:T(8,128)(2,1)}, u32[]{:S(2)}) copy-start(bf16[8,128,16]{1,2,0:T(8,128)(2,1)} %param.8) | copy-start | bytes 98308
  32.0 3.7 %collective-permute-start.6 = (bf16[4,144,384]{2,1,0:T(8,128)(2,1)S(1)}, bf16[4,144,384]{2,1,0:T(8,128)(2,1)S(1)}, u32[]{:S(2)}, u32[]{:S(2)}) collective-permute-start(bf16[4,144,384]{2,1,0:T(8,128)(2,1)S(1)} %get-tuple-element.24), channel_id=1, source_target_pairs={{0,4},{4,0},{8,12},{12,8},{16,20},{20,16},{24,28},{28,24},{32,36},... | collective-permute-start | bytes 1327112 | tf_op jit(solution)/shard_map/ppermute | solution.py:387
  38.0 41.8 %collective-permute-start.8 = (bf16[2,4,128,256]{3,2,1,0:T(8,128)(2,1)S(1)}, bf16[2,4,128,256]{3,2,1,0:T(8,128)(2,1)S(1)}, u32[]{:S(2)}, u32[]{:S(2)}) collective-permute-start(bf16[2,4,128,256]{3,2,1,0:T(8,128)(2,1)S(1)} %get-tuple-element.30.kv2), channel_id=1, source_target_pairs={{8,0},{12,4},{16,8},{20,12},{24,16},{28,20},{32,24},{36,28},{40,32... | collective-permute-start | bytes 1572872 | tf_op jit(solution)/shard_map/ppermute | solution.py:414
  48.9 16.7 %all-to-all-start = ((bf16[8,96,128]{2,1,0:T(8,128)(2,1)}), bf16[8,96,128]{2,1,0:T(8,128)(2,1)S(1)}, u32[]{:S(2)}, u32[]{:S(2)}) async-start(bf16[8,96,128]{2,1,0:T(8,128)(2,1)} %get-tuple-element.29.send1), calls=%async_computation | async-start | bytes 393216 | tf_op jit(solution)/shard_map/all_to_all | solution.py:336
  52.3 29.5 %collective-permute-start.7 = (bf16[2,4,128,256]{3,2,1,0:T(8,128)(2,1)S(1)}, bf16[2,4,128,256]{3,2,1,0:T(8,128)(2,1)S(1)}, u32[]{:S(2)}, u32[]{:S(2)}) collective-permute-start(bf16[2,4,128,256]{3,2,1,0:T(8,128)(2,1)S(1)} %get-tuple-element.30.kv2), channel_id=1, source_target_pairs={{0,8},{4,12},{8,16},{12,20},{16,24},{20,28},{24,32},{28,36},{32,40... | collective-permute-start | bytes 1572872 | tf_op jit(solution)/shard_map/ppermute | solution.py:413
  66.3 41.1 %copy-start.5 = (f32[1024]{0:T(1024)S(1)}, f32[1024]{0:T(1024)}, u32[]{:S(2)}) copy-start(f32[1024]{0:T(1024)} %param.9) | copy-start | bytes 12292
  66.3 19.5 %all-to-all-start.1 = ((bf16[8,96,128]{2,1,0:T(8,128)(2,1)}), bf16[8,96,128]{2,1,0:T(8,128)(2,1)S(1)}, u32[]{:S(2)}, u32[]{:S(2)}) async-start(bf16[8,96,128]{2,1,0:T(8,128)(2,1)} %get-tuple-element.32), calls=%async_computation.1 | async-start | bytes 393216 | tf_op jit(solution)/shard_map/all_to_all | solution.py:336
  79.8 8.3 %collective-permute-start.10 = (bf16[4,128,256]{2,1,0:T(8,128)(2,1)S(1)}, bf16[4,128,256]{2,1,0:T(8,128)(2,1)S(1)}, u32[]{:S(2)}, u32[]{:S(2)}) collective-permute-start(bf16[4,128,256]{2,1,0:T(8,128)(2,1)S(1)} %slice_bitcast_fusion), channel_id=1, source_target_pairs={{8,0},{12,4},{16,8},{20,12},{24,16},{28,20},{32,24},{36,28},{40,32... | collective-permute-start | bytes 786440 | tf_op jit(solution)/shard_map/ppermute | solution.py:427
  81.8 11.6 %collective-permute-start.9 = (bf16[4,128,256]{2,1,0:T(8,128)(2,1)S(1)}, bf16[4,128,256]{2,1,0:T(8,128)(2,1)S(1)}, u32[]{:S(2)}, u32[]{:S(2)}) collective-permute-start(bf16[4,128,256]{2,1,0:T(8,128)(2,1)S(1)} %slice_bitcast_fusion.1), channel_id=1, source_target_pairs={{0,8},{4,12},{8,16},{12,20},{16,24},{20,28},{24,32},{28,36},{32,40... | collective-permute-start | bytes 786440 | tf_op jit(solution)/shard_map/ppermute | solution.py:426
  94.6 12.7 %all-to-all-start.2 = ((bf16[8,80,128]{2,1,0:T(8,128)(2,1)}), bf16[8,80,128]{2,1,0:T(8,128)(2,1)S(1)}, u32[]{:S(2)}, u32[]{:S(2)}) async-start(bf16[8,80,128]{2,1,0:T(8,128)(2,1)} %shard_map.70), calls=%async_computation.2 | async-start | bytes 327680 | tf_op jit(solution)/shard_map/all_to_all | solution.py:336

commit v12 on v10

--- a/solution.py
+++ b/solution.py
@@ -57,10 +57,13 @@
     return mm(steps, jnp.where(row <= col, 1.0, 0.0).astype(F32), HIGH)
 
 
-def split_kernel(pat, tokens, steps, upper, lower):
+def lower_kernel(tokens, lower):
+    lower[...] = tokens[0]
+
+
+def upper_kernel(pat, tokens, steps, upper):
     for b in range(4):
-        upper[64 * b : 64 * b + 64] = tokens[0, :64, 512 * b : 512 * b + 512]
-    lower[...] = tokens[0, 64:]
+        upper[64 * b : 64 * b + 64] = tokens[0, :, 512 * b : 512 * b + 512]
     lane = lax.broadcasted_iota(jnp.int32, (8, TOK), 1)
     wanted = jnp.zeros((8, TOK), jnp.int32)
     for i in range(6):
@@ -346,20 +349,24 @@
     down = [(i, (i - 1) % 4) for i in range(4)]
     w3 = w_qkv.transpose(1, 0, 2)
     wft = w_feature.transpose(0, 2, 1)
-    upper, lower = pl.pallas_call(
-        split_kernel,
+    upper = pl.pallas_call(
+        upper_kernel,
         grid=(1,),
-        out_shape=[shape((272, 512), BF), shape((64, D), BF)],
+        out_shape=shape((272, 512), BF),
         in_specs=[
             pl.BlockSpec(memory_space=pltpu.SMEM),
-            pl.BlockSpec((1, TOK, D), lambda i: (0, 0, 0)),
+            pl.BlockSpec((1, 64, D), lambda i: (0, 0, 0)),
             pl.BlockSpec((1, 8, TOK), lambda i: (0, 0, 0)),
         ],
-        out_specs=[
-            pl.BlockSpec((272, 512), lambda i: (0, 0)),
-            pl.BlockSpec((64, D), lambda i: (0, 0)),
-        ],
+        out_specs=pl.BlockSpec((272, 512), lambda i: (0, 0)),
     )(pattern, tokens, log_decay)
+    lower = pl.pallas_call(
+        lower_kernel,
+        grid=(1,),
+        out_shape=shape((64, D), BF),
+        in_specs=[pl.BlockSpec((1, 64, D), lambda i: (0, 1, 0))],
+        out_specs=pl.BlockSpec((64, D), lambda i: (0, 0)),
+    )(tokens)
     ta1 = lax.ppermute(upper, "fsdp", up)
     tb2 = lax.ppermute(lower, "fsdp", down)
     ta2 = lax.ppermute(lower, "fsdp", up)

time: 109 us -> 110 us (level)
  Pallas kernels: 12.3 us -> 13.8 us
    pallas_call x1 -> x2, Pallas kernels: 1.88 us -> 3.36 us  [the longest x1 1.69 us: per_device(): pl.pallas_call(upper_kernel, grid=(1,), out_shape=shape((272, 512), BF),...]
  transfers between devices with their start and end apart: 14 -> 14, of which waited for: 7 -> 7; matrix products, arithmetic and copies ran while one was open for 0% -> 0% of each run, Pallas kernels for 3% -> 4%
where the time goes in v12:
time: 110 us; the launch traced here: 109 us
  starting transfers between devices  56.1 us (51%)
  waiting for transfers between devices  20.7 us (19%)
  blocking collectives  14.3 us (13%)
  Pallas kernels  13.8 us (13%)
  local copies, waits for them, and re-layouts  4.17 us (4%)
    all_to_all x3, starting transfers between devices, exchange(): return lax.all_to_all(a, axis, 0, 0, tiled=True, axis_index_groups=groups)  15.3 us
    all_to_all x1, blocking collectives, exchange(): return lax.all_to_all(a, axis, 0, 0, tiled=True, axis_index_groups=groups)  14.3 us
    ppermute x1, starting transfers between devices, per_device(): kvq_mate = lax.ppermute(kvq_other, 'seq', pairs(lambda q, c: (q, 1 - c)))  12 us
    pallas_call x7, Pallas kernels, call(): pl.pallas_call(kernel, out_shape=outs, in_specs=[pl.BlockSpec(memory_spac...  10.4 us
    all_to_all x3, waiting for transfers between devices, exchange(): return lax.all_to_all(a, axis, 0, 0, tiled=True, axis_index_groups=groups)  9.95 us
    ppermute x1, waiting for transfers between devices, chain(): tp = lax.ppermute(near_p, 'seq', pairs(lambda q, c: (q + 1, c)))  5.11 us
    ppermute x1, starting transfers between devices, per_device(): tb1 = lax.ppermute(upper, 'fsdp', down)  4.4 us
    ppermute x1, starting transfers between devices, per_device(): zp = lax.ppermute(kv2, 'seq', pairs(lambda q, c: (q + 1, c)))  4.03 us
  transfers between devices with their start and end apart: 14, of which 7 were waited for; matrix products, arithmetic and copies ran while one was open for 0% of the time, Pallas kernels for 4%

profile of v12, /device:TPU:1, one launch (start us, length us, event | category | flops | bytes accessed | tf_op | source)
XLA Modules:
  0.0 109.3 jit_solution(16566978533593263745)
XLA Ops:
  0.0 1.7 %shard_map.64.upper = bf16[272,512]{1,0:T(8,128)(2,1)} custom-call(s32[1,2,3]{2,1,0:T(2,128)} %pat.1, bf16[1,128,2048]{2,1,0:T(8,128)(2,1)} %tokens.3, f32[1,8,128]{2,1,0:T(8,128)} %steps.1), custom_call_target="tpu_custom_call" | custom-call | tf_op jit(solution)/shard_map/pallas_call | solution.py:352
  1.7 3.9 %collective-permute-start = (bf16[272,512]{1,0:T(8,128)(2,1)}, bf16[272,512]{1,0:T(8,128)(2,1)S(1)}, u32[]{:S(2)}, u32[]{:S(2)}) collective-permute-start(bf16[272,512]{1,0:T(8,128)(2,1)} %shard_map.64.upper), channel_id=1, source_target_pairs={{0,1},{1,2},{2,3},{3,0},{4,5},{5,6},{6,7},{7,4},{8,9},{9,10},{10,1... | collective-permute-start | bytes 835592 | tf_op jit(solution)/shard_map/ppermute | solution.py:370
  5.6 1.7 %shard_map.66 = bf16[64,2048]{1,0:T(8,128)(2,1)} custom-call(bf16[1,128,2048]{2,1,0:T(8,128)(2,1)} %tokens.3), custom_call_target="tpu_custom_call" | custom-call | tf_op jit(solution)/shard_map/pallas_call | solution.py:363
  7.3 3.2 %collective-permute-start.4 = (bf16[64,2048]{1,0:T(8,128)(2,1)}, bf16[64,2048]{1,0:T(8,128)(2,1)S(1)}, u32[]{:S(2)}, u32[]{:S(2)}) collective-permute-start(bf16[64,2048]{1,0:T(8,128)(2,1)} %shard_map.66), channel_id=1, source_target_pairs={{0,3},{1,0},{2,1},{3,2},{4,7},{5,4},{6,5},{7,6},{8,11},{9,8},{10,9... | collective-permute-start | bytes 786440 | tf_op jit(solution)/shard_map/ppermute | solution.py:371
  10.5 2.1 %collective-permute-start.3 = (bf16[64,2048]{1,0:T(8,128)(2,1)}, bf16[64,2048]{1,0:T(8,128)(2,1)S(1)}, u32[]{:S(2)}, u32[]{:S(2)}) collective-permute-start(bf16[64,2048]{1,0:T(8,128)(2,1)} %shard_map.66), channel_id=1, source_target_pairs={{0,1},{1,2},{2,3},{3,0},{4,5},{5,6},{6,7},{7,4},{8,9},{9,10},{10,1... | collective-permute-start | bytes 786440 | tf_op jit(solution)/shard_map/ppermute | solution.py:372
  12.6 4.4 %collective-permute-start.2 = (bf16[272,512]{1,0:T(8,128)(2,1)}, bf16[272,512]{1,0:T(8,128)(2,1)S(1)}, u32[]{:S(2)}, u32[]{:S(2)}) collective-permute-start(bf16[272,512]{1,0:T(8,128)(2,1)} %shard_map.64.upper), channel_id=1, source_target_pairs={{0,3},{1,0},{2,1},{3,2},{4,7},{5,4},{6,5},{7,6},{8,11},{9,8},{10,9... | collective-permute-start | bytes 835592 | tf_op jit(solution)/shard_map/ppermute | solution.py:373
  17.0 0.1 stack.27.scal
  17.1 0.0 collective-permute-done.4.tb2
  17.1 2.1 %collective-permute-start.5 = (bf16[64,2048]{1,0:T(8,128)(2,1)S(1)}, bf16[64,2048]{1,0:T(8,128)(2,1)S(1)}, u32[]{:S(2)}, u32[]{:S(2)}) collective-permute-start(bf16[64,2048]{1,0:T(8,128)(2,1)S(1)} %collective-permute-done.4.tb2), channel_id=1, source_target_pairs={{0,3},{1,0},{2,1},{3,2},{4,7},{5,4},{6,5},{7,6},{8,11},{9,8},{10,9... | collective-permute-start | bytes 786440 | tf_op jit(solution)/shard_map/ppermute | solution.py:375
  19.3 0.0 collective-permute-done.ta1
  19.3 3.1 %collective-permute-start.1 = (bf16[272,512]{1,0:T(8,128)(2,1)S(1)}, bf16[272,512]{1,0:T(8,128)(2,1)S(1)}, u32[]{:S(2)}, u32[]{:S(2)}) collective-permute-start(bf16[272,512]{1,0:T(8,128)(2,1)S(1)} %collective-permute-done.ta1), channel_id=1, source_target_pairs={{0,1},{1,2},{2,3},{3,0},{4,5},{5,6},{6,7},{7,4},{8,9},{9,10},{10,1... | collective-permute-start | bytes 835592 | tf_op jit(solution)/shard_map/ppermute | solution.py:374
  22.4 0.0 copy-start
  22.4 1.0 copy-done
  23.5 0.0 copy-start.2
  23.5 1.9 %copy-done.2 = bf16[2048,3,256]{2,0,1:T(8,128)(2,1)S(1)} copy-done((bf16[2048,3,256]{2,0,1:T(8,128)(2,1)S(1)}, bf16[2048,3,256]{2,0,1:T(8,128)(2,1)}, u32[]{:S(2)}) %copy-start.2) | copy-done | bytes 3145752
  25.4 0.0 copy-start.1
  25.4 0.0 copy-start.3
  25.4 0.6 shard_map.65.early
  26.0 0.0 copy-start.4
  26.0 0.0 collective-permute-done.3.ta2
  26.0 0.0 collective-permute-done.2.tb1
  26.0 1.5 %collective-permute-done.5.td2 = bf16[64,2048]{1,0:T(8,128)(2,1)S(1)} collective-permute-done((bf16[64,2048]{1,0:T(8,128)(2,1)S(1)}, bf16[64,2048]{1,0:T(8,128)(2,1)S(1)}, u32[]{:S(2)}, u32[]{:S(2)}) %collective-permute-start.5) | collective-permute-done | bytes 262176 | tf_op jit(solution)/shard_map/ppermute | solution.py:375
  27.5 1.8 %collective-permute-done.1.td1 = bf16[272,512]{1,0:T(8,128)(2,1)S(1)} collective-permute-done((bf16[272,512]{1,0:T(8,128)(2,1)S(1)}, bf16[272,512]{1,0:T(8,128)(2,1)S(1)}, u32[]{:S(2)}, u32[]{:S(2)}) %collective-permute-start.1) | collective-permute-done | bytes 278560 | tf_op jit(solution)/shard_map/ppermute | solution.py:374
  29.3 0.0 copy-done.1
  29.3 0.0 copy-done.3
  29.3 1.9 %shard_map.67 = (bf16[4,128,256]{2,1,0:T(8,128)(2,1)S(1)}, bf16[4,144,384]{2,1,0:T(8,128)(2,1)S(1)}, bf16[4,128,128]{2,1,0:T(8,128)(2,1)S(1)}, f32[4,8,128]{2,1,0:T(8,128)S(1)}, f32[4,8,128]{2,1,0:T(8,128)S(1)}) custom-call(s32[6]{0:T(128)S(1)} %stack.27.scal, bf16[3,128,256]{2,1,0:T(8,128)(2,1)S(1)} %shard_map.65.early, bf16[272,512]{1,0:T(8,128)(2,1)S(1)} %copy-done.1, ...), custom_call_target="tpu_custom_call" | custom-call | flops 3000000000 | bytes 9000000 | tf_op jit(solution)/shard_map/pallas_call | solution.py:305
  31.2 12.0 %collective-permute-start.6 = (bf16[4,144,384]{2,1,0:T(8,128)(2,1)S(1)}, bf16[4,144,384]{2,1,0:T(8,128)(2,1)S(1)}, u32[]{:S(2)}, u32[]{:S(2)}) collective-permute-start(bf16[4,144,384]{2,1,0:T(8,128)(2,1)S(1)} %get-tuple-element.20), channel_id=1, source_target_pairs={{0,4},{4,0},{8,12},{12,8},{16,20},{20,16},{24,28},{28,24},{32,36},... | collective-permute-start | bytes 1327112 | tf_op jit(solution)/shard_map/ppermute | solution.py:393
  43.2 1.4 %collective-permute-done.6.kvq_mate = bf16[4,144,384]{2,1,0:T(8,128)(2,1)S(1)} collective-permute-done((bf16[4,144,384]{2,1,0:T(8,128)(2,1)S(1)}, bf16[4,144,384]{2,1,0:T(8,128)(2,1)S(1)}, u32[]{:S(2)}, u32[]{:S(2)}) %collective-permute-start.6) | collective-permute-done | bytes 442400 | tf_op jit(solution)/shard_map/ppermute | solution.py:393
  44.6 0.0 copy-done.4
  44.6 1.7 %shard_map.68 = (bf16[8,96,128]{2,1,0:T(8,128)(2,1)}, f32[4,16,128]{2,1,0:T(8,128)S(1)}, f32[8,128]{1,0:T(8,128)S(1)}, f32[8,128]{1,0:T(8,128)S(1)}) custom-call(s32[6]{0:T(128)S(1)} %stack.27.scal, bf16[4,128,256]{2,1,0:T(8,128)(2,1)S(1)} %get-tuple-element.19.kv_own, bf16[4,144,384]{2,1,0:T(8,128)(2,1)S(1)} %collective-permute-done.6.kvq_mate, ...), custom_call_target="tpu_custom_call" | custom-call | flops 2000000000 | bytes 6000000 | tf_op jit(solution)/shard_map/pallas_call | solution.py:305
  46.3 3.7 %all-to-all-start = ((bf16[8,96,128]{2,1,0:T(8,128)(2,1)}), bf16[8,96,128]{2,1,0:T(8,128)(2,1)S(1)}, u32[]{:S(2)}, u32[]{:S(2)}) async-start(bf16[8,96,128]{2,1,0:T(8,128)(2,1)} %get-tuple-element.27), calls=%async_computation | async-start | bytes 393216 | tf_op jit(solution)/shard_map/all_to_all | solution.py:338
  50.0 0.6 shard_map.69
  50.6 1.3 %collective-permute-start.8 = (bf16[2,4,128,256]{3,2,1,0:T(8,128)(2,1)S(1)}, bf16[2,4,128,256]{3,2,1,0:T(8,128)(2,1)S(1)}, u32[]{:S(2)}, u32[]{:S(2)}) collective-permute-start(bf16[2,4,128,256]{3,2,1,0:T(8,128)(2,1)S(1)} %get-tuple-element.25.kv2), channel_id=1, source_target_pairs={{8,0},{12,4},{16,8},{20,12},{24,16},{28,20},{32,24},{36,28},{40,32... | collective-permute-start | bytes 1572872 | tf_op jit(solution)/shard_map/ppermute | solution.py:404
  51.9 4.0 %collective-permute-start.7 = (bf16[2,4,128,256]{3,2,1,0:T(8,128)(2,1)S(1)}, bf16[2,4,128,256]{3,2,1,0:T(8,128)(2,1)S(1)}, u32[]{:S(2)}, u32[]{:S(2)}) collective-permute-start(bf16[2,4,128,256]{3,2,1,0:T(8,128)(2,1)S(1)} %get-tuple-element.25.kv2), channel_id=1, source_target_pairs={{0,8},{4,12},{8,16},{12,20},{16,24},{20,28},{24,32},{28,36},{32,40... | collective-permute-start | bytes 1572872 | tf_op jit(solution)/shard_map/ppermute | solution.py:403
  56.0 3.5 %all-to-all-done.got = bf16[8,96,128]{2,1,0:T(8,128)(2,1)S(1)} async-done(((bf16[8,96,128]{2,1,0:T(8,128)(2,1)}), bf16[8,96,128]{2,1,0:T(8,128)(2,1)S(1)}, u32[]{:S(2)}, u32[]{:S(2)}) %all-to-all-start) | async-done | bytes 196640 | tf_op jit(solution)/shard_map/all_to_all | solution.py:338
  59.5 0.7 shard_map.70
  60.2 0.0 copy-start.5
  60.2 7.0 %all-to-all-start.1 = ((bf16[8,96,128]{2,1,0:T(8,128)(2,1)}), bf16[8,96,128]{2,1,0:T(8,128)(2,1)S(1)}, u32[]{:S(2)}, u32[]{:S(2)}) async-start(bf16[8,96,128]{2,1,0:T(8,128)(2,1)} %get-tuple-element.28), calls=%async_computation.1 | async-start | bytes 393216 | tf_op jit(solution)/shard_map/all_to_all | solution.py:338
  67.1 1.0 collective-permute-done.8.zm
  68.1 1.3 %collective-permute-start.10 = (bf16[4,128,256]{2,1,0:T(8,128)(2,1)S(1)}, bf16[4,128,256]{2,1,0:T(8,128)(2,1)S(1)}, u32[]{:S(2)}, u32[]{:S(2)}) collective-permute-start(bf16[4,128,256]{2,1,0:T(8,128)(2,1)S(1)} %slice_bitcast_fusion), channel_id=1, source_target_pairs={{8,0},{12,4},{16,8},{20,12},{24,16},{28,20},{32,24},{36,28},{40,32... | collective-permute-start | bytes 786440 | tf_op jit(solution)/shard_map/ppermute | solution.py:437
  69.4 6.5 %all-to-all-done.1.got = bf16[8,96,128]{2,1,0:T(8,128)(2,1)S(1)} async-done(((bf16[8,96,128]{2,1,0:T(8,128)(2,1)}), bf16[8,96,128]{2,1,0:T(8,128)(2,1)S(1)}, u32[]{:S(2)}, u32[]{:S(2)}) %all-to-all-start.1) | async-done | bytes 196640 | tf_op jit(solution)/shard_map/all_to_all | solution.py:338
  75.9 1.2 %shard_map.71 = bf16[8,80,128]{2,1,0:T(8,128)(2,1)} custom-call(s32[6]{0:T(128)S(1)} %stack.27.scal, bf16[8,96,128]{2,1,0:T(8,128)(2,1)S(1)} %all-to-all-done.1.got, f32[8,8,128]{2,1,0:T(8,128)S(1)} %get-tuple-element.29.inner, f32[8,8,128]{2,1,0:T(8,128)S(1)} %get-tuple-element.30.outer), custom_call_target="tpu_custom_call" | custom-call | flops 1000000000 | bytes 3000000 | tf_op jit(solution)/shard_map/pallas_call | solution.py:305
  77.1 4.6 %all-to-all-start.2 = ((bf16[8,80,128]{2,1,0:T(8,128)(2,1)}), bf16[8,80,128]{2,1,0:T(8,128)(2,1)S(1)}, u32[]{:S(2)}, u32[]{:S(2)}) async-start(bf16[8,80,128]{2,1,0:T(8,128)(2,1)} %shard_map.71), calls=%async_computation.2 | async-start | bytes 327680 | tf_op jit(solution)/shard_map/all_to_all | solution.py:338
  81.7 0.0 collective-permute-done.7.zp
  81.8 3.4 %collective-permute-start.9 = (bf16[4,128,256]{2,1,0:T(8,128)(2,1)S(1)}, bf16[4,128,256]{2,1,0:T(8,128)(2,1)S(1)}, u32[]{:S(2)}, u32[]{:S(2)}) collective-permute-start(bf16[4,128,256]{2,1,0:T(8,128)(2,1)S(1)} %slice_bitcast_fusion.1), channel_id=1, source_target_pairs={{0,8},{4,12},{8,16},{12,20},{16,24},{20,28},{24,32},{28,36},{32,40... | collective-permute-start | bytes 786440 | tf_op jit(solution)/shard_map/ppermute | solution.py:436
  85.2 0.1 min.12.pat
  85.2 0.0 collective-permute-done.10.tm
  85.2 5.1 %collective-permute-done.9.tp = bf16[4,128,256]{2,1,0:T(8,128)(2,1)S(1)} collective-permute-done((bf16[4,128,256]{2,1,0:T(8,128)(2,1)S(1)}, bf16[4,128,256]{2,1,0:T(8,128)(2,1)S(1)}, u32[]{:S(2)}, u32[]{:S(2)}) %collective-permute-start.9) | collective-permute-done | bytes 262176 | tf_op jit(solution)/shard_map/ppermute | solution.py:436
  90.4 0.0 all-to-all-done.2.got
  90.4 0.0 copy-done.5
  90.4 3.6 %shard_map.72 = bf16[8,128,128]{2,1,0:T(8,128)(2,1)S(1)} custom-call(s32[6]{0:T(128)S(1)} %stack.27.scal, s32[48]{0:T(128)S(1)} %min.12.pat, bf16[2,4,128,256]{3,2,1,0:T(8,128)(2,1)S(1)} %get-tuple-element.25.kv2, bf16[2,4,128,128]{3,2,1,0:T(8,128)(2,1)S(1)} %get-tuple-element.26.q2, bf16[2,4,128,256]{3,2,1,0:T(8,128)(2,1)S(1)} %collective-permute-done.7.zp, ...), custom_call_target="tpu_custom_call" | custom-call | flops 8000000000 | bytes 24000000 | tf_op jit(solution)/shard_map/pallas_call | solution.py:305
  94.0 14.3 %all_to_all.20 = bf16[8,128,128]{2,1,0:T(8,128)(2,1)S(1)} all-to-all(bf16[8,128,128]{2,1,0:T(8,128)(2,1)S(1)} %shard_map.72), channel_id=1, replica_groups={{0,4,1,5,2,6,3,7},{8,12,9,13,10,14,11,15},{16,20,17,21,18,22,19,23},{24..., dimensions={0} | all-to-all | bytes 524288 | tf_op jit(solution)/shard_map/all_to_all | solution.py:338
  108.2 0.2 copy.7
  108.4 0.9 copy.8
  (3 shorter events, 0.0 us)
Async XLA Ops:
  1.7 17.6 %collective-permute-start = (bf16[272,512]{1,0:T(8,128)(2,1)}, bf16[272,512]{1,0:T(8,128)(2,1)S(1)}, u32[]{:S(2)}, u32[]{:S(2)}) collective-permute-start(bf16[272,512]{1,0:T(8,128)(2,1)} %shard_map.64.upper), channel_id=1, source_target_pairs={{0,1},{1,2},{2,3},{3,0},{4,5},{5,6},{6,7},{7,4},{8,9},{9,10},{10,1... | collective-permute-start | bytes 835592 | tf_op jit(solution)/shard_map/ppermute | solution.py:370
  7.3 9.8 %collective-permute-start.4 = (bf16[64,2048]{1,0:T(8,128)(2,1)}, bf16[64,2048]{1,0:T(8,128)(2,1)S(1)}, u32[]{:S(2)}, u32[]{:S(2)}) collective-permute-start(bf16[64,2048]{1,0:T(8,128)(2,1)} %shard_map.66), channel_id=1, source_target_pairs={{0,3},{1,0},{2,1},{3,2},{4,7},{5,4},{6,5},{7,6},{8,11},{9,8},{10,9... | collective-permute-start | bytes 786440 | tf_op jit(solution)/shard_map/ppermute | solution.py:371
  10.5 15.5 %collective-permute-start.3 = (bf16[64,2048]{1,0:T(8,128)(2,1)}, bf16[64,2048]{1,0:T(8,128)(2,1)S(1)}, u32[]{:S(2)}, u32[]{:S(2)}) collective-permute-start(bf16[64,2048]{1,0:T(8,128)(2,1)} %shard_map.66), channel_id=1, source_target_pairs={{0,1},{1,2},{2,3},{3,0},{4,5},{5,6},{6,7},{7,4},{8,9},{9,10},{10,1... | collective-permute-start | bytes 786440 | tf_op jit(solution)/shard_map/ppermute | solution.py:372
  12.6 13.4 %collective-permute-start.2 = (bf16[272,512]{1,0:T(8,128)(2,1)}, bf16[272,512]{1,0:T(8,128)(2,1)S(1)}, u32[]{:S(2)}, u32[]{:S(2)}) collective-permute-start(bf16[272,512]{1,0:T(8,128)(2,1)} %shard_map.64.upper), channel_id=1, source_target_pairs={{0,3},{1,0},{2,1},{3,2},{4,7},{5,4},{6,5},{7,6},{8,11},{9,8},{10,9... | collective-permute-start | bytes 835592 | tf_op jit(solution)/shard_map/ppermute | solution.py:373
  17.1 10.3 %collective-permute-start.5 = (bf16[64,2048]{1,0:T(8,128)(2,1)S(1)}, bf16[64,2048]{1,0:T(8,128)(2,1)S(1)}, u32[]{:S(2)}, u32[]{:S(2)}) collective-permute-start(bf16[64,2048]{1,0:T(8,128)(2,1)S(1)} %collective-permute-done.4.tb2), channel_id=1, source_target_pairs={{0,3},{1,0},{2,1},{3,2},{4,7},{5,4},{6,5},{7,6},{8,11},{9,8},{10,9... | collective-permute-start | bytes 786440 | tf_op jit(solution)/shard_map/ppermute | solution.py:375
  19.3 10.0 %collective-permute-start.1 = (bf16[272,512]{1,0:T(8,128)(2,1)S(1)}, bf16[272,512]{1,0:T(8,128)(2,1)S(1)}, u32[]{:S(2)}, u32[]{:S(2)}) collective-permute-start(bf16[272,512]{1,0:T(8,128)(2,1)S(1)} %collective-permute-done.ta1), channel_id=1, source_target_pairs={{0,1},{1,2},{2,3},{3,0},{4,5},{5,6},{6,7},{7,4},{8,9},{9,10},{10,1... | collective-permute-start | bytes 835592 | tf_op jit(solution)/shard_map/ppermute | solution.py:374
  22.4 1.0 copy-start
  23.5 1.9 %copy-start.2 = (bf16[2048,3,256]{2,0,1:T(8,128)(2,1)S(1)}, bf16[2048,3,256]{2,0,1:T(8,128)(2,1)}, u32[]{:S(2)}) copy-start(bf16[2048,3,256]{2,0,1:T(8,128)(2,1)} %param.7) | copy-start | bytes 9437188
  25.4 3.9 %copy-start.1 = (bf16[272,512]{1,0:T(8,128)(2,1)S(1)}, bf16[272,512]{1,0:T(8,128)(2,1)}, u32[]{:S(2)}) copy-start(bf16[272,512]{1,0:T(8,128)(2,1)} %shard_map.64.upper) | copy-start | bytes 835588
  25.4 3.9 %copy-start.3 = (bf16[2048,3,256]{2,0,1:T(8,128)(2,1)S(1)}, bf16[2048,3,256]{2,0,1:T(8,128)(2,1)}, u32[]{:S(2)}) copy-start(bf16[2048,3,256]{2,0,1:T(8,128)(2,1)} %param.7) | copy-start | bytes 9437188
  26.0 18.7 %copy-start.4 = (bf16[8,128,16]{1,2,0:T(8,128)(2,1)S(1)}, bf16[8,128,16]{1,2,0:T(8,128)(2,1)}, u32[]{:S(2)}) copy-start(bf16[8,128,16]{1,2,0:T(8,128)(2,1)} %param.8) | copy-start | bytes 98308
  31.2 13.4 %collective-permute-start.6 = (bf16[4,144,384]{2,1,0:T(8,128)(2,1)S(1)}, bf16[4,144,384]{2,1,0:T(8,128)(2,1)S(1)}, u32[]{:S(2)}, u32[]{:S(2)}) collective-permute-start(bf16[4,144,384]{2,1,0:T(8,128)(2,1)S(1)} %get-tuple-element.20), channel_id=1, source_target_pairs={{0,4},{4,0},{8,12},{12,8},{16,20},{20,16},{24,28},{28,24},{32,36},... | collective-permute-start | bytes 1327112 | tf_op jit(solution)/shard_map/ppermute | solution.py:393
  46.3 13.1 %all-to-all-start = ((bf16[8,96,128]{2,1,0:T(8,128)(2,1)}), bf16[8,96,128]{2,1,0:T(8,128)(2,1)S(1)}, u32[]{:S(2)}, u32[]{:S(2)}) async-start(bf16[8,96,128]{2,1,0:T(8,128)(2,1)} %get-tuple-element.27), calls=%async_computation | async-start | bytes 393216 | tf_op jit(solution)/shard_map/all_to_all | solution.py:338
  50.6 17.5 %collective-permute-start.8 = (bf16[2,4,128,256]{3,2,1,0:T(8,128)(2,1)S(1)}, bf16[2,4,128,256]{3,2,1,0:T(8,128)(2,1)S(1)}, u32[]{:S(2)}, u32[]{:S(2)}) collective-permute-start(bf16[2,4,128,256]{3,2,1,0:T(8,128)(2,1)S(1)} %get-tuple-element.25.kv2), channel_id=1, source_target_pairs={{8,0},{12,4},{16,8},{20,12},{24,16},{28,20},{32,24},{36,28},{40,32... | collective-permute-start | bytes 1572872 | tf_op jit(solution)/shard_map/ppermute | solution.py:404
  51.9 29.8 %collective-permute-start.7 = (bf16[2,4,128,256]{3,2,1,0:T(8,128)(2,1)S(1)}, bf16[2,4,128,256]{3,2,1,0:T(8,128)(2,1)S(1)}, u32[]{:S(2)}, u32[]{:S(2)}) collective-permute-start(bf16[2,4,128,256]{3,2,1,0:T(8,128)(2,1)S(1)} %get-tuple-element.25.kv2), channel_id=1, source_target_pairs={{0,8},{4,12},{8,16},{12,20},{16,24},{20,28},{24,32},{28,36},{32,40... | collective-permute-start | bytes 1572872 | tf_op jit(solution)/shard_map/ppermute | solution.py:403
  60.2 30.2 %copy-start.5 = (f32[1024]{0:T(1024)S(1)}, f32[1024]{0:T(1024)}, u32[]{:S(2)}) copy-start(f32[1024]{0:T(1024)} %param.9) | copy-start | bytes 12292
  60.2 15.7 %all-to-all-start.1 = ((bf16[8,96,128]{2,1,0:T(8,128)(2,1)}), bf16[8,96,128]{2,1,0:T(8,128)(2,1)S(1)}, u32[]{:S(2)}, u32[]{:S(2)}) async-start(bf16[8,96,128]{2,1,0:T(8,128)(2,1)} %get-tuple-element.28), calls=%async_computation.1 | async-start | bytes 393216 | tf_op jit(solution)/shard_map/all_to_all | solution.py:338
  68.1 17.1 %collective-permute-start.10 = (bf16[4,128,256]{2,1,0:T(8,128)(2,1)S(1)}, bf16[4,128,256]{2,1,0:T(8,128)(2,1)S(1)}, u32[]{:S(2)}, u32[]{:S(2)}) collective-permute-start(bf16[4,128,256]{2,1,0:T(8,128)(2,1)S(1)} %slice_bitcast_fusion), channel_id=1, source_target_pairs={{8,0},{12,4},{16,8},{20,12},{24,16},{28,20},{32,24},{36,28},{40,32... | collective-permute-start | bytes 786440 | tf_op jit(solution)/shard_map/ppermute | solution.py:437
  77.1 13.2 %all-to-all-start.2 = ((bf16[8,80,128]{2,1,0:T(8,128)(2,1)}), bf16[8,80,128]{2,1,0:T(8,128)(2,1)S(1)}, u32[]{:S(2)}, u32[]{:S(2)}) async-start(bf16[8,80,128]{2,1,0:T(8,128)(2,1)} %shard_map.71), calls=%async_computation.2 | async-start | bytes 327680 | tf_op jit(solution)/shard_map/all_to_all | solution.py:338
  81.8 8.6 %collective-permute-start.9 = (bf16[4,128,256]{2,1,0:T(8,128)(2,1)S(1)}, bf16[4,128,256]{2,1,0:T(8,128)(2,1)S(1)}, u32[]{:S(2)}, u32[]{:S(2)}) collective-permute-start(bf16[4,128,256]{2,1,0:T(8,128)(2,1)S(1)} %slice_bitcast_fusion.1), channel_id=1, source_target_pairs={{0,8},{4,12},{8,16},{12,20},{16,24},{20,28},{24,32},{28,36},{32,40... | collective-permute-start | bytes 786440 | tf_op jit(solution)/shard_map/ppermute | solution.py:436
